TPU v7x, 512 devices: a whole 4x8x8 slice. The times are simulated.
512 devices in a mesh: dp: 32 (over y_lo, x, core), seq: 16 (over z, y_hi).
Axes of the slice: x: 4, y: 8 (y_hi: 2, y_lo: 4; y = y_hi * 4 + y_lo), z: 8, core: 2. Of those that a mesh axis runs over, the one named last changes fastest.
Arguments:
- tokens: bfloat16 [32, 2048, 1024], P('dp', 'seq'), may hold values from -8 to 8
- qkv_weight: bfloat16 [16, 192, 1024], P('seq', 'dp'), may hold values from -0.18 to 0.18
- key_tiles: int32 [32, 16, 4], P('dp'), may hold values from 0 to 15, as said below
- key_counts: int32 [32, 16], P('dp'), may hold values from 1 to 4, as said below
- cotangent: bfloat16 [32, 2048, 1024], P('dp', 'seq'), may hold values from -6 to 6
Outputs:
- attended: bfloat16 [32, 2048, 1024], P('dp', 'seq')
- grad_input: bfloat16 [32, 2048, 1024], P('dp', 'seq')
- grad_weight: float32 [16, 192, 1024], P('seq', 'dp')
Inputs may be any that keep to these rules, and one draw needn't show every extreme that they name: `key_tiles`: row a of a scene lists tile a first, then 4 - 1 other tiles; the 4 entries of a row are distinct, and those beyond the count are ignored. `key_counts`: some query tile of every scene has a count of 4.
All inputs are finite; a program needn't handle non-finite values.
Results may differ from a plain program's by a relative error of at most 0.025.
Values may be sent and summed in bfloat16 or wider, within the bound.
No kernel may reach another device: no remote copies, remote signals or barrier semaphores. Data moves between devices by JAX's collectives and lax.ppermute only.
A program may use at most 64 MiB of HBM per device.

v0:
```python
import jax
import jax.numpy as jnp
from jax import lax
from jax.sharding import PartitionSpec as P

HEAD_DIM = 64
TILE = 128
TOP = 4


def shards(tokens, qkv_weight, key_tiles, key_counts, cotangent):
    heads_dev = qkv_weight.shape[0]
    tok_dev = tokens.shape[1]
    seq_len = tok_dev * lax.axis_size("seq")
    tiles_n = seq_len // TILE
    scale = HEAD_DIM ** (-0.5)
    grad_scale = (lax.axis_size("dp") * seq_len) ** (-0.5)
    w_head = lax.all_gather(qkv_weight, "dp", axis=1, tiled=True)
    w_all = lax.all_gather(w_head, "seq", axis=0, tiled=True)
    scene = lax.all_gather(tokens, "seq", axis=1, tiled=True)[0]
    qkv = jnp.einsum("ld,hfd->lhf", scene, w_head, preferred_element_type=jnp.float32).astype(
        jnp.bfloat16
    )
    shape_tiles = (tiles_n, TILE, heads_dev, HEAD_DIM)
    query = qkv[:, :, :HEAD_DIM].reshape(shape_tiles)
    keys = qkv[:, :, HEAD_DIM : 2 * HEAD_DIM].reshape(shape_tiles)
    values = qkv[:, :, 2 * HEAD_DIM :].reshape(shape_tiles)
    tile_list = key_tiles[0]
    key_sel = jnp.take(keys, tile_list, axis=0)
    value_sel = jnp.take(values, tile_list, axis=0)
    live = jnp.arange(TOP, dtype=jnp.int32)[None, :] < key_counts[0][:, None]
    live = live[:, None, None, :, None]
    scores = (
        jnp.einsum("aqhd,atkhd->ahqtk", query, key_sel, preferred_element_type=jnp.float32) * scale
    )
    scores = jnp.where(live, scores, -1e30)
    top_score = jnp.max(scores, axis=(3, 4), keepdims=True)
    expo = jnp.exp(scores - top_score)
    probs = expo / jnp.sum(expo, axis=(3, 4), keepdims=True)
    probs_b = probs.astype(jnp.bfloat16)
    output = jnp.einsum(
        "ahqtk,atkhd->aqhd", probs_b, value_sel, preferred_element_type=jnp.float32
    ).astype(jnp.bfloat16)
    output = output.reshape(seq_len, heads_dev * HEAD_DIM)
    attended = lax.all_to_all(output, "seq", split_axis=0, concat_axis=1, tiled=True)[None]
    grad_heads = lax.all_to_all(
        cotangent[0], "seq", split_axis=1, concat_axis=0, tiled=True
    ).reshape(shape_tiles)
    dprobs = jnp.einsum(
        "aqhd,atkhd->ahqtk", grad_heads, value_sel, preferred_element_type=jnp.float32
    )
    delta = jnp.sum(probs * dprobs, axis=(3, 4), keepdims=True)
    dscores = (probs * (dprobs - delta) * scale).astype(jnp.bfloat16)
    dquery = jnp.einsum(
        "ahqtk,atkhd->aqhd", dscores, key_sel, preferred_element_type=jnp.float32
    ).astype(jnp.bfloat16)
    dkey_part = jnp.einsum("ahqtk,aqhd->atkhd", dscores, query, preferred_element_type=jnp.float32)
    dvalue_part = jnp.einsum(
        "ahqtk,aqhd->atkhd", probs_b, grad_heads, preferred_element_type=jnp.float32
    )
    selector = (
        tile_list.reshape(-1)[:, None] == jnp.arange(tiles_n, dtype=jnp.int32)[None, :]
    ).astype(jnp.float32)
    width = TILE * heads_dev * HEAD_DIM
    dkey = jnp.einsum(
        "ba,bx->ax",
        selector,
        dkey_part.reshape(tiles_n * TOP, width),
        precision=lax.Precision.HIGHEST,
    )
    dvalue = jnp.einsum(
        "ba,bx->ax",
        selector,
        dvalue_part.reshape(tiles_n * TOP, width),
        precision=lax.Precision.HIGHEST,
    )
    dkey = dkey.astype(jnp.bfloat16).reshape(shape_tiles)
    dvalue = dvalue.astype(jnp.bfloat16).reshape(shape_tiles)
    dqkv = jnp.concatenate([dquery, dkey, dvalue], axis=-1).reshape(
        seq_len, heads_dev, 3 * HEAD_DIM
    )
    token_grads = lax.all_to_all(dqkv, "seq", split_axis=0, concat_axis=1, tiled=True)
    grad_input = jnp.einsum(
        "lhf,hfd->ld", token_grads, w_all, preferred_element_type=jnp.float32
    ).astype(jnp.bfloat16)[None]
    weight_part = jnp.einsum("lhf,ld->hfd", dqkv, scene, preferred_element_type=jnp.float32)
    grad_weight = (
        lax.psum_scatter(
            weight_part.astype(jnp.bfloat16), "dp", scatter_dimension=1, tiled=True
        ).astype(jnp.float32)
        * grad_scale
    )
    return (attended, grad_input, grad_weight)


def solution(mesh):
    in_specs = (
        P("dp", "seq", None),
        P("seq", "dp", None),
        P("dp", None, None),
        P("dp", None),
        P("dp", "seq", None),
    )
    out_specs = (P("dp", "seq", None), P("dp", "seq", None), P("seq", "dp", None))
    return jax.shard_map(shards, mesh=mesh, in_specs=in_specs, out_specs=out_specs, check_vma=False)
```

profile of v0, /device:TPU:135, one launch (start us, length us, event | category | flops | bytes accessed | tf_op | source)
XLA Modules:
  0.0 388.5 jit_solution(16610460573768889426)
XLA Ops:
  7.9 0.7 copy.73
  8.7 37.2 %all_gather.10 = bf16[1,192,1024]{2,0,1:T(2,128)(2,1)S(1)} all-gather(bf16[1,6,1024]{2,0,1:T(2,128)(2,1)S(1)} %copy.73), channel_id=1, replica_groups=mesh['dp'=32,'seq'=16] {'dp'}, dimensions={1}, use_global_device_ids=true | all-gather | bytes 405504 | tf_op jit(solution)/shard_map/all_gather | solution.py:18
  45.9 0.9 copy.113
  46.8 1.8 copy.81
  48.6 13.8 %all-to-all-start.1 = ((bf16[128,16,64]{0,2,1:T(8,128)(2,1)}), bf16[128,16,64]{0,2,1:T(8,128)(2,1)S(1)}, u32[]{:S(2)}, u32[]{:S(2)}) async-start(bf16[128,16,64]{0,2,1:T(8,128)(2,1)} %bitcast.18), calls=%async_computation.1 | async-start | bytes 524288 | tf_op jit(solution)/shard_map/all_to_all | solution.py:46
  62.5 0.8 copy.84
  65.0 0.7 iota_compare_fusion.3
  65.7 70.4 %all-gather.3.cloned.1.call-done = bf16[1,2048,1024]{2,1,0:T(8,128)(2,1)} async-done(((bf16[1,128,1024]{2,1,0:T(8,128)(2,1)}), bf16[1,2048,1024]{2,1,0:T(8,128)(2,1)}) %all-gather.3.cloned.1.call-update) | async-done | bytes 4194320 | tf_op jit(solution)/shard_map/all_gather | solution.py:20
  136.1 3.8 fusion.17
  140.2 0.8 gather_fusion.1
  140.9 3.5 fusion.11
  144.5 0.7 gather_fusion
  145.2 3.1 fusion.13
  148.4 4.0 %fusion.3 = (f32[16,128]{1,0:T(8,128)S(1)}, f32[16,4,128,128]{3,2,1,0:T(8,128)S(1)}) fusion(f32[16,128]{1,0:T(8,128)S(1)} %fusion.13, f32[16,128]{1,0:T(8,128)S(1)} %get-tuple-element.19, f32[16,128,4,128]{1,3,2,0:T(8,128)} %get-tuple-element.20, pred[16,4]{1,0:T(8,128)(4,1)S(1)} %iota_compare_fusion.3, bf16[128,16,64]{0,2,1:T(8,128)(2,1)S(1)} %all-to-all-done.1, ...), kind=kOutput, calls=%fused_computation.8 | convolution fusion | flops 141031424 | bytes 9724032 | tf_op jit(solution)/shard_map/aqhd,atkhd->ahqtk/dot_general | solution.py:49
  152.4 1.7 fusion.6
  154.1 1.3 copy-done.1
  155.5 0.8 convolution_bitcast_fusion.1
  156.3 2.7 copy.87
  159.0 3.6 reshape.154
  162.6 0.9 convolution_convert_fusion.1
  164.3 2.4 fusion.37
  166.7 0.8 copy.136
  167.5 5.3 %convolution_bitcast_fusion = f32[16,4,128,1,64]{4,2,1,0,3:T(8,128)} fusion(bf16[128,16,64]{0,2,1:T(8,128)(2,1)S(1)} %copy-done.5, f32[16,128,4,128]{1,3,2,0:T(8,128)} %get-tuple-element.20, f32[16,128]{1,0:T(8,128)S(1)} %fusion.13, f32[16,128]{1,0:T(8,128)S(1)} %get-tuple-element.19, pred[16,4]{1,0:T(8,128)(4,1)S(1)} %iota_compare_fusion.3), kind=kOutput, calls=%fused_computation.23 | convolution fusion | flops 139460608 | bytes 6570048 | tf_op jit(solution)/shard_map/ahqtk,aqhd->atkhd/dot_general | solution.py:58
  172.7 3.7 reshape.155
  176.4 4.1 %fusion.38 = bf16[16,128,64]{1,2,0:T(8,128)(2,1)} fusion(bf16[16,4,128,1,64]{2,4,1,0,3:T(8,128)(2,1)S(1)} %bitcast.170, pred[16,4]{1,0:T(8,128)(4,1)S(1)} %copy.72, f32[16,128,4,128]{1,3,2,0:T(8,128)} %get-tuple-element.20, f32[16,128]{1,0:T(8,128)S(1)} %fusion.13, f32[16,128]{1,0:T(8,128)S(1)} %get-tuple-element.19, pred[16,4]{1,0:T(8,128)(4,1)S(1)} %iota_compare_fusion.3), kind=kOutput, calls=%fused_computation.35 | convolution fusion | flops 140115968 | bytes 5521536 | tf_op jit(solution)/shard_map/ahqtk,atkhd->aqhd/dot_general | solution.py:41
  180.5 5.8 %all-to-all-start = ((bf16[16,128,64]{1,2,0:T(8,128)(2,1)}), bf16[16,128,64]{1,2,0:T(8,128)(2,1)S(1)}, u32[]{:S(2)}, u32[]{:S(2)}) async-start(bf16[16,128,64]{1,2,0:T(8,128)(2,1)} %fusion.38), calls=%async_computation | async-start | bytes 524288 | tf_op jit(solution)/shard_map/all_to_all | solution.py:45
  186.3 0.9 convolution_convert_fusion
  188.6 1.2 reduce.6
  190.3 2.1 reshape.202
  192.4 5.0 %all-to-all-done = bf16[16,128,64]{1,2,0:T(8,128)(2,1)S(1)} async-done(((bf16[16,128,64]{1,2,0:T(8,128)(2,1)}), bf16[16,128,64]{1,2,0:T(8,128)(2,1)S(1)}, u32[]{:S(2)}, u32[]{:S(2)}) %all-to-all-start) | async-done | bytes 262176 | tf_op jit(solution)/shard_map/all_to_all | solution.py:45
  197.4 6.5 %all-to-all-start.2 = ((bf16[16,2,12288]{2,1,0:T(2,128)(2,1)}), bf16[16,2,12288]{2,1,0:T(2,128)(2,1)S(1)}, u32[]{:S(2)}, u32[]{:S(2)}) async-start(bf16[16,2,12288]{2,1,0:T(2,128)(2,1)} %reshape.202), calls=%async_computation.2 | async-start | bytes 1572864 | tf_op jit(solution)/shard_map/all_to_all | solution.py:82
  203.9 3.3 fusion.31
  207.1 127.1 %fusion = bf16[8,1024]{1,0:T(8,128)(2,1)S(1)} fusion(bf16[1,192,1024]{2,1,0:T(8,128)(2,1)S(1)} %fusion.31), kind=kCustom, calls=%all-reduce-scatter | all-reduce-scatter fusion | flops 262145 | bytes 411648
  334.2 6.3 %collective-permute-start = (bf16[8,1024]{1,0:T(8,128)(2,1)S(1)}, bf16[8,1024]{1,0:T(8,128)(2,1)S(1)}, u32[]{:S(2)}, u32[]{:S(2)}) collective-permute-start(bf16[8,1024]{1,0:T(8,128)(2,1)S(1)} %fusion), channel_id=1, source_target_pairs={{0,16},{16,32},{32,48},{48,64},{64,80},{80,96},{96,112},{112,128},... | collective-permute-start | bytes 49160
  340.6 1.9 collective-permute-start.1
  342.5 9.6 %collective-permute-start.7 = (bf16[6,1024]{1,0:T(8,128)(2,1)S(1)}, bf16[6,1024]{1,0:T(8,128)(2,1)S(1)}, u32[]{:S(2)}, u32[]{:S(2)}) collective-permute-start(bf16[6,1024]{1,0:T(8,128)(2,1)S(1)} %slice.19), channel_id=1, source_target_pairs={{0,128},{16,144},{32,160},{48,176},{64,192},{80,208},{96,224},{112... | collective-permute-start | bytes 36872
  352.1 1.9 collective-permute-start.2
  354.0 4.9 %collective-permute-start.3 = (bf16[8,1024]{1,0:T(8,128)(2,1)S(1)}, bf16[8,1024]{1,0:T(8,128)(2,1)S(1)}, u32[]{:S(2)}, u32[]{:S(2)}) collective-permute-start(bf16[8,1024]{1,0:T(8,128)(2,1)S(1)} %fusion), channel_id=1, source_target_pairs={{0,64},{16,80},{32,96},{48,112},{64,128},{80,144},{96,160},{112,17... | collective-permute-start | bytes 49160
  358.9 1.9 collective-permute-start.4
  360.9 1.9 collective-permute-start.5
  362.8 1.9 collective-permute-start.6
  364.7 1.3 dynamic-slice.4
  366.7 2.4 collective-permute-done.6
  369.1 0.9 concatenate.14
  370.7 0.8 copy.96
  371.5 1.5 reshape.203
  373.0 1.2 copy.93
  374.4 7.3 %fusion.34 = bf16[1,128,1024]{2,1,0:T(8,128)(2,1)} fusion(bf16[16,192,1024]{2,1,0:T(8,128)(2,1)} %all-gather.5.cloned.1.call-done, bf16[16,128,1,192]{1,0,3,2:T(8,128)(2,1)S(1)} %bitcast.179), kind=kOutput, calls=%fused_computation.33 | convolution fusion | flops 805437440 | bytes 7340032 | tf_op jit(solution)/shard_map/lhf,hfd->ld/dot_general | solution.py:83
  (46 shorter events, 6.2 us)
Async XLA Ops:
  7.2 129.0 %all-gather.3.cloned.1.call-start = ((), (), s32[]{:S(2)}) async-start(), calls=%async_computation.3 | async-start | bytes 4456448 | tf_op jit(solution)/shard_map/all_gather | solution.py:20
  7.9 366.5 %all-gather.5.cloned.1.call-start = ((), (), s32[]{:S(2)}) async-start(), calls=%async_computation.4 | async-start | bytes 6684672 | tf_op jit(solution)/shard_map/all_gather | solution.py:19
  48.6 99.7 %all-to-all-start.1 = ((bf16[128,16,64]{0,2,1:T(8,128)(2,1)}), bf16[128,16,64]{0,2,1:T(8,128)(2,1)S(1)}, u32[]{:S(2)}, u32[]{:S(2)}) async-start(bf16[128,16,64]{0,2,1:T(8,128)(2,1)} %bitcast.18), calls=%async_computation.1 | async-start | bytes 524288 | tf_op jit(solution)/shard_map/all_to_all | solution.py:46
  140.9 4.3 %copy-start.2 = (bf16[64,128,64]{1,2,0:T(8,128)(2,1)}, bf16[64,128,64]{1,2,0:T(8,128)(2,1)S(1)}, u32[]{:S(2)}) copy-start(bf16[64,128,64]{1,2,0:T(8,128)(2,1)S(1)} %gather_fusion.1) | copy-start | bytes 3145732
  148.4 4.0 %copy-start.4 = (bf16[128,16,64]{0,2,1:T(8,128)(2,1)}, bf16[128,16,64]{0,2,1:T(8,128)(2,1)S(1)}, u32[]{:S(2)}) copy-start(bf16[128,16,64]{0,2,1:T(8,128)(2,1)S(1)} %all-to-all-done.1) | copy-start | bytes 786436
  148.4 4.0 %copy-start = (f32[16,128,4,128]{1,3,2,0:T(8,128)S(1)}, f32[16,128,4,128]{1,3,2,0:T(8,128)}, u32[]{:S(2)}) copy-start(f32[16,128,4,128]{1,3,2,0:T(8,128)} %get-tuple-element.20) | copy-start | bytes 12582916
  154.1 1.3 copy-start.1
  163.5 3.9 %copy-start.5 = (bf16[128,16,64]{0,2,1:T(8,128)(2,1)S(1)}, bf16[128,16,64]{0,2,1:T(8,128)(2,1)}, u32[]{:S(2)}) copy-start(bf16[128,16,64]{0,2,1:T(8,128)(2,1)} %copy-done.4) | copy-start | bytes 786436
  180.5 7.4 %copy-start.3 = (bf16[1,16,8,8,128]{4,3,1,2,0:T(8,128)(2,1)S(1)}, bf16[1,16,8,8,128]{4,3,1,2,0:T(8,128)(2,1)}, u32[]{:S(2)}) copy-start(bf16[1,16,8,8,128]{4,3,1,2,0:T(8,128)(2,1)} %copy.136) | copy-start | bytes 786436
  180.5 16.8 %all-to-all-start = ((bf16[16,128,64]{1,2,0:T(8,128)(2,1)}), bf16[16,128,64]{1,2,0:T(8,128)(2,1)S(1)}, u32[]{:S(2)}, u32[]{:S(2)}) async-start(bf16[16,128,64]{1,2,0:T(8,128)(2,1)} %fusion.38), calls=%async_computation | async-start | bytes 524288 | tf_op jit(solution)/shard_map/all_to_all | solution.py:45
  197.4 174.1 %all-to-all-start.2 = ((bf16[16,2,12288]{2,1,0:T(2,128)(2,1)}), bf16[16,2,12288]{2,1,0:T(2,128)(2,1)S(1)}, u32[]{:S(2)}, u32[]{:S(2)}) async-start(bf16[16,2,12288]{2,1,0:T(2,128)(2,1)} %reshape.202), calls=%async_computation.2 | async-start | bytes 1572864 | tf_op jit(solution)/shard_map/all_to_all | solution.py:82
  334.2 26.6 %collective-permute-start = (bf16[8,1024]{1,0:T(8,128)(2,1)S(1)}, bf16[8,1024]{1,0:T(8,128)(2,1)S(1)}, u32[]{:S(2)}, u32[]{:S(2)}) collective-permute-start(bf16[8,1024]{1,0:T(8,128)(2,1)S(1)} %fusion), channel_id=1, source_target_pairs={{0,16},{16,32},{32,48},{48,64},{64,80},{80,96},{96,112},{112,128},... | collective-permute-start | bytes 49160
  340.6 22.2 %collective-permute-start.1 = (bf16[8,1024]{1,0:T(8,128)(2,1)S(1)}, bf16[8,1024]{1,0:T(8,128)(2,1)S(1)}, u32[]{:S(2)}, u32[]{:S(2)}) collective-permute-start(bf16[8,1024]{1,0:T(8,128)(2,1)S(1)} %fusion), channel_id=1, source_target_pairs={{0,32},{16,48},{32,64},{48,80},{64,96},{80,112},{96,128},{112,144}... | collective-permute-start | bytes 49160
  342.5 16.4 %collective-permute-start.7 = (bf16[6,1024]{1,0:T(8,128)(2,1)S(1)}, bf16[6,1024]{1,0:T(8,128)(2,1)S(1)}, u32[]{:S(2)}, u32[]{:S(2)}) collective-permute-start(bf16[6,1024]{1,0:T(8,128)(2,1)S(1)} %slice.19), channel_id=1, source_target_pairs={{0,128},{16,144},{32,160},{48,176},{64,192},{80,208},{96,224},{112... | collective-permute-start | bytes 36872
  352.1 14.6 %collective-permute-start.2 = (bf16[8,1024]{1,0:T(8,128)(2,1)S(1)}, bf16[8,1024]{1,0:T(8,128)(2,1)S(1)}, u32[]{:S(2)}, u32[]{:S(2)}) collective-permute-start(bf16[8,1024]{1,0:T(8,128)(2,1)S(1)} %fusion), channel_id=1, source_target_pairs={{0,48},{16,64},{32,80},{48,96},{64,112},{80,128},{96,144},{112,160... | collective-permute-start | bytes 49160
  354.0 12.6 %collective-permute-start.3 = (bf16[8,1024]{1,0:T(8,128)(2,1)S(1)}, bf16[8,1024]{1,0:T(8,128)(2,1)S(1)}, u32[]{:S(2)}, u32[]{:S(2)}) collective-permute-start(bf16[8,1024]{1,0:T(8,128)(2,1)S(1)} %fusion), channel_id=1, source_target_pairs={{0,64},{16,80},{32,96},{48,112},{64,128},{80,144},{96,160},{112,17... | collective-permute-start | bytes 49160
  358.9 7.8 %collective-permute-start.4 = (bf16[8,1024]{1,0:T(8,128)(2,1)S(1)}, bf16[8,1024]{1,0:T(8,128)(2,1)S(1)}, u32[]{:S(2)}, u32[]{:S(2)}) collective-permute-start(bf16[8,1024]{1,0:T(8,128)(2,1)S(1)} %fusion), channel_id=1, source_target_pairs={{0,80},{16,96},{32,112},{48,128},{64,144},{80,160},{96,176},{112,1... | collective-permute-start | bytes 49160
  360.9 5.8 %collective-permute-start.5 = (bf16[8,1024]{1,0:T(8,128)(2,1)S(1)}, bf16[8,1024]{1,0:T(8,128)(2,1)S(1)}, u32[]{:S(2)}, u32[]{:S(2)}) collective-permute-start(bf16[8,1024]{1,0:T(8,128)(2,1)S(1)} %fusion), channel_id=1, source_target_pairs={{0,96},{16,112},{32,128},{48,144},{64,160},{80,176},{96,192},{112,... | collective-permute-start | bytes 49160
  362.8 6.3 %collective-permute-start.6 = (bf16[8,1024]{1,0:T(8,128)(2,1)S(1)}, bf16[8,1024]{1,0:T(8,128)(2,1)S(1)}, u32[]{:S(2)}, u32[]{:S(2)}) collective-permute-start(bf16[8,1024]{1,0:T(8,128)(2,1)S(1)} %fusion), channel_id=1, source_target_pairs={{0,112},{16,128},{32,144},{48,160},{64,176},{80,192},{96,208},{112... | collective-permute-start | bytes 49160
Sparse Core Ops, SparseCore 0:
  11.2 124.9 all-gather.2
  139.3 185.7 all-gather.4
where the time goes:
time: 390 us; the launch traced here: 389 us
  blocking collectives  164 us (42%)
  waiting for transfers between devices  78.5 us (20%)
  starting transfers between devices  56.5 us (14%)
  matrix products  36.2 us (9%)
  local copies, waits for them, and re-layouts  29.5 us (8%)
  between operations  15.1 us (4%)
  other arithmetic  8.26 us (2%)
    unnamed x1, blocking collectives  127 us
    all_gather x1, waiting for transfers between devices, shards(): scene = lax.all_gather(tokens, 'seq', axis=1, tiled=True)[0]  70.4 us
    all_gather x1, blocking collectives, shards(): w_head = lax.all_gather(qkv_weight, 'dp', axis=1, tiled=True)  37.2 us
    unnamed x8, starting transfers between devices  30.4 us
    all_to_all x1, starting transfers between devices, shards(): lax.all_to_all(cotangent[0], 'seq', split_axis=1, concat_axis=0, tiled=True)  13.8 us
    unnamed x27, local copies, waits for them, and re-layouts  13.5 us
  transfers between devices with their start and end apart: 13, of which 3 were waited for; matrix products, arithmetic and copies ran while one was open for 50% of the time, Pallas kernels for 0%

commit v1 on v0

v1 whole, which is shorter than its diff:
```python
import functools

import jax
import jax.numpy as jnp
from jax import lax
from jax.experimental import pallas as pl
from jax.experimental.pallas import tpu as pltpu
from jax.sharding import PartitionSpec as P

HEAD_DIM = 64
TILE = 128
TOP = 4
BF = jnp.bfloat16
F32 = jnp.float32
VM = pl.BlockSpec(memory_space=pltpu.VMEM)
SM = pl.BlockSpec(memory_space=pltpu.SMEM)
PARAMS = pltpu.CompilerParams(vmem_limit_bytes=48 * 2**20)

YL, XN, CORES, ZN, YH = 4, 4, 2, 8, 2
DP = YL * XN * CORES
SEQ = ZN * YH


def dot(a, b, ca, cb):
    return lax.dot_general(a, b, (((ca,), (cb,)), ((), ())), preferred_element_type=F32)


def flip_y(x):
    return lax.ppermute(x, "seq", [(s, s ^ 1) for s in range(SEQ)])


def shift_z(x, k):
    return lax.ppermute(x, "seq", [(s, (s + YH * k) % SEQ) for s in range(SEQ)])


def swap_core(x):
    return lax.ppermute(x, "dp", [(d, d ^ 1) for d in range(DP)])


def shift_y(x, k):
    pairs = []
    for d in range(DP):
        for s in range(SEQ):
            y = (s % YH) * YL + d // (XN * CORES)
            to = (y + k) % (YL * YH)
            d_to = (to % YL) * XN * CORES + d % (XN * CORES)
            pairs.append((d * SEQ + s, d_to * SEQ + (s // YH) * YH + to // YL))
    return lax.ppermute(x, ("dp", "seq"), pairs)


def spread(x, axis, n, groups=None):
    copies = jnp.broadcast_to(x[None], (n, *x.shape))
    return lax.all_to_all(copies, axis, 0, 0, tiled=True, axis_index_groups=groups)


def attend(nblk, order_ref, list_ref, count_ref, *refs):
    blocks = refs[:nblk]
    w_ref, cot_ref, att_ref, dqkv_ref, kv_rows, kv_cols, q_cols, acc = refs[nblk:]
    scale = HEAD_DIM ** (-0.5)
    tiles = kv_rows.shape[0]
    w = w_ref[...]
    w = jnp.concatenate([w[HEAD_DIM:], w[:HEAD_DIM]], axis=0)
    slot = 0
    for blk in blocks:
        qkv = dot(blk[...], w, 1, 1).astype(BF)
        for r in range(blk.shape[0] // TILE):
            tile = order_ref[slot]
            slot += 1
            piece = qkv[r * TILE : (r + 1) * TILE]
            kv = piece[:, :TILE]
            kv_rows[tile] = kv
            kv_cols[tile] = kv.T
            q_cols[tile] = piece[:, TILE:].T
    acc[...] = jnp.zeros_like(acc)
    zero = jnp.zeros((HEAD_DIM, TILE), BF)

    def step(a, _):
        left = jnp.concatenate([q_cols[a], zero], axis=0)
        right = jnp.concatenate([zero, cot_ref[a]], axis=0)
        both = jnp.concatenate([left, right], axis=1)
        keys = [list_ref[a, t] for t in range(TOP)]
        count = count_ref[a]
        rows = jnp.concatenate([kv_rows[j] for j in keys], axis=0)
        prod = dot(rows, both, 1, 0)
        raw = prod[:, :TILE]
        dprobs = prod[:, TILE:]
        parts = [raw[t * TILE : (t + 1) * TILE] for t in range(TOP)]
        raw = jnp.concatenate(
            parts[:1] + [jnp.where(t < count, parts[t], -1e30) for t in range(1, TOP)], axis=0
        )
        top = jnp.max(raw, axis=0, keepdims=True)
        expo = jnp.exp((raw - top) * scale)
        probs = expo * (1.0 / jnp.sum(expo, axis=0, keepdims=True))
        delta = jnp.sum(probs * dprobs, axis=0, keepdims=True)
        dscores = (probs * ((dprobs - delta) * scale)).astype(BF)
        pair = jnp.concatenate([dscores, probs.astype(BF)], axis=1)
        cols = jnp.concatenate([kv_cols[j] for j in keys], axis=1)
        out = dot(cols, pair, 1, 0)
        dqkv_ref[a, :HEAD_DIM, :] = out[:HEAD_DIM, :TILE].astype(BF)
        att_ref[a] = out[HEAD_DIM:, TILE:].astype(BF)
        both_t = jnp.concatenate([left.T, right.T], axis=0)
        back = dot(pair, both_t, 1, 0)
        for t in range(TOP):
            acc[keys[t]] += back[t * TILE : (t + 1) * TILE]
        return 0

    lax.fori_loop(0, tiles, step, 0, unroll=2)
    for a in range(tiles):
        dqkv_ref[a, HEAD_DIM:, :] = acc[a].astype(BF).T


def attention(order, tile_list, counts, blocks, w_head, cot_t):
    tiles = tile_list.shape[0]
    return pl.pallas_call(
        functools.partial(attend, len(blocks)),
        out_shape=(
            jax.ShapeDtypeStruct((tiles, HEAD_DIM, TILE), BF),
            jax.ShapeDtypeStruct((tiles, 3 * HEAD_DIM, TILE), BF),
        ),
        in_specs=[SM, SM, SM] + [VM] * (len(blocks) + 2),
        out_specs=(VM, VM),
        scratch_shapes=[
            pltpu.VMEM((tiles, TILE, 2 * HEAD_DIM), BF),
            pltpu.VMEM((tiles, 2 * HEAD_DIM, TILE), BF),
            pltpu.VMEM((tiles, HEAD_DIM, TILE), BF),
            pltpu.VMEM((tiles, TILE, 2 * HEAD_DIM), F32),
        ],
        compiler_params=PARAMS,
        name="attend",
    )(order, tile_list, counts, *blocks, w_head, cot_t)


def weight_sum(nblk, order_ref, dqkv_ref, *refs):
    blocks, out_ref = refs[:nblk], refs[nblk]
    total, slot = None, 0
    for blk in blocks:
        n = blk.shape[0] // TILE
        left = jnp.concatenate([dqkv_ref[order_ref[slot + r]] for r in range(n)], axis=1)
        slot += n
        part = dot(left, blk[...], 1, 0)
        total = part if total is None else total + part
    owners, rows = out_ref.shape[:2]
    for i in range(owners):
        out_ref[i] = total[i * rows : (i + 1) * rows].astype(BF)


def weight_grad(order, dqkv_t, blocks, owners):
    rows, depth = dqkv_t.shape[1] // owners, blocks[0].shape[1]
    return pl.pallas_call(
        functools.partial(weight_sum, len(blocks)),
        out_shape=jax.ShapeDtypeStruct((owners, rows, depth), BF),
        in_specs=[SM, VM] + [VM] * len(blocks),
        out_specs=VM,
        compiler_params=PARAMS,
        name="weight_sum",
    )(order, dqkv_t, *blocks)


def input_sum(split, place_ref, dqkv_ref, *refs):
    weights, out_ref = refs[:-1], refs[-1]
    heads = dqkv_ref.shape[0]
    chunk = 3 * HEAD_DIM // XN
    cols = jnp.concatenate(
        [dqkv_ref[h, c * chunk : (c + 1) * chunk, :] for c in range(XN) for h in range(heads)],
        axis=0,
    )
    left = cols.T
    k = 0
    for p in range(YL):
        total, at = None, 0
        for _ in range(split[p]):
            mine, other = weights[2 * k][...], weights[2 * k + 1][...]
            k += 1
            depth = mine.shape[0] * mine.shape[1] * mine.shape[2]
            both = jnp.concatenate([mine.reshape(depth, TILE), other.reshape(depth, TILE)], axis=1)
            part = dot(left[:, at : at + depth], both, 1, 0)
            at += depth
            total = part if total is None else total + part
        for c in range(CORES):
            where = pl.multiple_of(place_ref[2 * p + c] * TILE, TILE)
            out_ref[:, pl.ds(where, TILE)] = total[:, c * TILE : (c + 1) * TILE].astype(BF)


def input_grad(place, dqkv_t, split, weights):
    return pl.pallas_call(
        functools.partial(input_sum, split),
        out_shape=jax.ShapeDtypeStruct((TILE, YL * CORES * TILE), BF),
        in_specs=[SM, VM] + [VM] * len(weights),
        out_specs=VM,
        compiler_params=PARAMS,
        name="input_sum",
    )(place, dqkv_t, *weights)


def shards(tokens, qkv_weight, key_tiles, key_counts, cotangent):
    heads = SEQ
    depth = tokens.shape[2]
    tiles = key_tiles.shape[1]
    dp, seq = lax.axis_index("dp"), lax.axis_index("seq")
    y_lo, x, core = dp // (XN * CORES), dp // CORES % XN, dp % CORES
    z, y_hi = seq // YH, seq % YH
    grad_scale = (DP * tiles * TILE) ** (-0.5)

    w_head = spread(qkv_weight[0], "dp", DP).reshape(3 * HEAD_DIM, depth)
    chunk = 3 * HEAD_DIM // XN
    w_block = lax.dynamic_slice(
        w_head, (x * chunk, (y_lo * CORES + core) * TILE), (chunk, TILE)
    )

    own = tokens[0]
    pair = jnp.concatenate([own, flip_y(own)], axis=0)
    right, left = [pair], [pair]
    for _ in range(ZN // 2 - 1):
        right.append(shift_z(right[-1], 1))
        left.append(shift_z(left[-1], -1))
    far = [shift_z(right[-1][:TILE], 1), shift_z(left[-1][TILE:], -1)]
    blocks = right + left[1:] + far
    zs = [(0, 0), (0, 1)]
    zs += [(-k, j) for k in range(1, ZN // 2) for j in range(2)]
    zs += [(k, j) for k in range(1, ZN // 2) for j in range(2)]
    zs += [(ZN // 2, 0), (ZN // 2, 1)]
    order = jnp.stack([(z + k) % ZN * YH + (y_hi + j) % YH for k, j in zs]).astype(jnp.int32)

    cot_t = cotangent[0].T.reshape(heads, HEAD_DIM, TILE)
    cot_t = lax.all_to_all(cot_t, "seq", 0, 0, tiled=True)

    w_seq = spread(w_block, "seq", SEQ)
    x_groups = [
        [(y * XN + i) * CORES + c for i in range(XN)] for y in range(YL) for c in range(CORES)
    ]
    w_0 = spread(w_seq, "dp", XN, x_groups)
    w_m, w_p = shift_y(w_0, 1), shift_y(w_0, -1)
    half = XN // 2
    w_f = [shift_y(w_m[:half], 1), shift_y(w_p[half:], -1)]
    pieces = [w_0, w_m, w_p, *w_f]
    weights = []
    for piece in pieces:
        weights += [piece, swap_core(piece)]
    place = jnp.stack(
        [
            (y_lo + k) % YL * CORES + (core + c) % CORES
            for k in (0, YL - 1, 1, 2)
            for c in range(CORES)
        ]
    ).astype(jnp.int32)

    att_t, dqkv_t = attention(order, key_tiles[0], key_counts[0], blocks, w_head, cot_t)
    token_grads = lax.all_to_all(dqkv_t, "seq", 0, 0, tiled=True)
    att_t = lax.all_to_all(att_t, "seq", 0, 0, tiled=True)
    attended = att_t.reshape(heads * HEAD_DIM, TILE).T[None]

    parts = weight_grad(order, dqkv_t, blocks, DP)
    parts = lax.all_to_all(parts, "dp", 0, 0, tiled=True)
    grad_weight = jnp.sum(parts.astype(F32), axis=0)[None] * grad_scale

    grad_input = input_grad(place, token_grads, (1, 1, 1, 2), weights)[None]
    return (attended, grad_input, grad_weight)


def solution(mesh):
    in_specs = (
        P("dp", "seq", None),
        P("seq", "dp", None),
        P("dp", None, None),
        P("dp", None),
        P("dp", "seq", None),
    )
    out_specs = (P("dp", "seq", None), P("dp", "seq", None), P("seq", "dp", None))
    return jax.shard_map(shards, mesh=mesh, in_specs=in_specs, out_specs=out_specs, check_vma=False)
```

time: 390 us -> 221 us (0.57)
  the two profiles are of different devices: /device:TPU:135 before, /device:TPU:1 now
where the time goes in v1:
time: 221 us; the launch traced here: 219 us
  starting transfers between devices  132 us (60%)
  waiting for transfers between devices  52.4 us (24%)
  Pallas kernels  18.4 us (8%)
  local copies, waits for them, and re-layouts  14.3 us (6%)
    ppermute x8, starting transfers between devices, shift_z(): return lax.ppermute(x, 'seq', [(s, (s + YH * k) % SEQ) for s in range(SEQ)])  30.9 us
    ppermute x4, starting transfers between devices, shift_y(): return lax.ppermute(x, ('dp', 'seq'), pairs)  30 us
    all_to_all x3, starting transfers between devices, spread(): lax.all_to_all(copies, axis, 0, 0, tiled=True, axis_index_groups=groups)  14.9 us
    all_to_all x1, starting transfers between devices, shards(): cot_t = lax.all_to_all(cot_t, 'seq', 0, 0, tiled=True)  12.4 us
    ppermute x5, starting transfers between devices, swap_core(): return lax.ppermute(x, 'dp', [(d, d ^ 1) for d in range(DP)])  12.2 us
    all_to_all x1, starting transfers between devices, shards(): att_t = lax.all_to_all(att_t, 'seq', 0, 0, tiled=True)  11.6 us
    pallas_call x1, Pallas kernels, attention(): pl.pallas_call(functools.partial(attend, len(blocks)), out_shape=(jax.Sha...  11.2 us
    all_to_all x1, waiting for transfers between devices, shards(): parts = lax.all_to_all(parts, 'dp', 0, 0, tiled=True)  11.1 us
  transfers between devices with their start and end apart: 25, of which 11 were waited for; matrix products, arithmetic and copies ran while one was open for 5% of the time, Pallas kernels for 7%

profile of v1, /device:TPU:1, one launch (start us, length us, event | category | flops | bytes accessed | tf_op | source)
XLA Modules:
  0.0 219.3 jit_solution(9775396798942251181)
XLA Ops:
  0.6 8.3 %collective-permute-start = (bf16[128,1024]{1,0:T(8,128)(2,1)}, bf16[128,1024]{1,0:T(8,128)(2,1)S(1)}, u32[]{:S(2)}, u32[]{:S(2)}) collective-permute-start(bf16[128,1024]{1,0:T(8,128)(2,1)} %bitcast.40), channel_id=1, source_target_pairs={{0,1},{1,0},{2,3},{3,2},{4,5},{5,4},{6,7},{7,6},{8,9},{9,8},{10,11... | collective-permute-start | bytes 786440 | tf_op jit(solution)/shard_map/ppermute | solution.py:29
  8.9 1.6 broadcast_in_dim.13
  10.5 5.9 %all-to-all-start = ((bf16[32,6,1024]{2,1,0:T(8,128)(2,1)}), bf16[32,6,1024]{2,1,0:T(8,128)(2,1)S(1)}, u32[]{:S(2)}, u32[]{:S(2)}) async-start(bf16[32,6,1024]{2,1,0:T(8,128)(2,1)} %broadcast_in_dim.13), calls=%async_computation | async-start | bytes 1048576 | tf_op jit(solution)/shard_map/all_to_all | solution.py:53
  16.4 1.3 collective-permute-done
  17.8 9.6 %collective-permute-start.4 = (bf16[256,1024]{1,0:T(8,128)(2,1)S(1)}, bf16[256,1024]{1,0:T(8,128)(2,1)S(1)}, u32[]{:S(2)}, u32[]{:S(2)}) collective-permute-start(bf16[256,1024]{1,0:T(8,128)(2,1)S(1)} %pad_maximum_fusion.refs_0_), channel_id=1, source_target_pairs={{0,14},{1,15},{2,0},{3,1},{4,2},{5,3},{6,4},{7,5},{8,6},{9,7},{10,... | collective-permute-start | bytes 1572872 | tf_op jit(solution)/shard_map/ppermute | solution.py:33
  27.4 1.9 collective-permute-start.1
  29.4 0.8 copy.11
  30.2 4.4 %all-to-all-done = bf16[32,6,1024]{2,1,0:T(8,128)(2,1)S(1)} async-done(((bf16[32,6,1024]{2,1,0:T(8,128)(2,1)}), bf16[32,6,1024]{2,1,0:T(8,128)(2,1)S(1)}, u32[]{:S(2)}, u32[]{:S(2)}) %all-to-all-start) | async-done | bytes 393248 | tf_op jit(solution)/shard_map/all_to_all | solution.py:53
  34.7 12.4 %all-to-all-start.1 = ((bf16[16,64,128]{2,1,0:T(8,128)(2,1)}), bf16[16,64,128]{2,1,0:T(8,128)(2,1)S(1)}, u32[]{:S(2)}, u32[]{:S(2)}) async-start(bf16[16,64,128]{2,1,0:T(8,128)(2,1)} %bitcast.22), calls=%async_computation.1 | async-start | bytes 524288 | tf_op jit(solution)/shard_map/all_to_all | solution.py:225
  47.1 4.5 %collective-permute-start.5 = (bf16[256,1024]{1,0:T(8,128)(2,1)S(1)}, bf16[256,1024]{1,0:T(8,128)(2,1)}, u32[]{:S(2)}, u32[]{:S(2)}) collective-permute-start(bf16[256,1024]{1,0:T(8,128)(2,1)S(1)} %collective-permute-done.4.refs_4_), channel_id=1, source_target_pairs={{0,14},{1,15},{2,0},{3,1},{4,2},{5,3},{6,4},{7,5},{8,6},{9,7},{10,... | collective-permute-start | bytes 1572872 | tf_op jit(solution)/shard_map/ppermute | solution.py:33
  51.6 1.9 collective-permute-start.2
  53.7 6.6 %all-to-all-done.1.refs_10_ = bf16[16,64,128]{2,1,0:T(8,128)(2,1)S(1)} async-done(((bf16[16,64,128]{2,1,0:T(8,128)(2,1)}), bf16[16,64,128]{2,1,0:T(8,128)(2,1)S(1)}, u32[]{:S(2)}, u32[]{:S(2)}) %all-to-all-start.1) | async-done | bytes 262176 | tf_op jit(solution)/shard_map/all_to_all | solution.py:225
  61.7 5.5 %all-to-all-start.4 = ((bf16[16,48,128]{2,1,0:T(8,128)(2,1)}), bf16[16,48,128]{2,1,0:T(8,128)(2,1)S(1)}, u32[]{:S(2)}, u32[]{:S(2)}) async-start(bf16[16,48,128]{2,1,0:T(8,128)(2,1)} %broadcast_in_dim.29), calls=%async_computation.4 | async-start | bytes 393216 | tf_op jit(solution)/shard_map/all_to_all | solution.py:53
  67.2 4.5 %collective-permute-start.6 = (bf16[256,1024]{1,0:T(8,128)(2,1)}, bf16[256,1024]{1,0:T(8,128)(2,1)S(1)}, u32[]{:S(2)}, u32[]{:S(2)}) collective-permute-start(bf16[256,1024]{1,0:T(8,128)(2,1)} %collective-permute-done.5.refs_5_), channel_id=1, source_target_pairs={{0,14},{1,15},{2,0},{3,1},{4,2},{5,3},{6,4},{7,5},{8,6},{9,7},{10,... | collective-permute-start | bytes 1572872 | tf_op jit(solution)/shard_map/ppermute | solution.py:33
  71.7 1.9 collective-permute-start.3
  73.7 5.9 %all-to-all-done.4 = bf16[16,48,128]{2,1,0:T(8,128)(2,1)S(1)} async-done(((bf16[16,48,128]{2,1,0:T(8,128)(2,1)}), bf16[16,48,128]{2,1,0:T(8,128)(2,1)S(1)}, u32[]{:S(2)}, u32[]{:S(2)}) %all-to-all-start.4) | async-done | bytes 196640 | tf_op jit(solution)/shard_map/all_to_all | solution.py:53
  79.6 1.0 broadcast_in_dim.30
  80.6 3.5 %all-to-all-start.5 = ((bf16[4,16,48,128]{3,2,1,0:T(8,128)(2,1)}), bf16[4,16,48,128]{3,2,1,0:T(8,128)(2,1)S(1)}, u32[]{:S(2)}, u32[]{:S(2)}) async-start(bf16[4,16,48,128]{3,2,1,0:T(8,128)(2,1)} %broadcast_in_dim.30), calls=%async_computation.5 | async-start | bytes 1572864 | tf_op jit(solution)/shard_map/all_to_all | solution.py:53
  84.1 1.1 collective-permute-done.6.refs_6_
  85.9 4.6 %collective-permute-start.8 = (bf16[128,1024]{1,0:T(8,128)(2,1)}, bf16[128,1024]{1,0:T(8,128)(2,1)}, u32[]{:S(2)}, u32[]{:S(2)}) collective-permute-start(bf16[128,1024]{1,0:T(8,128)(2,1)} %slice.17), channel_id=1, source_target_pairs={{0,14},{1,15},{2,0},{3,1},{4,2},{5,3},{6,4},{7,5},{8,6},{9,7},{10,... | collective-permute-start | bytes 786440 | tf_op jit(solution)/shard_map/ppermute | solution.py:33
  90.5 0.7 slice.16
  91.2 1.9 collective-permute-start.7
  94.7 5.8 %collective-permute-done.7.refs_7_ = bf16[128,1024]{1,0:T(8,128)(2,1)} collective-permute-done((bf16[128,1024]{1,0:T(8,128)(2,1)}, bf16[128,1024]{1,0:T(8,128)(2,1)}, u32[]{:S(2)}, u32[]{:S(2)}) %collective-permute-start.7) | collective-permute-done | bytes 262176 | tf_op jit(solution)/shard_map/ppermute | solution.py:33
  100.5 1.0 copy-done.1
  101.5 0.9 copy-done.3
  102.4 11.2 %attend.1 = (bf16[16,64,128]{2,1,0:T(8,128)(2,1)S(1)}, bf16[16,192,128]{2,1,0:T(8,128)(2,1)}) custom-call(s32[16]{0:T(128)S(1)} %stack.94.order_ref, s32[16,4]{1,0:T(8,128)S(1)} %copy.12.list_ref, s32[16]{0:T(128)S(1)} %bitcast.37, bf16[256,1024]{1,0:T(8,128)(2,1)S(1)} %pad_maximum_fusion.refs_0_, bf16[256,1024]{1,0:T(8,128)(2,1)S(1)} %collective-permute-done.1.refs_1_, ...), custom_call_target="tpu_custom_call" | custom-call | tf_op jit(solution)/shard_map/attend/pallas_call | solution.py:114
  114.3 11.6 %all-to-all-start.2 = ((bf16[16,64,128]{2,1,0:T(8,128)(2,1)}), bf16[16,64,128]{2,1,0:T(8,128)(2,1)}, u32[]{:S(2)}, u32[]{:S(2)}) async-start(bf16[16,64,128]{2,1,0:T(8,128)(2,1)} %copy-done.4), calls=%async_computation.2 | async-start | bytes 524288 | tf_op jit(solution)/shard_map/all_to_all | solution.py:249
  125.9 3.5 %weight_sum.1 = bf16[32,6,1024]{2,1,0:T(8,128)(2,1)} custom-call(s32[16]{0:T(128)S(1)} %stack.94.order_ref, bf16[16,192,128]{2,1,0:T(8,128)(2,1)} %get-tuple-element.6.dqkv_ref, bf16[256,1024]{1,0:T(8,128)(2,1)S(1)} %pad_maximum_fusion.refs_0_, bf16[256,1024]{1,0:T(8,128)(2,1)S(1)} %collective-permute-done.1.refs_1_, ...), custom_call_target="tpu_custom_call" | custom-call | tf_op jit(solution)/shard_map/weight_sum/pallas_call | solution.py:149
  129.4 9.1 %all-to-all-done.2 = bf16[16,64,128]{2,1,0:T(8,128)(2,1)} async-done(((bf16[16,64,128]{2,1,0:T(8,128)(2,1)}), bf16[16,64,128]{2,1,0:T(8,128)(2,1)}, u32[]{:S(2)}, u32[]{:S(2)}) %all-to-all-start.2) | async-done | bytes 262176 | tf_op jit(solution)/shard_map/all_to_all | solution.py:249
  138.5 7.9 %all-to-all-start.6 = ((bf16[32,6,1024]{2,1,0:T(8,128)(2,1)}), bf16[32,6,1024]{2,1,0:T(8,128)(2,1)S(1)}, u32[]{:S(2)}, u32[]{:S(2)}) async-start(bf16[32,6,1024]{2,1,0:T(8,128)(2,1)} %weight_sum.1), calls=%async_computation.6 | async-start | bytes 1048576 | tf_op jit(solution)/shard_map/all_to_all | solution.py:253
  146.4 3.4 %collective-permute-start.12 = (bf16[4,16,48,128]{3,2,1,0:T(8,128)(2,1)S(1)}, bf16[4,16,48,128]{3,2,1,0:T(8,128)(2,1)}, u32[]{:S(2)}, u32[]{:S(2)}) collective-permute-start(bf16[4,16,48,128]{3,2,1,0:T(8,128)(2,1)S(1)} %all-to-all-done.5.refs_0_), channel_id=1, source_target_pairs={{0,385},{1,384},{2,387},{3,386},{4,389},{5,388},{6,391},{7,390},{8... | collective-permute-start | bytes 2359304 | tf_op jit(solution)/shard_map/ppermute | solution.py:48
  149.8 1.9 collective-permute-start.10
  151.7 11.1 %all-to-all-done.6 = bf16[32,6,1024]{2,1,0:T(8,128)(2,1)S(1)} async-done(((bf16[32,6,1024]{2,1,0:T(8,128)(2,1)}), bf16[32,6,1024]{2,1,0:T(8,128)(2,1)S(1)}, u32[]{:S(2)}, u32[]{:S(2)}) %all-to-all-start.6) | async-done | bytes 393248 | tf_op jit(solution)/shard_map/all_to_all | solution.py:253
  162.9 0.8 copy-done.6
  163.6 3.6 %all-to-all-start.3 = ((bf16[16,192,128]{2,1,0:T(8,128)(2,1)}), bf16[16,192,128]{2,1,0:T(8,128)(2,1)S(1)}, u32[]{:S(2)}, u32[]{:S(2)}) async-start(bf16[16,192,128]{2,1,0:T(8,128)(2,1)} %get-tuple-element.6.dqkv_ref), calls=%async_computation.3 | async-start | bytes 1572864 | tf_op jit(solution)/shard_map/all_to_all | solution.py:248
  167.3 1.9 collective-permute-start.9
  169.2 4.9 %collective-permute-done.12.refs_4_ = bf16[4,16,48,128]{3,2,1,0:T(8,128)(2,1)} collective-permute-done((bf16[4,16,48,128]{3,2,1,0:T(8,128)(2,1)S(1)}, bf16[4,16,48,128]{3,2,1,0:T(8,128)(2,1)}, u32[]{:S(2)}, u32[]{:S(2)}) %collective-permute-start.12) | collective-permute-done | bytes 786464 | tf_op jit(solution)/shard_map/ppermute | solution.py:48
  174.1 1.0 slice.19
  175.1 1.9 collective-permute-start.16
  177.1 22.8 %collective-permute-start.14 = (bf16[2,16,48,128]{3,2,1,0:T(8,128)(2,1)S(1)}, bf16[2,16,48,128]{3,2,1,0:T(8,128)(2,1)}, u32[]{:S(2)}, u32[]{:S(2)}) collective-permute-start(bf16[2,16,48,128]{3,2,1,0:T(8,128)(2,1)S(1)} %slice.18), channel_id=1, source_target_pairs={{0,128},{1,129},{2,130},{3,131},{4,132},{5,133},{6,134},{7,135},{8... | collective-permute-start | bytes 1179656 | tf_op jit(solution)/shard_map/ppermute | solution.py:48
  199.8 3.1 %collective-permute-start.13 = (bf16[4,16,48,128]{3,2,1,0:T(8,128)(2,1)}, bf16[4,16,48,128]{3,2,1,0:T(8,128)(2,1)}, u32[]{:S(2)}, u32[]{:S(2)}) collective-permute-start(bf16[4,16,48,128]{3,2,1,0:T(8,128)(2,1)} %collective-permute-done.12.refs_4_), channel_id=1, source_target_pairs={{0,16},{16,0},{32,48},{48,32},{64,80},{80,64},{96,112},{112,96},{1... | collective-permute-start | bytes 2359304 | tf_op jit(solution)/shard_map/ppermute | solution.py:37
  202.9 1.9 collective-permute-start.11
  204.8 1.6 collective-permute-done.16.refs_8_
  206.5 3.4 %collective-permute-start.17 = (bf16[2,16,48,128]{3,2,1,0:T(8,128)(2,1)S(1)}, bf16[2,16,48,128]{3,2,1,0:T(8,128)(2,1)}, u32[]{:S(2)}, u32[]{:S(2)}) collective-permute-start(bf16[2,16,48,128]{3,2,1,0:T(8,128)(2,1)S(1)} %collective-permute-done.16.refs_8_), channel_id=1, source_target_pairs={{0,16},{16,0},{32,48},{48,32},{64,80},{80,64},{96,112},{112,96},{1... | collective-permute-start | bytes 1179656 | tf_op jit(solution)/shard_map/ppermute | solution.py:37
  209.8 1.9 collective-permute-start.15
  211.9 1.8 copy.13
  213.7 1.2 convert_reduce_fusion
  215.6 3.7 %input_sum.1 = bf16[128,1024]{1,0:T(8,128)(2,1)} custom-call(s32[8]{0:T(128)S(1)} %stack.103.place_ref, bf16[16,192,128]{2,1,0:T(8,128)(2,1)S(1)} %all-to-all-done.3.dqkv_ref, bf16[4,16,48,128]{3,2,1,0:T(8,128)(2,1)S(1)} %all-to-all-done.5.refs_0_, bf16[4,16,48,128]{3,2,1,0:T(8,128)(2,1)S(1)} %collective-permute-done.9.refs_1_, ...), custom_call_target="tpu_custom_call" | custom-call | tf_op jit(solution)/shard_map/input_sum/pallas_call | solution.py:185
  (43 shorter events, 5.1 us)
Async XLA Ops:
  0.6 17.1 %collective-permute-start = (bf16[128,1024]{1,0:T(8,128)(2,1)}, bf16[128,1024]{1,0:T(8,128)(2,1)S(1)}, u32[]{:S(2)}, u32[]{:S(2)}) collective-permute-start(bf16[128,1024]{1,0:T(8,128)(2,1)} %bitcast.40), channel_id=1, source_target_pairs={{0,1},{1,0},{2,3},{3,2},{4,5},{5,4},{6,7},{7,6},{8,9},{9,8},{10,11... | collective-permute-start | bytes 786440 | tf_op jit(solution)/shard_map/ppermute | solution.py:29
  10.5 7.2 %copy-start.8 = (bf16[1,128,1024]{2,1,0:T(8,128)(2,1)S(1)}, bf16[1,128,1024]{2,1,0:T(8,128)(2,1)}, u32[]{:S(2)}) copy-start(bf16[1,128,1024]{2,1,0:T(8,128)(2,1)} %param.5) | copy-start | bytes 786436
  10.5 24.1 %all-to-all-start = ((bf16[32,6,1024]{2,1,0:T(8,128)(2,1)}), bf16[32,6,1024]{2,1,0:T(8,128)(2,1)S(1)}, u32[]{:S(2)}, u32[]{:S(2)}) async-start(bf16[32,6,1024]{2,1,0:T(8,128)(2,1)} %broadcast_in_dim.13), calls=%async_computation | async-start | bytes 1048576 | tf_op jit(solution)/shard_map/all_to_all | solution.py:53
  16.4 13.0 %copy-start.7 = (bf16[1,128,1024]{2,1,0:T(8,128)(2,1)S(1)}, bf16[1,128,1024]{2,1,0:T(8,128)(2,1)}, u32[]{:S(2)}) copy-start(bf16[1,128,1024]{2,1,0:T(8,128)(2,1)} %param.9) | copy-start | bytes 786436
  17.8 29.3 %collective-permute-start.4 = (bf16[256,1024]{1,0:T(8,128)(2,1)S(1)}, bf16[256,1024]{1,0:T(8,128)(2,1)S(1)}, u32[]{:S(2)}, u32[]{:S(2)}) collective-permute-start(bf16[256,1024]{1,0:T(8,128)(2,1)S(1)} %pad_maximum_fusion.refs_0_), channel_id=1, source_target_pairs={{0,14},{1,15},{2,0},{3,1},{4,2},{5,3},{6,4},{7,5},{8,6},{9,7},{10,... | collective-permute-start | bytes 1572872 | tf_op jit(solution)/shard_map/ppermute | solution.py:33
  27.4 24.1 %collective-permute-start.1 = (bf16[256,1024]{1,0:T(8,128)(2,1)S(1)}, bf16[256,1024]{1,0:T(8,128)(2,1)S(1)}, u32[]{:S(2)}, u32[]{:S(2)}) collective-permute-start(bf16[256,1024]{1,0:T(8,128)(2,1)S(1)} %pad_maximum_fusion.refs_0_), channel_id=1, source_target_pairs={{0,2},{1,3},{2,4},{3,5},{4,6},{5,7},{6,8},{7,9},{8,10},{9,11},{10,... | collective-permute-start | bytes 1572872 | tf_op jit(solution)/shard_map/ppermute | solution.py:33
  34.7 25.6 %all-to-all-start.1 = ((bf16[16,64,128]{2,1,0:T(8,128)(2,1)}), bf16[16,64,128]{2,1,0:T(8,128)(2,1)S(1)}, u32[]{:S(2)}, u32[]{:S(2)}) async-start(bf16[16,64,128]{2,1,0:T(8,128)(2,1)} %bitcast.22), calls=%async_computation.1 | async-start | bytes 524288 | tf_op jit(solution)/shard_map/all_to_all | solution.py:225
  47.1 20.2 %collective-permute-start.5 = (bf16[256,1024]{1,0:T(8,128)(2,1)S(1)}, bf16[256,1024]{1,0:T(8,128)(2,1)}, u32[]{:S(2)}, u32[]{:S(2)}) collective-permute-start(bf16[256,1024]{1,0:T(8,128)(2,1)S(1)} %collective-permute-done.4.refs_4_), channel_id=1, source_target_pairs={{0,14},{1,15},{2,0},{3,1},{4,2},{5,3},{6,4},{7,5},{8,6},{9,7},{10,... | collective-permute-start | bytes 1572872 | tf_op jit(solution)/shard_map/ppermute | solution.py:33
  51.6 20.2 %collective-permute-start.2 = (bf16[256,1024]{1,0:T(8,128)(2,1)S(1)}, bf16[256,1024]{1,0:T(8,128)(2,1)}, u32[]{:S(2)}, u32[]{:S(2)}) collective-permute-start(bf16[256,1024]{1,0:T(8,128)(2,1)S(1)} %collective-permute-done.1.refs_1_), channel_id=1, source_target_pairs={{0,2},{1,3},{2,4},{3,5},{4,6},{5,7},{6,8},{7,9},{8,10},{9,11},{10,... | collective-permute-start | bytes 1572872 | tf_op jit(solution)/shard_map/ppermute | solution.py:33
  53.7 13.5 %copy-start = (bf16[192,1024]{1,0:T(8,128)(2,1)}, bf16[192,1024]{1,0:T(8,128)(2,1)S(1)}, u32[]{:S(2)}) copy-start(bf16[192,1024]{1,0:T(8,128)(2,1)S(1)} %reshape.27.refs_9_) | copy-start | bytes 1179652
  60.3 0.7 copy-start.2
  61.7 17.9 %all-to-all-start.4 = ((bf16[16,48,128]{2,1,0:T(8,128)(2,1)}), bf16[16,48,128]{2,1,0:T(8,128)(2,1)S(1)}, u32[]{:S(2)}, u32[]{:S(2)}) async-start(bf16[16,48,128]{2,1,0:T(8,128)(2,1)} %broadcast_in_dim.29), calls=%async_computation.4 | async-start | bytes 393216 | tf_op jit(solution)/shard_map/all_to_all | solution.py:53
  67.2 17.9 %collective-permute-start.6 = (bf16[256,1024]{1,0:T(8,128)(2,1)}, bf16[256,1024]{1,0:T(8,128)(2,1)S(1)}, u32[]{:S(2)}, u32[]{:S(2)}) collective-permute-start(bf16[256,1024]{1,0:T(8,128)(2,1)} %collective-permute-done.5.refs_5_), channel_id=1, source_target_pairs={{0,14},{1,15},{2,0},{3,1},{4,2},{5,3},{6,4},{7,5},{8,6},{9,7},{10,... | collective-permute-start | bytes 1572872 | tf_op jit(solution)/shard_map/ppermute | solution.py:33
  71.7 18.8 %collective-permute-start.3 = (bf16[256,1024]{1,0:T(8,128)(2,1)}, bf16[256,1024]{1,0:T(8,128)(2,1)S(1)}, u32[]{:S(2)}, u32[]{:S(2)}) collective-permute-start(bf16[256,1024]{1,0:T(8,128)(2,1)} %collective-permute-done.2.refs_2_), channel_id=1, source_target_pairs={{0,2},{1,3},{2,4},{3,5},{4,6},{5,7},{6,8},{7,9},{8,10},{9,11},{10,... | collective-permute-start | bytes 1572872 | tf_op jit(solution)/shard_map/ppermute | solution.py:33
  80.6 33.7 %all-to-all-start.5 = ((bf16[4,16,48,128]{3,2,1,0:T(8,128)(2,1)}), bf16[4,16,48,128]{3,2,1,0:T(8,128)(2,1)S(1)}, u32[]{:S(2)}, u32[]{:S(2)}) async-start(bf16[4,16,48,128]{3,2,1,0:T(8,128)(2,1)} %broadcast_in_dim.30), calls=%async_computation.5 | async-start | bytes 1572864 | tf_op jit(solution)/shard_map/all_to_all | solution.py:53
  85.9 8.8 %collective-permute-start.8 = (bf16[128,1024]{1,0:T(8,128)(2,1)}, bf16[128,1024]{1,0:T(8,128)(2,1)}, u32[]{:S(2)}, u32[]{:S(2)}) collective-permute-start(bf16[128,1024]{1,0:T(8,128)(2,1)} %slice.17), channel_id=1, source_target_pairs={{0,14},{1,15},{2,0},{3,1},{4,2},{5,3},{6,4},{7,5},{8,6},{9,7},{10,... | collective-permute-start | bytes 786440 | tf_op jit(solution)/shard_map/ppermute | solution.py:33
  91.2 9.2 %collective-permute-start.7 = (bf16[128,1024]{1,0:T(8,128)(2,1)}, bf16[128,1024]{1,0:T(8,128)(2,1)}, u32[]{:S(2)}, u32[]{:S(2)}) collective-permute-start(bf16[128,1024]{1,0:T(8,128)(2,1)} %slice.16), channel_id=1, source_target_pairs={{0,2},{1,3},{2,4},{3,5},{4,6},{5,7},{6,8},{7,9},{8,10},{9,11},{10,... | collective-permute-start | bytes 786440 | tf_op jit(solution)/shard_map/ppermute | solution.py:33
  93.3 0.7 copy-start.9
  94.2 6.3 %copy-start.5 = (s32[1,16]{1,0:T(1,128)S(1)}, s32[1,16]{1,0:T(1,128)}, u32[]{:S(2)}) copy-start(s32[1,16]{1,0:T(1,128)} %param.8) | copy-start | bytes 196
  100.5 1.0 copy-start.1
  101.5 0.9 copy-start.3
  113.6 0.7 copy-start.4
  114.3 24.2 %all-to-all-start.2 = ((bf16[16,64,128]{2,1,0:T(8,128)(2,1)}), bf16[16,64,128]{2,1,0:T(8,128)(2,1)}, u32[]{:S(2)}, u32[]{:S(2)}) async-start(bf16[16,64,128]{2,1,0:T(8,128)(2,1)} %copy-done.4), calls=%async_computation.2 | async-start | bytes 524288 | tf_op jit(solution)/shard_map/all_to_all | solution.py:249
  138.5 24.4 %all-to-all-start.6 = ((bf16[32,6,1024]{2,1,0:T(8,128)(2,1)}), bf16[32,6,1024]{2,1,0:T(8,128)(2,1)S(1)}, u32[]{:S(2)}, u32[]{:S(2)}) async-start(bf16[32,6,1024]{2,1,0:T(8,128)(2,1)} %weight_sum.1), calls=%async_computation.6 | async-start | bytes 1048576 | tf_op jit(solution)/shard_map/all_to_all | solution.py:253
  146.4 27.6 %collective-permute-start.12 = (bf16[4,16,48,128]{3,2,1,0:T(8,128)(2,1)S(1)}, bf16[4,16,48,128]{3,2,1,0:T(8,128)(2,1)}, u32[]{:S(2)}, u32[]{:S(2)}) collective-permute-start(bf16[4,16,48,128]{3,2,1,0:T(8,128)(2,1)S(1)} %all-to-all-done.5.refs_0_), channel_id=1, source_target_pairs={{0,385},{1,384},{2,387},{3,386},{4,389},{5,388},{6,391},{7,390},{8... | collective-permute-start | bytes 2359304 | tf_op jit(solution)/shard_map/ppermute | solution.py:48
  149.8 27.2 %collective-permute-start.10 = (bf16[4,16,48,128]{3,2,1,0:T(8,128)(2,1)S(1)}, bf16[4,16,48,128]{3,2,1,0:T(8,128)(2,1)S(1)}, u32[]{:S(2)}, u32[]{:S(2)}) collective-permute-start(bf16[4,16,48,128]{3,2,1,0:T(8,128)(2,1)S(1)} %all-to-all-done.5.refs_0_), channel_id=1, source_target_pairs={{0,128},{1,129},{2,130},{3,131},{4,132},{5,133},{6,134},{7,135},{8... | collective-permute-start | bytes 2359304 | tf_op jit(solution)/shard_map/ppermute | solution.py:48
  162.9 0.8 copy-start.6
  163.6 51.9 %all-to-all-start.3 = ((bf16[16,192,128]{2,1,0:T(8,128)(2,1)}), bf16[16,192,128]{2,1,0:T(8,128)(2,1)S(1)}, u32[]{:S(2)}, u32[]{:S(2)}) async-start(bf16[16,192,128]{2,1,0:T(8,128)(2,1)} %get-tuple-element.6.dqkv_ref), calls=%async_computation.3 | async-start | bytes 1572864 | tf_op jit(solution)/shard_map/all_to_all | solution.py:248
  167.3 48.3 %collective-permute-start.9 = (bf16[4,16,48,128]{3,2,1,0:T(8,128)(2,1)S(1)}, bf16[4,16,48,128]{3,2,1,0:T(8,128)(2,1)S(1)}, u32[]{:S(2)}, u32[]{:S(2)}) collective-permute-start(bf16[4,16,48,128]{3,2,1,0:T(8,128)(2,1)S(1)} %all-to-all-done.5.refs_0_), channel_id=1, source_target_pairs={{0,16},{16,0},{32,48},{48,32},{64,80},{80,64},{96,112},{112,96},{1... | collective-permute-start | bytes 2359304 | tf_op jit(solution)/shard_map/ppermute | solution.py:37
  175.1 31.4 %collective-permute-start.16 = (bf16[2,16,48,128]{3,2,1,0:T(8,128)(2,1)S(1)}, bf16[2,16,48,128]{3,2,1,0:T(8,128)(2,1)S(1)}, u32[]{:S(2)}, u32[]{:S(2)}) collective-permute-start(bf16[2,16,48,128]{3,2,1,0:T(8,128)(2,1)S(1)} %slice.19), channel_id=1, source_target_pairs={{0,385},{1,384},{2,387},{3,386},{4,389},{5,388},{6,391},{7,390},{8... | collective-permute-start | bytes 1179656 | tf_op jit(solution)/shard_map/ppermute | solution.py:48
  177.1 32.8 %collective-permute-start.14 = (bf16[2,16,48,128]{3,2,1,0:T(8,128)(2,1)S(1)}, bf16[2,16,48,128]{3,2,1,0:T(8,128)(2,1)}, u32[]{:S(2)}, u32[]{:S(2)}) collective-permute-start(bf16[2,16,48,128]{3,2,1,0:T(8,128)(2,1)S(1)} %slice.18), channel_id=1, source_target_pairs={{0,128},{1,129},{2,130},{3,131},{4,132},{5,133},{6,134},{7,135},{8... | collective-permute-start | bytes 1179656 | tf_op jit(solution)/shard_map/ppermute | solution.py:48
  199.8 15.7 %collective-permute-start.13 = (bf16[4,16,48,128]{3,2,1,0:T(8,128)(2,1)}, bf16[4,16,48,128]{3,2,1,0:T(8,128)(2,1)}, u32[]{:S(2)}, u32[]{:S(2)}) collective-permute-start(bf16[4,16,48,128]{3,2,1,0:T(8,128)(2,1)} %collective-permute-done.12.refs_4_), channel_id=1, source_target_pairs={{0,16},{16,0},{32,48},{48,32},{64,80},{80,64},{96,112},{112,96},{1... | collective-permute-start | bytes 2359304 | tf_op jit(solution)/shard_map/ppermute | solution.py:37
  202.9 12.7 %collective-permute-start.11 = (bf16[4,16,48,128]{3,2,1,0:T(8,128)(2,1)S(1)}, bf16[4,16,48,128]{3,2,1,0:T(8,128)(2,1)}, u32[]{:S(2)}, u32[]{:S(2)}) collective-permute-start(bf16[4,16,48,128]{3,2,1,0:T(8,128)(2,1)S(1)} %collective-permute-done.10.refs_2_), channel_id=1, source_target_pairs={{0,16},{16,0},{32,48},{48,32},{64,80},{80,64},{96,112},{112,96},{1... | collective-permute-start | bytes 2359304 | tf_op jit(solution)/shard_map/ppermute | solution.py:37
  206.5 9.1 %collective-permute-start.17 = (bf16[2,16,48,128]{3,2,1,0:T(8,128)(2,1)S(1)}, bf16[2,16,48,128]{3,2,1,0:T(8,128)(2,1)}, u32[]{:S(2)}, u32[]{:S(2)}) collective-permute-start(bf16[2,16,48,128]{3,2,1,0:T(8,128)(2,1)S(1)} %collective-permute-done.16.refs_8_), channel_id=1, source_target_pairs={{0,16},{16,0},{32,48},{48,32},{64,80},{80,64},{96,112},{112,96},{1... | collective-permute-start | bytes 1179656 | tf_op jit(solution)/shard_map/ppermute | solution.py:37
  209.8 5.7 %collective-permute-start.15 = (bf16[2,16,48,128]{3,2,1,0:T(8,128)(2,1)}, bf16[2,16,48,128]{3,2,1,0:T(8,128)(2,1)}, u32[]{:S(2)}, u32[]{:S(2)}) collective-permute-start(bf16[2,16,48,128]{3,2,1,0:T(8,128)(2,1)} %collective-permute-done.14.refs_6_), channel_id=1, source_target_pairs={{0,16},{16,0},{32,48},{48,32},{64,80},{80,64},{96,112},{112,96},{1... | collective-permute-start | bytes 1179656 | tf_op jit(solution)/shard_map/ppermute | solution.py:37

commit v2 on v1

v2 whole, which is shorter than its diff:
```python
import functools

import jax
import jax.numpy as jnp
from jax import lax
from jax.experimental import pallas as pl
from jax.experimental.pallas import tpu as pltpu
from jax.sharding import PartitionSpec as P

HEAD_DIM = 64
TILE = 128
TOP = 4
BF = jnp.bfloat16
F32 = jnp.float32
VM = pl.BlockSpec(memory_space=pltpu.VMEM)
SM = pl.BlockSpec(memory_space=pltpu.SMEM)
PARAMS = pltpu.CompilerParams(vmem_limit_bytes=48 * 2**20)

YL, XN, CORES, ZN, YH = 4, 4, 2, 8, 2
DP = YL * XN * CORES
SEQ = ZN * YH


def dot(a, b, ca, cb):
    return lax.dot_general(a, b, (((ca,), (cb,)), ((), ())), preferred_element_type=F32)


def flip_y(x):
    return lax.ppermute(x, "seq", [(s, s ^ 1) for s in range(SEQ)])


def shift_z(x, k):
    return lax.ppermute(x, "seq", [(s, (s + YH * k) % SEQ) for s in range(SEQ)])


def swap_core(x):
    return lax.ppermute(x, "dp", [(d, d ^ 1) for d in range(DP)])


def shift_x(x, k):
    pairs = []
    for d in range(DP):
        to = (d // CORES + k) % XN
        pairs.append((d, d // (XN * CORES) * XN * CORES + to * CORES + d % CORES))
    return lax.ppermute(x, "dp", pairs)


def shift_y(x, k):
    return lax.ppermute(x, "dp", [(d, (d + k * XN * CORES) % DP) for d in range(DP)])


def spread(x, axis, n):
    copies = jnp.broadcast_to(x[None], (n, *x.shape))
    return lax.all_to_all(copies, axis, 0, 0, tiled=True)


def attend(nblk, order_ref, list_ref, count_ref, *refs):
    blocks = refs[:nblk]
    w_ref, cot_ref, out_ref, kv_rows, kv_cols, q_cols, acc = refs[nblk:]
    scale = HEAD_DIM ** (-0.5)
    tiles = kv_rows.shape[0]
    w = w_ref[...]
    w = jnp.concatenate([w[HEAD_DIM:], w[:HEAD_DIM]], axis=0)
    slot = 0
    for blk in blocks:
        qkv = dot(blk[...], w, 1, 1).astype(BF)
        for r in range(blk.shape[0] // TILE):
            tile = order_ref[slot]
            slot += 1
            piece = qkv[r * TILE : (r + 1) * TILE]
            kv = piece[:, :TILE]
            kv_rows[tile] = kv
            kv_cols[tile] = kv.T
            q_cols[tile] = piece[:, TILE:].T
    acc[...] = jnp.zeros_like(acc)
    zero = jnp.zeros((HEAD_DIM, TILE), BF)

    def step(a, _):
        left = jnp.concatenate([q_cols[a], zero], axis=0)
        right = jnp.concatenate([zero, cot_ref[a, :HEAD_DIM, :]], axis=0)
        both = jnp.concatenate([left, right], axis=1)
        keys = [list_ref[a, t] for t in range(TOP)]
        count = count_ref[a]
        rows = jnp.concatenate([kv_rows[j] for j in keys], axis=0)
        prod = dot(rows, both, 1, 0)
        raw = prod[:, :TILE]
        dprobs = prod[:, TILE:]
        parts = [raw[t * TILE : (t + 1) * TILE] for t in range(TOP)]
        raw = jnp.concatenate(
            parts[:1] + [jnp.where(t < count, parts[t], -1e30) for t in range(1, TOP)], axis=0
        )
        top = jnp.max(raw, axis=0, keepdims=True)
        expo = jnp.exp((raw - top) * scale)
        probs = expo * (1.0 / jnp.sum(expo, axis=0, keepdims=True))
        delta = jnp.sum(probs * dprobs, axis=0, keepdims=True)
        dscores = (probs * ((dprobs - delta) * scale)).astype(BF)
        pair = jnp.concatenate([dscores, probs.astype(BF)], axis=1)
        cols = jnp.concatenate([kv_cols[j] for j in keys], axis=1)
        out = dot(cols, pair, 1, 0)
        out_ref[a, :HEAD_DIM, :] = out[:HEAD_DIM, :TILE].astype(BF)
        out_ref[a, 3 * HEAD_DIM :, :] = out[HEAD_DIM:, TILE:].astype(BF)
        both_t = jnp.concatenate([left.T, right.T], axis=0)
        back = dot(pair, both_t, 1, 0)
        for t in range(TOP):
            acc[keys[t]] += back[t * TILE : (t + 1) * TILE]
        return 0

    lax.fori_loop(0, tiles, step, 0, unroll=2)
    for a in range(tiles):
        out_ref[a, HEAD_DIM : 3 * HEAD_DIM, :] = acc[a].astype(BF).T


def attention(order, tile_list, counts, blocks, w_head, cot_t):
    tiles = tile_list.shape[0]
    return pl.pallas_call(
        functools.partial(attend, len(blocks)),
        out_shape=jax.ShapeDtypeStruct((tiles, 4 * HEAD_DIM, TILE), BF),
        in_specs=[SM, SM, SM] + [VM] * (len(blocks) + 2),
        out_specs=VM,
        scratch_shapes=[
            pltpu.VMEM((tiles, TILE, 2 * HEAD_DIM), BF),
            pltpu.VMEM((tiles, 2 * HEAD_DIM, TILE), BF),
            pltpu.VMEM((tiles, HEAD_DIM, TILE), BF),
            pltpu.VMEM((tiles, TILE, 2 * HEAD_DIM), F32),
        ],
        compiler_params=PARAMS,
        name="attend",
    )(order, tile_list, counts, *blocks, w_head, cot_t)


def weight_sum(nblk, here_ref, order_ref, dqkv_ref, *refs):
    blocks, out_ref = refs[:nblk], refs[nblk]
    total, slot = None, 0
    for blk in blocks:
        n = blk.shape[0] // TILE
        left = [dqkv_ref[order_ref[slot + r], : 3 * HEAD_DIM, :] for r in range(n)]
        slot += n
        part = dot(jnp.concatenate(left, axis=1), blk[...], 1, 0)
        total = part if total is None else total + part
    rows = out_ref.shape[3]
    core, x, y = here_ref[0], here_ref[1], here_ref[2]
    for i in range(DP):
        c = lax.rem(i % CORES + CORES - core, CORES)
        u = lax.rem(i // CORES % XN + XN - x, XN)
        v = lax.rem(i // (CORES * XN) + YL - y, YL)
        out_ref[c, u, v] = total[i * rows : (i + 1) * rows]


def weight_grad(here, order, dqkv_t, blocks):
    rows, depth = 3 * HEAD_DIM // DP, blocks[0].shape[1]
    return pl.pallas_call(
        functools.partial(weight_sum, len(blocks)),
        out_shape=jax.ShapeDtypeStruct((CORES, XN, YL, rows, depth), F32),
        in_specs=[SM, SM, VM] + [VM] * len(blocks),
        out_specs=VM,
        compiler_params=PARAMS,
        name="weight_sum",
    )(here, order, dqkv_t, *blocks)


def input_sum(both_ref, w_ref, att_ref, out_ref):
    heads = both_ref.shape[0]
    chunk = 3 * HEAD_DIM // XN
    att_ref[...] = jnp.concatenate(
        [both_ref[h, 3 * HEAD_DIM :, :] for h in range(heads)], axis=0
    ).T
    left = jnp.concatenate(
        [both_ref[h, c * chunk : (c + 1) * chunk, :] for c in range(XN) for h in range(heads)],
        axis=0,
    ).T
    for y in range(YL):
        cols = []
        for c in range(CORES):
            part = [w_ref[(y * XN + u) * CORES + c] for u in range(XN)]
            cols.append(jnp.concatenate([p.reshape(heads * chunk, TILE) for p in part], axis=0))
        total = dot(left, jnp.concatenate(cols, axis=1), 1, 0)
        at = y * CORES * TILE
        out_ref[:, at : at + CORES * TILE] = total.astype(BF)


def input_grad(both, w_all):
    heads = both.shape[0]
    return pl.pallas_call(
        input_sum,
        out_shape=(
            jax.ShapeDtypeStruct((TILE, heads * HEAD_DIM), BF),
            jax.ShapeDtypeStruct((TILE, YL * CORES * TILE), BF),
        ),
        in_specs=[VM, VM],
        out_specs=(VM, VM),
        compiler_params=PARAMS,
        name="input_sum",
    )(both, w_all)


def shards(tokens, qkv_weight, key_tiles, key_counts, cotangent):
    heads = SEQ
    depth = tokens.shape[2]
    tiles = key_tiles.shape[1]
    dp, seq = lax.axis_index("dp"), lax.axis_index("seq")
    y_lo, x, core = dp // (XN * CORES), dp // CORES % XN, dp % CORES
    z, y_hi = seq // YH, seq % YH
    grad_scale = (DP * tiles * TILE) ** (-0.5)

    w_head = spread(qkv_weight[0], "dp", DP).reshape(3 * HEAD_DIM, depth)
    chunk = 3 * HEAD_DIM // XN
    w_block = lax.dynamic_slice(
        w_head, (x * chunk, (y_lo * CORES + core) * TILE), (chunk, TILE)
    )

    own = tokens[0]
    pair = jnp.concatenate([own, flip_y(own)], axis=0)
    right, left = [pair], [pair]
    for _ in range(ZN // 2 - 1):
        right.append(shift_z(right[-1], 1))
        left.append(shift_z(left[-1], -1))
    far = [shift_z(right[-1][:TILE], 1), shift_z(left[-1][TILE:], -1)]
    blocks = right + left[1:] + far
    zs = [(0, 0), (0, 1)]
    zs += [(-k, j) for k in range(1, ZN // 2) for j in range(2)]
    zs += [(k, j) for k in range(1, ZN // 2) for j in range(2)]
    zs += [(ZN // 2, 0), (ZN // 2, 1)]
    order = jnp.stack([(z + k) % ZN * YH + (y_hi + j) % YH for k, j in zs]).astype(jnp.int32)

    cot_t = cotangent[0].T.reshape(heads, HEAD_DIM, TILE)
    copies = jnp.broadcast_to(w_block[None], (heads, *w_block.shape))
    mixed = jnp.concatenate([cot_t, copies], axis=1)
    mixed, _ = lax.optimization_barrier((mixed, pair))
    mixed = lax.all_to_all(mixed, "seq", 0, 0, tiled=True)
    w_seq, _ = lax.optimization_barrier((mixed[:, HEAD_DIM:], (right[1], left[1])))
    w_all = lax.all_gather(w_seq, "dp", axis=0)

    both = attention(order, key_tiles[0], key_counts[0], blocks, w_head, mixed)
    here = jnp.stack([core, x, y_lo]).astype(jnp.int32)
    sums = weight_grad(here, order, both, blocks)
    both = lax.all_to_all(both, "seq", 0, 0, tiled=True)

    sums = sums[0] + swap_core(sums[1])
    sums = sums[0] + sum(shift_x(sums[k], k) for k in range(1, XN))
    sums = sums[0] + sum(shift_y(sums[k], k) for k in range(1, YL))
    grad_weight = sums[None] * grad_scale

    attended, grad_input = input_grad(both, w_all)
    return (attended[None], grad_input[None], grad_weight)


def solution(mesh):
    in_specs = (
        P("dp", "seq", None),
        P("seq", "dp", None),
        P("dp", None, None),
        P("dp", None),
        P("dp", "seq", None),
    )
    out_specs = (P("dp", "seq", None), P("dp", "seq", None), P("seq", "dp", None))
    return jax.shard_map(shards, mesh=mesh, in_specs=in_specs, out_specs=out_specs, check_vma=False)
```

time: 221 us -> 204 us (0.923)
  the two profiles are of different devices: /device:TPU:1 before, /device:TPU:56 now
where the time goes in v2:
time: 204 us; the launch traced here: 203 us
  starting transfers between devices  88.6 us (43%)
  waiting for transfers between devices  66.7 us (33%)
  Pallas kernels  18 us (9%)
  between operations  14.6 us (7%)
  local copies, waits for them, and re-layouts  12.8 us (6%)
    ppermute x8, waiting for transfers between devices, shift_z(): return lax.ppermute(x, 'seq', [(s, (s + YH * k) % SEQ) for s in range(SEQ)])  29.4 us
    ppermute x8, starting transfers between devices, shift_z(): return lax.ppermute(x, 'seq', [(s, (s + YH * k) % SEQ) for s in range(SEQ)])  28.2 us
    ppermute x1, waiting for transfers between devices, flip_y(): return lax.ppermute(x, 'seq', [(s, s ^ 1) for s in range(SEQ)])  17.6 us
    all_to_all x1, starting transfers between devices, shards(): mixed = lax.all_to_all(mixed, 'seq', 0, 0, tiled=True)  14.2 us
    all_to_all x1, starting transfers between devices, shards(): both = lax.all_to_all(both, 'seq', 0, 0, tiled=True)  11.1 us
    pallas_call x1, Pallas kernels, attention(): pl.pallas_call(functools.partial(attend, len(blocks)), out_shape=jax.Shap...  10.9 us
    ppermute x3, starting transfers between devices, shift_y(): lax.ppermute(x, 'dp', [(d, (d + k * XN * CORES) % DP) for d in range(DP)])  9.62 us
    ppermute x3, starting transfers between devices, shift_x(): return lax.ppermute(x, 'dp', pairs)  9.57 us
  transfers between devices with their start and end apart: 20, of which 12 were waited for; matrix products, arithmetic and copies ran while one was open for 3% of the time, Pallas kernels for 7%

profile of v2, /device:TPU:56, one launch (start us, length us, event | category | flops | bytes accessed | tf_op | source)
XLA Modules:
  0.0 202.6 jit_solution(14644509861336044461)
XLA Ops:
  7.2 1.6 broadcast_in_dim.21
  8.8 7.8 %all-to-all-start = ((bf16[32,6,1024]{2,1,0:T(8,128)(2,1)}), bf16[32,6,1024]{2,1,0:T(8,128)(2,1)S(1)}, u32[]{:S(2)}, u32[]{:S(2)}) async-start(bf16[32,6,1024]{2,1,0:T(8,128)(2,1)} %broadcast_in_dim.21), calls=%async_computation | async-start | bytes 1048576 | tf_op jit(solution)/shard_map/all_to_all | solution.py:54
  16.5 6.3 %collective-permute-start = (bf16[128,1024]{1,0:T(8,128)(2,1)}, bf16[128,1024]{1,0:T(8,128)(2,1)S(1)}, u32[]{:S(2)}, u32[]{:S(2)}) collective-permute-start(bf16[128,1024]{1,0:T(8,128)(2,1)} %bitcast.66), channel_id=1, source_target_pairs={{0,1},{1,0},{2,3},{3,2},{4,5},{5,4},{6,7},{7,6},{8,9},{9,8},{10,11... | collective-permute-start | bytes 786440 | tf_op jit(solution)/shard_map/ppermute | solution.py:29
  22.8 1.1 copy.14
  24.0 17.6 %collective-permute-done = bf16[128,1024]{1,0:T(8,128)(2,1)S(1)} collective-permute-done((bf16[128,1024]{1,0:T(8,128)(2,1)}, bf16[128,1024]{1,0:T(8,128)(2,1)S(1)}, u32[]{:S(2)}, u32[]{:S(2)}) %collective-permute-start) | collective-permute-done | bytes 262176 | tf_op jit(solution)/shard_map/ppermute | solution.py:29
  41.6 1.0 pad_maximum_fusion.refs_0_
  42.8 0.8 pad_maximum_fusion.1
  43.6 14.2 %all-to-all-start.1 = ((bf16[16,112,128]{2,1,0:T(8,128)(2,1)}), bf16[16,112,128]{2,1,0:T(8,128)(2,1)S(1)}, u32[]{:S(2)}, u32[]{:S(2)}) async-start(bf16[16,112,128]{2,1,0:T(8,128)(2,1)} %pad_maximum_fusion.1), calls=%async_computation.1 | async-start | bytes 917504 | tf_op jit(solution)/shard_map/all_to_all | solution.py:229
  57.9 3.4 %collective-permute-start.1 = (bf16[256,1024]{1,0:T(8,128)(2,1)S(1)}, bf16[256,1024]{1,0:T(8,128)(2,1)S(1)}, u32[]{:S(2)}, u32[]{:S(2)}) collective-permute-start(bf16[256,1024]{1,0:T(8,128)(2,1)S(1)} %pad_maximum_fusion.refs_0_), channel_id=1, source_target_pairs={{0,2},{1,3},{2,4},{3,5},{4,6},{5,7},{6,8},{7,9},{8,10},{9,11},{10,... | collective-permute-start | bytes 1572872 | tf_op jit(solution)/shard_map/ppermute | solution.py:33
  61.3 3.7 %collective-permute-start.4 = (bf16[256,1024]{1,0:T(8,128)(2,1)S(1)}, bf16[256,1024]{1,0:T(8,128)(2,1)S(1)}, u32[]{:S(2)}, u32[]{:S(2)}) collective-permute-start(bf16[256,1024]{1,0:T(8,128)(2,1)S(1)} %pad_maximum_fusion.refs_0_), channel_id=1, source_target_pairs={{0,14},{1,15},{2,0},{3,1},{4,2},{5,3},{6,4},{7,5},{8,6},{9,7},{10,... | collective-permute-start | bytes 1572872 | tf_op jit(solution)/shard_map/ppermute | solution.py:33
  64.9 9.3 %all-to-all-done.1.refs_10_ = bf16[16,112,128]{2,1,0:T(8,128)(2,1)S(1)} async-done(((bf16[16,112,128]{2,1,0:T(8,128)(2,1)}), bf16[16,112,128]{2,1,0:T(8,128)(2,1)S(1)}, u32[]{:S(2)}, u32[]{:S(2)}) %all-to-all-start.1) | async-done | bytes 458784 | tf_op jit(solution)/shard_map/all_to_all | solution.py:229
  74.2 0.7 slice.54
  74.9 8.3 %collective-permute-done.1.refs_1_ = bf16[256,1024]{1,0:T(8,128)(2,1)S(1)} collective-permute-done((bf16[256,1024]{1,0:T(8,128)(2,1)S(1)}, bf16[256,1024]{1,0:T(8,128)(2,1)S(1)}, u32[]{:S(2)}, u32[]{:S(2)}) %collective-permute-start.1) | collective-permute-done | bytes 524320 | tf_op jit(solution)/shard_map/ppermute | solution.py:33
  83.3 3.4 %collective-permute-start.2 = (bf16[256,1024]{1,0:T(8,128)(2,1)S(1)}, bf16[256,1024]{1,0:T(8,128)(2,1)S(1)}, u32[]{:S(2)}, u32[]{:S(2)}) collective-permute-start(bf16[256,1024]{1,0:T(8,128)(2,1)S(1)} %collective-permute-done.1.refs_1_), channel_id=1, source_target_pairs={{0,2},{1,3},{2,4},{3,5},{4,6},{5,7},{6,8},{7,9},{8,10},{9,11},{10,... | collective-permute-start | bytes 1572872 | tf_op jit(solution)/shard_map/ppermute | solution.py:33
  86.7 3.7 %collective-permute-start.5 = (bf16[256,1024]{1,0:T(8,128)(2,1)S(1)}, bf16[256,1024]{1,0:T(8,128)(2,1)S(1)}, u32[]{:S(2)}, u32[]{:S(2)}) collective-permute-start(bf16[256,1024]{1,0:T(8,128)(2,1)S(1)} %collective-permute-done.4.refs_4_), channel_id=1, source_target_pairs={{0,14},{1,15},{2,0},{3,1},{4,2},{5,3},{6,4},{7,5},{8,6},{9,7},{10,... | collective-permute-start | bytes 1572872 | tf_op jit(solution)/shard_map/ppermute | solution.py:33
  90.3 9.9 %collective-permute-done.2.refs_2_ = bf16[256,1024]{1,0:T(8,128)(2,1)S(1)} collective-permute-done((bf16[256,1024]{1,0:T(8,128)(2,1)S(1)}, bf16[256,1024]{1,0:T(8,128)(2,1)S(1)}, u32[]{:S(2)}, u32[]{:S(2)}) %collective-permute-start.2) | collective-permute-done | bytes 524320 | tf_op jit(solution)/shard_map/ppermute | solution.py:33
  100.2 2.2 %collective-permute-start.3 = (bf16[256,1024]{1,0:T(8,128)(2,1)S(1)}, bf16[256,1024]{1,0:T(8,128)(2,1)S(1)}, u32[]{:S(2)}, u32[]{:S(2)}) collective-permute-start(bf16[256,1024]{1,0:T(8,128)(2,1)S(1)} %collective-permute-done.2.refs_2_), channel_id=1, source_target_pairs={{0,2},{1,3},{2,4},{3,5},{4,6},{5,7},{6,8},{7,9},{8,10},{9,11},{10,... | collective-permute-start | bytes 1572872 | tf_op jit(solution)/shard_map/ppermute | solution.py:33
  102.4 0.8 copy-done.2
  103.3 4.9 %collective-permute-start.6 = (bf16[256,1024]{1,0:T(8,128)(2,1)S(1)}, bf16[256,1024]{1,0:T(8,128)(2,1)S(1)}, u32[]{:S(2)}, u32[]{:S(2)}) collective-permute-start(bf16[256,1024]{1,0:T(8,128)(2,1)S(1)} %collective-permute-done.5.refs_5_), channel_id=1, source_target_pairs={{0,14},{1,15},{2,0},{3,1},{4,2},{5,3},{6,4},{7,5},{8,6},{9,7},{10,... | collective-permute-start | bytes 1572872 | tf_op jit(solution)/shard_map/ppermute | solution.py:33
  108.1 0.8 copy-done.5
  109.0 7.4 %collective-permute-done.3.refs_3_ = bf16[256,1024]{1,0:T(8,128)(2,1)S(1)} collective-permute-done((bf16[256,1024]{1,0:T(8,128)(2,1)S(1)}, bf16[256,1024]{1,0:T(8,128)(2,1)S(1)}, u32[]{:S(2)}, u32[]{:S(2)}) %collective-permute-start.3) | collective-permute-done | bytes 524320 | tf_op jit(solution)/shard_map/ppermute | solution.py:33
  116.3 0.7 slice.52
  117.1 1.9 collective-permute-start.7
  119.0 0.7 slice.53
  119.7 5.1 %collective-permute-start.8 = (bf16[128,1024]{1,0:T(8,128)(2,1)}, bf16[128,1024]{1,0:T(8,128)(2,1)}, u32[]{:S(2)}, u32[]{:S(2)}) collective-permute-start(bf16[128,1024]{1,0:T(8,128)(2,1)} %slice.53), channel_id=1, source_target_pairs={{0,14},{1,15},{2,0},{3,1},{4,2},{5,3},{6,4},{7,5},{8,6},{9,7},{10,... | collective-permute-start | bytes 786440 | tf_op jit(solution)/shard_map/ppermute | solution.py:33
  125.2 1.7 collective-permute-done.7.refs_7_
  127.0 2.1 %collective-permute-done.8.refs_8_ = bf16[128,1024]{1,0:T(8,128)(2,1)} collective-permute-done((bf16[128,1024]{1,0:T(8,128)(2,1)}, bf16[128,1024]{1,0:T(8,128)(2,1)}, u32[]{:S(2)}, u32[]{:S(2)}) %collective-permute-start.8) | collective-permute-done | bytes 262176 | tf_op jit(solution)/shard_map/ppermute | solution.py:33
  129.0 1.0 copy-done.3
  130.1 1.0 copy-done.6
  131.1 10.9 %attend.1.dqkv_ref = bf16[16,256,128]{2,1,0:T(8,128)(2,1)} custom-call(s32[16]{0:T(128)S(1)} %stack.79.order_ref, s32[16,4]{1,0:T(8,128)S(1)} %copy.15.list_ref, s32[16]{0:T(128)S(1)} %bitcast.62, bf16[256,1024]{1,0:T(8,128)(2,1)S(1)} %pad_maximum_fusion.refs_0_, bf16[256,1024]{1,0:T(8,128)(2,1)S(1)} %collective-permute-done.1.refs_1_, ...), custom_call_target="tpu_custom_call" | custom-call | tf_op jit(solution)/shard_map/attend/pallas_call | solution.py:115
  142.0 11.1 %all-to-all-start.2 = ((bf16[16,256,128]{2,1,0:T(8,128)(2,1)}), bf16[16,256,128]{2,1,0:T(8,128)(2,1)S(1)}, u32[]{:S(2)}, u32[]{:S(2)}) async-start(bf16[16,256,128]{2,1,0:T(8,128)(2,1)} %attend.1.dqkv_ref), calls=%async_computation.2 | async-start | bytes 2097152 | tf_op jit(solution)/shard_map/all_to_all | solution.py:236
  153.2 1.0 copy-done.1
  154.3 1.0 copy-done.4
  155.3 1.0 copy-done.7
  156.4 2.5 %weight_sum.1 = f32[2,4,4,6,1024]{4,3,2,1,0:T(8,128)S(1)} custom-call(s32[3]{0:T(128)S(1)} %pad_add_fusion.here_ref, s32[16]{0:T(128)S(1)} %stack.79.order_ref, bf16[16,256,128]{2,1,0:T(8,128)(2,1)} %attend.1.dqkv_ref, bf16[256,1024]{1,0:T(8,128)(2,1)S(1)} %pad_maximum_fusion.refs_0_, bf16[256,1024]{1,0:T(8,128)(2,1)S(1)} %collective-permute-done.1.refs_1_, ...), custom_call_target="tpu_custom_call" | custom-call | tf_op jit(solution)/shard_map/weight_sum/pallas_call | solution.py:151
  158.9 1.9 collective-permute-start.9
  160.8 1.9 collective-permute-done.9
  162.8 1.9 collective-permute-start.10
  164.7 4.7 %collective-permute-start.11 = (f32[4,6,1024]{2,1,0:T(8,128)S(1)}, f32[4,6,1024]{2,1,0:T(8,128)S(1)}, u32[]{:S(2)}, u32[]{:S(2)}) collective-permute-start(f32[4,6,1024]{2,1,0:T(8,128)S(1)} %get-tuple-element.20), channel_id=1, source_target_pairs={{0,64},{16,80},{32,96},{48,112},{64,0},{80,16},{96,32},{112,48},{1... | collective-permute-start | bytes 294920 | tf_op jit(solution)/shard_map/ppermute | solution.py:45
  169.4 3.0 %collective-permute-start.12 = (f32[4,6,1024]{2,1,0:T(8,128)S(1)}, f32[4,6,1024]{2,1,0:T(8,128)S(1)}, u32[]{:S(2)}, u32[]{:S(2)}) collective-permute-start(f32[4,6,1024]{2,1,0:T(8,128)S(1)} %get-tuple-element.21), channel_id=1, source_target_pairs={{0,96},{16,112},{32,0},{48,16},{64,32},{80,48},{96,64},{112,80},{1... | collective-permute-start | bytes 294920 | tf_op jit(solution)/shard_map/ppermute | solution.py:45
  172.4 1.9 collective-permute-done.10
  174.3 2.5 %collective-permute-done.12 = f32[4,6,1024]{2,1,0:T(8,128)S(1)} collective-permute-done((f32[4,6,1024]{2,1,0:T(8,128)S(1)}, f32[4,6,1024]{2,1,0:T(8,128)S(1)}, u32[]{:S(2)}, u32[]{:S(2)}) %collective-permute-start.12) | collective-permute-done | bytes 98336 | tf_op jit(solution)/shard_map/ppermute | solution.py:45
  176.8 4.1 %collective-permute-start.13 = (f32[6,1024]{1,0:T(8,128)S(1)}, f32[6,1024]{1,0:T(8,128)S(1)}, u32[]{:S(2)}, u32[]{:S(2)}) collective-permute-start(f32[6,1024]{1,0:T(8,128)S(1)} %get-tuple-element.25), channel_id=1, source_target_pairs={{0,128},{16,144},{32,160},{48,176},{64,192},{80,208},{96,224},{112... | collective-permute-start | bytes 73736 | tf_op jit(solution)/shard_map/ppermute | solution.py:49
  180.9 2.0 collective-permute-start.14
  182.9 3.5 %collective-permute-start.15 = (f32[6,1024]{1,0:T(8,128)S(1)}, f32[6,1024]{1,0:T(8,128)S(1)}, u32[]{:S(2)}, u32[]{:S(2)}) collective-permute-start(f32[6,1024]{1,0:T(8,128)S(1)} %get-tuple-element.24), channel_id=1, source_target_pairs={{0,384},{16,400},{32,416},{48,432},{64,448},{80,464},{96,480},{112... | collective-permute-start | bytes 73736 | tf_op jit(solution)/shard_map/ppermute | solution.py:49
  186.4 1.2 collective-permute-done.14
  187.7 2.9 %collective-permute-done.15 = f32[6,1024]{1,0:T(8,128)S(1)} collective-permute-done((f32[6,1024]{1,0:T(8,128)S(1)}, f32[6,1024]{1,0:T(8,128)S(1)}, u32[]{:S(2)}, u32[]{:S(2)}) %collective-permute-start.15) | collective-permute-done | bytes 24608 | tf_op jit(solution)/shard_map/ppermute | solution.py:49
  191.2 4.6 %input_sum.1 = (bf16[128,1024]{1,0:T(8,128)(2,1)}, bf16[128,1024]{1,0:T(8,128)(2,1)}) custom-call(bf16[16,256,128]{2,1,0:T(8,128)(2,1)S(1)} %all-to-all-done.2.both_ref, bf16[32,16,48,128]{3,2,1,0:T(8,128)(2,1)} %bitcast.63), custom_call_target="tpu_custom_call" | custom-call | tf_op jit(solution)/shard_map/input_sum/pallas_call | solution.py:183
  (36 shorter events, 1.3 us)
Async XLA Ops:
  7.2 117.9 %copy-start.9 = (s32[1,16,4]{1,2,0:T(4,128)S(1)}, s32[1,16,4]{1,2,0:T(4,128)}, u32[]{:S(2)}) copy-start(s32[1,16,4]{1,2,0:T(4,128)} %param.7) | copy-start | bytes 772
  7.2 121.9 %copy-start.8 = (s32[1,16]{1,0:T(1,128)S(1)}, s32[1,16]{1,0:T(1,128)}, u32[]{:S(2)}) copy-start(s32[1,16]{1,0:T(1,128)} %param.8) | copy-start | bytes 196
  8.8 33.9 %all-to-all-start = ((bf16[32,6,1024]{2,1,0:T(8,128)(2,1)}), bf16[32,6,1024]{2,1,0:T(8,128)(2,1)S(1)}, u32[]{:S(2)}, u32[]{:S(2)}) async-start(bf16[32,6,1024]{2,1,0:T(8,128)(2,1)} %broadcast_in_dim.21), calls=%async_computation | async-start | bytes 1048576 | tf_op jit(solution)/shard_map/all_to_all | solution.py:54
  16.5 25.1 %collective-permute-start = (bf16[128,1024]{1,0:T(8,128)(2,1)}, bf16[128,1024]{1,0:T(8,128)(2,1)S(1)}, u32[]{:S(2)}, u32[]{:S(2)}) collective-permute-start(bf16[128,1024]{1,0:T(8,128)(2,1)} %bitcast.66), channel_id=1, source_target_pairs={{0,1},{1,0},{2,3},{3,2},{4,5},{5,4},{6,7},{7,6},{8,9},{9,8},{10,11... | collective-permute-start | bytes 786440 | tf_op jit(solution)/shard_map/ppermute | solution.py:29
  43.6 30.6 %all-to-all-start.1 = ((bf16[16,112,128]{2,1,0:T(8,128)(2,1)}), bf16[16,112,128]{2,1,0:T(8,128)(2,1)S(1)}, u32[]{:S(2)}, u32[]{:S(2)}) async-start(bf16[16,112,128]{2,1,0:T(8,128)(2,1)} %pad_maximum_fusion.1), calls=%async_computation.1 | async-start | bytes 917504 | tf_op jit(solution)/shard_map/all_to_all | solution.py:229
  57.8 133.3 %all-gather.3.cloned.1.call-start = ((), (), s32[]{:S(2)}) async-start(), calls=%async_computation.3 | async-start | bytes 6488064 | tf_op jit(solution)/shard_map/all_gather | solution.py:231
  57.9 25.4 %collective-permute-start.1 = (bf16[256,1024]{1,0:T(8,128)(2,1)S(1)}, bf16[256,1024]{1,0:T(8,128)(2,1)S(1)}, u32[]{:S(2)}, u32[]{:S(2)}) collective-permute-start(bf16[256,1024]{1,0:T(8,128)(2,1)S(1)} %pad_maximum_fusion.refs_0_), channel_id=1, source_target_pairs={{0,2},{1,3},{2,4},{3,5},{4,6},{5,7},{6,8},{7,9},{8,10},{9,11},{10,... | collective-permute-start | bytes 1572872 | tf_op jit(solution)/shard_map/ppermute | solution.py:33
  61.3 22.0 %collective-permute-start.4 = (bf16[256,1024]{1,0:T(8,128)(2,1)S(1)}, bf16[256,1024]{1,0:T(8,128)(2,1)S(1)}, u32[]{:S(2)}, u32[]{:S(2)}) collective-permute-start(bf16[256,1024]{1,0:T(8,128)(2,1)S(1)} %pad_maximum_fusion.refs_0_), channel_id=1, source_target_pairs={{0,14},{1,15},{2,0},{3,1},{4,2},{5,3},{6,4},{7,5},{8,6},{9,7},{10,... | collective-permute-start | bytes 1572872 | tf_op jit(solution)/shard_map/ppermute | solution.py:33
  83.2 58.8 %copy-start = (bf16[256,1024]{1,0:T(8,128)(2,1)}, bf16[256,1024]{1,0:T(8,128)(2,1)S(1)}, u32[]{:S(2)}) copy-start(bf16[256,1024]{1,0:T(8,128)(2,1)S(1)} %collective-permute-done.4.refs_4_) | copy-start | bytes 1572868
  83.3 17.0 %collective-permute-start.2 = (bf16[256,1024]{1,0:T(8,128)(2,1)S(1)}, bf16[256,1024]{1,0:T(8,128)(2,1)S(1)}, u32[]{:S(2)}, u32[]{:S(2)}) collective-permute-start(bf16[256,1024]{1,0:T(8,128)(2,1)S(1)} %collective-permute-done.1.refs_1_), channel_id=1, source_target_pairs={{0,2},{1,3},{2,4},{3,5},{4,6},{5,7},{6,8},{7,9},{8,10},{9,11},{10,... | collective-permute-start | bytes 1572872 | tf_op jit(solution)/shard_map/ppermute | solution.py:33
  86.7 16.6 %collective-permute-start.5 = (bf16[256,1024]{1,0:T(8,128)(2,1)S(1)}, bf16[256,1024]{1,0:T(8,128)(2,1)S(1)}, u32[]{:S(2)}, u32[]{:S(2)}) collective-permute-start(bf16[256,1024]{1,0:T(8,128)(2,1)S(1)} %collective-permute-done.4.refs_4_), channel_id=1, source_target_pairs={{0,14},{1,15},{2,0},{3,1},{4,2},{5,3},{6,4},{7,5},{8,6},{9,7},{10,... | collective-permute-start | bytes 1572872 | tf_op jit(solution)/shard_map/ppermute | solution.py:33
  100.2 16.1 %collective-permute-start.3 = (bf16[256,1024]{1,0:T(8,128)(2,1)S(1)}, bf16[256,1024]{1,0:T(8,128)(2,1)S(1)}, u32[]{:S(2)}, u32[]{:S(2)}) collective-permute-start(bf16[256,1024]{1,0:T(8,128)(2,1)S(1)} %collective-permute-done.2.refs_2_), channel_id=1, source_target_pairs={{0,2},{1,3},{2,4},{3,5},{4,6},{5,7},{6,8},{7,9},{8,10},{9,11},{10,... | collective-permute-start | bytes 1572872 | tf_op jit(solution)/shard_map/ppermute | solution.py:33
  102.4 0.8 copy-start.2
  103.3 15.7 %collective-permute-start.6 = (bf16[256,1024]{1,0:T(8,128)(2,1)S(1)}, bf16[256,1024]{1,0:T(8,128)(2,1)S(1)}, u32[]{:S(2)}, u32[]{:S(2)}) collective-permute-start(bf16[256,1024]{1,0:T(8,128)(2,1)S(1)} %collective-permute-done.5.refs_5_), channel_id=1, source_target_pairs={{0,14},{1,15},{2,0},{3,1},{4,2},{5,3},{6,4},{7,5},{8,6},{9,7},{10,... | collective-permute-start | bytes 1572872 | tf_op jit(solution)/shard_map/ppermute | solution.py:33
  108.1 0.8 copy-start.5
  117.1 9.9 %collective-permute-start.7 = (bf16[128,1024]{1,0:T(8,128)(2,1)}, bf16[128,1024]{1,0:T(8,128)(2,1)}, u32[]{:S(2)}, u32[]{:S(2)}) collective-permute-start(bf16[128,1024]{1,0:T(8,128)(2,1)} %slice.52), channel_id=1, source_target_pairs={{0,2},{1,3},{2,4},{3,5},{4,6},{5,7},{6,8},{7,9},{8,10},{9,11},{10,... | collective-permute-start | bytes 786440 | tf_op jit(solution)/shard_map/ppermute | solution.py:33
  119.7 9.3 %collective-permute-start.8 = (bf16[128,1024]{1,0:T(8,128)(2,1)}, bf16[128,1024]{1,0:T(8,128)(2,1)}, u32[]{:S(2)}, u32[]{:S(2)}) collective-permute-start(bf16[128,1024]{1,0:T(8,128)(2,1)} %slice.53), channel_id=1, source_target_pairs={{0,14},{1,15},{2,0},{3,1},{4,2},{5,3},{6,4},{7,5},{8,6},{9,7},{10,... | collective-permute-start | bytes 786440 | tf_op jit(solution)/shard_map/ppermute | solution.py:33
  129.0 1.0 copy-start.3
  130.1 1.0 copy-start.6
  142.0 49.1 %all-to-all-start.2 = ((bf16[16,256,128]{2,1,0:T(8,128)(2,1)}), bf16[16,256,128]{2,1,0:T(8,128)(2,1)S(1)}, u32[]{:S(2)}, u32[]{:S(2)}) async-start(bf16[16,256,128]{2,1,0:T(8,128)(2,1)} %attend.1.dqkv_ref), calls=%async_computation.2 | async-start | bytes 2097152 | tf_op jit(solution)/shard_map/all_to_all | solution.py:236
  153.2 1.0 copy-start.1
  154.3 1.0 copy-start.4
  155.3 1.0 copy-start.7
  158.9 3.8 %collective-permute-start.9 = (f32[4,4,6,1024]{3,2,1,0:T(8,128)S(1)}, f32[4,4,6,1024]{3,2,1,0:T(8,128)S(1)}, u32[]{:S(2)}, u32[]{:S(2)}) collective-permute-start(f32[4,4,6,1024]{3,2,1,0:T(8,128)S(1)} %slice_bitcast_fusion), channel_id=1, source_target_pairs={{0,16},{16,0},{32,48},{48,32},{64,80},{80,64},{96,112},{112,96},{1... | collective-permute-start | bytes 1179656 | tf_op jit(solution)/shard_map/ppermute | solution.py:37
  162.8 11.5 %collective-permute-start.10 = (f32[4,6,1024]{2,1,0:T(8,128)S(1)}, f32[4,6,1024]{2,1,0:T(8,128)S(1)}, u32[]{:S(2)}, u32[]{:S(2)}) collective-permute-start(f32[4,6,1024]{2,1,0:T(8,128)S(1)} %get-tuple-element.22), channel_id=1, source_target_pairs={{0,32},{16,48},{32,64},{48,80},{64,96},{80,112},{96,0},{112,16},{1... | collective-permute-start | bytes 294920 | tf_op jit(solution)/shard_map/ppermute | solution.py:45
  164.7 9.5 %collective-permute-start.11 = (f32[4,6,1024]{2,1,0:T(8,128)S(1)}, f32[4,6,1024]{2,1,0:T(8,128)S(1)}, u32[]{:S(2)}, u32[]{:S(2)}) collective-permute-start(f32[4,6,1024]{2,1,0:T(8,128)S(1)} %get-tuple-element.20), channel_id=1, source_target_pairs={{0,64},{16,80},{32,96},{48,112},{64,0},{80,16},{96,32},{112,48},{1... | collective-permute-start | bytes 294920 | tf_op jit(solution)/shard_map/ppermute | solution.py:45
  169.4 7.3 %collective-permute-start.12 = (f32[4,6,1024]{2,1,0:T(8,128)S(1)}, f32[4,6,1024]{2,1,0:T(8,128)S(1)}, u32[]{:S(2)}, u32[]{:S(2)}) collective-permute-start(f32[4,6,1024]{2,1,0:T(8,128)S(1)} %get-tuple-element.21), channel_id=1, source_target_pairs={{0,96},{16,112},{32,0},{48,16},{64,32},{80,48},{96,64},{112,80},{1... | collective-permute-start | bytes 294920 | tf_op jit(solution)/shard_map/ppermute | solution.py:45
  176.8 9.6 %collective-permute-start.13 = (f32[6,1024]{1,0:T(8,128)S(1)}, f32[6,1024]{1,0:T(8,128)S(1)}, u32[]{:S(2)}, u32[]{:S(2)}) collective-permute-start(f32[6,1024]{1,0:T(8,128)S(1)} %get-tuple-element.25), channel_id=1, source_target_pairs={{0,128},{16,144},{32,160},{48,176},{64,192},{80,208},{96,224},{112... | collective-permute-start | bytes 73736 | tf_op jit(solution)/shard_map/ppermute | solution.py:49
  180.9 6.7 %collective-permute-start.14 = (f32[6,1024]{1,0:T(8,128)S(1)}, f32[6,1024]{1,0:T(8,128)S(1)}, u32[]{:S(2)}, u32[]{:S(2)}) collective-permute-start(f32[6,1024]{1,0:T(8,128)S(1)} %get-tuple-element.23), channel_id=1, source_target_pairs={{0,256},{16,272},{32,288},{48,304},{64,320},{80,336},{96,352},{112... | collective-permute-start | bytes 73736 | tf_op jit(solution)/shard_map/ppermute | solution.py:49
  182.9 7.6 %collective-permute-start.15 = (f32[6,1024]{1,0:T(8,128)S(1)}, f32[6,1024]{1,0:T(8,128)S(1)}, u32[]{:S(2)}, u32[]{:S(2)}) collective-permute-start(f32[6,1024]{1,0:T(8,128)S(1)} %get-tuple-element.24), channel_id=1, source_target_pairs={{0,384},{16,400},{32,416},{48,432},{64,448},{80,464},{96,480},{112... | collective-permute-start | bytes 73736 | tf_op jit(solution)/shard_map/ppermute | solution.py:49
Sparse Core Ops, SparseCore 0:
  83.4 65.1 all-gather.2

commit v3 on v2

--- a/solution.py
+++ b/solution.py
@@ -54,16 +54,46 @@
     return lax.all_to_all(copies, axis, 0, 0, tiled=True)
 
 
-def attend(nblk, order_ref, list_ref, count_ref, *refs):
+def tiles_of(blocks):
+    own, flip, r1, l1, r2, r3, l2, l3, r4, l4, r5, l5 = blocks
+    half = TILE // 2
+    yield from (own[...], flip[...], r1[...], l1[...])
+    for pair in (r2, r3, l2, l3):
+        yield pair[...]
+    yield r4[:TILE]
+    yield l4[half:]
+    yield jnp.concatenate([r4[TILE:], l4[:half]], axis=0)
+    yield jnp.concatenate([r5[...], l5[...]], axis=0)
+
+
+def tile_places(z, y_hi):
+    steps = [(0, 0), (0, 1), (-1, 0), (1, 0), (-1, 1), (-2, 0), (-2, 1), (-3, 0)]
+    steps += [(2, 0), (1, 1), (3, 0), (2, 1), (-3, 1), (3, 1), (4, 0), (4, 1)]
+    places = [lax.rem(z + k + ZN, ZN) * YH + lax.rem(y_hi + j, YH) for k, j in steps]
+    return jnp.stack(places).astype(jnp.int32)
+
+
+def gather_scene(own):
+    flip, r1, l1 = flip_y(own), shift_z(own, 1), shift_z(own, -1)
+    r2 = shift_z(jnp.concatenate([flip, r1], axis=0), 1)
+    l2 = shift_z(jnp.concatenate([l1, flip], axis=0), -1)
+    r3, l3 = shift_z(r2, 1), shift_z(l2, -1)
+    half = TILE // 2
+    r4, l4 = shift_z(r3[: TILE + half], 1), shift_z(l3[half:], -1)
+    r5, l5 = shift_z(r4[:half], 1), shift_z(l4[TILE:], -1)
+    return own, flip, r1, l1, r2, r3, l2, l3, r4, l4, r5, l5
+
+
+def attend(nblk, here_ref, order_ref, list_ref, count_ref, *refs):
     blocks = refs[:nblk]
-    w_ref, cot_ref, out_ref, kv_rows, kv_cols, q_cols, acc = refs[nblk:]
+    w_ref, cot_ref, out_ref, sum_ref, kv_rows, kv_cols, q_cols, acc = refs[nblk:]
     scale = HEAD_DIM ** (-0.5)
     tiles = kv_rows.shape[0]
     w = w_ref[...]
     w = jnp.concatenate([w[HEAD_DIM:], w[:HEAD_DIM]], axis=0)
     slot = 0
-    for blk in blocks:
-        qkv = dot(blk[...], w, 1, 1).astype(BF)
+    for blk in tiles_of(blocks):
+        qkv = dot(blk, w, 1, 1).astype(BF)
         for r in range(blk.shape[0] // TILE):
             tile = order_ref[slot]
             slot += 1
@@ -109,14 +139,33 @@
     for a in range(tiles):
         out_ref[a, HEAD_DIM : 3 * HEAD_DIM, :] = acc[a].astype(BF).T
 
-
-def attention(order, tile_list, counts, blocks, w_head, cot_t):
+    total, slot = None, 0
+    for blk in tiles_of(blocks):
+        n = blk.shape[0] // TILE
+        left = [out_ref[order_ref[slot + r], : 3 * HEAD_DIM, :] for r in range(n)]
+        slot += n
+        part = dot(jnp.concatenate(left, axis=1), blk, 1, 0)
+        total = part if total is None else total + part
+    rows = sum_ref.shape[3]
+    core, x, y = here_ref[0], here_ref[1], here_ref[2]
+    for i in range(DP):
+        c = lax.rem(i % CORES + CORES - core, CORES)
+        u = lax.rem(i // CORES % XN + XN - x, XN)
+        v = lax.rem(i // (CORES * XN) + YL - y, YL)
+        sum_ref[c, u, v] = total[i * rows : (i + 1) * rows]
+
+
+def attention(here, order, tile_list, counts, blocks, w_head, cot_t):
     tiles = tile_list.shape[0]
+    rows, depth = w_head.shape[0] // DP, w_head.shape[1]
     return pl.pallas_call(
         functools.partial(attend, len(blocks)),
-        out_shape=jax.ShapeDtypeStruct((tiles, 4 * HEAD_DIM, TILE), BF),
-        in_specs=[SM, SM, SM] + [VM] * (len(blocks) + 2),
-        out_specs=VM,
+        out_shape=(
+            jax.ShapeDtypeStruct((tiles, 4 * HEAD_DIM, TILE), BF),
+            jax.ShapeDtypeStruct((CORES, XN, YL, rows, depth), F32),
+        ),
+        in_specs=[SM, SM, SM, SM] + [VM] * (len(blocks) + 2),
+        out_specs=(VM, VM),
         scratch_shapes=[
             pltpu.VMEM((tiles, TILE, 2 * HEAD_DIM), BF),
             pltpu.VMEM((tiles, 2 * HEAD_DIM, TILE), BF),
@@ -125,37 +174,7 @@
         ],
         compiler_params=PARAMS,
         name="attend",
-    )(order, tile_list, counts, *blocks, w_head, cot_t)
-
-
-def weight_sum(nblk, here_ref, order_ref, dqkv_ref, *refs):
-    blocks, out_ref = refs[:nblk], refs[nblk]
-    total, slot = None, 0
-    for blk in blocks:
-        n = blk.shape[0] // TILE
-        left = [dqkv_ref[order_ref[slot + r], : 3 * HEAD_DIM, :] for r in range(n)]
-        slot += n
-        part = dot(jnp.concatenate(left, axis=1), blk[...], 1, 0)
-        total = part if total is None else total + part
-    rows = out_ref.shape[3]
-    core, x, y = here_ref[0], here_ref[1], here_ref[2]
-    for i in range(DP):
-        c = lax.rem(i % CORES + CORES - core, CORES)
-        u = lax.rem(i // CORES % XN + XN - x, XN)
-        v = lax.rem(i // (CORES * XN) + YL - y, YL)
-        out_ref[c, u, v] = total[i * rows : (i + 1) * rows]
-
-
-def weight_grad(here, order, dqkv_t, blocks):
-    rows, depth = 3 * HEAD_DIM // DP, blocks[0].shape[1]
-    return pl.pallas_call(
-        functools.partial(weight_sum, len(blocks)),
-        out_shape=jax.ShapeDtypeStruct((CORES, XN, YL, rows, depth), F32),
-        in_specs=[SM, SM, VM] + [VM] * len(blocks),
-        out_specs=VM,
-        compiler_params=PARAMS,
-        name="weight_sum",
-    )(here, order, dqkv_t, *blocks)
+    )(here, order, tile_list, counts, *blocks, w_head, cot_t)
 
 
 def input_sum(both_ref, w_ref, att_ref, out_ref):
@@ -202,37 +221,27 @@
     z, y_hi = seq // YH, seq % YH
     grad_scale = (DP * tiles * TILE) ** (-0.5)
 
-    w_head = spread(qkv_weight[0], "dp", DP).reshape(3 * HEAD_DIM, depth)
+    blocks = gather_scene(tokens[0])
+    flip, r1, l1, r2, r3, l2, l3 = blocks[1:8]
+
+    w_own, _ = lax.optimization_barrier((qkv_weight[0], (flip, r1, l1)))
+    w_head = spread(w_own, "dp", DP).reshape(3 * HEAD_DIM, depth)
     chunk = 3 * HEAD_DIM // XN
     w_block = lax.dynamic_slice(
         w_head, (x * chunk, (y_lo * CORES + core) * TILE), (chunk, TILE)
     )
 
-    own = tokens[0]
-    pair = jnp.concatenate([own, flip_y(own)], axis=0)
-    right, left = [pair], [pair]
-    for _ in range(ZN // 2 - 1):
-        right.append(shift_z(right[-1], 1))
-        left.append(shift_z(left[-1], -1))
-    far = [shift_z(right[-1][:TILE], 1), shift_z(left[-1][TILE:], -1)]
-    blocks = right + left[1:] + far
-    zs = [(0, 0), (0, 1)]
-    zs += [(-k, j) for k in range(1, ZN // 2) for j in range(2)]
-    zs += [(k, j) for k in range(1, ZN // 2) for j in range(2)]
-    zs += [(ZN // 2, 0), (ZN // 2, 1)]
-    order = jnp.stack([(z + k) % ZN * YH + (y_hi + j) % YH for k, j in zs]).astype(jnp.int32)
-
     cot_t = cotangent[0].T.reshape(heads, HEAD_DIM, TILE)
     copies = jnp.broadcast_to(w_block[None], (heads, *w_block.shape))
     mixed = jnp.concatenate([cot_t, copies], axis=1)
-    mixed, _ = lax.optimization_barrier((mixed, pair))
+    mixed, _ = lax.optimization_barrier((mixed, (r2, l2)))
     mixed = lax.all_to_all(mixed, "seq", 0, 0, tiled=True)
-    w_seq, _ = lax.optimization_barrier((mixed[:, HEAD_DIM:], (right[1], left[1])))
+    w_seq, _ = lax.optimization_barrier((mixed[:, HEAD_DIM:], (r3, l3)))
     w_all = lax.all_gather(w_seq, "dp", axis=0)
 
-    both = attention(order, key_tiles[0], key_counts[0], blocks, w_head, mixed)
     here = jnp.stack([core, x, y_lo]).astype(jnp.int32)
-    sums = weight_grad(here, order, both, blocks)
+    order = tile_places(z, y_hi)
+    both, sums = attention(here, order, key_tiles[0], key_counts[0], blocks, w_head, mixed)
     both = lax.all_to_all(both, "seq", 0, 0, tiled=True)
 
     sums = sums[0] + swap_core(sums[1])

time: 204 us -> 197 us (0.966)
  waiting for transfers between devices: 66.7 us -> 53.6 us
  starting transfers between devices: 88.6 us -> 97.4 us
  local copies, waits for them, and re-layouts: 12.8 us -> 9.97 us
    ppermute x1, waiting for transfers between devices: 17.6 us -> 2.11 us  [flip_y(): return lax.ppermute(x, 'seq', [(s, s ^ 1) for s in range(SEQ)])]
    ppermute x8 -> x10, starting transfers between devices: 28.2 us -> 41 us  [shift_z(): return lax.ppermute(x, 'seq', [(s, (s + YH * k) % SEQ) for s in range(SEQ)])]
    unnamed x21 -> x13, local copies, waits for them, and re-layouts: 7.51 us -> 3.74 us
    all_to_all x1, starting transfers between devices: 14.2 us -> 10.7 us  [shards(): mixed = lax.all_to_all(mixed, 'seq', 0, 0, tiled=True)]
    ppermute x8 -> x10, waiting for transfers between devices: 29.4 us -> 31.7 us  [shift_z(): return lax.ppermute(x, 'seq', [(s, (s + YH * k) % SEQ) for s in range(SEQ)])]
    pallas_call x2 -> x1, Pallas kernels: 13.4 us -> 12.8 us  [attention(): pl.pallas_call(functools.partial(attend, len(blocks)), out_shape=(jax.Sha...]
  transfers between devices with their start and end apart: 20 -> 22, of which waited for: 12 -> 16; matrix products, arithmetic and copies ran while one was open for 3% -> 4% of each run, Pallas kernels for 7% -> 7%
where the time goes in v3:
time: 197 us; the launch traced here: 196 us
  starting transfers between devices  97.4 us (49%)
  waiting for transfers between devices  53.6 us (27%)
  Pallas kernels  17.4 us (9%)
  between operations  14.5 us (7%)
  local copies, waits for them, and re-layouts  9.97 us (5%)
  other arithmetic  2.94 us (1%)
    ppermute x10, starting transfers between devices, shift_z(): return lax.ppermute(x, 'seq', [(s, (s + YH * k) % SEQ) for s in range(SEQ)])  41 us
    ppermute x10, waiting for transfers between devices, shift_z(): return lax.ppermute(x, 'seq', [(s, (s + YH * k) % SEQ) for s in range(SEQ)])  31.7 us
    pallas_call x1, Pallas kernels, attention(): pl.pallas_call(functools.partial(attend, len(blocks)), out_shape=(jax.Sha...  12.8 us
    all_to_all x1, starting transfers between devices, shards(): both = lax.all_to_all(both, 'seq', 0, 0, tiled=True)  11.5 us
    ppermute x3, starting transfers between devices, shift_x(): return lax.ppermute(x, 'dp', pairs)  11.4 us
    all_to_all x1, starting transfers between devices, shards(): mixed = lax.all_to_all(mixed, 'seq', 0, 0, tiled=True)  10.7 us
    ppermute x3, starting transfers between devices, shift_y(): lax.ppermute(x, 'dp', [(d, (d + k * XN * CORES) % DP) for d in range(DP)])  8.23 us
    all_to_all x1, waiting for transfers between devices, shards(): mixed = lax.all_to_all(mixed, 'seq', 0, 0, tiled=True)  8.01 us
  transfers between devices with their start and end apart: 22, of which 16 were waited for; matrix products, arithmetic and copies ran while one was open for 4% of the time, Pallas kernels for 7%

profile of v3, /device:TPU:56, one launch (start us, length us, event | category | flops | bytes accessed | tf_op | source)
XLA Modules:
  0.0 195.8 jit_solution(9611969219116195377)
XLA Ops:
  7.2 4.8 %collective-permute-start = (bf16[128,1024]{1,0:T(8,128)(2,1)}, bf16[128,1024]{1,0:T(8,128)(2,1)S(1)}, u32[]{:S(2)}, u32[]{:S(2)}) collective-permute-start(bf16[128,1024]{1,0:T(8,128)(2,1)} %bitcast.60), channel_id=1, source_target_pairs={{0,1},{1,0},{2,3},{3,2},{4,5},{5,4},{6,7},{7,6},{8,9},{9,8},{10,11... | collective-permute-start | bytes 786440 | tf_op jit(solution)/shard_map/ppermute | solution.py:29
  12.0 4.3 %collective-permute-start.1 = (bf16[128,1024]{1,0:T(8,128)(2,1)}, bf16[128,1024]{1,0:T(8,128)(2,1)S(1)}, u32[]{:S(2)}, u32[]{:S(2)}) collective-permute-start(bf16[128,1024]{1,0:T(8,128)(2,1)} %bitcast.61), channel_id=1, source_target_pairs={{0,2},{1,3},{2,4},{3,5},{4,6},{5,7},{6,8},{7,9},{8,10},{9,11},{10,... | collective-permute-start | bytes 786440 | tf_op jit(solution)/shard_map/ppermute | solution.py:33
  16.3 8.6 %collective-permute-start.2 = (bf16[128,1024]{1,0:T(8,128)(2,1)}, bf16[128,1024]{1,0:T(8,128)(2,1)S(1)}, u32[]{:S(2)}, u32[]{:S(2)}) collective-permute-start(bf16[128,1024]{1,0:T(8,128)(2,1)} %bitcast.62), channel_id=1, source_target_pairs={{0,14},{1,15},{2,0},{3,1},{4,2},{5,3},{6,4},{7,5},{8,6},{9,7},{10,... | collective-permute-start | bytes 786440 | tf_op jit(solution)/shard_map/ppermute | solution.py:33
  24.9 2.1 %collective-permute-done.refs_1_ = bf16[128,1024]{1,0:T(8,128)(2,1)S(1)} collective-permute-done((bf16[128,1024]{1,0:T(8,128)(2,1)}, bf16[128,1024]{1,0:T(8,128)(2,1)S(1)}, u32[]{:S(2)}, u32[]{:S(2)}) %collective-permute-start) | collective-permute-done | bytes 262176 | tf_op jit(solution)/shard_map/ppermute | solution.py:29
  27.0 2.2 %collective-permute-done.1.refs_2_ = bf16[128,1024]{1,0:T(8,128)(2,1)S(1)} collective-permute-done((bf16[128,1024]{1,0:T(8,128)(2,1)}, bf16[128,1024]{1,0:T(8,128)(2,1)S(1)}, u32[]{:S(2)}, u32[]{:S(2)}) %collective-permute-start.1) | collective-permute-done | bytes 262176 | tf_op jit(solution)/shard_map/ppermute | solution.py:33
  29.2 1.3 collective-permute-done.2.refs_3_
  30.5 1.6 broadcast_in_dim.8
  32.1 7.8 %all-to-all-start = ((bf16[32,6,1024]{2,1,0:T(8,128)(2,1)}), bf16[32,6,1024]{2,1,0:T(8,128)(2,1)S(1)}, u32[]{:S(2)}, u32[]{:S(2)}) async-start(bf16[32,6,1024]{2,1,0:T(8,128)(2,1)} %broadcast_in_dim.8), calls=%async_computation | async-start | bytes 1048576 | tf_op jit(solution)/shard_map/all_to_all | solution.py:54
  39.9 0.9 pad_maximum_fusion.1
  40.8 1.9 collective-permute-start.3
  42.7 7.5 %collective-permute-start.5 = (bf16[256,1024]{1,0:T(8,128)(2,1)S(1)}, bf16[256,1024]{1,0:T(8,128)(2,1)}, u32[]{:S(2)}, u32[]{:S(2)}) collective-permute-start(bf16[256,1024]{1,0:T(8,128)(2,1)S(1)} %get-tuple-element.29), channel_id=1, source_target_pairs={{0,14},{1,15},{2,0},{3,1},{4,2},{5,3},{6,4},{7,5},{8,6},{9,7},{10,... | collective-permute-start | bytes 1572872 | tf_op jit(solution)/shard_map/ppermute | solution.py:33
  50.2 1.1 copy.14
  51.4 1.8 all-to-all-done
  53.4 0.8 pad_maximum_fusion.2
  54.2 6.5 %collective-permute-done.3.refs_4_ = bf16[256,1024]{1,0:T(8,128)(2,1)S(1)} collective-permute-done((bf16[256,1024]{1,0:T(8,128)(2,1)}, bf16[256,1024]{1,0:T(8,128)(2,1)S(1)}, u32[]{:S(2)}, u32[]{:S(2)}) %collective-permute-start.3) | collective-permute-done | bytes 524320 | tf_op jit(solution)/shard_map/ppermute | solution.py:33
  60.7 1.0 collective-permute-done.5.refs_6_
  61.7 10.7 %all-to-all-start.1 = ((bf16[16,112,128]{2,1,0:T(8,128)(2,1)}), bf16[16,112,128]{2,1,0:T(8,128)(2,1)S(1)}, u32[]{:S(2)}, u32[]{:S(2)}) async-start(bf16[16,112,128]{2,1,0:T(8,128)(2,1)} %pad_maximum_fusion.2), calls=%async_computation.1 | async-start | bytes 917504 | tf_op jit(solution)/shard_map/all_to_all | solution.py:238
  72.4 4.6 %collective-permute-start.6 = (bf16[256,1024]{1,0:T(8,128)(2,1)}, bf16[256,1024]{1,0:T(8,128)(2,1)S(1)}, u32[]{:S(2)}, u32[]{:S(2)}) collective-permute-start(bf16[256,1024]{1,0:T(8,128)(2,1)} %collective-permute-done.5.refs_6_), channel_id=1, source_target_pairs={{0,14},{1,15},{2,0},{3,1},{4,2},{5,3},{6,4},{7,5},{8,6},{9,7},{10,... | collective-permute-start | bytes 1572872 | tf_op jit(solution)/shard_map/ppermute | solution.py:33
  77.0 1.9 collective-permute-start.4
  78.9 8.0 %all-to-all-done.1.refs_13_ = bf16[16,112,128]{2,1,0:T(8,128)(2,1)S(1)} async-done(((bf16[16,112,128]{2,1,0:T(8,128)(2,1)}), bf16[16,112,128]{2,1,0:T(8,128)(2,1)S(1)}, u32[]{:S(2)}, u32[]{:S(2)}) %all-to-all-start.1) | async-done | bytes 458784 | tf_op jit(solution)/shard_map/all_to_all | solution.py:238
  86.9 0.7 slice.64
  87.6 7.5 %collective-permute-done.6.refs_7_ = bf16[256,1024]{1,0:T(8,128)(2,1)S(1)} collective-permute-done((bf16[256,1024]{1,0:T(8,128)(2,1)}, bf16[256,1024]{1,0:T(8,128)(2,1)S(1)}, u32[]{:S(2)}, u32[]{:S(2)}) %collective-permute-start.6) | collective-permute-done | bytes 524320 | tf_op jit(solution)/shard_map/ppermute | solution.py:33
  95.7 3.4 %collective-permute-start.8 = (bf16[192,1024]{1,0:T(8,128)(2,1)S(1)}, bf16[192,1024]{1,0:T(8,128)(2,1)S(1)}, u32[]{:S(2)}, u32[]{:S(2)}) collective-permute-start(bf16[192,1024]{1,0:T(8,128)(2,1)S(1)} %slice.61), channel_id=1, source_target_pairs={{0,14},{1,15},{2,0},{3,1},{4,2},{5,3},{6,4},{7,5},{8,6},{9,7},{10,... | collective-permute-start | bytes 1179656 | tf_op jit(solution)/shard_map/ppermute | solution.py:33
  99.2 2.5 %collective-permute-start.7 = (bf16[192,1024]{1,0:T(8,128)(2,1)S(1)}, bf16[192,1024]{1,0:T(8,128)(2,1)S(1)}, u32[]{:S(2)}, u32[]{:S(2)}) collective-permute-start(bf16[192,1024]{1,0:T(8,128)(2,1)S(1)} %slice.60), channel_id=1, source_target_pairs={{0,2},{1,3},{2,4},{3,5},{4,6},{5,7},{6,8},{7,9},{8,10},{9,11},{10,... | collective-permute-start | bytes 1179656 | tf_op jit(solution)/shard_map/ppermute | solution.py:33
  101.6 6.7 %collective-permute-done.8.refs_9_ = bf16[192,1024]{1,0:T(8,128)(2,1)S(1)} collective-permute-done((bf16[192,1024]{1,0:T(8,128)(2,1)S(1)}, bf16[192,1024]{1,0:T(8,128)(2,1)S(1)}, u32[]{:S(2)}, u32[]{:S(2)}) %collective-permute-start.8) | collective-permute-done | bytes 393248 | tf_op jit(solution)/shard_map/ppermute | solution.py:33
  109.0 4.5 %collective-permute-start.10 = (bf16[64,1024]{1,0:T(8,128)(2,1)}, bf16[64,1024]{1,0:T(8,128)(2,1)}, u32[]{:S(2)}, u32[]{:S(2)}) collective-permute-start(bf16[64,1024]{1,0:T(8,128)(2,1)} %slice.63), channel_id=1, source_target_pairs={{0,14},{1,15},{2,0},{3,1},{4,2},{5,3},{6,4},{7,5},{8,6},{9,7},{10,... | collective-permute-start | bytes 393224 | tf_op jit(solution)/shard_map/ppermute | solution.py:33
  114.1 1.9 collective-permute-start.9
  116.4 6.1 %collective-permute-done.9.refs_10_ = bf16[64,1024]{1,0:T(8,128)(2,1)} collective-permute-done((bf16[64,1024]{1,0:T(8,128)(2,1)}, bf16[64,1024]{1,0:T(8,128)(2,1)}, u32[]{:S(2)}, u32[]{:S(2)}) %collective-permute-start.9) | collective-permute-done | bytes 131104 | tf_op jit(solution)/shard_map/ppermute | solution.py:33
  122.5 1.1 copy-done.2
  123.6 0.9 copy-done.3
  124.5 12.8 %attend.1 = (bf16[16,256,128]{2,1,0:T(8,128)(2,1)S(1)}, f32[2,4,4,6,1024]{4,3,2,1,0:T(8,128)}) custom-call(s32[3]{0:T(128)S(1)} %pad_add_fusion.here_ref, s32[16]{0:T(128)S(1)} %stack.83.order_ref, s32[16,4]{1,0:T(8,128)S(1)} %copy.15.list_ref, s32[16]{0:T(128)S(1)} %bitcast.64, bf16[128,1024]{1,0:T(8,128)(2,1)S(1)} %bitcast.63, ...), custom_call_target="tpu_custom_call" | custom-call | tf_op jit(solution)/shard_map/attend/pallas_call | solution.py:161
  137.3 1.1 copy-done
  138.4 11.5 %all-to-all-start.2 = ((bf16[16,256,128]{2,1,0:T(8,128)(2,1)}), bf16[16,256,128]{2,1,0:T(8,128)(2,1)S(1)}, u32[]{:S(2)}, u32[]{:S(2)}) async-start(bf16[16,256,128]{2,1,0:T(8,128)(2,1)} %copy-done), calls=%async_computation.2 | async-start | bytes 2097152 | tf_op jit(solution)/shard_map/all_to_all | solution.py:245
  149.9 1.1 slice_bitcast_fusion
  151.0 1.9 collective-permute-start.11
  152.9 1.9 collective-permute-done.11
  154.8 1.1 bitcast_add_fusion
  156.0 3.4 %collective-permute-start.12 = (f32[4,6,1024]{2,1,0:T(8,128)S(1)}, f32[4,6,1024]{2,1,0:T(8,128)S(1)}, u32[]{:S(2)}, u32[]{:S(2)}) collective-permute-start(f32[4,6,1024]{2,1,0:T(8,128)S(1)} %get-tuple-element.28), channel_id=1, source_target_pairs={{0,32},{16,48},{32,64},{48,80},{64,96},{80,112},{96,0},{112,16},{1... | collective-permute-start | bytes 294920 | tf_op jit(solution)/shard_map/ppermute | solution.py:45
  159.4 4.7 %collective-permute-start.13 = (f32[4,6,1024]{2,1,0:T(8,128)S(1)}, f32[4,6,1024]{2,1,0:T(8,128)S(1)}, u32[]{:S(2)}, u32[]{:S(2)}) collective-permute-start(f32[4,6,1024]{2,1,0:T(8,128)S(1)} %get-tuple-element.26), channel_id=1, source_target_pairs={{0,64},{16,80},{32,96},{48,112},{64,0},{80,16},{96,32},{112,48},{1... | collective-permute-start | bytes 294920 | tf_op jit(solution)/shard_map/ppermute | solution.py:45
  164.0 3.4 %collective-permute-start.14 = (f32[4,6,1024]{2,1,0:T(8,128)S(1)}, f32[4,6,1024]{2,1,0:T(8,128)S(1)}, u32[]{:S(2)}, u32[]{:S(2)}) collective-permute-start(f32[4,6,1024]{2,1,0:T(8,128)S(1)} %get-tuple-element.27), channel_id=1, source_target_pairs={{0,96},{16,112},{32,0},{48,16},{64,32},{80,48},{96,64},{112,80},{1... | collective-permute-start | bytes 294920 | tf_op jit(solution)/shard_map/ppermute | solution.py:45
  167.4 1.3 collective-permute-done.13
  168.7 2.2 %collective-permute-done.14 = f32[4,6,1024]{2,1,0:T(8,128)S(1)} collective-permute-done((f32[4,6,1024]{2,1,0:T(8,128)S(1)}, f32[4,6,1024]{2,1,0:T(8,128)S(1)}, u32[]{:S(2)}, u32[]{:S(2)}) %collective-permute-start.14) | collective-permute-done | bytes 98336 | tf_op jit(solution)/shard_map/ppermute | solution.py:45
  171.0 2.4 %collective-permute-start.15 = (f32[6,1024]{1,0:T(8,128)S(1)}, f32[6,1024]{1,0:T(8,128)S(1)}, u32[]{:S(2)}, u32[]{:S(2)}) collective-permute-start(f32[6,1024]{1,0:T(8,128)S(1)} %get-tuple-element.33), channel_id=1, source_target_pairs={{0,128},{16,144},{32,160},{48,176},{64,192},{80,208},{96,224},{112... | collective-permute-start | bytes 73736 | tf_op jit(solution)/shard_map/ppermute | solution.py:49
  173.3 2.8 %collective-permute-start.16 = (f32[6,1024]{1,0:T(8,128)S(1)}, f32[6,1024]{1,0:T(8,128)S(1)}, u32[]{:S(2)}, u32[]{:S(2)}) collective-permute-start(f32[6,1024]{1,0:T(8,128)S(1)} %get-tuple-element.31), channel_id=1, source_target_pairs={{0,256},{16,272},{32,288},{48,304},{64,320},{80,336},{96,352},{112... | collective-permute-start | bytes 73736 | tf_op jit(solution)/shard_map/ppermute | solution.py:49
  176.2 3.1 %collective-permute-start.17 = (f32[6,1024]{1,0:T(8,128)S(1)}, f32[6,1024]{1,0:T(8,128)S(1)}, u32[]{:S(2)}, u32[]{:S(2)}) collective-permute-start(f32[6,1024]{1,0:T(8,128)S(1)} %get-tuple-element.32), channel_id=1, source_target_pairs={{0,384},{16,400},{32,416},{48,432},{64,448},{80,464},{96,480},{112... | collective-permute-start | bytes 73736 | tf_op jit(solution)/shard_map/ppermute | solution.py:49
  179.2 0.8 collective-permute-done.16
  180.0 3.7 %collective-permute-done.17 = f32[6,1024]{1,0:T(8,128)S(1)} collective-permute-done((f32[6,1024]{1,0:T(8,128)S(1)}, f32[6,1024]{1,0:T(8,128)S(1)}, u32[]{:S(2)}, u32[]{:S(2)}) %collective-permute-start.17) | collective-permute-done | bytes 24608 | tf_op jit(solution)/shard_map/ppermute | solution.py:49
  184.4 4.6 %input_sum.1 = (bf16[128,1024]{1,0:T(8,128)(2,1)}, bf16[128,1024]{1,0:T(8,128)(2,1)}) custom-call(bf16[16,256,128]{2,1,0:T(8,128)(2,1)S(1)} %all-to-all-done.2.both_ref, bf16[32,16,48,128]{3,2,1,0:T(8,128)(2,1)} %bitcast.65), custom_call_target="tpu_custom_call" | custom-call | tf_op jit(solution)/shard_map/input_sum/pallas_call | solution.py:202
  (33 shorter events, 3.1 us)
Async XLA Ops:
  7.2 109.0 %copy-start.5 = (s32[1,16,4]{1,2,0:T(4,128)S(1)}, s32[1,16,4]{1,2,0:T(4,128)}, u32[]{:S(2)}) copy-start(s32[1,16,4]{1,2,0:T(4,128)} %param.7) | copy-start | bytes 772
  7.2 115.3 %copy-start.4 = (s32[1,16]{1,0:T(1,128)S(1)}, s32[1,16]{1,0:T(1,128)}, u32[]{:S(2)}) copy-start(s32[1,16]{1,0:T(1,128)} %param.8) | copy-start | bytes 196
  7.2 19.9 %collective-permute-start = (bf16[128,1024]{1,0:T(8,128)(2,1)}, bf16[128,1024]{1,0:T(8,128)(2,1)S(1)}, u32[]{:S(2)}, u32[]{:S(2)}) collective-permute-start(bf16[128,1024]{1,0:T(8,128)(2,1)} %bitcast.60), channel_id=1, source_target_pairs={{0,1},{1,0},{2,3},{3,2},{4,5},{5,4},{6,7},{7,6},{8,9},{9,8},{10,11... | collective-permute-start | bytes 786440 | tf_op jit(solution)/shard_map/ppermute | solution.py:29
  12.0 17.2 %collective-permute-start.1 = (bf16[128,1024]{1,0:T(8,128)(2,1)}, bf16[128,1024]{1,0:T(8,128)(2,1)S(1)}, u32[]{:S(2)}, u32[]{:S(2)}) collective-permute-start(bf16[128,1024]{1,0:T(8,128)(2,1)} %bitcast.61), channel_id=1, source_target_pairs={{0,2},{1,3},{2,4},{3,5},{4,6},{5,7},{6,8},{7,9},{8,10},{9,11},{10,... | collective-permute-start | bytes 786440 | tf_op jit(solution)/shard_map/ppermute | solution.py:33
  16.3 14.2 %collective-permute-start.2 = (bf16[128,1024]{1,0:T(8,128)(2,1)}, bf16[128,1024]{1,0:T(8,128)(2,1)S(1)}, u32[]{:S(2)}, u32[]{:S(2)}) collective-permute-start(bf16[128,1024]{1,0:T(8,128)(2,1)} %bitcast.62), channel_id=1, source_target_pairs={{0,14},{1,15},{2,0},{3,1},{4,2},{5,3},{6,4},{7,5},{8,6},{9,7},{10,... | collective-permute-start | bytes 786440 | tf_op jit(solution)/shard_map/ppermute | solution.py:33
  32.1 21.1 %all-to-all-start = ((bf16[32,6,1024]{2,1,0:T(8,128)(2,1)}), bf16[32,6,1024]{2,1,0:T(8,128)(2,1)S(1)}, u32[]{:S(2)}, u32[]{:S(2)}) async-start(bf16[32,6,1024]{2,1,0:T(8,128)(2,1)} %broadcast_in_dim.8), calls=%async_computation | async-start | bytes 1048576 | tf_op jit(solution)/shard_map/all_to_all | solution.py:54
  40.8 19.9 %collective-permute-start.3 = (bf16[256,1024]{1,0:T(8,128)(2,1)}, bf16[256,1024]{1,0:T(8,128)(2,1)S(1)}, u32[]{:S(2)}, u32[]{:S(2)}) collective-permute-start(bf16[256,1024]{1,0:T(8,128)(2,1)} %get-tuple-element.30), channel_id=1, source_target_pairs={{0,2},{1,3},{2,4},{3,5},{4,6},{5,7},{6,8},{7,9},{8,10},{9,11},{10,... | collective-permute-start | bytes 1572872 | tf_op jit(solution)/shard_map/ppermute | solution.py:33
  42.7 19.0 %collective-permute-start.5 = (bf16[256,1024]{1,0:T(8,128)(2,1)S(1)}, bf16[256,1024]{1,0:T(8,128)(2,1)}, u32[]{:S(2)}, u32[]{:S(2)}) collective-permute-start(bf16[256,1024]{1,0:T(8,128)(2,1)S(1)} %get-tuple-element.29), channel_id=1, source_target_pairs={{0,14},{1,15},{2,0},{3,1},{4,2},{5,3},{6,4},{7,5},{8,6},{9,7},{10,... | collective-permute-start | bytes 1572872 | tf_op jit(solution)/shard_map/ppermute | solution.py:33
  60.7 35.0 %copy-start.1 = (bf16[256,1024]{1,0:T(8,128)(2,1)}, bf16[256,1024]{1,0:T(8,128)(2,1)S(1)}, u32[]{:S(2)}) copy-start(bf16[256,1024]{1,0:T(8,128)(2,1)S(1)} %collective-permute-done.3.refs_4_) | copy-start | bytes 1572868
  61.7 25.3 %all-to-all-start.1 = ((bf16[16,112,128]{2,1,0:T(8,128)(2,1)}), bf16[16,112,128]{2,1,0:T(8,128)(2,1)S(1)}, u32[]{:S(2)}, u32[]{:S(2)}) async-start(bf16[16,112,128]{2,1,0:T(8,128)(2,1)} %pad_maximum_fusion.2), calls=%async_computation.1 | async-start | bytes 917504 | tf_op jit(solution)/shard_map/all_to_all | solution.py:238
  72.4 112.1 %all-gather.3.cloned.1.call-start = ((), (), s32[]{:S(2)}) async-start(), calls=%async_computation.3 | async-start | bytes 6488064 | tf_op jit(solution)/shard_map/all_gather | solution.py:240
  72.4 22.8 %collective-permute-start.6 = (bf16[256,1024]{1,0:T(8,128)(2,1)}, bf16[256,1024]{1,0:T(8,128)(2,1)S(1)}, u32[]{:S(2)}, u32[]{:S(2)}) collective-permute-start(bf16[256,1024]{1,0:T(8,128)(2,1)} %collective-permute-done.5.refs_6_), channel_id=1, source_target_pairs={{0,14},{1,15},{2,0},{3,1},{4,2},{5,3},{6,4},{7,5},{8,6},{9,7},{10,... | collective-permute-start | bytes 1572872 | tf_op jit(solution)/shard_map/ppermute | solution.py:33
  77.0 18.7 %collective-permute-start.4 = (bf16[256,1024]{1,0:T(8,128)(2,1)S(1)}, bf16[256,1024]{1,0:T(8,128)(2,1)S(1)}, u32[]{:S(2)}, u32[]{:S(2)}) collective-permute-start(bf16[256,1024]{1,0:T(8,128)(2,1)S(1)} %collective-permute-done.3.refs_4_), channel_id=1, source_target_pairs={{0,2},{1,3},{2,4},{3,5},{4,6},{5,7},{6,8},{7,9},{8,10},{9,11},{10,... | collective-permute-start | bytes 1572872 | tf_op jit(solution)/shard_map/ppermute | solution.py:33
  95.7 12.6 %collective-permute-start.8 = (bf16[192,1024]{1,0:T(8,128)(2,1)S(1)}, bf16[192,1024]{1,0:T(8,128)(2,1)S(1)}, u32[]{:S(2)}, u32[]{:S(2)}) collective-permute-start(bf16[192,1024]{1,0:T(8,128)(2,1)S(1)} %slice.61), channel_id=1, source_target_pairs={{0,14},{1,15},{2,0},{3,1},{4,2},{5,3},{6,4},{7,5},{8,6},{9,7},{10,... | collective-permute-start | bytes 1179656 | tf_op jit(solution)/shard_map/ppermute | solution.py:33
  99.2 14.3 %collective-permute-start.7 = (bf16[192,1024]{1,0:T(8,128)(2,1)S(1)}, bf16[192,1024]{1,0:T(8,128)(2,1)S(1)}, u32[]{:S(2)}, u32[]{:S(2)}) collective-permute-start(bf16[192,1024]{1,0:T(8,128)(2,1)S(1)} %slice.60), channel_id=1, source_target_pairs={{0,2},{1,3},{2,4},{3,5},{4,6},{5,7},{6,8},{7,9},{8,10},{9,11},{10,... | collective-permute-start | bytes 1179656 | tf_op jit(solution)/shard_map/ppermute | solution.py:33
  109.0 7.4 %collective-permute-start.10 = (bf16[64,1024]{1,0:T(8,128)(2,1)}, bf16[64,1024]{1,0:T(8,128)(2,1)}, u32[]{:S(2)}, u32[]{:S(2)}) collective-permute-start(bf16[64,1024]{1,0:T(8,128)(2,1)} %slice.63), channel_id=1, source_target_pairs={{0,14},{1,15},{2,0},{3,1},{4,2},{5,3},{6,4},{7,5},{8,6},{9,7},{10,... | collective-permute-start | bytes 393224 | tf_op jit(solution)/shard_map/ppermute | solution.py:33
  114.1 8.4 %collective-permute-start.9 = (bf16[64,1024]{1,0:T(8,128)(2,1)}, bf16[64,1024]{1,0:T(8,128)(2,1)}, u32[]{:S(2)}, u32[]{:S(2)}) collective-permute-start(bf16[64,1024]{1,0:T(8,128)(2,1)} %slice.62), channel_id=1, source_target_pairs={{0,2},{1,3},{2,4},{3,5},{4,6},{5,7},{6,8},{7,9},{8,10},{9,11},{10,... | collective-permute-start | bytes 393224 | tf_op jit(solution)/shard_map/ppermute | solution.py:33
  122.5 1.1 copy-start.2
  123.5 0.9 copy-start.3
  137.3 1.1 copy-start
  138.4 46.0 %all-to-all-start.2 = ((bf16[16,256,128]{2,1,0:T(8,128)(2,1)}), bf16[16,256,128]{2,1,0:T(8,128)(2,1)S(1)}, u32[]{:S(2)}, u32[]{:S(2)}) async-start(bf16[16,256,128]{2,1,0:T(8,128)(2,1)} %copy-done), calls=%async_computation.2 | async-start | bytes 2097152 | tf_op jit(solution)/shard_map/all_to_all | solution.py:245
  151.0 3.8 %collective-permute-start.11 = (f32[4,4,6,1024]{3,2,1,0:T(8,128)S(1)}, f32[4,4,6,1024]{3,2,1,0:T(8,128)S(1)}, u32[]{:S(2)}, u32[]{:S(2)}) collective-permute-start(f32[4,4,6,1024]{3,2,1,0:T(8,128)S(1)} %slice_bitcast_fusion), channel_id=1, source_target_pairs={{0,16},{16,0},{32,48},{48,32},{64,80},{80,64},{96,112},{112,96},{1... | collective-permute-start | bytes 1179656 | tf_op jit(solution)/shard_map/ppermute | solution.py:37
  156.0 11.4 %collective-permute-start.12 = (f32[4,6,1024]{2,1,0:T(8,128)S(1)}, f32[4,6,1024]{2,1,0:T(8,128)S(1)}, u32[]{:S(2)}, u32[]{:S(2)}) collective-permute-start(f32[4,6,1024]{2,1,0:T(8,128)S(1)} %get-tuple-element.28), channel_id=1, source_target_pairs={{0,32},{16,48},{32,64},{48,80},{64,96},{80,112},{96,0},{112,16},{1... | collective-permute-start | bytes 294920 | tf_op jit(solution)/shard_map/ppermute | solution.py:45
  159.4 9.3 %collective-permute-start.13 = (f32[4,6,1024]{2,1,0:T(8,128)S(1)}, f32[4,6,1024]{2,1,0:T(8,128)S(1)}, u32[]{:S(2)}, u32[]{:S(2)}) collective-permute-start(f32[4,6,1024]{2,1,0:T(8,128)S(1)} %get-tuple-element.26), channel_id=1, source_target_pairs={{0,64},{16,80},{32,96},{48,112},{64,0},{80,16},{96,32},{112,48},{1... | collective-permute-start | bytes 294920 | tf_op jit(solution)/shard_map/ppermute | solution.py:45
  164.0 6.9 %collective-permute-start.14 = (f32[4,6,1024]{2,1,0:T(8,128)S(1)}, f32[4,6,1024]{2,1,0:T(8,128)S(1)}, u32[]{:S(2)}, u32[]{:S(2)}) collective-permute-start(f32[4,6,1024]{2,1,0:T(8,128)S(1)} %get-tuple-element.27), channel_id=1, source_target_pairs={{0,96},{16,112},{32,0},{48,16},{64,32},{80,48},{96,64},{112,80},{1... | collective-permute-start | bytes 294920 | tf_op jit(solution)/shard_map/ppermute | solution.py:45
  171.0 8.3 %collective-permute-start.15 = (f32[6,1024]{1,0:T(8,128)S(1)}, f32[6,1024]{1,0:T(8,128)S(1)}, u32[]{:S(2)}, u32[]{:S(2)}) collective-permute-start(f32[6,1024]{1,0:T(8,128)S(1)} %get-tuple-element.33), channel_id=1, source_target_pairs={{0,128},{16,144},{32,160},{48,176},{64,192},{80,208},{96,224},{112... | collective-permute-start | bytes 73736 | tf_op jit(solution)/shard_map/ppermute | solution.py:49
  173.3 6.7 %collective-permute-start.16 = (f32[6,1024]{1,0:T(8,128)S(1)}, f32[6,1024]{1,0:T(8,128)S(1)}, u32[]{:S(2)}, u32[]{:S(2)}) collective-permute-start(f32[6,1024]{1,0:T(8,128)S(1)} %get-tuple-element.31), channel_id=1, source_target_pairs={{0,256},{16,272},{32,288},{48,304},{64,320},{80,336},{96,352},{112... | collective-permute-start | bytes 73736 | tf_op jit(solution)/shard_map/ppermute | solution.py:49
  176.2 7.6 %collective-permute-start.17 = (f32[6,1024]{1,0:T(8,128)S(1)}, f32[6,1024]{1,0:T(8,128)S(1)}, u32[]{:S(2)}, u32[]{:S(2)}) collective-permute-start(f32[6,1024]{1,0:T(8,128)S(1)} %get-tuple-element.32), channel_id=1, source_target_pairs={{0,384},{16,400},{32,416},{48,432},{64,448},{80,464},{96,480},{112... | collective-permute-start | bytes 73736 | tf_op jit(solution)/shard_map/ppermute | solution.py:49
Sparse Core Ops, SparseCore 0:
  95.8 75.1 all-gather.2

commit v4 on v3

--- a/solution.py
+++ b/solution.py
@@ -33,25 +33,17 @@
     return lax.ppermute(x, "seq", [(s, (s + YH * k) % SEQ) for s in range(SEQ)])
 
 
-def swap_core(x):
-    return lax.ppermute(x, "dp", [(d, d ^ 1) for d in range(DP)])
-
-
-def shift_x(x, k):
-    pairs = []
-    for d in range(DP):
-        to = (d // CORES + k) % XN
-        pairs.append((d, d // (XN * CORES) * XN * CORES + to * CORES + d % CORES))
-    return lax.ppermute(x, "dp", pairs)
-
-
-def shift_y(x, k):
-    return lax.ppermute(x, "dp", [(d, (d + k * XN * CORES) % DP) for d in range(DP)])
+def swap_dp(x, bit):
+    return lax.ppermute(x, "dp", [(d, d ^ bit) for d in range(DP)])
 
 
 def spread(x, axis, n):
     copies = jnp.broadcast_to(x[None], (n, *x.shape))
     return lax.all_to_all(copies, axis, 0, 0, tiled=True)
+
+
+def mirror(dp):
+    return sum(((dp >> k) & 1) << (4 - k) for k in range(5))
 
 
 def tiles_of(blocks):
@@ -146,13 +138,10 @@
         slot += n
         part = dot(jnp.concatenate(left, axis=1), blk, 1, 0)
         total = part if total is None else total + part
-    rows = sum_ref.shape[3]
-    core, x, y = here_ref[0], here_ref[1], here_ref[2]
+    rows = sum_ref.shape[1]
+    here = here_ref[0]
     for i in range(DP):
-        c = lax.rem(i % CORES + CORES - core, CORES)
-        u = lax.rem(i // CORES % XN + XN - x, XN)
-        v = lax.rem(i // (CORES * XN) + YL - y, YL)
-        sum_ref[c, u, v] = total[i * rows : (i + 1) * rows]
+        sum_ref[mirror(i) ^ here] = total[i * rows : (i + 1) * rows]
 
 
 def attention(here, order, tile_list, counts, blocks, w_head, cot_t):
@@ -162,7 +151,7 @@
         functools.partial(attend, len(blocks)),
         out_shape=(
             jax.ShapeDtypeStruct((tiles, 4 * HEAD_DIM, TILE), BF),
-            jax.ShapeDtypeStruct((CORES, XN, YL, rows, depth), F32),
+            jax.ShapeDtypeStruct((DP, rows, depth), F32),
         ),
         in_specs=[SM, SM, SM, SM] + [VM] * (len(blocks) + 2),
         out_specs=(VM, VM),
@@ -177,24 +166,19 @@
     )(here, order, tile_list, counts, *blocks, w_head, cot_t)
 
 
-def input_sum(both_ref, w_ref, att_ref, out_ref):
+def input_sum(both_ref, w_ref, att_ref, out_ref, sorted_ref):
     heads = both_ref.shape[0]
-    chunk = 3 * HEAD_DIM // XN
     att_ref[...] = jnp.concatenate(
         [both_ref[h, 3 * HEAD_DIM :, :] for h in range(heads)], axis=0
     ).T
-    left = jnp.concatenate(
-        [both_ref[h, c * chunk : (c + 1) * chunk, :] for c in range(XN) for h in range(heads)],
-        axis=0,
-    ).T
-    for y in range(YL):
-        cols = []
-        for c in range(CORES):
-            part = [w_ref[(y * XN + u) * CORES + c] for u in range(XN)]
-            cols.append(jnp.concatenate([p.reshape(heads * chunk, TILE) for p in part], axis=0))
-        total = dot(left, jnp.concatenate(cols, axis=1), 1, 0)
-        at = y * CORES * TILE
-        out_ref[:, at : at + CORES * TILE] = total.astype(BF)
+    rows = 3 * HEAD_DIM // DP
+    for h in range(heads):
+        part = both_ref[h, : 3 * HEAD_DIM, :].astype(F32)
+        for d in range(DP):
+            at = (d * heads + h) * rows
+            sorted_ref[at : at + rows, :] = part[d * rows : (d + 1) * rows]
+    left = sorted_ref[...].astype(BF).T
+    out_ref[...] = dot(left, w_ref[...], 1, 0).astype(BF)
 
 
 def input_grad(both, w_all):
@@ -203,10 +187,11 @@
         input_sum,
         out_shape=(
             jax.ShapeDtypeStruct((TILE, heads * HEAD_DIM), BF),
-            jax.ShapeDtypeStruct((TILE, YL * CORES * TILE), BF),
+            jax.ShapeDtypeStruct((TILE, w_all.shape[1]), BF),
         ),
         in_specs=[VM, VM],
         out_specs=(VM, VM),
+        scratch_shapes=[pltpu.VMEM((w_all.shape[0], TILE), F32)],
         compiler_params=PARAMS,
         name="input_sum",
     )(both, w_all)
@@ -217,37 +202,34 @@
     depth = tokens.shape[2]
     tiles = key_tiles.shape[1]
     dp, seq = lax.axis_index("dp"), lax.axis_index("seq")
-    y_lo, x, core = dp // (XN * CORES), dp // CORES % XN, dp % CORES
     z, y_hi = seq // YH, seq % YH
     grad_scale = (DP * tiles * TILE) ** (-0.5)
 
     blocks = gather_scene(tokens[0])
-    flip, r1, l1, r2, r3, l2, l3 = blocks[1:8]
-
-    w_own, _ = lax.optimization_barrier((qkv_weight[0], (flip, r1, l1)))
-    w_head = spread(w_own, "dp", DP).reshape(3 * HEAD_DIM, depth)
-    chunk = 3 * HEAD_DIM // XN
-    w_block = lax.dynamic_slice(
-        w_head, (x * chunk, (y_lo * CORES + core) * TILE), (chunk, TILE)
-    )
-
+
+    own_rows = qkv_weight[0]
+    rows = own_rows.shape[0]
+    lanes = rows * depth // TILE
     cot_t = cotangent[0].T.reshape(heads, HEAD_DIM, TILE)
-    copies = jnp.broadcast_to(w_block[None], (heads, *w_block.shape))
+    copies = jnp.broadcast_to(own_rows.reshape(lanes, TILE)[None], (heads, lanes, TILE))
     mixed = jnp.concatenate([cot_t, copies], axis=1)
-    mixed, _ = lax.optimization_barrier((mixed, (r2, l2)))
     mixed = lax.all_to_all(mixed, "seq", 0, 0, tiled=True)
-    w_seq, _ = lax.optimization_barrier((mixed[:, HEAD_DIM:], (r3, l3)))
-    w_all = lax.all_gather(w_seq, "dp", axis=0)
-
-    here = jnp.stack([core, x, y_lo]).astype(jnp.int32)
+    w_seq = mixed[:, HEAD_DIM:].reshape(heads * rows, depth)
+    w_seq, _ = lax.optimization_barrier((w_seq, blocks[1:4]))
+    w_all = lax.all_gather(w_seq, "dp", axis=0, tiled=True)
+
+    own_rows, _ = lax.optimization_barrier((own_rows, mixed))
+    w_head = spread(own_rows, "dp", DP).reshape(DP * rows, depth)
+
+    here = mirror(dp)[None].astype(jnp.int32)
     order = tile_places(z, y_hi)
     both, sums = attention(here, order, key_tiles[0], key_counts[0], blocks, w_head, mixed)
     both = lax.all_to_all(both, "seq", 0, 0, tiled=True)
 
-    sums = sums[0] + swap_core(sums[1])
-    sums = sums[0] + sum(shift_x(sums[k], k) for k in range(1, XN))
-    sums = sums[0] + sum(shift_y(sums[k], k) for k in range(1, YL))
-    grad_weight = sums[None] * grad_scale
+    for bit in (1, 2, 4, 8, 16):
+        half = sums.shape[0] // 2
+        sums = sums[:half] + swap_dp(sums[half:], bit)
+    grad_weight = sums * grad_scale
 
     attended, grad_input = input_grad(both, w_all)
     return (attended[None], grad_input[None], grad_weight)

time: 197 us -> 187 us (0.949)
  starting transfers between devices: 97.4 us -> 89.9 us
  waiting for transfers between devices: 53.6 us -> 49.4 us
    ppermute x10, waiting for transfers between devices: 31.7 us -> 17.5 us  [shift_z(): return lax.ppermute(x, 'seq', [(s, (s + YH * k) % SEQ) for s in range(SEQ)])]
    ppermute x7 -> x5, waiting for transfers between devices: 9.9 us -> 20.6 us  [swap_dp(): return lax.ppermute(x, 'dp', [(d, d ^ bit) for d in range(DP)])]
    ppermute x7 -> x5, starting transfers between devices: 21.6 us -> 14.9 us  [swap_dp(): return lax.ppermute(x, 'dp', [(d, d ^ bit) for d in range(DP)])]
    ppermute x10, starting transfers between devices: 41 us -> 34.9 us  [shift_z(): return lax.ppermute(x, 'seq', [(s, (s + YH * k) % SEQ) for s in range(SEQ)])]
    all_to_all x1, starting transfers between devices: 10.7 us -> 15.7 us  [shards(): mixed = lax.all_to_all(mixed, 'seq', 0, 0, tiled=True)]
    all_to_all x1, starting transfers between devices: 7.76 us -> 12.4 us  [spread(): return lax.all_to_all(copies, axis, 0, 0, tiled=True)]
    ppermute x1, waiting for transfers between devices: 2.11 us -> 5.08 us  [flip_y(): return lax.ppermute(x, 'seq', [(s, s ^ 1) for s in range(SEQ)])]
    ppermute x1, starting transfers between devices: 4.85 us -> 2.02 us  [flip_y(): return lax.ppermute(x, 'seq', [(s, s ^ 1) for s in range(SEQ)])]
  transfers between devices with their start and end apart: 22 -> 20, of which waited for: 16 -> 11; matrix products, arithmetic and copies ran while one was open for 4% -> 4% of each run, Pallas kernels for 7% -> 7%
where the time goes in v4:
time: 187 us; the launch traced here: 185 us
  starting transfers between devices  89.9 us (48%)
  waiting for transfers between devices  49.4 us (26%)
  Pallas kernels  17.4 us (9%)
  between operations  14.5 us (8%)
  local copies, waits for them, and re-layouts  11.9 us (6%)
  other arithmetic  2.1 us (1%)
    ppermute x10, starting transfers between devices, shift_z(): return lax.ppermute(x, 'seq', [(s, (s + YH * k) % SEQ) for s in range(SEQ)])  34.9 us
    ppermute x5, waiting for transfers between devices, swap_dp(): return lax.ppermute(x, 'dp', [(d, d ^ bit) for d in range(DP)])  20.6 us
    ppermute x10, waiting for transfers between devices, shift_z(): return lax.ppermute(x, 'seq', [(s, (s + YH * k) % SEQ) for s in range(SEQ)])  17.5 us
    all_to_all x1, starting transfers between devices, shards(): mixed = lax.all_to_all(mixed, 'seq', 0, 0, tiled=True)  15.7 us
    ppermute x5, starting transfers between devices, swap_dp(): return lax.ppermute(x, 'dp', [(d, d ^ bit) for d in range(DP)])  14.9 us
    pallas_call x1, Pallas kernels, attention(): pl.pallas_call(functools.partial(attend, len(blocks)), out_shape=(jax.Sha...  12.8 us
    all_to_all x1, starting transfers between devices, spread(): return lax.all_to_all(copies, axis, 0, 0, tiled=True)  12.4 us
    all_to_all x1, starting transfers between devices, shards(): both = lax.all_to_all(both, 'seq', 0, 0, tiled=True)  9.93 us
  transfers between devices with their start and end apart: 20, of which 11 were waited for; matrix products, arithmetic and copies ran while one was open for 4% of the time, Pallas kernels for 7%

profile of v4, /device:TPU:56, one launch (start us, length us, event | category | flops | bytes accessed | tf_op | source)
XLA Modules:
  0.0 185.2 jit_solution(8864738960164095096)
XLA Ops:
  7.2 1.1 copy.11
  8.3 0.8 broadcast_in_dim.23
  9.1 0.8 pad_maximum_fusion.2
  9.9 15.7 %all-to-all-start = ((bf16[16,112,128]{2,1,0:T(8,128)(2,1)}), bf16[16,112,128]{2,1,0:T(8,128)(2,1)S(1)}, u32[]{:S(2)}, u32[]{:S(2)}) async-start(bf16[16,112,128]{2,1,0:T(8,128)(2,1)} %pad_maximum_fusion.2), calls=%async_computation | async-start | bytes 917504 | tf_op jit(solution)/shard_map/all_to_all | solution.py:216
  25.7 2.0 %collective-permute-start = (bf16[128,1024]{1,0:T(8,128)(2,1)}, bf16[128,1024]{1,0:T(8,128)(2,1)S(1)}, u32[]{:S(2)}, u32[]{:S(2)}) collective-permute-start(bf16[128,1024]{1,0:T(8,128)(2,1)} %bitcast.27), channel_id=1, source_target_pairs={{0,1},{1,0},{2,3},{3,2},{4,5},{5,4},{6,7},{7,6},{8,9},{9,8},{10,11... | collective-permute-start | bytes 786440 | tf_op jit(solution)/shard_map/ppermute | solution.py:29
  27.7 3.8 %collective-permute-start.1 = (bf16[128,1024]{1,0:T(8,128)(2,1)}, bf16[128,1024]{1,0:T(8,128)(2,1)S(1)}, u32[]{:S(2)}, u32[]{:S(2)}) collective-permute-start(bf16[128,1024]{1,0:T(8,128)(2,1)} %bitcast.28), channel_id=1, source_target_pairs={{0,2},{1,3},{2,4},{3,5},{4,6},{5,7},{6,8},{7,9},{8,10},{9,11},{10,... | collective-permute-start | bytes 786440 | tf_op jit(solution)/shard_map/ppermute | solution.py:33
  31.5 3.2 %collective-permute-start.2 = (bf16[128,1024]{1,0:T(8,128)(2,1)}, bf16[128,1024]{1,0:T(8,128)(2,1)S(1)}, u32[]{:S(2)}, u32[]{:S(2)}) collective-permute-start(bf16[128,1024]{1,0:T(8,128)(2,1)} %bitcast.29), channel_id=1, source_target_pairs={{0,14},{1,15},{2,0},{3,1},{4,2},{5,3},{6,4},{7,5},{8,6},{9,7},{10,... | collective-permute-start | bytes 786440 | tf_op jit(solution)/shard_map/ppermute | solution.py:33
  34.8 6.2 %all-to-all-done.refs_13_ = bf16[16,112,128]{2,1,0:T(8,128)(2,1)S(1)} async-done(((bf16[16,112,128]{2,1,0:T(8,128)(2,1)}), bf16[16,112,128]{2,1,0:T(8,128)(2,1)S(1)}, u32[]{:S(2)}, u32[]{:S(2)}) %all-to-all-start) | async-done | bytes 458784 | tf_op jit(solution)/shard_map/all_to_all | solution.py:216
  41.0 0.8 reshape.19
  41.7 5.1 %collective-permute-done.refs_1_ = bf16[128,1024]{1,0:T(8,128)(2,1)S(1)} collective-permute-done((bf16[128,1024]{1,0:T(8,128)(2,1)}, bf16[128,1024]{1,0:T(8,128)(2,1)S(1)}, u32[]{:S(2)}, u32[]{:S(2)}) %collective-permute-start) | collective-permute-done | bytes 262176 | tf_op jit(solution)/shard_map/ppermute | solution.py:29
  46.8 0.1 pad_maximum_fusion.1
  47.0 4.8 %collective-permute-start.5 = (bf16[256,1024]{1,0:T(8,128)(2,1)S(1)}, bf16[256,1024]{1,0:T(8,128)(2,1)S(1)}, u32[]{:S(2)}, u32[]{:S(2)}) collective-permute-start(bf16[256,1024]{1,0:T(8,128)(2,1)S(1)} %get-tuple-element.21), channel_id=1, source_target_pairs={{0,14},{1,15},{2,0},{3,1},{4,2},{5,3},{6,4},{7,5},{8,6},{9,7},{10,... | collective-permute-start | bytes 1572872 | tf_op jit(solution)/shard_map/ppermute | solution.py:33
  51.8 1.9 %collective-permute-start.3 = (bf16[256,1024]{1,0:T(8,128)(2,1)S(1)}, bf16[256,1024]{1,0:T(8,128)(2,1)}, u32[]{:S(2)}, u32[]{:S(2)}) collective-permute-start(bf16[256,1024]{1,0:T(8,128)(2,1)S(1)} %get-tuple-element.22), channel_id=1, source_target_pairs={{0,2},{1,3},{2,4},{3,5},{4,6},{5,7},{6,8},{7,9},{8,10},{9,11},{10,... | collective-permute-start | bytes 1572872 | tf_op jit(solution)/shard_map/ppermute | solution.py:33
  53.7 5.8 %collective-permute-done.5.refs_6_ = bf16[256,1024]{1,0:T(8,128)(2,1)S(1)} collective-permute-done((bf16[256,1024]{1,0:T(8,128)(2,1)S(1)}, bf16[256,1024]{1,0:T(8,128)(2,1)S(1)}, u32[]{:S(2)}, u32[]{:S(2)}) %collective-permute-start.5) | collective-permute-done | bytes 524320 | tf_op jit(solution)/shard_map/ppermute | solution.py:33
  59.5 4.6 %collective-permute-start.6 = (bf16[256,1024]{1,0:T(8,128)(2,1)S(1)}, bf16[256,1024]{1,0:T(8,128)(2,1)S(1)}, u32[]{:S(2)}, u32[]{:S(2)}) collective-permute-start(bf16[256,1024]{1,0:T(8,128)(2,1)S(1)} %collective-permute-done.5.refs_6_), channel_id=1, source_target_pairs={{0,14},{1,15},{2,0},{3,1},{4,2},{5,3},{6,4},{7,5},{8,6},{9,7},{10,... | collective-permute-start | bytes 1572872 | tf_op jit(solution)/shard_map/ppermute | solution.py:33
  64.2 1.9 %collective-permute-start.4 = (bf16[256,1024]{1,0:T(8,128)(2,1)}, bf16[256,1024]{1,0:T(8,128)(2,1)S(1)}, u32[]{:S(2)}, u32[]{:S(2)}) collective-permute-start(bf16[256,1024]{1,0:T(8,128)(2,1)} %collective-permute-done.3.refs_4_), channel_id=1, source_target_pairs={{0,2},{1,3},{2,4},{3,5},{4,6},{5,7},{6,8},{7,9},{8,10},{9,11},{10,... | collective-permute-start | bytes 1572872 | tf_op jit(solution)/shard_map/ppermute | solution.py:33
  66.1 1.6 broadcast_in_dim.25
  67.8 12.4 %all-to-all-start.1 = ((bf16[32,6,1024]{2,1,0:T(8,128)(2,1)}), bf16[32,6,1024]{2,1,0:T(8,128)(2,1)}, u32[]{:S(2)}, u32[]{:S(2)}) async-start(bf16[32,6,1024]{2,1,0:T(8,128)(2,1)} %broadcast_in_dim.25), calls=%async_computation.1 | async-start | bytes 1048576 | tf_op jit(solution)/shard_map/all_to_all | solution.py:42
  80.3 5.1 %collective-permute-start.8 = (bf16[192,1024]{1,0:T(8,128)(2,1)S(1)}, bf16[192,1024]{1,0:T(8,128)(2,1)S(1)}, u32[]{:S(2)}, u32[]{:S(2)}) collective-permute-start(bf16[192,1024]{1,0:T(8,128)(2,1)S(1)} %slice.61), channel_id=1, source_target_pairs={{0,14},{1,15},{2,0},{3,1},{4,2},{5,3},{6,4},{7,5},{8,6},{9,7},{10,... | collective-permute-start | bytes 1179656 | tf_op jit(solution)/shard_map/ppermute | solution.py:33
  85.4 1.9 %collective-permute-start.7 = (bf16[192,1024]{1,0:T(8,128)(2,1)S(1)}, bf16[192,1024]{1,0:T(8,128)(2,1)S(1)}, u32[]{:S(2)}, u32[]{:S(2)}) collective-permute-start(bf16[192,1024]{1,0:T(8,128)(2,1)S(1)} %slice.60), channel_id=1, source_target_pairs={{0,2},{1,3},{2,4},{3,5},{4,6},{5,7},{6,8},{7,9},{8,10},{9,11},{10,... | collective-permute-start | bytes 1179656 | tf_op jit(solution)/shard_map/ppermute | solution.py:33
  87.4 6.7 %collective-permute-done.8.refs_9_ = bf16[192,1024]{1,0:T(8,128)(2,1)S(1)} collective-permute-done((bf16[192,1024]{1,0:T(8,128)(2,1)S(1)}, bf16[192,1024]{1,0:T(8,128)(2,1)S(1)}, u32[]{:S(2)}, u32[]{:S(2)}) %collective-permute-start.8) | collective-permute-done | bytes 393248 | tf_op jit(solution)/shard_map/ppermute | solution.py:33
  94.1 0.7 slice.63
  94.7 5.6 %collective-permute-start.10 = (bf16[64,1024]{1,0:T(8,128)(2,1)}, bf16[64,1024]{1,0:T(8,128)(2,1)}, u32[]{:S(2)}, u32[]{:S(2)}) collective-permute-start(bf16[64,1024]{1,0:T(8,128)(2,1)} %slice.63), channel_id=1, source_target_pairs={{0,14},{1,15},{2,0},{3,1},{4,2},{5,3},{6,4},{7,5},{8,6},{9,7},{10,... | collective-permute-start | bytes 393224 | tf_op jit(solution)/shard_map/ppermute | solution.py:33
  100.3 0.7 slice.62
  101.0 1.9 %collective-permute-start.9 = (bf16[64,1024]{1,0:T(8,128)(2,1)}, bf16[64,1024]{1,0:T(8,128)(2,1)}, u32[]{:S(2)}, u32[]{:S(2)}) collective-permute-start(bf16[64,1024]{1,0:T(8,128)(2,1)} %slice.62), channel_id=1, source_target_pairs={{0,2},{1,3},{2,4},{3,5},{4,6},{5,7},{6,8},{7,9},{8,10},{9,11},{10,... | collective-permute-start | bytes 393224 | tf_op jit(solution)/shard_map/ppermute | solution.py:33
  103.0 0.1 copy.12.list_ref
  103.1 0.1 stack.67.order_ref
  103.2 1.2 reshape.18.refs_12_
  104.4 4.9 %collective-permute-done.9.refs_10_ = bf16[64,1024]{1,0:T(8,128)(2,1)} collective-permute-done((bf16[64,1024]{1,0:T(8,128)(2,1)}, bf16[64,1024]{1,0:T(8,128)(2,1)}, u32[]{:S(2)}, u32[]{:S(2)}) %collective-permute-start.9) | collective-permute-done | bytes 131104 | tf_op jit(solution)/shard_map/ppermute | solution.py:33
  109.4 1.1 copy-done.2
  110.4 1.0 copy-done.3
  111.4 12.8 %attend.1 = (bf16[16,256,128]{2,1,0:T(8,128)(2,1)S(1)}, f32[32,6,1024]{2,1,0:T(8,128)}) custom-call(s32[1]{0:T(128)} %bitcast.here_ref, s32[16]{0:T(128)S(1)} %stack.67.order_ref, s32[16,4]{1,0:T(8,128)S(1)} %copy.12.list_ref, s32[16]{0:T(128)S(1)} %bitcast.31, bf16[128,1024]{1,0:T(8,128)(2,1)S(1)} %bitcast.30, ...), custom_call_target="tpu_custom_call" | custom-call | tf_op jit(solution)/shard_map/attend/pallas_call | solution.py:150
  124.2 1.1 copy-done
  125.3 9.9 %all-to-all-start.2 = ((bf16[16,256,128]{2,1,0:T(8,128)(2,1)}), bf16[16,256,128]{2,1,0:T(8,128)(2,1)S(1)}, u32[]{:S(2)}, u32[]{:S(2)}) async-start(bf16[16,256,128]{2,1,0:T(8,128)(2,1)} %copy-done), calls=%async_computation.2 | async-start | bytes 2097152 | tf_op jit(solution)/shard_map/all_to_all | solution.py:227
  135.2 1.1 slice.51
  136.3 1.9 %collective-permute-start.11 = (f32[16,6,1024]{2,1,0:T(8,128)S(1)}, f32[16,6,1024]{2,1,0:T(8,128)S(1)}, u32[]{:S(2)}, u32[]{:S(2)}) collective-permute-start(f32[16,6,1024]{2,1,0:T(8,128)S(1)} %slice.51), channel_id=1, source_target_pairs={{0,16},{16,0},{32,48},{48,32},{64,80},{80,64},{96,112},{112,96},{1... | collective-permute-start | bytes 1179656 | tf_op jit(solution)/shard_map/ppermute | solution.py:37
  138.2 1.9 %collective-permute-done.11 = f32[16,6,1024]{2,1,0:T(8,128)S(1)} collective-permute-done((f32[16,6,1024]{2,1,0:T(8,128)S(1)}, f32[16,6,1024]{2,1,0:T(8,128)S(1)}, u32[]{:S(2)}, u32[]{:S(2)}) %collective-permute-start.11) | collective-permute-done | bytes 393248 | tf_op jit(solution)/shard_map/ppermute | solution.py:37
  140.1 1.1 slice_add_fusion
  141.2 3.3 %collective-permute-start.12 = (f32[8,6,1024]{2,1,0:T(8,128)S(1)}, f32[8,6,1024]{2,1,0:T(8,128)S(1)}, u32[]{:S(2)}, u32[]{:S(2)}) collective-permute-start(f32[8,6,1024]{2,1,0:T(8,128)S(1)} %slice.66), channel_id=1, source_target_pairs={{0,32},{16,48},{32,0},{48,16},{64,96},{80,112},{96,64},{112,80},{1... | collective-permute-start | bytes 589832 | tf_op jit(solution)/shard_map/ppermute | solution.py:37
  144.6 6.9 %collective-permute-done.12 = f32[8,6,1024]{2,1,0:T(8,128)S(1)} collective-permute-done((f32[8,6,1024]{2,1,0:T(8,128)S(1)}, f32[8,6,1024]{2,1,0:T(8,128)S(1)}, u32[]{:S(2)}, u32[]{:S(2)}) %collective-permute-start.12) | collective-permute-done | bytes 196640 | tf_op jit(solution)/shard_map/ppermute | solution.py:37
  151.5 4.9 %collective-permute-start.13 = (f32[4,6,1024]{2,1,0:T(8,128)S(1)}, f32[4,6,1024]{2,1,0:T(8,128)S(1)}, u32[]{:S(2)}, u32[]{:S(2)}) collective-permute-start(f32[4,6,1024]{2,1,0:T(8,128)S(1)} %slice.68), channel_id=1, source_target_pairs={{0,64},{16,80},{32,96},{48,112},{64,0},{80,16},{96,32},{112,48},{1... | collective-permute-start | bytes 294920 | tf_op jit(solution)/shard_map/ppermute | solution.py:37
  156.4 3.5 %collective-permute-done.13 = f32[4,6,1024]{2,1,0:T(8,128)S(1)} collective-permute-done((f32[4,6,1024]{2,1,0:T(8,128)S(1)}, f32[4,6,1024]{2,1,0:T(8,128)S(1)}, u32[]{:S(2)}, u32[]{:S(2)}) %collective-permute-start.13) | collective-permute-done | bytes 98336 | tf_op jit(solution)/shard_map/ppermute | solution.py:37
  159.9 2.4 %collective-permute-start.14 = (f32[2,6,1024]{2,1,0:T(8,128)S(1)}, f32[2,6,1024]{2,1,0:T(8,128)S(1)}, u32[]{:S(2)}, u32[]{:S(2)}) collective-permute-start(f32[2,6,1024]{2,1,0:T(8,128)S(1)} %slice.70), channel_id=1, source_target_pairs={{0,128},{16,144},{32,160},{48,176},{64,192},{80,208},{96,224},{112... | collective-permute-start | bytes 147464 | tf_op jit(solution)/shard_map/ppermute | solution.py:37
  162.3 3.8 %collective-permute-done.14 = f32[2,6,1024]{2,1,0:T(8,128)S(1)} collective-permute-done((f32[2,6,1024]{2,1,0:T(8,128)S(1)}, f32[2,6,1024]{2,1,0:T(8,128)S(1)}, u32[]{:S(2)}, u32[]{:S(2)}) %collective-permute-start.14) | collective-permute-done | bytes 49184 | tf_op jit(solution)/shard_map/ppermute | solution.py:37
  166.1 2.4 %collective-permute-start.15 = (f32[1,6,1024]{2,1,0:T(8,128)S(1)}, f32[1,6,1024]{2,1,0:T(8,128)S(1)}, u32[]{:S(2)}, u32[]{:S(2)}) collective-permute-start(f32[1,6,1024]{2,1,0:T(8,128)S(1)} %slice.72), channel_id=1, source_target_pairs={{0,256},{16,272},{32,288},{48,304},{64,320},{80,336},{96,352},{112... | collective-permute-start | bytes 73736 | tf_op jit(solution)/shard_map/ppermute | solution.py:37
  168.5 4.6 %collective-permute-done.15 = f32[1,6,1024]{2,1,0:T(8,128)S(1)} collective-permute-done((f32[1,6,1024]{2,1,0:T(8,128)S(1)}, f32[1,6,1024]{2,1,0:T(8,128)S(1)}, u32[]{:S(2)}, u32[]{:S(2)}) %collective-permute-start.15) | collective-permute-done | bytes 24608 | tf_op jit(solution)/shard_map/ppermute | solution.py:37
  173.1 0.6 copy.13
  173.7 4.6 %input_sum.1 = (bf16[128,1024]{1,0:T(8,128)(2,1)}, bf16[128,1024]{1,0:T(8,128)(2,1)}) custom-call(bf16[16,256,128]{2,1,0:T(8,128)(2,1)S(1)} %all-to-all-done.2.both_ref, bf16[3072,1024]{1,0:T(8,128)(2,1)} %all-gather.2.cloned.1.call-done.w_ref), custom_call_target="tpu_custom_call" | custom-call | tf_op jit(solution)/shard_map/input_sum/pallas_call | solution.py:186
  (33 shorter events, 0.4 us)
Async XLA Ops:
  7.2 95.9 %copy-start.5 = (s32[1,16,4]{1,2,0:T(4,128)S(1)}, s32[1,16,4]{1,2,0:T(4,128)}, u32[]{:S(2)}) copy-start(s32[1,16,4]{1,2,0:T(4,128)} %param.7) | copy-start | bytes 772
  7.2 102.2 %copy-start.4 = (s32[1,16]{1,0:T(1,128)S(1)}, s32[1,16]{1,0:T(1,128)}, u32[]{:S(2)}) copy-start(s32[1,16]{1,0:T(1,128)} %param.8) | copy-start | bytes 196
  9.9 31.0 %all-to-all-start = ((bf16[16,112,128]{2,1,0:T(8,128)(2,1)}), bf16[16,112,128]{2,1,0:T(8,128)(2,1)S(1)}, u32[]{:S(2)}, u32[]{:S(2)}) async-start(bf16[16,112,128]{2,1,0:T(8,128)(2,1)} %pad_maximum_fusion.2), calls=%async_computation | async-start | bytes 917504 | tf_op jit(solution)/shard_map/all_to_all | solution.py:216
  25.6 148.1 %all-gather.2.cloned.1.call-start = ((), (), s32[]{:S(2)}) async-start(), calls=%async_computation.3 | async-start | bytes 6488064 | tf_op jit(solution)/shard_map/all_gather | solution.py:219
  25.7 21.2 %collective-permute-start = (bf16[128,1024]{1,0:T(8,128)(2,1)}, bf16[128,1024]{1,0:T(8,128)(2,1)S(1)}, u32[]{:S(2)}, u32[]{:S(2)}) collective-permute-start(bf16[128,1024]{1,0:T(8,128)(2,1)} %bitcast.27), channel_id=1, source_target_pairs={{0,1},{1,0},{2,3},{3,2},{4,5},{5,4},{6,7},{7,6},{8,9},{9,8},{10,11... | collective-permute-start | bytes 786440 | tf_op jit(solution)/shard_map/ppermute | solution.py:29
  27.7 19.1 %collective-permute-start.1 = (bf16[128,1024]{1,0:T(8,128)(2,1)}, bf16[128,1024]{1,0:T(8,128)(2,1)S(1)}, u32[]{:S(2)}, u32[]{:S(2)}) collective-permute-start(bf16[128,1024]{1,0:T(8,128)(2,1)} %bitcast.28), channel_id=1, source_target_pairs={{0,2},{1,3},{2,4},{3,5},{4,6},{5,7},{6,8},{7,9},{8,10},{9,11},{10,... | collective-permute-start | bytes 786440 | tf_op jit(solution)/shard_map/ppermute | solution.py:33
  31.5 15.3 %collective-permute-start.2 = (bf16[128,1024]{1,0:T(8,128)(2,1)}, bf16[128,1024]{1,0:T(8,128)(2,1)S(1)}, u32[]{:S(2)}, u32[]{:S(2)}) collective-permute-start(bf16[128,1024]{1,0:T(8,128)(2,1)} %bitcast.29), channel_id=1, source_target_pairs={{0,14},{1,15},{2,0},{3,1},{4,2},{5,3},{6,4},{7,5},{8,6},{9,7},{10,... | collective-permute-start | bytes 786440 | tf_op jit(solution)/shard_map/ppermute | solution.py:33
  47.0 12.5 %collective-permute-start.5 = (bf16[256,1024]{1,0:T(8,128)(2,1)S(1)}, bf16[256,1024]{1,0:T(8,128)(2,1)S(1)}, u32[]{:S(2)}, u32[]{:S(2)}) collective-permute-start(bf16[256,1024]{1,0:T(8,128)(2,1)S(1)} %get-tuple-element.21), channel_id=1, source_target_pairs={{0,14},{1,15},{2,0},{3,1},{4,2},{5,3},{6,4},{7,5},{8,6},{9,7},{10,... | collective-permute-start | bytes 1572872 | tf_op jit(solution)/shard_map/ppermute | solution.py:33
  51.8 12.4 %collective-permute-start.3 = (bf16[256,1024]{1,0:T(8,128)(2,1)S(1)}, bf16[256,1024]{1,0:T(8,128)(2,1)}, u32[]{:S(2)}, u32[]{:S(2)}) collective-permute-start(bf16[256,1024]{1,0:T(8,128)(2,1)S(1)} %get-tuple-element.22), channel_id=1, source_target_pairs={{0,2},{1,3},{2,4},{3,5},{4,6},{5,7},{6,8},{7,9},{8,10},{9,11},{10,... | collective-permute-start | bytes 1572872 | tf_op jit(solution)/shard_map/ppermute | solution.py:33
  59.5 20.7 %copy-start.1 = (bf16[256,1024]{1,0:T(8,128)(2,1)}, bf16[256,1024]{1,0:T(8,128)(2,1)S(1)}, u32[]{:S(2)}) copy-start(bf16[256,1024]{1,0:T(8,128)(2,1)S(1)} %collective-permute-done.5.refs_6_) | copy-start | bytes 1572868
  59.5 20.7 %collective-permute-start.6 = (bf16[256,1024]{1,0:T(8,128)(2,1)S(1)}, bf16[256,1024]{1,0:T(8,128)(2,1)S(1)}, u32[]{:S(2)}, u32[]{:S(2)}) collective-permute-start(bf16[256,1024]{1,0:T(8,128)(2,1)S(1)} %collective-permute-done.5.refs_6_), channel_id=1, source_target_pairs={{0,14},{1,15},{2,0},{3,1},{4,2},{5,3},{6,4},{7,5},{8,6},{9,7},{10,... | collective-permute-start | bytes 1572872 | tf_op jit(solution)/shard_map/ppermute | solution.py:33
  64.2 21.2 %collective-permute-start.4 = (bf16[256,1024]{1,0:T(8,128)(2,1)}, bf16[256,1024]{1,0:T(8,128)(2,1)S(1)}, u32[]{:S(2)}, u32[]{:S(2)}) collective-permute-start(bf16[256,1024]{1,0:T(8,128)(2,1)} %collective-permute-done.3.refs_4_), channel_id=1, source_target_pairs={{0,2},{1,3},{2,4},{3,5},{4,6},{5,7},{6,8},{7,9},{8,10},{9,11},{10,... | collective-permute-start | bytes 1572872 | tf_op jit(solution)/shard_map/ppermute | solution.py:33
  67.8 35.5 %all-to-all-start.1 = ((bf16[32,6,1024]{2,1,0:T(8,128)(2,1)}), bf16[32,6,1024]{2,1,0:T(8,128)(2,1)}, u32[]{:S(2)}, u32[]{:S(2)}) async-start(bf16[32,6,1024]{2,1,0:T(8,128)(2,1)} %broadcast_in_dim.25), calls=%async_computation.1 | async-start | bytes 1048576 | tf_op jit(solution)/shard_map/all_to_all | solution.py:42
  80.3 13.8 %collective-permute-start.8 = (bf16[192,1024]{1,0:T(8,128)(2,1)S(1)}, bf16[192,1024]{1,0:T(8,128)(2,1)S(1)}, u32[]{:S(2)}, u32[]{:S(2)}) collective-permute-start(bf16[192,1024]{1,0:T(8,128)(2,1)S(1)} %slice.61), channel_id=1, source_target_pairs={{0,14},{1,15},{2,0},{3,1},{4,2},{5,3},{6,4},{7,5},{8,6},{9,7},{10,... | collective-permute-start | bytes 1179656 | tf_op jit(solution)/shard_map/ppermute | solution.py:33
  85.4 14.9 %collective-permute-start.7 = (bf16[192,1024]{1,0:T(8,128)(2,1)S(1)}, bf16[192,1024]{1,0:T(8,128)(2,1)S(1)}, u32[]{:S(2)}, u32[]{:S(2)}) collective-permute-start(bf16[192,1024]{1,0:T(8,128)(2,1)S(1)} %slice.60), channel_id=1, source_target_pairs={{0,2},{1,3},{2,4},{3,5},{4,6},{5,7},{6,8},{7,9},{8,10},{9,11},{10,... | collective-permute-start | bytes 1179656 | tf_op jit(solution)/shard_map/ppermute | solution.py:33
  94.7 9.7 %collective-permute-start.10 = (bf16[64,1024]{1,0:T(8,128)(2,1)}, bf16[64,1024]{1,0:T(8,128)(2,1)}, u32[]{:S(2)}, u32[]{:S(2)}) collective-permute-start(bf16[64,1024]{1,0:T(8,128)(2,1)} %slice.63), channel_id=1, source_target_pairs={{0,14},{1,15},{2,0},{3,1},{4,2},{5,3},{6,4},{7,5},{8,6},{9,7},{10,... | collective-permute-start | bytes 393224 | tf_op jit(solution)/shard_map/ppermute | solution.py:33
  101.0 8.4 %collective-permute-start.9 = (bf16[64,1024]{1,0:T(8,128)(2,1)}, bf16[64,1024]{1,0:T(8,128)(2,1)}, u32[]{:S(2)}, u32[]{:S(2)}) collective-permute-start(bf16[64,1024]{1,0:T(8,128)(2,1)} %slice.62), channel_id=1, source_target_pairs={{0,2},{1,3},{2,4},{3,5},{4,6},{5,7},{6,8},{7,9},{8,10},{9,11},{10,... | collective-permute-start | bytes 393224 | tf_op jit(solution)/shard_map/ppermute | solution.py:33
  109.4 1.1 copy-start.2
  110.4 1.0 copy-start.3
  124.2 1.1 copy-start
  125.3 48.5 %all-to-all-start.2 = ((bf16[16,256,128]{2,1,0:T(8,128)(2,1)}), bf16[16,256,128]{2,1,0:T(8,128)(2,1)S(1)}, u32[]{:S(2)}, u32[]{:S(2)}) async-start(bf16[16,256,128]{2,1,0:T(8,128)(2,1)} %copy-done), calls=%async_computation.2 | async-start | bytes 2097152 | tf_op jit(solution)/shard_map/all_to_all | solution.py:227
  136.3 3.8 %collective-permute-start.11 = (f32[16,6,1024]{2,1,0:T(8,128)S(1)}, f32[16,6,1024]{2,1,0:T(8,128)S(1)}, u32[]{:S(2)}, u32[]{:S(2)}) collective-permute-start(f32[16,6,1024]{2,1,0:T(8,128)S(1)} %slice.51), channel_id=1, source_target_pairs={{0,16},{16,0},{32,48},{48,32},{64,80},{80,64},{96,112},{112,96},{1... | collective-permute-start | bytes 1179656 | tf_op jit(solution)/shard_map/ppermute | solution.py:37
  141.2 10.2 %collective-permute-start.12 = (f32[8,6,1024]{2,1,0:T(8,128)S(1)}, f32[8,6,1024]{2,1,0:T(8,128)S(1)}, u32[]{:S(2)}, u32[]{:S(2)}) collective-permute-start(f32[8,6,1024]{2,1,0:T(8,128)S(1)} %slice.66), channel_id=1, source_target_pairs={{0,32},{16,48},{32,0},{48,16},{64,96},{80,112},{96,64},{112,80},{1... | collective-permute-start | bytes 589832 | tf_op jit(solution)/shard_map/ppermute | solution.py:37
  151.5 8.4 %collective-permute-start.13 = (f32[4,6,1024]{2,1,0:T(8,128)S(1)}, f32[4,6,1024]{2,1,0:T(8,128)S(1)}, u32[]{:S(2)}, u32[]{:S(2)}) collective-permute-start(f32[4,6,1024]{2,1,0:T(8,128)S(1)} %slice.68), channel_id=1, source_target_pairs={{0,64},{16,80},{32,96},{48,112},{64,0},{80,16},{96,32},{112,48},{1... | collective-permute-start | bytes 294920 | tf_op jit(solution)/shard_map/ppermute | solution.py:37
  159.9 6.2 %collective-permute-start.14 = (f32[2,6,1024]{2,1,0:T(8,128)S(1)}, f32[2,6,1024]{2,1,0:T(8,128)S(1)}, u32[]{:S(2)}, u32[]{:S(2)}) collective-permute-start(f32[2,6,1024]{2,1,0:T(8,128)S(1)} %slice.70), channel_id=1, source_target_pairs={{0,128},{16,144},{32,160},{48,176},{64,192},{80,208},{96,224},{112... | collective-permute-start | bytes 147464 | tf_op jit(solution)/shard_map/ppermute | solution.py:37
  166.1 7.0 %collective-permute-start.15 = (f32[1,6,1024]{2,1,0:T(8,128)S(1)}, f32[1,6,1024]{2,1,0:T(8,128)S(1)}, u32[]{:S(2)}, u32[]{:S(2)}) collective-permute-start(f32[1,6,1024]{2,1,0:T(8,128)S(1)} %slice.72), channel_id=1, source_target_pairs={{0,256},{16,272},{32,288},{48,304},{64,320},{80,336},{96,352},{112... | collective-permute-start | bytes 73736 | tf_op jit(solution)/shard_map/ppermute | solution.py:37
Sparse Core Ops, SparseCore 0:
  47.0 79.9 all-gather.1

commit v5 on v4

--- a/solution.py
+++ b/solution.py
@@ -14,7 +14,7 @@
 F32 = jnp.float32
 VM = pl.BlockSpec(memory_space=pltpu.VMEM)
 SM = pl.BlockSpec(memory_space=pltpu.SMEM)
-PARAMS = pltpu.CompilerParams(vmem_limit_bytes=48 * 2**20)
+PARAMS = pltpu.CompilerParams(vmem_limit_bytes=32 * 2**20)
 
 YL, XN, CORES, ZN, YH = 4, 4, 2, 8, 2
 DP = YL * XN * CORES
@@ -215,7 +215,7 @@
     mixed = jnp.concatenate([cot_t, copies], axis=1)
     mixed = lax.all_to_all(mixed, "seq", 0, 0, tiled=True)
     w_seq = mixed[:, HEAD_DIM:].reshape(heads * rows, depth)
-    w_seq, _ = lax.optimization_barrier((w_seq, blocks[1:4]))
+    w_seq, _ = lax.optimization_barrier((w_seq, (blocks[4], blocks[6])))
     w_all = lax.all_gather(w_seq, "dp", axis=0, tiled=True)
 
     own_rows, _ = lax.optimization_barrier((own_rows, mixed))
@@ -228,7 +228,9 @@
 
     for bit in (1, 2, 4, 8, 16):
         half = sums.shape[0] // 2
-        sums = sums[:half] + swap_dp(sums[half:], bit)
+        sums = sums[:half] + swap_dp(sums[half:].astype(BF), bit).astype(F32)
+        if bit == 1:
+            w_all, sums = lax.optimization_barrier((w_all, sums))
     grad_weight = sums * grad_scale
 
     attended, grad_input = input_grad(both, w_all)

time: 187 us -> 192 us (1.027)
  starting transfers between devices: 89.9 us -> 107 us
  waiting for transfers between devices: 49.4 us -> 37.7 us
  Pallas kernels: 17.4 us -> 13.5 us
  local copies, waits for them, and re-layouts: 11.9 us -> 15.6 us
    ppermute x5, starting transfers between devices: 14.9 us -> 33.8 us  [swap_dp(): return lax.ppermute(x, 'dp', [(d, d ^ bit) for d in range(DP)])]
    ppermute x5, waiting for transfers between devices: 20.6 us -> 10.1 us  [swap_dp(): return lax.ppermute(x, 'dp', [(d, d ^ bit) for d in range(DP)])]
    all_to_all x1, starting transfers between devices: 15.7 us -> 9.85 us  [shards(): mixed = lax.all_to_all(mixed, 'seq', 0, 0, tiled=True)]
    ppermute x1, waiting for transfers between devices: 5.08 us -> 0.01 us  [flip_y(): return lax.ppermute(x, 'seq', [(s, s ^ 1) for s in range(SEQ)])]
    all_to_all x1, starting transfers between devices: 12.4 us -> 7.81 us  [spread(): return lax.all_to_all(copies, axis, 0, 0, tiled=True)]
    ppermute x10, starting transfers between devices: 34.9 us -> 39.2 us  [shift_z(): return lax.ppermute(x, 'seq', [(s, (s + YH * k) % SEQ) for s in range(SEQ)])]
    unnamed x13 -> x17, local copies, waits for them, and re-layouts: 3.75 us -> 7.45 us
    ppermute x1, starting transfers between devices: 2.02 us -> 4.85 us  [flip_y(): return lax.ppermute(x, 'seq', [(s, s ^ 1) for s in range(SEQ)])]
  transfers between devices with their start and end apart: 20 -> 20, of which waited for: 11 -> 10; matrix products, arithmetic and copies ran while one was open for 4% -> 5% of each run, Pallas kernels for 7% -> 7%
where the time goes in v5:
time: 192 us; the launch traced here: 190 us
  starting transfers between devices  107 us (56%)
  waiting for transfers between devices  37.7 us (20%)
  local copies, waits for them, and re-layouts  15.6 us (8%)
  between operations  14.5 us (8%)
  Pallas kernels  13.5 us (7%)
  other arithmetic  2.11 us (1%)
    ppermute x10, starting transfers between devices, shift_z(): return lax.ppermute(x, 'seq', [(s, (s + YH * k) % SEQ) for s in range(SEQ)])  39.2 us
    ppermute x5, starting transfers between devices, swap_dp(): return lax.ppermute(x, 'dp', [(d, d ^ bit) for d in range(DP)])  33.8 us
    ppermute x10, waiting for transfers between devices, shift_z(): return lax.ppermute(x, 'seq', [(s, (s + YH * k) % SEQ) for s in range(SEQ)])  19.8 us
    pallas_call x1, Pallas kernels, attention(): pl.pallas_call(functools.partial(attend, len(blocks)), out_shape=(jax.Sha...  11.7 us
    all_to_all x1, starting transfers between devices, shards(): both = lax.all_to_all(both, 'seq', 0, 0, tiled=True)  11 us
    ppermute x5, waiting for transfers between devices, swap_dp(): return lax.ppermute(x, 'dp', [(d, d ^ bit) for d in range(DP)])  10.1 us
    all_to_all x1, starting transfers between devices, shards(): mixed = lax.all_to_all(mixed, 'seq', 0, 0, tiled=True)  9.85 us
    all_to_all x1, starting transfers between devices, spread(): return lax.all_to_all(copies, axis, 0, 0, tiled=True)  7.81 us
  transfers between devices with their start and end apart: 20, of which 10 were waited for; matrix products, arithmetic and copies ran while one was open for 5% of the time, Pallas kernels for 7%

profile of v5, /device:TPU:56, one launch (start us, length us, event | category | flops | bytes accessed | tf_op | source)
XLA Modules:
  0.0 190.1 jit_solution(11721540353397834649)
XLA Ops:
  7.2 4.8 %collective-permute-start = (bf16[128,1024]{1,0:T(8,128)(2,1)}, bf16[128,1024]{1,0:T(8,128)(2,1)S(1)}, u32[]{:S(2)}, u32[]{:S(2)}) collective-permute-start(bf16[128,1024]{1,0:T(8,128)(2,1)} %bitcast.27), channel_id=1, source_target_pairs={{0,1},{1,0},{2,3},{3,2},{4,5},{5,4},{6,7},{7,6},{8,9},{9,8},{10,11... | collective-permute-start | bytes 786440 | tf_op jit(solution)/shard_map/ppermute | solution.py:29
  12.0 4.3 %collective-permute-start.1 = (bf16[128,1024]{1,0:T(8,128)(2,1)}, bf16[128,1024]{1,0:T(8,128)(2,1)S(1)}, u32[]{:S(2)}, u32[]{:S(2)}) collective-permute-start(bf16[128,1024]{1,0:T(8,128)(2,1)} %bitcast.28), channel_id=1, source_target_pairs={{0,2},{1,3},{2,4},{3,5},{4,6},{5,7},{6,8},{7,9},{8,10},{9,11},{10,... | collective-permute-start | bytes 786440 | tf_op jit(solution)/shard_map/ppermute | solution.py:33
  16.3 8.6 %collective-permute-start.2 = (bf16[128,1024]{1,0:T(8,128)(2,1)}, bf16[128,1024]{1,0:T(8,128)(2,1)S(1)}, u32[]{:S(2)}, u32[]{:S(2)}) collective-permute-start(bf16[128,1024]{1,0:T(8,128)(2,1)} %bitcast.29), channel_id=1, source_target_pairs={{0,14},{1,15},{2,0},{3,1},{4,2},{5,3},{6,4},{7,5},{8,6},{9,7},{10,... | collective-permute-start | bytes 786440 | tf_op jit(solution)/shard_map/ppermute | solution.py:33
  24.9 1.1 copy.11
  26.1 0.8 broadcast_in_dim.23
  26.9 0.8 pad_maximum_fusion.2
  27.7 9.8 %all-to-all-start = ((bf16[16,112,128]{2,1,0:T(8,128)(2,1)}), bf16[16,112,128]{2,1,0:T(8,128)(2,1)S(1)}, u32[]{:S(2)}, u32[]{:S(2)}) async-start(bf16[16,112,128]{2,1,0:T(8,128)(2,1)} %pad_maximum_fusion.2), calls=%async_computation | async-start | bytes 917504 | tf_op jit(solution)/shard_map/all_to_all | solution.py:216
  37.6 0.1 pad_maximum_fusion.1
  37.7 4.6 %collective-permute-start.5 = (bf16[256,1024]{1,0:T(8,128)(2,1)S(1)}, bf16[256,1024]{1,0:T(8,128)(2,1)S(1)}, u32[]{:S(2)}, u32[]{:S(2)}) collective-permute-start(bf16[256,1024]{1,0:T(8,128)(2,1)S(1)} %get-tuple-element.25), channel_id=1, source_target_pairs={{0,14},{1,15},{2,0},{3,1},{4,2},{5,3},{6,4},{7,5},{8,6},{9,7},{10,... | collective-permute-start | bytes 1572872 | tf_op jit(solution)/shard_map/ppermute | solution.py:33
  42.3 1.9 %collective-permute-start.3 = (bf16[256,1024]{1,0:T(8,128)(2,1)S(1)}, bf16[256,1024]{1,0:T(8,128)(2,1)}, u32[]{:S(2)}, u32[]{:S(2)}) collective-permute-start(bf16[256,1024]{1,0:T(8,128)(2,1)S(1)} %get-tuple-element.26), channel_id=1, source_target_pairs={{0,2},{1,3},{2,4},{3,5},{4,6},{5,7},{6,8},{7,9},{8,10},{9,11},{10,... | collective-permute-start | bytes 1572872 | tf_op jit(solution)/shard_map/ppermute | solution.py:33
  44.2 7.8 %all-to-all-done.refs_13_ = bf16[16,112,128]{2,1,0:T(8,128)(2,1)S(1)} async-done(((bf16[16,112,128]{2,1,0:T(8,128)(2,1)}), bf16[16,112,128]{2,1,0:T(8,128)(2,1)S(1)}, u32[]{:S(2)}, u32[]{:S(2)}) %all-to-all-start) | async-done | bytes 458784 | tf_op jit(solution)/shard_map/all_to_all | solution.py:216
  52.0 0.8 reshape.19
  52.8 7.6 %collective-permute-done.5.refs_6_ = bf16[256,1024]{1,0:T(8,128)(2,1)S(1)} collective-permute-done((bf16[256,1024]{1,0:T(8,128)(2,1)S(1)}, bf16[256,1024]{1,0:T(8,128)(2,1)S(1)}, u32[]{:S(2)}, u32[]{:S(2)}) %collective-permute-start.5) | collective-permute-done | bytes 524320 | tf_op jit(solution)/shard_map/ppermute | solution.py:33
  60.4 0.4 collective-permute-done.3.refs_4_
  60.9 3.4 %collective-permute-start.6 = (bf16[256,1024]{1,0:T(8,128)(2,1)S(1)}, bf16[256,1024]{1,0:T(8,128)(2,1)S(1)}, u32[]{:S(2)}, u32[]{:S(2)}) collective-permute-start(bf16[256,1024]{1,0:T(8,128)(2,1)S(1)} %collective-permute-done.5.refs_6_), channel_id=1, source_target_pairs={{0,14},{1,15},{2,0},{3,1},{4,2},{5,3},{6,4},{7,5},{8,6},{9,7},{10,... | collective-permute-start | bytes 1572872 | tf_op jit(solution)/shard_map/ppermute | solution.py:33
  64.2 2.5 %collective-permute-start.4 = (bf16[256,1024]{1,0:T(8,128)(2,1)}, bf16[256,1024]{1,0:T(8,128)(2,1)S(1)}, u32[]{:S(2)}, u32[]{:S(2)}) collective-permute-start(bf16[256,1024]{1,0:T(8,128)(2,1)} %collective-permute-done.3.refs_4_), channel_id=1, source_target_pairs={{0,2},{1,3},{2,4},{3,5},{4,6},{5,7},{6,8},{7,9},{8,10},{9,11},{10,... | collective-permute-start | bytes 1572872 | tf_op jit(solution)/shard_map/ppermute | solution.py:33
  66.7 1.6 broadcast_in_dim.25
  68.3 7.8 %all-to-all-start.1 = ((bf16[32,6,1024]{2,1,0:T(8,128)(2,1)}), bf16[32,6,1024]{2,1,0:T(8,128)(2,1)}, u32[]{:S(2)}, u32[]{:S(2)}) async-start(bf16[32,6,1024]{2,1,0:T(8,128)(2,1)} %broadcast_in_dim.25), calls=%async_computation.1 | async-start | bytes 1048576 | tf_op jit(solution)/shard_map/all_to_all | solution.py:42
  76.3 4.5 %collective-permute-start.8 = (bf16[192,1024]{1,0:T(8,128)(2,1)S(1)}, bf16[192,1024]{1,0:T(8,128)(2,1)S(1)}, u32[]{:S(2)}, u32[]{:S(2)}) collective-permute-start(bf16[192,1024]{1,0:T(8,128)(2,1)S(1)} %slice.66), channel_id=1, source_target_pairs={{0,14},{1,15},{2,0},{3,1},{4,2},{5,3},{6,4},{7,5},{8,6},{9,7},{10,... | collective-permute-start | bytes 1179656 | tf_op jit(solution)/shard_map/ppermute | solution.py:33
  80.8 1.9 %collective-permute-start.7 = (bf16[192,1024]{1,0:T(8,128)(2,1)S(1)}, bf16[192,1024]{1,0:T(8,128)(2,1)S(1)}, u32[]{:S(2)}, u32[]{:S(2)}) collective-permute-start(bf16[192,1024]{1,0:T(8,128)(2,1)S(1)} %slice.65), channel_id=1, source_target_pairs={{0,2},{1,3},{2,4},{3,5},{4,6},{5,7},{6,8},{7,9},{8,10},{9,11},{10,... | collective-permute-start | bytes 1179656 | tf_op jit(solution)/shard_map/ppermute | solution.py:33
  82.8 6.7 %collective-permute-done.8.refs_9_ = bf16[192,1024]{1,0:T(8,128)(2,1)S(1)} collective-permute-done((bf16[192,1024]{1,0:T(8,128)(2,1)S(1)}, bf16[192,1024]{1,0:T(8,128)(2,1)S(1)}, u32[]{:S(2)}, u32[]{:S(2)}) %collective-permute-start.8) | collective-permute-done | bytes 393248 | tf_op jit(solution)/shard_map/ppermute | solution.py:33
  89.5 0.7 slice.68
  90.1 5.6 %collective-permute-start.10 = (bf16[64,1024]{1,0:T(8,128)(2,1)}, bf16[64,1024]{1,0:T(8,128)(2,1)}, u32[]{:S(2)}, u32[]{:S(2)}) collective-permute-start(bf16[64,1024]{1,0:T(8,128)(2,1)} %slice.68), channel_id=1, source_target_pairs={{0,14},{1,15},{2,0},{3,1},{4,2},{5,3},{6,4},{7,5},{8,6},{9,7},{10,... | collective-permute-start | bytes 393224 | tf_op jit(solution)/shard_map/ppermute | solution.py:33
  95.7 0.7 slice.67
  96.4 1.9 %collective-permute-start.9 = (bf16[64,1024]{1,0:T(8,128)(2,1)}, bf16[64,1024]{1,0:T(8,128)(2,1)}, u32[]{:S(2)}, u32[]{:S(2)}) collective-permute-start(bf16[64,1024]{1,0:T(8,128)(2,1)} %slice.67), channel_id=1, source_target_pairs={{0,2},{1,3},{2,4},{3,5},{4,6},{5,7},{6,8},{7,9},{8,10},{9,11},{10,... | collective-permute-start | bytes 393224 | tf_op jit(solution)/shard_map/ppermute | solution.py:33
  98.5 0.1 stack.67.order_ref
  98.6 1.2 reshape.18.refs_12_
  99.8 4.9 %collective-permute-done.9.refs_10_ = bf16[64,1024]{1,0:T(8,128)(2,1)} collective-permute-done((bf16[64,1024]{1,0:T(8,128)(2,1)}, bf16[64,1024]{1,0:T(8,128)(2,1)}, u32[]{:S(2)}, u32[]{:S(2)}) %collective-permute-start.9) | collective-permute-done | bytes 131104 | tf_op jit(solution)/shard_map/ppermute | solution.py:33
  104.8 1.1 copy-done.4
  105.8 1.0 copy-done.5
  106.8 11.7 %attend.1 = (bf16[16,256,128]{2,1,0:T(8,128)(2,1)S(1)}, f32[32,6,1024]{2,1,0:T(8,128)S(1)}) custom-call(s32[1]{0:T(128)} %bitcast.here_ref, s32[16]{0:T(128)S(1)} %stack.67.order_ref, s32[16,4]{1,0:T(8,128)S(1)} %copy.12.list_ref, s32[16]{0:T(128)S(1)} %bitcast.31, bf16[128,1024]{1,0:T(8,128)(2,1)S(1)} %bitcast.30, ...), custom_call_target="tpu_custom_call" | custom-call | tf_op jit(solution)/shard_map/attend/pallas_call | solution.py:150
  118.5 1.0 copy-done.1
  119.5 1.1 copy-done.2
  120.5 11.0 %all-to-all-start.2 = ((bf16[16,256,128]{2,1,0:T(8,128)(2,1)}), bf16[16,256,128]{2,1,0:T(8,128)(2,1)S(1)}, u32[]{:S(2)}, u32[]{:S(2)}) async-start(bf16[16,256,128]{2,1,0:T(8,128)(2,1)} %copy-done.1), calls=%async_computation.2 | async-start | bytes 2097152 | tf_op jit(solution)/shard_map/all_to_all | solution.py:227
  131.6 1.1 slice.90
  132.7 1.9 %collective-permute-start.11 = (bf16[16,6,1024]{2,1,0:T(8,128)(2,1)S(1)}, bf16[16,6,1024]{2,1,0:T(8,128)(2,1)S(1)}, u32[]{:S(2)}, u32[]{:S(2)}) collective-permute-start(bf16[16,6,1024]{2,1,0:T(8,128)(2,1)S(1)} %slice.90), channel_id=1, source_target_pairs={{0,16},{16,0},{32,48},{48,32},{64,80},{80,64},{96,112},{112,96},{1... | collective-permute-start | bytes 589832 | tf_op jit(solution)/shard_map/ppermute | solution.py:37
  134.6 1.5 collective-permute-done.11
  136.1 1.1 convert_add_fusion
  137.3 3.4 %collective-permute-start.12 = (bf16[8,6,1024]{2,1,0:T(8,128)(2,1)S(1)}, bf16[8,6,1024]{2,1,0:T(8,128)(2,1)S(1)}, u32[]{:S(2)}, u32[]{:S(2)}) collective-permute-start(bf16[8,6,1024]{2,1,0:T(8,128)(2,1)S(1)} %slice.91), channel_id=1, source_target_pairs={{0,32},{16,48},{32,0},{48,16},{64,96},{80,112},{96,64},{112,80},{1... | collective-permute-start | bytes 294920 | tf_op jit(solution)/shard_map/ppermute | solution.py:37
  140.7 4.0 %collective-permute-done.12 = bf16[8,6,1024]{2,1,0:T(8,128)(2,1)S(1)} collective-permute-done((bf16[8,6,1024]{2,1,0:T(8,128)(2,1)S(1)}, bf16[8,6,1024]{2,1,0:T(8,128)(2,1)S(1)}, u32[]{:S(2)}, u32[]{:S(2)}) %collective-permute-start.12) | collective-permute-done | bytes 98336 | tf_op jit(solution)/shard_map/ppermute | solution.py:37
  144.8 4.9 %collective-permute-start.13 = (bf16[4,6,1024]{2,1,0:T(8,128)(2,1)S(1)}, bf16[4,6,1024]{2,1,0:T(8,128)(2,1)S(1)}, u32[]{:S(2)}, u32[]{:S(2)}) collective-permute-start(bf16[4,6,1024]{2,1,0:T(8,128)(2,1)S(1)} %slice.92), channel_id=1, source_target_pairs={{0,64},{16,80},{32,96},{48,112},{64,0},{80,16},{96,32},{112,48},{1... | collective-permute-start | bytes 147464 | tf_op jit(solution)/shard_map/ppermute | solution.py:37
  149.7 2.8 %collective-permute-done.13 = bf16[4,6,1024]{2,1,0:T(8,128)(2,1)S(1)} collective-permute-done((bf16[4,6,1024]{2,1,0:T(8,128)(2,1)S(1)}, bf16[4,6,1024]{2,1,0:T(8,128)(2,1)S(1)}, u32[]{:S(2)}, u32[]{:S(2)}) %collective-permute-start.13) | collective-permute-done | bytes 49184 | tf_op jit(solution)/shard_map/ppermute | solution.py:37
  152.5 15.0 %collective-permute-start.14 = (bf16[2,6,1024]{2,1,0:T(8,128)(2,1)S(1)}, bf16[2,6,1024]{2,1,0:T(8,128)(2,1)S(1)}, u32[]{:S(2)}, u32[]{:S(2)}) collective-permute-start(bf16[2,6,1024]{2,1,0:T(8,128)(2,1)S(1)} %slice.93), channel_id=1, source_target_pairs={{0,128},{16,144},{32,160},{48,176},{64,192},{80,208},{96,224},{112... | collective-permute-start | bytes 73736 | tf_op jit(solution)/shard_map/ppermute | solution.py:37
  167.5 1.9 collective-permute-done.14
  169.4 8.6 %collective-permute-start.15 = (bf16[1,6,1024]{2,1,0:T(8,128)(2,1)S(1)}, bf16[1,6,1024]{2,1,0:T(8,128)(2,1)S(1)}, u32[]{:S(2)}, u32[]{:S(2)}) collective-permute-start(bf16[1,6,1024]{2,1,0:T(8,128)(2,1)S(1)} %slice.94), channel_id=1, source_target_pairs={{0,256},{16,272},{32,288},{48,304},{64,320},{80,336},{96,352},{112... | collective-permute-start | bytes 36872 | tf_op jit(solution)/shard_map/ppermute | solution.py:37
  178.0 2.8 %copy-done = bf16[3072,1024]{1,0:T(8,128)(2,1)S(1)} copy-done((bf16[3072,1024]{1,0:T(8,128)(2,1)S(1)}, bf16[3072,1024]{1,0:T(8,128)(2,1)}, u32[]{:S(2)}) %copy-start) | copy-done | bytes 6291480
  180.8 1.8 input_sum.1
  182.6 0.6 copy.13
  (37 shorter events, 0.5 us)
Async XLA Ops:
  7.2 91.3 %copy-start.7 = (s32[1,16,4]{1,2,0:T(4,128)S(1)}, s32[1,16,4]{1,2,0:T(4,128)}, u32[]{:S(2)}) copy-start(s32[1,16,4]{1,2,0:T(4,128)} %param.7) | copy-start | bytes 772
  7.2 97.6 %copy-start.6 = (s32[1,16]{1,0:T(1,128)S(1)}, s32[1,16]{1,0:T(1,128)}, u32[]{:S(2)}) copy-start(s32[1,16]{1,0:T(1,128)} %param.8) | copy-start | bytes 196
  7.2 30.4 %collective-permute-start = (bf16[128,1024]{1,0:T(8,128)(2,1)}, bf16[128,1024]{1,0:T(8,128)(2,1)S(1)}, u32[]{:S(2)}, u32[]{:S(2)}) collective-permute-start(bf16[128,1024]{1,0:T(8,128)(2,1)} %bitcast.27), channel_id=1, source_target_pairs={{0,1},{1,0},{2,3},{3,2},{4,5},{5,4},{6,7},{7,6},{8,9},{9,8},{10,11... | collective-permute-start | bytes 786440 | tf_op jit(solution)/shard_map/ppermute | solution.py:29
  12.0 25.5 %collective-permute-start.1 = (bf16[128,1024]{1,0:T(8,128)(2,1)}, bf16[128,1024]{1,0:T(8,128)(2,1)S(1)}, u32[]{:S(2)}, u32[]{:S(2)}) collective-permute-start(bf16[128,1024]{1,0:T(8,128)(2,1)} %bitcast.28), channel_id=1, source_target_pairs={{0,2},{1,3},{2,4},{3,5},{4,6},{5,7},{6,8},{7,9},{8,10},{9,11},{10,... | collective-permute-start | bytes 786440 | tf_op jit(solution)/shard_map/ppermute | solution.py:33
  16.3 21.2 %collective-permute-start.2 = (bf16[128,1024]{1,0:T(8,128)(2,1)}, bf16[128,1024]{1,0:T(8,128)(2,1)S(1)}, u32[]{:S(2)}, u32[]{:S(2)}) collective-permute-start(bf16[128,1024]{1,0:T(8,128)(2,1)} %bitcast.29), channel_id=1, source_target_pairs={{0,14},{1,15},{2,0},{3,1},{4,2},{5,3},{6,4},{7,5},{8,6},{9,7},{10,... | collective-permute-start | bytes 786440 | tf_op jit(solution)/shard_map/ppermute | solution.py:33
  27.7 24.3 %all-to-all-start = ((bf16[16,112,128]{2,1,0:T(8,128)(2,1)}), bf16[16,112,128]{2,1,0:T(8,128)(2,1)S(1)}, u32[]{:S(2)}, u32[]{:S(2)}) async-start(bf16[16,112,128]{2,1,0:T(8,128)(2,1)} %pad_maximum_fusion.2), calls=%async_computation | async-start | bytes 917504 | tf_op jit(solution)/shard_map/all_to_all | solution.py:216
  37.5 99.7 %all-gather.2.cloned.1.call-start = ((), (), s32[]{:S(2)}) async-start(), calls=%async_computation.3 | async-start | bytes 6488064 | tf_op jit(solution)/shard_map/all_gather | solution.py:219
  37.7 22.7 %collective-permute-start.5 = (bf16[256,1024]{1,0:T(8,128)(2,1)S(1)}, bf16[256,1024]{1,0:T(8,128)(2,1)S(1)}, u32[]{:S(2)}, u32[]{:S(2)}) collective-permute-start(bf16[256,1024]{1,0:T(8,128)(2,1)S(1)} %get-tuple-element.25), channel_id=1, source_target_pairs={{0,14},{1,15},{2,0},{3,1},{4,2},{5,3},{6,4},{7,5},{8,6},{9,7},{10,... | collective-permute-start | bytes 1572872 | tf_op jit(solution)/shard_map/ppermute | solution.py:33
  42.3 18.5 %collective-permute-start.3 = (bf16[256,1024]{1,0:T(8,128)(2,1)S(1)}, bf16[256,1024]{1,0:T(8,128)(2,1)}, u32[]{:S(2)}, u32[]{:S(2)}) collective-permute-start(bf16[256,1024]{1,0:T(8,128)(2,1)S(1)} %get-tuple-element.26), channel_id=1, source_target_pairs={{0,2},{1,3},{2,4},{3,5},{4,6},{5,7},{6,8},{7,9},{8,10},{9,11},{10,... | collective-permute-start | bytes 1572872 | tf_op jit(solution)/shard_map/ppermute | solution.py:33
  60.4 15.8 %copy-start.3 = (bf16[256,1024]{1,0:T(8,128)(2,1)}, bf16[256,1024]{1,0:T(8,128)(2,1)S(1)}, u32[]{:S(2)}) copy-start(bf16[256,1024]{1,0:T(8,128)(2,1)S(1)} %collective-permute-done.5.refs_6_) | copy-start | bytes 1572868
  60.9 15.4 %collective-permute-start.6 = (bf16[256,1024]{1,0:T(8,128)(2,1)S(1)}, bf16[256,1024]{1,0:T(8,128)(2,1)S(1)}, u32[]{:S(2)}, u32[]{:S(2)}) collective-permute-start(bf16[256,1024]{1,0:T(8,128)(2,1)S(1)} %collective-permute-done.5.refs_6_), channel_id=1, source_target_pairs={{0,14},{1,15},{2,0},{3,1},{4,2},{5,3},{6,4},{7,5},{8,6},{9,7},{10,... | collective-permute-start | bytes 1572872 | tf_op jit(solution)/shard_map/ppermute | solution.py:33
  64.2 16.6 %collective-permute-start.4 = (bf16[256,1024]{1,0:T(8,128)(2,1)}, bf16[256,1024]{1,0:T(8,128)(2,1)S(1)}, u32[]{:S(2)}, u32[]{:S(2)}) collective-permute-start(bf16[256,1024]{1,0:T(8,128)(2,1)} %collective-permute-done.3.refs_4_), channel_id=1, source_target_pairs={{0,2},{1,3},{2,4},{3,5},{4,6},{5,7},{6,8},{7,9},{8,10},{9,11},{10,... | collective-permute-start | bytes 1572872 | tf_op jit(solution)/shard_map/ppermute | solution.py:33
  68.3 30.3 %all-to-all-start.1 = ((bf16[32,6,1024]{2,1,0:T(8,128)(2,1)}), bf16[32,6,1024]{2,1,0:T(8,128)(2,1)}, u32[]{:S(2)}, u32[]{:S(2)}) async-start(bf16[32,6,1024]{2,1,0:T(8,128)(2,1)} %broadcast_in_dim.25), calls=%async_computation.1 | async-start | bytes 1048576 | tf_op jit(solution)/shard_map/all_to_all | solution.py:42
  76.3 13.2 %collective-permute-start.8 = (bf16[192,1024]{1,0:T(8,128)(2,1)S(1)}, bf16[192,1024]{1,0:T(8,128)(2,1)S(1)}, u32[]{:S(2)}, u32[]{:S(2)}) collective-permute-start(bf16[192,1024]{1,0:T(8,128)(2,1)S(1)} %slice.66), channel_id=1, source_target_pairs={{0,14},{1,15},{2,0},{3,1},{4,2},{5,3},{6,4},{7,5},{8,6},{9,7},{10,... | collective-permute-start | bytes 1179656 | tf_op jit(solution)/shard_map/ppermute | solution.py:33
  80.8 14.9 %collective-permute-start.7 = (bf16[192,1024]{1,0:T(8,128)(2,1)S(1)}, bf16[192,1024]{1,0:T(8,128)(2,1)S(1)}, u32[]{:S(2)}, u32[]{:S(2)}) collective-permute-start(bf16[192,1024]{1,0:T(8,128)(2,1)S(1)} %slice.65), channel_id=1, source_target_pairs={{0,2},{1,3},{2,4},{3,5},{4,6},{5,7},{6,8},{7,9},{8,10},{9,11},{10,... | collective-permute-start | bytes 1179656 | tf_op jit(solution)/shard_map/ppermute | solution.py:33
  90.1 9.7 %collective-permute-start.10 = (bf16[64,1024]{1,0:T(8,128)(2,1)}, bf16[64,1024]{1,0:T(8,128)(2,1)}, u32[]{:S(2)}, u32[]{:S(2)}) collective-permute-start(bf16[64,1024]{1,0:T(8,128)(2,1)} %slice.68), channel_id=1, source_target_pairs={{0,14},{1,15},{2,0},{3,1},{4,2},{5,3},{6,4},{7,5},{8,6},{9,7},{10,... | collective-permute-start | bytes 393224 | tf_op jit(solution)/shard_map/ppermute | solution.py:33
  96.4 8.4 %collective-permute-start.9 = (bf16[64,1024]{1,0:T(8,128)(2,1)}, bf16[64,1024]{1,0:T(8,128)(2,1)}, u32[]{:S(2)}, u32[]{:S(2)}) collective-permute-start(bf16[64,1024]{1,0:T(8,128)(2,1)} %slice.67), channel_id=1, source_target_pairs={{0,2},{1,3},{2,4},{3,5},{4,6},{5,7},{6,8},{7,9},{8,10},{9,11},{10,... | collective-permute-start | bytes 393224 | tf_op jit(solution)/shard_map/ppermute | solution.py:33
  104.8 1.1 copy-start.4
  105.8 1.0 copy-start.5
  118.5 1.0 copy-start.1
  119.5 1.1 copy-start.2
  120.5 57.4 %all-to-all-start.2 = ((bf16[16,256,128]{2,1,0:T(8,128)(2,1)}), bf16[16,256,128]{2,1,0:T(8,128)(2,1)S(1)}, u32[]{:S(2)}, u32[]{:S(2)}) async-start(bf16[16,256,128]{2,1,0:T(8,128)(2,1)} %copy-done.1), calls=%async_computation.2 | async-start | bytes 2097152 | tf_op jit(solution)/shard_map/all_to_all | solution.py:227
  132.7 3.4 %collective-permute-start.11 = (bf16[16,6,1024]{2,1,0:T(8,128)(2,1)S(1)}, bf16[16,6,1024]{2,1,0:T(8,128)(2,1)S(1)}, u32[]{:S(2)}, u32[]{:S(2)}) collective-permute-start(bf16[16,6,1024]{2,1,0:T(8,128)(2,1)S(1)} %slice.90), channel_id=1, source_target_pairs={{0,16},{16,0},{32,48},{48,32},{64,80},{80,64},{96,112},{112,96},{1... | collective-permute-start | bytes 589832 | tf_op jit(solution)/shard_map/ppermute | solution.py:37
  137.3 7.4 %collective-permute-start.12 = (bf16[8,6,1024]{2,1,0:T(8,128)(2,1)S(1)}, bf16[8,6,1024]{2,1,0:T(8,128)(2,1)S(1)}, u32[]{:S(2)}, u32[]{:S(2)}) collective-permute-start(bf16[8,6,1024]{2,1,0:T(8,128)(2,1)S(1)} %slice.91), channel_id=1, source_target_pairs={{0,32},{16,48},{32,0},{48,16},{64,96},{80,112},{96,64},{112,80},{1... | collective-permute-start | bytes 294920 | tf_op jit(solution)/shard_map/ppermute | solution.py:37
  144.8 7.7 %collective-permute-start.13 = (bf16[4,6,1024]{2,1,0:T(8,128)(2,1)S(1)}, bf16[4,6,1024]{2,1,0:T(8,128)(2,1)S(1)}, u32[]{:S(2)}, u32[]{:S(2)}) collective-permute-start(bf16[4,6,1024]{2,1,0:T(8,128)(2,1)S(1)} %slice.92), channel_id=1, source_target_pairs={{0,64},{16,80},{32,96},{48,112},{64,0},{80,16},{96,32},{112,48},{1... | collective-permute-start | bytes 147464 | tf_op jit(solution)/shard_map/ppermute | solution.py:37
  152.5 16.9 %collective-permute-start.14 = (bf16[2,6,1024]{2,1,0:T(8,128)(2,1)S(1)}, bf16[2,6,1024]{2,1,0:T(8,128)(2,1)S(1)}, u32[]{:S(2)}, u32[]{:S(2)}) collective-permute-start(bf16[2,6,1024]{2,1,0:T(8,128)(2,1)S(1)} %slice.93), channel_id=1, source_target_pairs={{0,128},{16,144},{32,160},{48,176},{64,192},{80,208},{96,224},{112... | collective-permute-start | bytes 73736 | tf_op jit(solution)/shard_map/ppermute | solution.py:37
  169.4 13.2 %collective-permute-start.15 = (bf16[1,6,1024]{2,1,0:T(8,128)(2,1)S(1)}, bf16[1,6,1024]{2,1,0:T(8,128)(2,1)S(1)}, u32[]{:S(2)}, u32[]{:S(2)}) collective-permute-start(bf16[1,6,1024]{2,1,0:T(8,128)(2,1)S(1)} %slice.94), channel_id=1, source_target_pairs={{0,256},{16,272},{32,288},{48,304},{64,320},{80,336},{96,352},{112... | collective-permute-start | bytes 36872 | tf_op jit(solution)/shard_map/ppermute | solution.py:37
  178.0 2.8 %copy-start = (bf16[3072,1024]{1,0:T(8,128)(2,1)S(1)}, bf16[3072,1024]{1,0:T(8,128)(2,1)}, u32[]{:S(2)}) copy-start(bf16[3072,1024]{1,0:T(8,128)(2,1)} %all-gather.2.cloned.1.call-done.w_ref) | copy-start | bytes 18874372
Sparse Core Ops, SparseCore 0:
  61.0 75.1 all-gather.1

commit v6 on v5

--- a/solution.py
+++ b/solution.py
@@ -47,7 +47,7 @@
 
 
 def tiles_of(blocks):
-    own, flip, r1, l1, r2, r3, l2, l3, r4, l4, r5, l5 = blocks
+    own, flip, r1, l1, r2, r3, l2, l3, r4, l4, far = blocks
     half = TILE // 2
     yield from (own[...], flip[...], r1[...], l1[...])
     for pair in (r2, r3, l2, l3):
@@ -55,7 +55,7 @@
     yield r4[:TILE]
     yield l4[half:]
     yield jnp.concatenate([r4[TILE:], l4[:half]], axis=0)
-    yield jnp.concatenate([r5[...], l5[...]], axis=0)
+    yield far[...]
 
 
 def tile_places(z, y_hi):
@@ -72,8 +72,8 @@
     r3, l3 = shift_z(r2, 1), shift_z(l2, -1)
     half = TILE // 2
     r4, l4 = shift_z(r3[: TILE + half], 1), shift_z(l3[half:], -1)
-    r5, l5 = shift_z(r4[:half], 1), shift_z(l4[TILE:], -1)
-    return own, flip, r1, l1, r2, r3, l2, l3, r4, l4, r5, l5
+    far = shift_z(flip, ZN // 2)
+    return own, flip, r1, l1, r2, r3, l2, l3, r4, l4, far
 
 
 def attend(nblk, here_ref, order_ref, list_ref, count_ref, *refs):

time: 192 us -> 190 us (0.990)
  the two profiles are of different devices: /device:TPU:56 before, /device:TPU:314 now
where the time goes in v6:
time: 190 us; the launch traced here: 189 us
  starting transfers between devices  104 us (55%)
  waiting for transfers between devices  38.7 us (20%)
  local copies, waits for them, and re-layouts  15.8 us (8%)
  between operations  14.5 us (8%)
  Pallas kernels  13.7 us (7%)
  other arithmetic  2.92 us (2%)
    ppermute x5, starting transfers between devices, swap_dp(): return lax.ppermute(x, 'dp', [(d, d ^ bit) for d in range(DP)])  32.8 us
    ppermute x9, starting transfers between devices, shift_z(): return lax.ppermute(x, 'seq', [(s, (s + YH * k) % SEQ) for s in range(SEQ)])  32.1 us
    ppermute x9, waiting for transfers between devices, shift_z(): return lax.ppermute(x, 'seq', [(s, (s + YH * k) % SEQ) for s in range(SEQ)])  18.9 us
    all_to_all x1, starting transfers between devices, shards(): both = lax.all_to_all(both, 'seq', 0, 0, tiled=True)  13.2 us
    all_to_all x1, starting transfers between devices, shards(): mixed = lax.all_to_all(mixed, 'seq', 0, 0, tiled=True)  12 us
    pallas_call x1, Pallas kernels, attention(): pl.pallas_call(functools.partial(attend, len(blocks)), out_shape=(jax.Sha...  11.8 us
    ppermute x5, waiting for transfers between devices, swap_dp(): return lax.ppermute(x, 'dp', [(d, d ^ bit) for d in range(DP)])  11.8 us
    all_to_all x1, starting transfers between devices, spread(): return lax.all_to_all(copies, axis, 0, 0, tiled=True)  8.52 us
  transfers between devices with their start and end apart: 19, of which 9 were waited for; matrix products, arithmetic and copies ran while one was open for 6% of the time, Pallas kernels for 7%

profile of v6, /device:TPU:314, one launch (start us, length us, event | category | flops | bytes accessed | tf_op | source)
XLA Modules:
  0.0 189.2 jit_solution(231544414267543211)
XLA Ops:
  7.2 4.8 %collective-permute-start = (bf16[128,1024]{1,0:T(8,128)(2,1)}, bf16[128,1024]{1,0:T(8,128)(2,1)S(1)}, u32[]{:S(2)}, u32[]{:S(2)}) collective-permute-start(bf16[128,1024]{1,0:T(8,128)(2,1)} %bitcast.27), channel_id=1, source_target_pairs={{0,1},{1,0},{2,3},{3,2},{4,5},{5,4},{6,7},{7,6},{8,9},{9,8},{10,11... | collective-permute-start | bytes 786440 | tf_op jit(solution)/shard_map/ppermute | solution.py:29
  12.0 3.4 %collective-permute-start.1 = (bf16[128,1024]{1,0:T(8,128)(2,1)}, bf16[128,1024]{1,0:T(8,128)(2,1)S(1)}, u32[]{:S(2)}, u32[]{:S(2)}) collective-permute-start(bf16[128,1024]{1,0:T(8,128)(2,1)} %bitcast.28), channel_id=1, source_target_pairs={{0,2},{1,3},{2,4},{3,5},{4,6},{5,7},{6,8},{7,9},{8,10},{9,11},{10,... | collective-permute-start | bytes 786440 | tf_op jit(solution)/shard_map/ppermute | solution.py:33
  15.4 3.7 %collective-permute-start.2 = (bf16[128,1024]{1,0:T(8,128)(2,1)}, bf16[128,1024]{1,0:T(8,128)(2,1)S(1)}, u32[]{:S(2)}, u32[]{:S(2)}) collective-permute-start(bf16[128,1024]{1,0:T(8,128)(2,1)} %bitcast.29), channel_id=1, source_target_pairs={{0,14},{1,15},{2,0},{3,1},{4,2},{5,3},{6,4},{7,5},{8,6},{9,7},{10,... | collective-permute-start | bytes 786440 | tf_op jit(solution)/shard_map/ppermute | solution.py:33
  19.1 1.1 copy.11
  20.2 0.8 broadcast_in_dim.23
  21.0 0.8 pad_maximum_fusion.2
  21.8 12.0 %all-to-all-start = ((bf16[16,112,128]{2,1,0:T(8,128)(2,1)}), bf16[16,112,128]{2,1,0:T(8,128)(2,1)S(1)}, u32[]{:S(2)}, u32[]{:S(2)}) async-start(bf16[16,112,128]{2,1,0:T(8,128)(2,1)} %pad_maximum_fusion.2), calls=%async_computation | async-start | bytes 917504 | tf_op jit(solution)/shard_map/all_to_all | solution.py:216
  34.0 0.9 pad_maximum_fusion.1
  34.9 2.5 %collective-permute-start.3 = (bf16[256,1024]{1,0:T(8,128)(2,1)}, bf16[256,1024]{1,0:T(8,128)(2,1)S(1)}, u32[]{:S(2)}, u32[]{:S(2)}) collective-permute-start(bf16[256,1024]{1,0:T(8,128)(2,1)} %get-tuple-element.26), channel_id=1, source_target_pairs={{0,2},{1,3},{2,4},{3,5},{4,6},{5,7},{6,8},{7,9},{8,10},{9,11},{10,... | collective-permute-start | bytes 1572872 | tf_op jit(solution)/shard_map/ppermute | solution.py:33
  37.3 4.6 %collective-permute-start.5 = (bf16[256,1024]{1,0:T(8,128)(2,1)S(1)}, bf16[256,1024]{1,0:T(8,128)(2,1)S(1)}, u32[]{:S(2)}, u32[]{:S(2)}) collective-permute-start(bf16[256,1024]{1,0:T(8,128)(2,1)S(1)} %get-tuple-element.25), channel_id=1, source_target_pairs={{0,14},{1,15},{2,0},{3,1},{4,2},{5,3},{6,4},{7,5},{8,6},{9,7},{10,... | collective-permute-start | bytes 1572872 | tf_op jit(solution)/shard_map/ppermute | solution.py:33
  41.9 2.5 %all-to-all-done.refs_12_ = bf16[16,112,128]{2,1,0:T(8,128)(2,1)S(1)} async-done(((bf16[16,112,128]{2,1,0:T(8,128)(2,1)}), bf16[16,112,128]{2,1,0:T(8,128)(2,1)S(1)}, u32[]{:S(2)}, u32[]{:S(2)}) %all-to-all-start) | async-done | bytes 458784 | tf_op jit(solution)/shard_map/all_to_all | solution.py:216
  44.5 0.8 reshape.19
  45.2 9.8 %collective-permute-done.3.refs_4_ = bf16[256,1024]{1,0:T(8,128)(2,1)S(1)} collective-permute-done((bf16[256,1024]{1,0:T(8,128)(2,1)}, bf16[256,1024]{1,0:T(8,128)(2,1)S(1)}, u32[]{:S(2)}, u32[]{:S(2)}) %collective-permute-start.3) | collective-permute-done | bytes 524320 | tf_op jit(solution)/shard_map/ppermute | solution.py:33
  55.0 3.4 %collective-permute-start.4 = (bf16[256,1024]{1,0:T(8,128)(2,1)S(1)}, bf16[256,1024]{1,0:T(8,128)(2,1)S(1)}, u32[]{:S(2)}, u32[]{:S(2)}) collective-permute-start(bf16[256,1024]{1,0:T(8,128)(2,1)S(1)} %collective-permute-done.3.refs_4_), channel_id=1, source_target_pairs={{0,2},{1,3},{2,4},{3,5},{4,6},{5,7},{6,8},{7,9},{8,10},{9,11},{10,... | collective-permute-start | bytes 1572872 | tf_op jit(solution)/shard_map/ppermute | solution.py:33
  58.4 3.7 %collective-permute-start.6 = (bf16[256,1024]{1,0:T(8,128)(2,1)S(1)}, bf16[256,1024]{1,0:T(8,128)(2,1)S(1)}, u32[]{:S(2)}, u32[]{:S(2)}) collective-permute-start(bf16[256,1024]{1,0:T(8,128)(2,1)S(1)} %collective-permute-done.5.refs_6_), channel_id=1, source_target_pairs={{0,14},{1,15},{2,0},{3,1},{4,2},{5,3},{6,4},{7,5},{8,6},{9,7},{10,... | collective-permute-start | bytes 1572872 | tf_op jit(solution)/shard_map/ppermute | solution.py:33
  62.1 1.6 broadcast_in_dim.25
  63.7 8.5 %all-to-all-start.1 = ((bf16[32,6,1024]{2,1,0:T(8,128)(2,1)}), bf16[32,6,1024]{2,1,0:T(8,128)(2,1)}, u32[]{:S(2)}, u32[]{:S(2)}) async-start(bf16[32,6,1024]{2,1,0:T(8,128)(2,1)} %broadcast_in_dim.25), calls=%async_computation.1 | async-start | bytes 1048576 | tf_op jit(solution)/shard_map/all_to_all | solution.py:42
  72.2 0.8 slice.57
  73.0 1.9 %collective-permute-start.7 = (bf16[192,1024]{1,0:T(8,128)(2,1)}, bf16[192,1024]{1,0:T(8,128)(2,1)}, u32[]{:S(2)}, u32[]{:S(2)}) collective-permute-start(bf16[192,1024]{1,0:T(8,128)(2,1)} %slice.57), channel_id=1, source_target_pairs={{0,2},{1,3},{2,4},{3,5},{4,6},{5,7},{6,8},{7,9},{8,10},{9,11},{10,... | collective-permute-start | bytes 1179656 | tf_op jit(solution)/shard_map/ppermute | solution.py:33
  75.0 0.8 slice.58
  75.7 5.1 %collective-permute-start.8 = (bf16[192,1024]{1,0:T(8,128)(2,1)}, bf16[192,1024]{1,0:T(8,128)(2,1)}, u32[]{:S(2)}, u32[]{:S(2)}) collective-permute-start(bf16[192,1024]{1,0:T(8,128)(2,1)} %slice.58), channel_id=1, source_target_pairs={{0,14},{1,15},{2,0},{3,1},{4,2},{5,3},{6,4},{7,5},{8,6},{9,7},{10,... | collective-permute-start | bytes 1179656 | tf_op jit(solution)/shard_map/ppermute | solution.py:33
  80.9 3.9 %collective-permute-start.9 = (bf16[128,1024]{1,0:T(8,128)(2,1)S(1)}, bf16[128,1024]{1,0:T(8,128)(2,1)}, u32[]{:S(2)}, u32[]{:S(2)}) collective-permute-start(bf16[128,1024]{1,0:T(8,128)(2,1)S(1)} %collective-permute-done.refs_1_), channel_id=1, source_target_pairs={{0,8},{1,9},{2,10},{3,11},{4,12},{5,13},{6,14},{7,15},{8,0},{9,1},... | collective-permute-start | bytes 786440 | tf_op jit(solution)/shard_map/ppermute | solution.py:33
  84.9 0.1 copy.12.list_ref
  85.0 0.1 stack.67.order_ref
  85.1 5.5 %all-to-all-done.1 = bf16[32,6,1024]{2,1,0:T(8,128)(2,1)} async-done(((bf16[32,6,1024]{2,1,0:T(8,128)(2,1)}), bf16[32,6,1024]{2,1,0:T(8,128)(2,1)}, u32[]{:S(2)}, u32[]{:S(2)}) %all-to-all-start.1) | async-done | bytes 393248 | tf_op jit(solution)/shard_map/all_to_all | solution.py:42
  90.6 1.2 reshape.18.refs_11_
  91.7 8.5 %collective-permute-done.9.refs_10_ = bf16[128,1024]{1,0:T(8,128)(2,1)} collective-permute-done((bf16[128,1024]{1,0:T(8,128)(2,1)S(1)}, bf16[128,1024]{1,0:T(8,128)(2,1)}, u32[]{:S(2)}, u32[]{:S(2)}) %collective-permute-start.9) | collective-permute-done | bytes 262176 | tf_op jit(solution)/shard_map/ppermute | solution.py:33
  100.2 0.6 collective-permute-done.8.refs_9_
  100.8 1.1 copy-done.4
  101.9 1.0 copy-done.5
  102.9 11.8 %attend.1 = (bf16[16,256,128]{2,1,0:T(8,128)(2,1)S(1)}, f32[32,6,1024]{2,1,0:T(8,128)S(1)}) custom-call(s32[1]{0:T(128)} %bitcast.here_ref, s32[16]{0:T(128)S(1)} %stack.67.order_ref, s32[16,4]{1,0:T(8,128)S(1)} %copy.12.list_ref, s32[16]{0:T(128)S(1)} %bitcast.31, bf16[128,1024]{1,0:T(8,128)(2,1)S(1)} %bitcast.30, ...), custom_call_target="tpu_custom_call" | custom-call | tf_op jit(solution)/shard_map/attend/pallas_call | solution.py:150
  114.7 0.9 copy-done.1
  115.7 1.1 copy-done.2
  116.7 13.2 %all-to-all-start.2 = ((bf16[16,256,128]{2,1,0:T(8,128)(2,1)}), bf16[16,256,128]{2,1,0:T(8,128)(2,1)S(1)}, u32[]{:S(2)}, u32[]{:S(2)}) async-start(bf16[16,256,128]{2,1,0:T(8,128)(2,1)} %copy-done.1), calls=%async_computation.2 | async-start | bytes 2097152 | tf_op jit(solution)/shard_map/all_to_all | solution.py:227
  130.0 1.1 slice.80
  131.1 1.9 %collective-permute-start.10 = (bf16[16,6,1024]{2,1,0:T(8,128)(2,1)S(1)}, bf16[16,6,1024]{2,1,0:T(8,128)(2,1)S(1)}, u32[]{:S(2)}, u32[]{:S(2)}) collective-permute-start(bf16[16,6,1024]{2,1,0:T(8,128)(2,1)S(1)} %slice.80), channel_id=1, source_target_pairs={{0,16},{16,0},{32,48},{48,32},{64,80},{80,64},{96,112},{112,96},{1... | collective-permute-start | bytes 589832 | tf_op jit(solution)/shard_map/ppermute | solution.py:37
  133.0 1.5 collective-permute-done.10
  134.5 1.1 convert_add_fusion
  135.7 2.6 %collective-permute-start.11 = (bf16[8,6,1024]{2,1,0:T(8,128)(2,1)S(1)}, bf16[8,6,1024]{2,1,0:T(8,128)(2,1)S(1)}, u32[]{:S(2)}, u32[]{:S(2)}) collective-permute-start(bf16[8,6,1024]{2,1,0:T(8,128)(2,1)S(1)} %slice.81), channel_id=1, source_target_pairs={{0,32},{16,48},{32,0},{48,16},{64,96},{80,112},{96,64},{112,80},{1... | collective-permute-start | bytes 294920 | tf_op jit(solution)/shard_map/ppermute | solution.py:37
  138.3 4.8 %collective-permute-done.11 = bf16[8,6,1024]{2,1,0:T(8,128)(2,1)S(1)} collective-permute-done((bf16[8,6,1024]{2,1,0:T(8,128)(2,1)S(1)}, bf16[8,6,1024]{2,1,0:T(8,128)(2,1)S(1)}, u32[]{:S(2)}, u32[]{:S(2)}) %collective-permute-start.11) | collective-permute-done | bytes 98336 | tf_op jit(solution)/shard_map/ppermute | solution.py:37
  143.1 4.0 %collective-permute-start.12 = (bf16[4,6,1024]{2,1,0:T(8,128)(2,1)S(1)}, bf16[4,6,1024]{2,1,0:T(8,128)(2,1)S(1)}, u32[]{:S(2)}, u32[]{:S(2)}) collective-permute-start(bf16[4,6,1024]{2,1,0:T(8,128)(2,1)S(1)} %slice.82), channel_id=1, source_target_pairs={{0,64},{16,80},{32,96},{48,112},{64,0},{80,16},{96,32},{112,48},{1... | collective-permute-start | bytes 147464 | tf_op jit(solution)/shard_map/ppermute | solution.py:37
  147.2 3.6 %collective-permute-done.12 = bf16[4,6,1024]{2,1,0:T(8,128)(2,1)S(1)} collective-permute-done((bf16[4,6,1024]{2,1,0:T(8,128)(2,1)S(1)}, bf16[4,6,1024]{2,1,0:T(8,128)(2,1)S(1)}, u32[]{:S(2)}, u32[]{:S(2)}) %collective-permute-start.12) | collective-permute-done | bytes 49184 | tf_op jit(solution)/shard_map/ppermute | solution.py:37
  150.8 18.3 %collective-permute-start.13 = (bf16[2,6,1024]{2,1,0:T(8,128)(2,1)S(1)}, bf16[2,6,1024]{2,1,0:T(8,128)(2,1)S(1)}, u32[]{:S(2)}, u32[]{:S(2)}) collective-permute-start(bf16[2,6,1024]{2,1,0:T(8,128)(2,1)S(1)} %slice.83), channel_id=1, source_target_pairs={{0,128},{16,144},{32,160},{48,176},{64,192},{80,208},{96,224},{112... | collective-permute-start | bytes 73736 | tf_op jit(solution)/shard_map/ppermute | solution.py:37
  169.1 1.9 collective-permute-done.13
  171.1 5.9 %collective-permute-start.14 = (bf16[1,6,1024]{2,1,0:T(8,128)(2,1)S(1)}, bf16[1,6,1024]{2,1,0:T(8,128)(2,1)S(1)}, u32[]{:S(2)}, u32[]{:S(2)}) collective-permute-start(bf16[1,6,1024]{2,1,0:T(8,128)(2,1)S(1)} %slice.84), channel_id=1, source_target_pairs={{0,256},{16,272},{32,288},{48,304},{64,320},{80,336},{96,352},{112... | collective-permute-start | bytes 36872 | tf_op jit(solution)/shard_map/ppermute | solution.py:37
  177.0 2.8 %copy-done = bf16[3072,1024]{1,0:T(8,128)(2,1)S(1)} copy-done((bf16[3072,1024]{1,0:T(8,128)(2,1)S(1)}, bf16[3072,1024]{1,0:T(8,128)(2,1)}, u32[]{:S(2)}) %copy-start) | copy-done | bytes 6291480
  179.8 1.9 input_sum.1
  181.7 0.6 copy.13
  (33 shorter events, 0.3 us)
Async XLA Ops:
  7.2 77.7 %copy-start.7 = (s32[1,16,4]{1,2,0:T(4,128)S(1)}, s32[1,16,4]{1,2,0:T(4,128)}, u32[]{:S(2)}) copy-start(s32[1,16,4]{1,2,0:T(4,128)} %param.7) | copy-start | bytes 772
  7.2 93.7 %copy-start.6 = (s32[1,16]{1,0:T(1,128)S(1)}, s32[1,16]{1,0:T(1,128)}, u32[]{:S(2)}) copy-start(s32[1,16]{1,0:T(1,128)} %param.8) | copy-start | bytes 196
  7.2 26.7 %collective-permute-start = (bf16[128,1024]{1,0:T(8,128)(2,1)}, bf16[128,1024]{1,0:T(8,128)(2,1)S(1)}, u32[]{:S(2)}, u32[]{:S(2)}) collective-permute-start(bf16[128,1024]{1,0:T(8,128)(2,1)} %bitcast.27), channel_id=1, source_target_pairs={{0,1},{1,0},{2,3},{3,2},{4,5},{5,4},{6,7},{7,6},{8,9},{9,8},{10,11... | collective-permute-start | bytes 786440 | tf_op jit(solution)/shard_map/ppermute | solution.py:29
  12.0 21.9 %collective-permute-start.1 = (bf16[128,1024]{1,0:T(8,128)(2,1)}, bf16[128,1024]{1,0:T(8,128)(2,1)S(1)}, u32[]{:S(2)}, u32[]{:S(2)}) collective-permute-start(bf16[128,1024]{1,0:T(8,128)(2,1)} %bitcast.28), channel_id=1, source_target_pairs={{0,2},{1,3},{2,4},{3,5},{4,6},{5,7},{6,8},{7,9},{8,10},{9,11},{10,... | collective-permute-start | bytes 786440 | tf_op jit(solution)/shard_map/ppermute | solution.py:33
  15.4 18.5 %collective-permute-start.2 = (bf16[128,1024]{1,0:T(8,128)(2,1)}, bf16[128,1024]{1,0:T(8,128)(2,1)S(1)}, u32[]{:S(2)}, u32[]{:S(2)}) collective-permute-start(bf16[128,1024]{1,0:T(8,128)(2,1)} %bitcast.29), channel_id=1, source_target_pairs={{0,14},{1,15},{2,0},{3,1},{4,2},{5,3},{6,4},{7,5},{8,6},{9,7},{10,... | collective-permute-start | bytes 786440 | tf_op jit(solution)/shard_map/ppermute | solution.py:33
  21.8 22.6 %all-to-all-start = ((bf16[16,112,128]{2,1,0:T(8,128)(2,1)}), bf16[16,112,128]{2,1,0:T(8,128)(2,1)S(1)}, u32[]{:S(2)}, u32[]{:S(2)}) async-start(bf16[16,112,128]{2,1,0:T(8,128)(2,1)} %pad_maximum_fusion.2), calls=%async_computation | async-start | bytes 917504 | tf_op jit(solution)/shard_map/all_to_all | solution.py:216
  33.9 101.7 %all-gather.2.cloned.1.call-start = ((), (), s32[]{:S(2)}) async-start(), calls=%async_computation.3 | async-start | bytes 6488064 | tf_op jit(solution)/shard_map/all_gather | solution.py:219
  34.9 20.1 %collective-permute-start.3 = (bf16[256,1024]{1,0:T(8,128)(2,1)}, bf16[256,1024]{1,0:T(8,128)(2,1)S(1)}, u32[]{:S(2)}, u32[]{:S(2)}) collective-permute-start(bf16[256,1024]{1,0:T(8,128)(2,1)} %get-tuple-element.26), channel_id=1, source_target_pairs={{0,2},{1,3},{2,4},{3,5},{4,6},{5,7},{6,8},{7,9},{8,10},{9,11},{10,... | collective-permute-start | bytes 1572872 | tf_op jit(solution)/shard_map/ppermute | solution.py:33
  37.3 17.6 %collective-permute-start.5 = (bf16[256,1024]{1,0:T(8,128)(2,1)S(1)}, bf16[256,1024]{1,0:T(8,128)(2,1)S(1)}, u32[]{:S(2)}, u32[]{:S(2)}) collective-permute-start(bf16[256,1024]{1,0:T(8,128)(2,1)S(1)} %get-tuple-element.25), channel_id=1, source_target_pairs={{0,14},{1,15},{2,0},{3,1},{4,2},{5,3},{6,4},{7,5},{8,6},{9,7},{10,... | collective-permute-start | bytes 1572872 | tf_op jit(solution)/shard_map/ppermute | solution.py:33
  55.0 30.1 %copy-start.3 = (bf16[256,1024]{1,0:T(8,128)(2,1)}, bf16[256,1024]{1,0:T(8,128)(2,1)S(1)}, u32[]{:S(2)}) copy-start(bf16[256,1024]{1,0:T(8,128)(2,1)S(1)} %collective-permute-done.5.refs_6_) | copy-start | bytes 1572868
  55.0 17.2 %collective-permute-start.4 = (bf16[256,1024]{1,0:T(8,128)(2,1)S(1)}, bf16[256,1024]{1,0:T(8,128)(2,1)S(1)}, u32[]{:S(2)}, u32[]{:S(2)}) collective-permute-start(bf16[256,1024]{1,0:T(8,128)(2,1)S(1)} %collective-permute-done.3.refs_4_), channel_id=1, source_target_pairs={{0,2},{1,3},{2,4},{3,5},{4,6},{5,7},{6,8},{7,9},{8,10},{9,11},{10,... | collective-permute-start | bytes 1572872 | tf_op jit(solution)/shard_map/ppermute | solution.py:33
  58.4 16.6 %collective-permute-start.6 = (bf16[256,1024]{1,0:T(8,128)(2,1)S(1)}, bf16[256,1024]{1,0:T(8,128)(2,1)S(1)}, u32[]{:S(2)}, u32[]{:S(2)}) collective-permute-start(bf16[256,1024]{1,0:T(8,128)(2,1)S(1)} %collective-permute-done.5.refs_6_), channel_id=1, source_target_pairs={{0,14},{1,15},{2,0},{3,1},{4,2},{5,3},{6,4},{7,5},{8,6},{9,7},{10,... | collective-permute-start | bytes 1572872 | tf_op jit(solution)/shard_map/ppermute | solution.py:33
  63.7 26.9 %all-to-all-start.1 = ((bf16[32,6,1024]{2,1,0:T(8,128)(2,1)}), bf16[32,6,1024]{2,1,0:T(8,128)(2,1)}, u32[]{:S(2)}, u32[]{:S(2)}) async-start(bf16[32,6,1024]{2,1,0:T(8,128)(2,1)} %broadcast_in_dim.25), calls=%async_computation.1 | async-start | bytes 1048576 | tf_op jit(solution)/shard_map/all_to_all | solution.py:42
  73.0 27.2 %collective-permute-start.7 = (bf16[192,1024]{1,0:T(8,128)(2,1)}, bf16[192,1024]{1,0:T(8,128)(2,1)}, u32[]{:S(2)}, u32[]{:S(2)}) collective-permute-start(bf16[192,1024]{1,0:T(8,128)(2,1)} %slice.57), channel_id=1, source_target_pairs={{0,2},{1,3},{2,4},{3,5},{4,6},{5,7},{6,8},{7,9},{8,10},{9,11},{10,... | collective-permute-start | bytes 1179656 | tf_op jit(solution)/shard_map/ppermute | solution.py:33
  75.7 25.1 %collective-permute-start.8 = (bf16[192,1024]{1,0:T(8,128)(2,1)}, bf16[192,1024]{1,0:T(8,128)(2,1)}, u32[]{:S(2)}, u32[]{:S(2)}) collective-permute-start(bf16[192,1024]{1,0:T(8,128)(2,1)} %slice.58), channel_id=1, source_target_pairs={{0,14},{1,15},{2,0},{3,1},{4,2},{5,3},{6,4},{7,5},{8,6},{9,7},{10,... | collective-permute-start | bytes 1179656 | tf_op jit(solution)/shard_map/ppermute | solution.py:33
  80.9 19.4 %collective-permute-start.9 = (bf16[128,1024]{1,0:T(8,128)(2,1)S(1)}, bf16[128,1024]{1,0:T(8,128)(2,1)}, u32[]{:S(2)}, u32[]{:S(2)}) collective-permute-start(bf16[128,1024]{1,0:T(8,128)(2,1)S(1)} %collective-permute-done.refs_1_), channel_id=1, source_target_pairs={{0,8},{1,9},{2,10},{3,11},{4,12},{5,13},{6,14},{7,15},{8,0},{9,1},... | collective-permute-start | bytes 786440 | tf_op jit(solution)/shard_map/ppermute | solution.py:33
  100.8 1.1 copy-start.4
  101.9 1.0 copy-start.5
  114.7 1.0 copy-start.1
  115.6 1.1 copy-start.2
  116.7 60.3 %all-to-all-start.2 = ((bf16[16,256,128]{2,1,0:T(8,128)(2,1)}), bf16[16,256,128]{2,1,0:T(8,128)(2,1)S(1)}, u32[]{:S(2)}, u32[]{:S(2)}) async-start(bf16[16,256,128]{2,1,0:T(8,128)(2,1)} %copy-done.1), calls=%async_computation.2 | async-start | bytes 2097152 | tf_op jit(solution)/shard_map/all_to_all | solution.py:227
  131.1 3.4 %collective-permute-start.10 = (bf16[16,6,1024]{2,1,0:T(8,128)(2,1)S(1)}, bf16[16,6,1024]{2,1,0:T(8,128)(2,1)S(1)}, u32[]{:S(2)}, u32[]{:S(2)}) collective-permute-start(bf16[16,6,1024]{2,1,0:T(8,128)(2,1)S(1)} %slice.80), channel_id=1, source_target_pairs={{0,16},{16,0},{32,48},{48,32},{64,80},{80,64},{96,112},{112,96},{1... | collective-permute-start | bytes 589832 | tf_op jit(solution)/shard_map/ppermute | solution.py:37
  135.7 7.4 %collective-permute-start.11 = (bf16[8,6,1024]{2,1,0:T(8,128)(2,1)S(1)}, bf16[8,6,1024]{2,1,0:T(8,128)(2,1)S(1)}, u32[]{:S(2)}, u32[]{:S(2)}) collective-permute-start(bf16[8,6,1024]{2,1,0:T(8,128)(2,1)S(1)} %slice.81), channel_id=1, source_target_pairs={{0,32},{16,48},{32,0},{48,16},{64,96},{80,112},{96,64},{112,80},{1... | collective-permute-start | bytes 294920 | tf_op jit(solution)/shard_map/ppermute | solution.py:37
  143.1 7.7 %collective-permute-start.12 = (bf16[4,6,1024]{2,1,0:T(8,128)(2,1)S(1)}, bf16[4,6,1024]{2,1,0:T(8,128)(2,1)S(1)}, u32[]{:S(2)}, u32[]{:S(2)}) collective-permute-start(bf16[4,6,1024]{2,1,0:T(8,128)(2,1)S(1)} %slice.82), channel_id=1, source_target_pairs={{0,64},{16,80},{32,96},{48,112},{64,0},{80,16},{96,32},{112,48},{1... | collective-permute-start | bytes 147464 | tf_op jit(solution)/shard_map/ppermute | solution.py:37
  150.8 20.2 %collective-permute-start.13 = (bf16[2,6,1024]{2,1,0:T(8,128)(2,1)S(1)}, bf16[2,6,1024]{2,1,0:T(8,128)(2,1)S(1)}, u32[]{:S(2)}, u32[]{:S(2)}) collective-permute-start(bf16[2,6,1024]{2,1,0:T(8,128)(2,1)S(1)} %slice.83), channel_id=1, source_target_pairs={{0,128},{16,144},{32,160},{48,176},{64,192},{80,208},{96,224},{112... | collective-permute-start | bytes 73736 | tf_op jit(solution)/shard_map/ppermute | solution.py:37
  171.1 10.6 %collective-permute-start.14 = (bf16[1,6,1024]{2,1,0:T(8,128)(2,1)S(1)}, bf16[1,6,1024]{2,1,0:T(8,128)(2,1)S(1)}, u32[]{:S(2)}, u32[]{:S(2)}) collective-permute-start(bf16[1,6,1024]{2,1,0:T(8,128)(2,1)S(1)} %slice.84), channel_id=1, source_target_pairs={{0,256},{16,272},{32,288},{48,304},{64,320},{80,336},{96,352},{112... | collective-permute-start | bytes 36872 | tf_op jit(solution)/shard_map/ppermute | solution.py:37
  177.0 2.8 %copy-start = (bf16[3072,1024]{1,0:T(8,128)(2,1)S(1)}, bf16[3072,1024]{1,0:T(8,128)(2,1)}, u32[]{:S(2)}) copy-start(bf16[3072,1024]{1,0:T(8,128)(2,1)} %all-gather.2.cloned.1.call-done.w_ref) | copy-start | bytes 18874372
Sparse Core Ops, SparseCore 0:
  55.1 76.3 all-gather.1

commit v7 on v6

--- a/solution.py
+++ b/solution.py
@@ -14,6 +14,7 @@
 F32 = jnp.float32
 VM = pl.BlockSpec(memory_space=pltpu.VMEM)
 SM = pl.BlockSpec(memory_space=pltpu.SMEM)
+HBM = pl.BlockSpec(memory_space=pltpu.HBM)
 PARAMS = pltpu.CompilerParams(vmem_limit_bytes=32 * 2**20)
 
 YL, XN, CORES, ZN, YH = 4, 4, 2, 8, 2
@@ -78,7 +79,7 @@
 
 def attend(nblk, here_ref, order_ref, list_ref, count_ref, *refs):
     blocks = refs[:nblk]
-    w_ref, cot_ref, out_ref, sum_ref, kv_rows, kv_cols, q_cols, acc = refs[nblk:]
+    w_ref, cot_ref, out_ref, keep_ref, send_ref, kv_rows, kv_cols, q_cols, acc = refs[nblk:]
     scale = HEAD_DIM ** (-0.5)
     tiles = kv_rows.shape[0]
     w = w_ref[...]
@@ -138,23 +139,29 @@
         slot += n
         part = dot(jnp.concatenate(left, axis=1), blk, 1, 0)
         total = part if total is None else total + part
-    rows = sum_ref.shape[1]
+    rows = keep_ref.shape[1]
     here = here_ref[0]
-    for i in range(DP):
-        sum_ref[mirror(i) ^ here] = total[i * rows : (i + 1) * rows]
+    first = here < DP // 2
+    for i in range(0, DP, CORES):
+        even, odd = total[i * rows : (i + 1) * rows], total[(i + 1) * rows : (i + 2) * rows]
+        at = (mirror(i) ^ here) % (DP // 2)
+        keep_ref[at] = jnp.where(first, even, odd)
+        send_ref[at] = jnp.where(first, odd, even).astype(BF)
 
 
 def attention(here, order, tile_list, counts, blocks, w_head, cot_t):
     tiles = tile_list.shape[0]
     rows, depth = w_head.shape[0] // DP, w_head.shape[1]
+    outs = (
+        ((tiles, 4 * HEAD_DIM, TILE), BF),
+        ((DP // CORES, rows, depth), F32),
+        ((DP // CORES, rows, depth), BF),
+    )
     return pl.pallas_call(
         functools.partial(attend, len(blocks)),
-        out_shape=(
-            jax.ShapeDtypeStruct((tiles, 4 * HEAD_DIM, TILE), BF),
-            jax.ShapeDtypeStruct((DP, rows, depth), F32),
-        ),
+        out_shape=tuple(jax.ShapeDtypeStruct(*o) for o in outs),
+        out_specs=(VM,) * 3,
         in_specs=[SM, SM, SM, SM] + [VM] * (len(blocks) + 2),
-        out_specs=(VM, VM),
         scratch_shapes=[
             pltpu.VMEM((tiles, TILE, 2 * HEAD_DIM), BF),
             pltpu.VMEM((tiles, 2 * HEAD_DIM, TILE), BF),
@@ -166,8 +173,15 @@
     )(here, order, tile_list, counts, *blocks, w_head, cot_t)
 
 
-def input_sum(both_ref, w_ref, att_ref, out_ref, sorted_ref):
+def input_sum(both_ref, w_ref, att_ref, out_ref, w_here, sorted_ref, sems):
     heads = both_ref.shape[0]
+    parts = sems.shape[0]
+    deep = w_here.shape[0] // parts
+    copies = []
+    for p in range(parts):
+        span = pl.ds(p * deep, deep)
+        copies.append(pltpu.make_async_copy(w_ref.at[span], w_here.at[span], sems.at[p]))
+        copies[-1].start()
     att_ref[...] = jnp.concatenate(
         [both_ref[h, 3 * HEAD_DIM :, :] for h in range(heads)], axis=0
     ).T
@@ -177,22 +191,32 @@
         for d in range(DP):
             at = (d * heads + h) * rows
             sorted_ref[at : at + rows, :] = part[d * rows : (d + 1) * rows]
-    left = sorted_ref[...].astype(BF).T
-    out_ref[...] = dot(left, w_ref[...], 1, 0).astype(BF)
+    total = None
+    for p in range(parts):
+        left = sorted_ref[p * deep : (p + 1) * deep, :].astype(BF).T
+        copies[p].wait()
+        part = dot(left, w_here[p * deep : (p + 1) * deep, :], 1, 0)
+        total = part if total is None else total + part
+    out_ref[...] = total.astype(BF)
 
 
 def input_grad(both, w_all):
     heads = both.shape[0]
+    deep, depth = w_all.shape
     return pl.pallas_call(
         input_sum,
         out_shape=(
             jax.ShapeDtypeStruct((TILE, heads * HEAD_DIM), BF),
-            jax.ShapeDtypeStruct((TILE, w_all.shape[1]), BF),
+            jax.ShapeDtypeStruct((TILE, depth), BF),
         ),
-        in_specs=[VM, VM],
+        in_specs=[VM, HBM],
         out_specs=(VM, VM),
-        scratch_shapes=[pltpu.VMEM((w_all.shape[0], TILE), F32)],
-        compiler_params=PARAMS,
+        scratch_shapes=[
+            pltpu.VMEM((deep, depth), BF),
+            pltpu.VMEM((deep, TILE), F32),
+            pltpu.SemaphoreType.DMA((4,)),
+        ],
+        compiler_params=pltpu.CompilerParams(vmem_limit_bytes=58 * 2**20),
         name="input_sum",
     )(both, w_all)
 
@@ -223,17 +247,20 @@
 
     here = mirror(dp)[None].astype(jnp.int32)
     order = tile_places(z, y_hi)
-    both, sums = attention(here, order, key_tiles[0], key_counts[0], blocks, w_head, mixed)
+    both, keep, send = attention(here, order, key_tiles[0], key_counts[0], blocks, w_head, mixed)
     both = lax.all_to_all(both, "seq", 0, 0, tiled=True)
 
-    for bit in (1, 2, 4, 8, 16):
+    sums = keep + swap_dp(send, 1).astype(F32)
+    for bit in (2, 4, 8, 16):
+        if bit == 8:
+            sums, both = lax.optimization_barrier((sums, both))
         half = sums.shape[0] // 2
         sums = sums[:half] + swap_dp(sums[half:].astype(BF), bit).astype(F32)
-        if bit == 1:
-            w_all, sums = lax.optimization_barrier((w_all, sums))
+        if bit == 8:
+            attended, grad_input = input_grad(both, w_all)
+            sums, attended = lax.optimization_barrier((sums, attended))
     grad_weight = sums * grad_scale
 
-    attended, grad_input = input_grad(both, w_all)
     return (attended[None], grad_input[None], grad_weight)
 
 

time: 190 us -> 194 us (1.021)
  the two profiles are of different devices: /device:TPU:314 before, /device:TPU:56 now
where the time goes in v7:
time: 194 us; the launch traced here: 191 us
  starting transfers between devices  96.4 us (50%)
  waiting for transfers between devices  47.8 us (25%)
  Pallas kernels  17.1 us (9%)
  between operations  14.5 us (7%)
  local copies, waits for them, and re-layouts  12.4 us (6%)
  other arithmetic  2.92 us (2%)
    ppermute x9, starting transfers between devices, shift_z(): return lax.ppermute(x, 'seq', [(s, (s + YH * k) % SEQ) for s in range(SEQ)])  39.9 us
    ppermute x5, starting transfers between devices, swap_dp(): return lax.ppermute(x, 'dp', [(d, d ^ bit) for d in range(DP)])  21.2 us
    ppermute x9, waiting for transfers between devices, shift_z(): return lax.ppermute(x, 'seq', [(s, (s + YH * k) % SEQ) for s in range(SEQ)])  16.2 us
    ppermute x5, waiting for transfers between devices, swap_dp(): return lax.ppermute(x, 'dp', [(d, d ^ bit) for d in range(DP)])  15 us
    all_to_all x1, starting transfers between devices, shards(): both = lax.all_to_all(both, 'seq', 0, 0, tiled=True)  12.7 us
    pallas_call x1, Pallas kernels, attention(): pl.pallas_call(functools.partial(attend, len(blocks)), out_shape=tuple((j...  11.9 us
    all_to_all x1, starting transfers between devices, shards(): mixed = lax.all_to_all(mixed, 'seq', 0, 0, tiled=True)  9.85 us
    all_to_all x1, starting transfers between devices, spread(): return lax.all_to_all(copies, axis, 0, 0, tiled=True)  7.81 us
  transfers between devices with their start and end apart: 19, of which 10 were waited for; matrix products, arithmetic and copies ran while one was open for 5% of the time, Pallas kernels for 6%

profile of v7, /device:TPU:56, one launch (start us, length us, event | category | flops | bytes accessed | tf_op | source)
XLA Modules:
  0.0 191.1 jit_solution(15362952088863838023)
XLA Ops:
  7.2 4.8 %collective-permute-start = (bf16[128,1024]{1,0:T(8,128)(2,1)}, bf16[128,1024]{1,0:T(8,128)(2,1)S(1)}, u32[]{:S(2)}, u32[]{:S(2)}) collective-permute-start(bf16[128,1024]{1,0:T(8,128)(2,1)} %bitcast.27), channel_id=1, source_target_pairs={{0,1},{1,0},{2,3},{3,2},{4,5},{5,4},{6,7},{7,6},{8,9},{9,8},{10,11... | collective-permute-start | bytes 786440 | tf_op jit(solution)/shard_map/ppermute | solution.py:30
  12.0 4.3 %collective-permute-start.1 = (bf16[128,1024]{1,0:T(8,128)(2,1)}, bf16[128,1024]{1,0:T(8,128)(2,1)S(1)}, u32[]{:S(2)}, u32[]{:S(2)}) collective-permute-start(bf16[128,1024]{1,0:T(8,128)(2,1)} %bitcast.28), channel_id=1, source_target_pairs={{0,2},{1,3},{2,4},{3,5},{4,6},{5,7},{6,8},{7,9},{8,10},{9,11},{10,... | collective-permute-start | bytes 786440 | tf_op jit(solution)/shard_map/ppermute | solution.py:34
  16.3 8.6 %collective-permute-start.2 = (bf16[128,1024]{1,0:T(8,128)(2,1)}, bf16[128,1024]{1,0:T(8,128)(2,1)S(1)}, u32[]{:S(2)}, u32[]{:S(2)}) collective-permute-start(bf16[128,1024]{1,0:T(8,128)(2,1)} %bitcast.29), channel_id=1, source_target_pairs={{0,14},{1,15},{2,0},{3,1},{4,2},{5,3},{6,4},{7,5},{8,6},{9,7},{10,... | collective-permute-start | bytes 786440 | tf_op jit(solution)/shard_map/ppermute | solution.py:34
  24.9 0.8 broadcast_in_dim.23
  25.7 1.1 copy.11
  26.8 0.8 pad_maximum_fusion.2
  27.7 9.8 %all-to-all-start = ((bf16[16,112,128]{2,1,0:T(8,128)(2,1)}), bf16[16,112,128]{2,1,0:T(8,128)(2,1)S(1)}, u32[]{:S(2)}, u32[]{:S(2)}) async-start(bf16[16,112,128]{2,1,0:T(8,128)(2,1)} %pad_maximum_fusion.2), calls=%async_computation | async-start | bytes 917504 | tf_op jit(solution)/shard_map/all_to_all | solution.py:240
  37.6 0.9 pad_maximum_fusion.1
  38.5 3.4 %collective-permute-start.3 = (bf16[256,1024]{1,0:T(8,128)(2,1)}, bf16[256,1024]{1,0:T(8,128)(2,1)S(1)}, u32[]{:S(2)}, u32[]{:S(2)}) collective-permute-start(bf16[256,1024]{1,0:T(8,128)(2,1)} %get-tuple-element.32), channel_id=1, source_target_pairs={{0,2},{1,3},{2,4},{3,5},{4,6},{5,7},{6,8},{7,9},{8,10},{9,11},{10,... | collective-permute-start | bytes 1572872 | tf_op jit(solution)/shard_map/ppermute | solution.py:34
  41.9 3.7 %collective-permute-start.5 = (bf16[256,1024]{1,0:T(8,128)(2,1)S(1)}, bf16[256,1024]{1,0:T(8,128)(2,1)S(1)}, u32[]{:S(2)}, u32[]{:S(2)}) collective-permute-start(bf16[256,1024]{1,0:T(8,128)(2,1)S(1)} %get-tuple-element.31), channel_id=1, source_target_pairs={{0,14},{1,15},{2,0},{3,1},{4,2},{5,3},{6,4},{7,5},{8,6},{9,7},{10,... | collective-permute-start | bytes 1572872 | tf_op jit(solution)/shard_map/ppermute | solution.py:34
  45.6 6.5 %all-to-all-done.refs_12_ = bf16[16,112,128]{2,1,0:T(8,128)(2,1)S(1)} async-done(((bf16[16,112,128]{2,1,0:T(8,128)(2,1)}), bf16[16,112,128]{2,1,0:T(8,128)(2,1)S(1)}, u32[]{:S(2)}, u32[]{:S(2)}) %all-to-all-start) | async-done | bytes 458784 | tf_op jit(solution)/shard_map/all_to_all | solution.py:240
  52.0 0.8 reshape.19
  52.8 8.0 %collective-permute-done.3.refs_4_ = bf16[256,1024]{1,0:T(8,128)(2,1)S(1)} collective-permute-done((bf16[256,1024]{1,0:T(8,128)(2,1)}, bf16[256,1024]{1,0:T(8,128)(2,1)S(1)}, u32[]{:S(2)}, u32[]{:S(2)}) %collective-permute-start.3) | collective-permute-done | bytes 524320 | tf_op jit(solution)/shard_map/ppermute | solution.py:34
  60.8 3.8 %collective-permute-start.4 = (bf16[256,1024]{1,0:T(8,128)(2,1)S(1)}, bf16[256,1024]{1,0:T(8,128)(2,1)S(1)}, u32[]{:S(2)}, u32[]{:S(2)}) collective-permute-start(bf16[256,1024]{1,0:T(8,128)(2,1)S(1)} %collective-permute-done.3.refs_4_), channel_id=1, source_target_pairs={{0,2},{1,3},{2,4},{3,5},{4,6},{5,7},{6,8},{7,9},{8,10},{9,11},{10,... | collective-permute-start | bytes 1572872 | tf_op jit(solution)/shard_map/ppermute | solution.py:34
  64.6 3.2 %collective-permute-start.6 = (bf16[256,1024]{1,0:T(8,128)(2,1)S(1)}, bf16[256,1024]{1,0:T(8,128)(2,1)S(1)}, u32[]{:S(2)}, u32[]{:S(2)}) collective-permute-start(bf16[256,1024]{1,0:T(8,128)(2,1)S(1)} %collective-permute-done.5.refs_6_), channel_id=1, source_target_pairs={{0,14},{1,15},{2,0},{3,1},{4,2},{5,3},{6,4},{7,5},{8,6},{9,7},{10,... | collective-permute-start | bytes 1572872 | tf_op jit(solution)/shard_map/ppermute | solution.py:34
  67.9 1.6 broadcast_in_dim.25
  69.5 7.8 %all-to-all-start.1 = ((bf16[32,6,1024]{2,1,0:T(8,128)(2,1)}), bf16[32,6,1024]{2,1,0:T(8,128)(2,1)}, u32[]{:S(2)}, u32[]{:S(2)}) async-start(bf16[32,6,1024]{2,1,0:T(8,128)(2,1)} %broadcast_in_dim.25), calls=%async_computation.1 | async-start | bytes 1048576 | tf_op jit(solution)/shard_map/all_to_all | solution.py:43
  77.3 0.8 slice.48
  78.1 2.7 %collective-permute-start.7 = (bf16[192,1024]{1,0:T(8,128)(2,1)}, bf16[192,1024]{1,0:T(8,128)(2,1)}, u32[]{:S(2)}, u32[]{:S(2)}) collective-permute-start(bf16[192,1024]{1,0:T(8,128)(2,1)} %slice.48), channel_id=1, source_target_pairs={{0,2},{1,3},{2,4},{3,5},{4,6},{5,7},{6,8},{7,9},{8,10},{9,11},{10,... | collective-permute-start | bytes 1179656 | tf_op jit(solution)/shard_map/ppermute | solution.py:34
  80.9 0.8 slice.49
  81.6 4.3 %collective-permute-start.8 = (bf16[192,1024]{1,0:T(8,128)(2,1)}, bf16[192,1024]{1,0:T(8,128)(2,1)}, u32[]{:S(2)}, u32[]{:S(2)}) collective-permute-start(bf16[192,1024]{1,0:T(8,128)(2,1)} %slice.49), channel_id=1, source_target_pairs={{0,14},{1,15},{2,0},{3,1},{4,2},{5,3},{6,4},{7,5},{8,6},{9,7},{10,... | collective-permute-start | bytes 1179656 | tf_op jit(solution)/shard_map/ppermute | solution.py:34
  85.9 5.9 %collective-permute-start.9 = (bf16[128,1024]{1,0:T(8,128)(2,1)S(1)}, bf16[128,1024]{1,0:T(8,128)(2,1)}, u32[]{:S(2)}, u32[]{:S(2)}) collective-permute-start(bf16[128,1024]{1,0:T(8,128)(2,1)S(1)} %collective-permute-done.refs_1_), channel_id=1, source_target_pairs={{0,8},{1,9},{2,10},{3,11},{4,12},{5,13},{6,14},{7,15},{8,0},{9,1},... | collective-permute-start | bytes 786440 | tf_op jit(solution)/shard_map/ppermute | solution.py:34
  91.9 0.1 copy.12.list_ref
  92.0 0.1 stack.67.order_ref
  92.1 3.4 %all-to-all-done.1 = bf16[32,6,1024]{2,1,0:T(8,128)(2,1)} async-done(((bf16[32,6,1024]{2,1,0:T(8,128)(2,1)}), bf16[32,6,1024]{2,1,0:T(8,128)(2,1)}, u32[]{:S(2)}, u32[]{:S(2)}) %all-to-all-start.1) | async-done | bytes 393248 | tf_op jit(solution)/shard_map/all_to_all | solution.py:43
  95.6 1.2 reshape.18.refs_11_
  96.8 8.2 %collective-permute-done.9.refs_10_ = bf16[128,1024]{1,0:T(8,128)(2,1)} collective-permute-done((bf16[128,1024]{1,0:T(8,128)(2,1)S(1)}, bf16[128,1024]{1,0:T(8,128)(2,1)}, u32[]{:S(2)}, u32[]{:S(2)}) %collective-permute-start.9) | collective-permute-done | bytes 262176 | tf_op jit(solution)/shard_map/ppermute | solution.py:34
  105.0 1.0 copy-done.2
  106.0 1.0 copy-done.4
  107.0 11.9 %attend.1 = (bf16[16,256,128]{2,1,0:T(8,128)(2,1)S(1)}, f32[16,6,1024]{2,1,0:T(8,128)S(1)}, bf16[16,6,1024]{2,1,0:T(8,128)(2,1)S(1)}) custom-call(s32[1]{0:T(128)} %bitcast.here_ref, s32[16]{0:T(128)S(1)} %stack.67.order_ref, s32[16,4]{1,0:T(8,128)S(1)} %copy.12.list_ref, s32[16]{0:T(128)S(1)} %bitcast.31, bf16[128,1024]{1,0:T(8,128)(2,1)S(1)} %bitcast.30, ...), custom_call_target="tpu_custom_call" | custom-call | tf_op jit(solution)/shard_map/attend/pallas_call | solution.py:160
  118.9 1.0 copy-done
  119.9 0.8 copy-done.3
  120.7 0.7 copy-done.6
  121.4 12.7 %all-to-all-start.2 = ((bf16[16,256,128]{2,1,0:T(8,128)(2,1)}), bf16[16,256,128]{2,1,0:T(8,128)(2,1)S(1)}, u32[]{:S(2)}, u32[]{:S(2)}) async-start(bf16[16,256,128]{2,1,0:T(8,128)(2,1)} %copy-done), calls=%async_computation.2 | async-start | bytes 2097152 | tf_op jit(solution)/shard_map/all_to_all | solution.py:251
  134.1 1.9 collective-permute-start.10
  136.1 1.7 collective-permute-done.10
  137.8 1.1 convert_add_fusion
  138.9 3.4 %collective-permute-start.11 = (bf16[8,6,1024]{2,1,0:T(8,128)(2,1)S(1)}, bf16[8,6,1024]{2,1,0:T(8,128)(2,1)S(1)}, u32[]{:S(2)}, u32[]{:S(2)}) collective-permute-start(bf16[8,6,1024]{2,1,0:T(8,128)(2,1)S(1)} %slice.65), channel_id=1, source_target_pairs={{0,32},{16,48},{32,0},{48,16},{64,96},{80,112},{96,64},{112,80},{1... | collective-permute-start | bytes 294920 | tf_op jit(solution)/shard_map/ppermute | solution.py:38
  142.3 4.0 %collective-permute-done.11 = bf16[8,6,1024]{2,1,0:T(8,128)(2,1)S(1)} collective-permute-done((bf16[8,6,1024]{2,1,0:T(8,128)(2,1)S(1)}, bf16[8,6,1024]{2,1,0:T(8,128)(2,1)S(1)}, u32[]{:S(2)}, u32[]{:S(2)}) %collective-permute-start.11) | collective-permute-done | bytes 98336 | tf_op jit(solution)/shard_map/ppermute | solution.py:38
  146.4 4.9 %collective-permute-start.12 = (bf16[4,6,1024]{2,1,0:T(8,128)(2,1)S(1)}, bf16[4,6,1024]{2,1,0:T(8,128)(2,1)S(1)}, u32[]{:S(2)}, u32[]{:S(2)}) collective-permute-start(bf16[4,6,1024]{2,1,0:T(8,128)(2,1)S(1)} %slice.66), channel_id=1, source_target_pairs={{0,64},{16,80},{32,96},{48,112},{64,0},{80,16},{96,32},{112,48},{1... | collective-permute-start | bytes 147464 | tf_op jit(solution)/shard_map/ppermute | solution.py:38
  151.3 2.7 %collective-permute-done.12 = bf16[4,6,1024]{2,1,0:T(8,128)(2,1)S(1)} collective-permute-done((bf16[4,6,1024]{2,1,0:T(8,128)(2,1)S(1)}, bf16[4,6,1024]{2,1,0:T(8,128)(2,1)S(1)}, u32[]{:S(2)}, u32[]{:S(2)}) %collective-permute-start.12) | collective-permute-done | bytes 49184 | tf_op jit(solution)/shard_map/ppermute | solution.py:38
  154.1 6.7 %all-to-all-done.2.both_ref = bf16[16,256,128]{2,1,0:T(8,128)(2,1)S(1)} async-done(((bf16[16,256,128]{2,1,0:T(8,128)(2,1)}), bf16[16,256,128]{2,1,0:T(8,128)(2,1)S(1)}, u32[]{:S(2)}, u32[]{:S(2)}) %all-to-all-start.2) | async-done | bytes 1048608 | tf_op jit(solution)/shard_map/all_to_all | solution.py:251
  160.8 9.1 %collective-permute-start.13 = (bf16[2,6,1024]{2,1,0:T(8,128)(2,1)S(1)}, bf16[2,6,1024]{2,1,0:T(8,128)(2,1)S(1)}, u32[]{:S(2)}, u32[]{:S(2)}) collective-permute-start(bf16[2,6,1024]{2,1,0:T(8,128)(2,1)S(1)} %slice.67), channel_id=1, source_target_pairs={{0,128},{16,144},{32,160},{48,176},{64,192},{80,208},{96,224},{112... | collective-permute-start | bytes 73736 | tf_op jit(solution)/shard_map/ppermute | solution.py:38
  169.9 1.9 collective-permute-done.13
  171.9 5.2 %input_sum.1 = (bf16[128,1024]{1,0:T(8,128)(2,1)}, bf16[128,1024]{1,0:T(8,128)(2,1)}) custom-call(bf16[16,256,128]{2,1,0:T(8,128)(2,1)} %copy-done.7, bf16[3072,1024]{1,0:T(8,128)(2,1)} %all-gather.2.cloned.1.call-done.w_ref), custom_call_target="tpu_custom_call" | custom-call | tf_op jit(solution)/shard_map/input_sum/pallas_call | solution.py:206
  177.1 1.9 %collective-permute-start.14 = (bf16[1,6,1024]{2,1,0:T(8,128)(2,1)S(1)}, bf16[1,6,1024]{2,1,0:T(8,128)(2,1)S(1)}, u32[]{:S(2)}, u32[]{:S(2)}) collective-permute-start(bf16[1,6,1024]{2,1,0:T(8,128)(2,1)S(1)} %slice.68), channel_id=1, source_target_pairs={{0,256},{16,272},{32,288},{48,304},{64,320},{80,336},{96,352},{112... | collective-permute-start | bytes 36872 | tf_op jit(solution)/shard_map/ppermute | solution.py:38
  179.0 4.6 %collective-permute-done.14 = bf16[1,6,1024]{2,1,0:T(8,128)(2,1)S(1)} collective-permute-done((bf16[1,6,1024]{2,1,0:T(8,128)(2,1)S(1)}, bf16[1,6,1024]{2,1,0:T(8,128)(2,1)S(1)}, u32[]{:S(2)}, u32[]{:S(2)}) %collective-permute-start.14) | collective-permute-done | bytes 12320 | tf_op jit(solution)/shard_map/ppermute | solution.py:38
  183.6 0.6 copy.13
  (34 shorter events, 0.3 us)
Async XLA Ops:
  7.2 84.8 %copy-start.8 = (s32[1,16,4]{1,2,0:T(4,128)S(1)}, s32[1,16,4]{1,2,0:T(4,128)}, u32[]{:S(2)}) copy-start(s32[1,16,4]{1,2,0:T(4,128)} %param.7) | copy-start | bytes 772
  7.2 97.8 %copy-start.5 = (s32[1,16]{1,0:T(1,128)S(1)}, s32[1,16]{1,0:T(1,128)}, u32[]{:S(2)}) copy-start(s32[1,16]{1,0:T(1,128)} %param.8) | copy-start | bytes 196
  7.2 30.4 %collective-permute-start = (bf16[128,1024]{1,0:T(8,128)(2,1)}, bf16[128,1024]{1,0:T(8,128)(2,1)S(1)}, u32[]{:S(2)}, u32[]{:S(2)}) collective-permute-start(bf16[128,1024]{1,0:T(8,128)(2,1)} %bitcast.27), channel_id=1, source_target_pairs={{0,1},{1,0},{2,3},{3,2},{4,5},{5,4},{6,7},{7,6},{8,9},{9,8},{10,11... | collective-permute-start | bytes 786440 | tf_op jit(solution)/shard_map/ppermute | solution.py:30
  12.0 25.5 %collective-permute-start.1 = (bf16[128,1024]{1,0:T(8,128)(2,1)}, bf16[128,1024]{1,0:T(8,128)(2,1)S(1)}, u32[]{:S(2)}, u32[]{:S(2)}) collective-permute-start(bf16[128,1024]{1,0:T(8,128)(2,1)} %bitcast.28), channel_id=1, source_target_pairs={{0,2},{1,3},{2,4},{3,5},{4,6},{5,7},{6,8},{7,9},{8,10},{9,11},{10,... | collective-permute-start | bytes 786440 | tf_op jit(solution)/shard_map/ppermute | solution.py:34
  16.3 21.3 %collective-permute-start.2 = (bf16[128,1024]{1,0:T(8,128)(2,1)}, bf16[128,1024]{1,0:T(8,128)(2,1)S(1)}, u32[]{:S(2)}, u32[]{:S(2)}) collective-permute-start(bf16[128,1024]{1,0:T(8,128)(2,1)} %bitcast.29), channel_id=1, source_target_pairs={{0,14},{1,15},{2,0},{3,1},{4,2},{5,3},{6,4},{7,5},{8,6},{9,7},{10,... | collective-permute-start | bytes 786440 | tf_op jit(solution)/shard_map/ppermute | solution.py:34
  27.7 24.3 %all-to-all-start = ((bf16[16,112,128]{2,1,0:T(8,128)(2,1)}), bf16[16,112,128]{2,1,0:T(8,128)(2,1)S(1)}, u32[]{:S(2)}, u32[]{:S(2)}) async-start(bf16[16,112,128]{2,1,0:T(8,128)(2,1)} %pad_maximum_fusion.2), calls=%async_computation | async-start | bytes 917504 | tf_op jit(solution)/shard_map/all_to_all | solution.py:240
  37.5 134.3 %all-gather.2.cloned.1.call-start = ((), (), s32[]{:S(2)}) async-start(), calls=%async_computation.3 | async-start | bytes 6488064 | tf_op jit(solution)/shard_map/all_gather | solution.py:243
  38.5 22.2 %collective-permute-start.3 = (bf16[256,1024]{1,0:T(8,128)(2,1)}, bf16[256,1024]{1,0:T(8,128)(2,1)S(1)}, u32[]{:S(2)}, u32[]{:S(2)}) collective-permute-start(bf16[256,1024]{1,0:T(8,128)(2,1)} %get-tuple-element.32), channel_id=1, source_target_pairs={{0,2},{1,3},{2,4},{3,5},{4,6},{5,7},{6,8},{7,9},{8,10},{9,11},{10,... | collective-permute-start | bytes 1572872 | tf_op jit(solution)/shard_map/ppermute | solution.py:34
  41.9 18.9 %collective-permute-start.5 = (bf16[256,1024]{1,0:T(8,128)(2,1)S(1)}, bf16[256,1024]{1,0:T(8,128)(2,1)S(1)}, u32[]{:S(2)}, u32[]{:S(2)}) collective-permute-start(bf16[256,1024]{1,0:T(8,128)(2,1)S(1)} %get-tuple-element.31), channel_id=1, source_target_pairs={{0,14},{1,15},{2,0},{3,1},{4,2},{5,3},{6,4},{7,5},{8,6},{9,7},{10,... | collective-permute-start | bytes 1572872 | tf_op jit(solution)/shard_map/ppermute | solution.py:34
  60.8 31.4 %copy-start.1 = (bf16[256,1024]{1,0:T(8,128)(2,1)}, bf16[256,1024]{1,0:T(8,128)(2,1)S(1)}, u32[]{:S(2)}) copy-start(bf16[256,1024]{1,0:T(8,128)(2,1)S(1)} %collective-permute-done.5.refs_6_) | copy-start | bytes 1572868
  60.8 16.5 %collective-permute-start.4 = (bf16[256,1024]{1,0:T(8,128)(2,1)S(1)}, bf16[256,1024]{1,0:T(8,128)(2,1)S(1)}, u32[]{:S(2)}, u32[]{:S(2)}) collective-permute-start(bf16[256,1024]{1,0:T(8,128)(2,1)S(1)} %collective-permute-done.3.refs_4_), channel_id=1, source_target_pairs={{0,2},{1,3},{2,4},{3,5},{4,6},{5,7},{6,8},{7,9},{8,10},{9,11},{10,... | collective-permute-start | bytes 1572872 | tf_op jit(solution)/shard_map/ppermute | solution.py:34
  64.6 16.2 %collective-permute-start.6 = (bf16[256,1024]{1,0:T(8,128)(2,1)S(1)}, bf16[256,1024]{1,0:T(8,128)(2,1)S(1)}, u32[]{:S(2)}, u32[]{:S(2)}) collective-permute-start(bf16[256,1024]{1,0:T(8,128)(2,1)S(1)} %collective-permute-done.5.refs_6_), channel_id=1, source_target_pairs={{0,14},{1,15},{2,0},{3,1},{4,2},{5,3},{6,4},{7,5},{8,6},{9,7},{10,... | collective-permute-start | bytes 1572872 | tf_op jit(solution)/shard_map/ppermute | solution.py:34
  69.5 26.1 %all-to-all-start.1 = ((bf16[32,6,1024]{2,1,0:T(8,128)(2,1)}), bf16[32,6,1024]{2,1,0:T(8,128)(2,1)}, u32[]{:S(2)}, u32[]{:S(2)}) async-start(bf16[32,6,1024]{2,1,0:T(8,128)(2,1)} %broadcast_in_dim.25), calls=%async_computation.1 | async-start | bytes 1048576 | tf_op jit(solution)/shard_map/all_to_all | solution.py:43
  78.1 26.9 %collective-permute-start.7 = (bf16[192,1024]{1,0:T(8,128)(2,1)}, bf16[192,1024]{1,0:T(8,128)(2,1)}, u32[]{:S(2)}, u32[]{:S(2)}) collective-permute-start(bf16[192,1024]{1,0:T(8,128)(2,1)} %slice.48), channel_id=1, source_target_pairs={{0,2},{1,3},{2,4},{3,5},{4,6},{5,7},{6,8},{7,9},{8,10},{9,11},{10,... | collective-permute-start | bytes 1179656 | tf_op jit(solution)/shard_map/ppermute | solution.py:34
  81.6 23.3 %collective-permute-start.8 = (bf16[192,1024]{1,0:T(8,128)(2,1)}, bf16[192,1024]{1,0:T(8,128)(2,1)}, u32[]{:S(2)}, u32[]{:S(2)}) collective-permute-start(bf16[192,1024]{1,0:T(8,128)(2,1)} %slice.49), channel_id=1, source_target_pairs={{0,14},{1,15},{2,0},{3,1},{4,2},{5,3},{6,4},{7,5},{8,6},{9,7},{10,... | collective-permute-start | bytes 1179656 | tf_op jit(solution)/shard_map/ppermute | solution.py:34
  85.9 19.0 %collective-permute-start.9 = (bf16[128,1024]{1,0:T(8,128)(2,1)S(1)}, bf16[128,1024]{1,0:T(8,128)(2,1)}, u32[]{:S(2)}, u32[]{:S(2)}) collective-permute-start(bf16[128,1024]{1,0:T(8,128)(2,1)S(1)} %collective-permute-done.refs_1_), channel_id=1, source_target_pairs={{0,8},{1,9},{2,10},{3,11},{4,12},{5,13},{6,14},{7,15},{8,0},{9,1},... | collective-permute-start | bytes 786440 | tf_op jit(solution)/shard_map/ppermute | solution.py:34
  105.0 1.0 copy-start.2
  106.0 1.0 copy-start.4
  118.9 1.0 copy-start
  119.9 0.8 copy-start.3
  120.7 0.7 copy-start.6
  121.4 39.4 %all-to-all-start.2 = ((bf16[16,256,128]{2,1,0:T(8,128)(2,1)}), bf16[16,256,128]{2,1,0:T(8,128)(2,1)S(1)}, u32[]{:S(2)}, u32[]{:S(2)}) async-start(bf16[16,256,128]{2,1,0:T(8,128)(2,1)} %copy-done), calls=%async_computation.2 | async-start | bytes 2097152 | tf_op jit(solution)/shard_map/all_to_all | solution.py:251
  134.1 3.6 %collective-permute-start.10 = (bf16[16,6,1024]{2,1,0:T(8,128)(2,1)}, bf16[16,6,1024]{2,1,0:T(8,128)(2,1)S(1)}, u32[]{:S(2)}, u32[]{:S(2)}) collective-permute-start(bf16[16,6,1024]{2,1,0:T(8,128)(2,1)} %copy-done.6), channel_id=1, source_target_pairs={{0,16},{16,0},{32,48},{48,32},{64,80},{80,64},{96,112},{112,96},{1... | collective-permute-start | bytes 589832 | tf_op jit(solution)/shard_map/ppermute | solution.py:38
  138.9 7.4 %collective-permute-start.11 = (bf16[8,6,1024]{2,1,0:T(8,128)(2,1)S(1)}, bf16[8,6,1024]{2,1,0:T(8,128)(2,1)S(1)}, u32[]{:S(2)}, u32[]{:S(2)}) collective-permute-start(bf16[8,6,1024]{2,1,0:T(8,128)(2,1)S(1)} %slice.65), channel_id=1, source_target_pairs={{0,32},{16,48},{32,0},{48,16},{64,96},{80,112},{96,64},{112,80},{1... | collective-permute-start | bytes 294920 | tf_op jit(solution)/shard_map/ppermute | solution.py:38
  146.4 7.7 %collective-permute-start.12 = (bf16[4,6,1024]{2,1,0:T(8,128)(2,1)S(1)}, bf16[4,6,1024]{2,1,0:T(8,128)(2,1)S(1)}, u32[]{:S(2)}, u32[]{:S(2)}) collective-permute-start(bf16[4,6,1024]{2,1,0:T(8,128)(2,1)S(1)} %slice.66), channel_id=1, source_target_pairs={{0,64},{16,80},{32,96},{48,112},{64,0},{80,16},{96,32},{112,48},{1... | collective-permute-start | bytes 147464 | tf_op jit(solution)/shard_map/ppermute | solution.py:38
  160.8 11.0 %copy-start.7 = (bf16[16,256,128]{2,1,0:T(8,128)(2,1)}, bf16[16,256,128]{2,1,0:T(8,128)(2,1)S(1)}, u32[]{:S(2)}) copy-start(bf16[16,256,128]{2,1,0:T(8,128)(2,1)S(1)} %all-to-all-done.2.both_ref) | copy-start | bytes 3145732
  160.8 11.0 %collective-permute-start.13 = (bf16[2,6,1024]{2,1,0:T(8,128)(2,1)S(1)}, bf16[2,6,1024]{2,1,0:T(8,128)(2,1)S(1)}, u32[]{:S(2)}, u32[]{:S(2)}) collective-permute-start(bf16[2,6,1024]{2,1,0:T(8,128)(2,1)S(1)} %slice.67), channel_id=1, source_target_pairs={{0,128},{16,144},{32,160},{48,176},{64,192},{80,208},{96,224},{112... | collective-permute-start | bytes 73736 | tf_op jit(solution)/shard_map/ppermute | solution.py:38
  177.1 6.5 %collective-permute-start.14 = (bf16[1,6,1024]{2,1,0:T(8,128)(2,1)S(1)}, bf16[1,6,1024]{2,1,0:T(8,128)(2,1)S(1)}, u32[]{:S(2)}, u32[]{:S(2)}) collective-permute-start(bf16[1,6,1024]{2,1,0:T(8,128)(2,1)S(1)} %slice.68), channel_id=1, source_target_pairs={{0,256},{16,272},{32,288},{48,304},{64,320},{80,336},{96,352},{112... | collective-permute-start | bytes 36872 | tf_op jit(solution)/shard_map/ppermute | solution.py:38
Sparse Core Ops, SparseCore 0:
  60.9 74.2 all-gather.1

commit v8 on v6

--- a/solution.py
+++ b/solution.py
@@ -47,38 +47,40 @@
 
 
 def tiles_of(blocks):
-    own, flip, r1, l1, r2, r3, l2, l3, r4, l4, far = blocks
+    *whole, r3, l3, r4, l4 = blocks
     half = TILE // 2
-    yield from (own[...], flip[...], r1[...], l1[...])
-    for pair in (r2, r3, l2, l3):
-        yield pair[...]
-    yield r4[:TILE]
-    yield l4[half:]
-    yield jnp.concatenate([r4[TILE:], l4[:half]], axis=0)
-    yield far[...]
+    for block in whole:
+        yield block[...]
+    yield r3[:TILE]
+    yield l3[half:]
+    yield jnp.concatenate([r3[TILE:], l3[:half]], axis=0)
+    yield jnp.concatenate([r4[...], l4[...]], axis=0)
 
 
 def tile_places(z, y_hi):
-    steps = [(0, 0), (0, 1), (-1, 0), (1, 0), (-1, 1), (-2, 0), (-2, 1), (-3, 0)]
-    steps += [(2, 0), (1, 1), (3, 0), (2, 1), (-3, 1), (3, 1), (4, 0), (4, 1)]
+    steps = [(0, 0), (0, 1), (-1, 0), (1, 0), (-2, 0), (2, 0), (-1, 1), (-3, 0), (3, 0), (1, 1)]
+    steps += [(-2, 1), (2, 1), (-3, 1), (3, 1), (4, 0), (4, 1)]
     places = [lax.rem(z + k + ZN, ZN) * YH + lax.rem(y_hi + j, YH) for k, j in steps]
     return jnp.stack(places).astype(jnp.int32)
 
 
 def gather_scene(own):
-    flip, r1, l1 = flip_y(own), shift_z(own, 1), shift_z(own, -1)
-    r2 = shift_z(jnp.concatenate([flip, r1], axis=0), 1)
-    l2 = shift_z(jnp.concatenate([l1, flip], axis=0), -1)
-    r3, l3 = shift_z(r2, 1), shift_z(l2, -1)
     half = TILE // 2
-    r4, l4 = shift_z(r3[: TILE + half], 1), shift_z(l3[half:], -1)
-    far = shift_z(flip, ZN // 2)
-    return own, flip, r1, l1, r2, r3, l2, l3, r4, l4, far
+    flip = flip_y(own)
+    r1, l1, r2, l2 = (shift_z(own, k) for k in (1, -1, 2, -2))
+    flip, r1, l1 = lax.optimization_barrier((flip, r1, l1))
+    right = shift_z(jnp.concatenate([flip, r2], axis=0), 1)
+    left = shift_z(jnp.concatenate([l2, flip], axis=0), -1)
+    ry, ly = shift_z(flip, 2), shift_z(flip, -2)
+    r3 = shift_z(jnp.concatenate([ry, right[TILE : TILE + half]], axis=0), 1)
+    l3 = shift_z(jnp.concatenate([left[half:TILE], ly], axis=0), -1)
+    r4, l4 = shift_z(ry[:half], 2), shift_z(ly[half:], -2)
+    return own, flip, r1, l1, r2, l2, right, left, ry, ly, r3, l3, r4, l4
 
 
 def attend(nblk, here_ref, order_ref, list_ref, count_ref, *refs):
     blocks = refs[:nblk]
-    w_ref, cot_ref, out_ref, sum_ref, kv_rows, kv_cols, q_cols, acc = refs[nblk:]
+    w_ref, cot_ref, out_ref, keep_ref, send_ref, kv_rows, kv_cols, q_cols, acc = refs[nblk:]
     scale = HEAD_DIM ** (-0.5)
     tiles = kv_rows.shape[0]
     w = w_ref[...]
@@ -138,23 +140,29 @@
         slot += n
         part = dot(jnp.concatenate(left, axis=1), blk, 1, 0)
         total = part if total is None else total + part
-    rows = sum_ref.shape[1]
+    rows = keep_ref.shape[1]
     here = here_ref[0]
-    for i in range(DP):
-        sum_ref[mirror(i) ^ here] = total[i * rows : (i + 1) * rows]
+    first = here < DP // 2
+    for i in range(0, DP, CORES):
+        even, odd = total[i * rows : (i + 1) * rows], total[(i + 1) * rows : (i + 2) * rows]
+        at = (mirror(i) ^ here) % (DP // 2)
+        keep_ref[at] = jnp.where(first, even, odd)
+        send_ref[at] = jnp.where(first, odd, even).astype(BF)
 
 
 def attention(here, order, tile_list, counts, blocks, w_head, cot_t):
     tiles = tile_list.shape[0]
     rows, depth = w_head.shape[0] // DP, w_head.shape[1]
+    outs = (
+        ((tiles, 4 * HEAD_DIM, TILE), BF),
+        ((DP // CORES, rows, depth), F32),
+        ((DP // CORES, rows, depth), BF),
+    )
     return pl.pallas_call(
         functools.partial(attend, len(blocks)),
-        out_shape=(
-            jax.ShapeDtypeStruct((tiles, 4 * HEAD_DIM, TILE), BF),
-            jax.ShapeDtypeStruct((DP, rows, depth), F32),
-        ),
+        out_shape=tuple(jax.ShapeDtypeStruct(*o) for o in outs),
+        out_specs=(VM,) * 3,
         in_specs=[SM, SM, SM, SM] + [VM] * (len(blocks) + 2),
-        out_specs=(VM, VM),
         scratch_shapes=[
             pltpu.VMEM((tiles, TILE, 2 * HEAD_DIM), BF),
             pltpu.VMEM((tiles, 2 * HEAD_DIM, TILE), BF),
@@ -215,7 +223,7 @@
     mixed = jnp.concatenate([cot_t, copies], axis=1)
     mixed = lax.all_to_all(mixed, "seq", 0, 0, tiled=True)
     w_seq = mixed[:, HEAD_DIM:].reshape(heads * rows, depth)
-    w_seq, _ = lax.optimization_barrier((w_seq, (blocks[4], blocks[6])))
+    w_seq, _ = lax.optimization_barrier((w_seq, blocks[6:10]))
     w_all = lax.all_gather(w_seq, "dp", axis=0, tiled=True)
 
     own_rows, _ = lax.optimization_barrier((own_rows, mixed))
@@ -223,14 +231,14 @@
 
     here = mirror(dp)[None].astype(jnp.int32)
     order = tile_places(z, y_hi)
-    both, sums = attention(here, order, key_tiles[0], key_counts[0], blocks, w_head, mixed)
+    both, keep, send = attention(here, order, key_tiles[0], key_counts[0], blocks, w_head, mixed)
     both = lax.all_to_all(both, "seq", 0, 0, tiled=True)
 
-    for bit in (1, 2, 4, 8, 16):
+    sums = keep + swap_dp(send, 1).astype(F32)
+    w_all, sums = lax.optimization_barrier((w_all, sums))
+    for bit in (2, 4, 8, 16):
         half = sums.shape[0] // 2
         sums = sums[:half] + swap_dp(sums[half:].astype(BF), bit).astype(F32)
-        if bit == 1:
-            w_all, sums = lax.optimization_barrier((w_all, sums))
     grad_weight = sums * grad_scale
 
     attended, grad_input = input_grad(both, w_all)

time: 190 us -> 209 us (1.10)
  the two profiles are of different devices: /device:TPU:314 before, /device:TPU:56 now
where the time goes in v8:
time: 209 us; the launch traced here: 207 us
  starting transfers between devices  113 us (54%)
  waiting for transfers between devices  46 us (22%)
  Pallas kernels  15.1 us (7%)
  between operations  14.6 us (7%)
  local copies, waits for them, and re-layouts  13.9 us (7%)
  other arithmetic  4.7 us (2%)
    ppermute x12, starting transfers between devices, shift_z(): return lax.ppermute(x, 'seq', [(s, (s + YH * k) % SEQ) for s in range(SEQ)])  48.4 us
    ppermute x5, starting transfers between devices, swap_dp(): return lax.ppermute(x, 'dp', [(d, d ^ bit) for d in range(DP)])  30.9 us
    ppermute x12, waiting for transfers between devices, shift_z(): return lax.ppermute(x, 'seq', [(s, (s + YH * k) % SEQ) for s in range(SEQ)])  24.4 us
    pallas_call x1, Pallas kernels, attention(): pl.pallas_call(functools.partial(attend, len(blocks)), out_shape=tuple((j...  13.2 us
    ppermute x5, waiting for transfers between devices, swap_dp(): return lax.ppermute(x, 'dp', [(d, d ^ bit) for d in range(DP)])  11.4 us
    all_to_all x1, starting transfers between devices, shards(): both = lax.all_to_all(both, 'seq', 0, 0, tiled=True)  11.4 us
    all_gather x1, waiting for transfers between devices, shards(): w_all = lax.all_gather(w_seq, 'dp', axis=0, tiled=True)  10.2 us
    all_to_all x1, starting transfers between devices, shards(): mixed = lax.all_to_all(mixed, 'seq', 0, 0, tiled=True)  9.85 us
  transfers between devices with their start and end apart: 22, of which 8 were waited for; matrix products, arithmetic and copies ran while one was open for 6% of the time, Pallas kernels for 7%

profile of v8, /device:TPU:56, one launch (start us, length us, event | category | flops | bytes accessed | tf_op | source)
XLA Modules:
  0.0 207.5 jit_solution(13179415969392646897)
XLA Ops:
  7.2 4.8 %collective-permute-start = (bf16[128,1024]{1,0:T(8,128)(2,1)}, bf16[128,1024]{1,0:T(8,128)(2,1)S(1)}, u32[]{:S(2)}, u32[]{:S(2)}) collective-permute-start(bf16[128,1024]{1,0:T(8,128)(2,1)} %bitcast.27), channel_id=1, source_target_pairs={{0,1},{1,0},{2,3},{3,2},{4,5},{5,4},{6,7},{7,6},{8,9},{9,8},{10,11... | collective-permute-start | bytes 786440 | tf_op jit(solution)/shard_map/ppermute | solution.py:29
  12.0 4.3 %collective-permute-start.1 = (bf16[128,1024]{1,0:T(8,128)(2,1)}, bf16[128,1024]{1,0:T(8,128)(2,1)S(1)}, u32[]{:S(2)}, u32[]{:S(2)}) collective-permute-start(bf16[128,1024]{1,0:T(8,128)(2,1)} %bitcast.28), channel_id=1, source_target_pairs={{0,2},{1,3},{2,4},{3,5},{4,6},{5,7},{6,8},{7,9},{8,10},{9,11},{10,... | collective-permute-start | bytes 786440 | tf_op jit(solution)/shard_map/ppermute | solution.py:33
  16.3 8.6 %collective-permute-start.2 = (bf16[128,1024]{1,0:T(8,128)(2,1)}, bf16[128,1024]{1,0:T(8,128)(2,1)S(1)}, u32[]{:S(2)}, u32[]{:S(2)}) collective-permute-start(bf16[128,1024]{1,0:T(8,128)(2,1)} %bitcast.29), channel_id=1, source_target_pairs={{0,14},{1,15},{2,0},{3,1},{4,2},{5,3},{6,4},{7,5},{8,6},{9,7},{10,... | collective-permute-start | bytes 786440 | tf_op jit(solution)/shard_map/ppermute | solution.py:33
  24.9 1.9 collective-permute-start.3
  26.9 6.0 %collective-permute-start.4 = (bf16[128,1024]{1,0:T(8,128)(2,1)}, bf16[128,1024]{1,0:T(8,128)(2,1)S(1)}, u32[]{:S(2)}, u32[]{:S(2)}) collective-permute-start(bf16[128,1024]{1,0:T(8,128)(2,1)} %bitcast.31), channel_id=1, source_target_pairs={{0,12},{1,13},{2,14},{3,15},{4,0},{5,1},{6,2},{7,3},{8,4},{9,5},{1... | collective-permute-start | bytes 786440 | tf_op jit(solution)/shard_map/ppermute | solution.py:33
  32.9 1.1 copy.11
  34.0 0.8 broadcast_in_dim.23
  34.8 0.8 pad_maximum_fusion.2
  35.6 9.8 %all-to-all-start = ((bf16[16,112,128]{2,1,0:T(8,128)(2,1)}), bf16[16,112,128]{2,1,0:T(8,128)(2,1)S(1)}, u32[]{:S(2)}, u32[]{:S(2)}) async-start(bf16[16,112,128]{2,1,0:T(8,128)(2,1)} %pad_maximum_fusion.2), calls=%async_computation | async-start | bytes 917504 | tf_op jit(solution)/shard_map/all_to_all | solution.py:224
  45.6 1.1 pad_maximum_fusion.1
  46.7 4.6 %collective-permute-start.6 = (bf16[256,1024]{1,0:T(8,128)(2,1)}, bf16[256,1024]{1,0:T(8,128)(2,1)S(1)}, u32[]{:S(2)}, u32[]{:S(2)}) collective-permute-start(bf16[256,1024]{1,0:T(8,128)(2,1)} %get-tuple-element.33), channel_id=1, source_target_pairs={{0,14},{1,15},{2,0},{3,1},{4,2},{5,3},{6,4},{7,5},{8,6},{9,7},{10,... | collective-permute-start | bytes 1572872 | tf_op jit(solution)/shard_map/ppermute | solution.py:33
  51.3 1.9 collective-permute-start.5
  53.2 4.8 %collective-permute-start.8 = (bf16[128,1024]{1,0:T(8,128)(2,1)S(1)}, bf16[128,1024]{1,0:T(8,128)(2,1)S(1)}, u32[]{:S(2)}, u32[]{:S(2)}) collective-permute-start(bf16[128,1024]{1,0:T(8,128)(2,1)S(1)} %collective-permute-done.refs_1_), channel_id=1, source_target_pairs={{0,12},{1,13},{2,14},{3,15},{4,0},{5,1},{6,2},{7,3},{8,4},{9,5},{1... | collective-permute-start | bytes 786440 | tf_op jit(solution)/shard_map/ppermute | solution.py:33
  58.1 1.9 collective-permute-start.7
  60.0 0.8 reshape.19
  60.8 18.3 %collective-permute-done.8.refs_9_ = bf16[128,1024]{1,0:T(8,128)(2,1)S(1)} collective-permute-done((bf16[128,1024]{1,0:T(8,128)(2,1)S(1)}, bf16[128,1024]{1,0:T(8,128)(2,1)S(1)}, u32[]{:S(2)}, u32[]{:S(2)}) %collective-permute-start.8) | collective-permute-done | bytes 262176 | tf_op jit(solution)/shard_map/ppermute | solution.py:33
  79.1 1.6 broadcast_in_dim.25
  80.7 7.8 %all-to-all-start.1 = ((bf16[32,6,1024]{2,1,0:T(8,128)(2,1)}), bf16[32,6,1024]{2,1,0:T(8,128)(2,1)}, u32[]{:S(2)}, u32[]{:S(2)}) async-start(bf16[32,6,1024]{2,1,0:T(8,128)(2,1)} %broadcast_in_dim.25), calls=%async_computation.1 | async-start | bytes 1048576 | tf_op jit(solution)/shard_map/all_to_all | solution.py:42
  88.5 0.8 pad_maximum_fusion.4
  89.3 4.6 %collective-permute-start.10 = (bf16[192,1024]{1,0:T(8,128)(2,1)}, bf16[192,1024]{1,0:T(8,128)(2,1)}, u32[]{:S(2)}, u32[]{:S(2)}) collective-permute-start(bf16[192,1024]{1,0:T(8,128)(2,1)} %pad_maximum_fusion.4), channel_id=1, source_target_pairs={{0,14},{1,15},{2,0},{3,1},{4,2},{5,3},{6,4},{7,5},{8,6},{9,7},{10,... | collective-permute-start | bytes 1179656 | tf_op jit(solution)/shard_map/ppermute | solution.py:33
  93.9 0.8 pad_maximum_fusion.3
  94.7 1.9 collective-permute-start.9
  96.6 0.7 slice.58
  97.3 4.8 %collective-permute-start.11 = (bf16[64,1024]{1,0:T(8,128)(2,1)}, bf16[64,1024]{1,0:T(8,128)(2,1)}, u32[]{:S(2)}, u32[]{:S(2)}) collective-permute-start(bf16[64,1024]{1,0:T(8,128)(2,1)} %slice.58), channel_id=1, source_target_pairs={{0,4},{1,5},{2,6},{3,7},{4,8},{5,9},{6,10},{7,11},{8,12},{9,13},{1... | collective-permute-start | bytes 393224 | tf_op jit(solution)/shard_map/ppermute | solution.py:33
  102.1 0.7 slice.59
  102.8 3.1 %collective-permute-start.12 = (bf16[64,1024]{1,0:T(8,128)(2,1)}, bf16[64,1024]{1,0:T(8,128)(2,1)}, u32[]{:S(2)}, u32[]{:S(2)}) collective-permute-start(bf16[64,1024]{1,0:T(8,128)(2,1)} %slice.59), channel_id=1, source_target_pairs={{0,12},{1,13},{2,14},{3,15},{4,0},{5,1},{6,2},{7,3},{8,4},{9,5},{1... | collective-permute-start | bytes 393224 | tf_op jit(solution)/shard_map/ppermute | solution.py:33
  106.2 1.2 reshape.18.refs_14_
  107.4 4.0 %collective-permute-done.11.refs_12_ = bf16[64,1024]{1,0:T(8,128)(2,1)} collective-permute-done((bf16[64,1024]{1,0:T(8,128)(2,1)}, bf16[64,1024]{1,0:T(8,128)(2,1)}, u32[]{:S(2)}, u32[]{:S(2)}) %collective-permute-start.11) | collective-permute-done | bytes 131104 | tf_op jit(solution)/shard_map/ppermute | solution.py:33
  111.4 2.0 collective-permute-done.12.refs_13_
  113.5 0.9 copy-done.4
  114.4 1.0 copy-done.6
  115.4 13.2 %attend.1 = (bf16[16,256,128]{2,1,0:T(8,128)(2,1)}, f32[16,6,1024]{2,1,0:T(8,128)S(1)}, bf16[16,6,1024]{2,1,0:T(8,128)(2,1)S(1)}) custom-call(s32[1]{0:T(128)} %bitcast.here_ref, s32[16]{0:T(128)S(1)} %stack.67.order_ref, s32[16,4]{1,0:T(8,128)S(1)} %copy.12.list_ref, s32[16]{0:T(128)S(1)} %bitcast.33, bf16[128,1024]{1,0:T(8,128)(2,1)S(1)} %bitcast.32, ...), custom_call_target="tpu_custom_call" | custom-call | tf_op jit(solution)/shard_map/attend/pallas_call | solution.py:161
  128.6 0.8 copy-done.1
  129.4 0.7 copy-done.8
  130.1 11.4 %all-to-all-start.2 = ((bf16[16,256,128]{2,1,0:T(8,128)(2,1)}), bf16[16,256,128]{2,1,0:T(8,128)(2,1)S(1)}, u32[]{:S(2)}, u32[]{:S(2)}) async-start(bf16[16,256,128]{2,1,0:T(8,128)(2,1)} %get-tuple-element.19), calls=%async_computation.2 | async-start | bytes 2097152 | tf_op jit(solution)/shard_map/all_to_all | solution.py:235
  141.5 1.9 collective-permute-start.13
  143.5 1.7 collective-permute-done.13
  145.2 1.1 convert_add_fusion
  146.3 10.2 %all-gather.2.cloned.1.call-done.w_ref = bf16[3072,1024]{1,0:T(8,128)(2,1)} async-done(((bf16[96,1024]{1,0:T(8,128)(2,1)}), bf16[3072,1024]{1,0:T(8,128)(2,1)}) %all-gather.2.cloned.1.call-update) | async-done | bytes 6291472 | tf_op jit(solution)/shard_map/all_gather | solution.py:227
  156.5 1.9 collective-permute-start.14
  158.4 5.6 %collective-permute-done.14 = bf16[8,6,1024]{2,1,0:T(8,128)(2,1)S(1)} collective-permute-done((bf16[8,6,1024]{2,1,0:T(8,128)(2,1)S(1)}, bf16[8,6,1024]{2,1,0:T(8,128)(2,1)S(1)}, u32[]{:S(2)}, u32[]{:S(2)}) %collective-permute-start.14) | collective-permute-done | bytes 98336 | tf_op jit(solution)/shard_map/ppermute | solution.py:37
  164.1 8.9 %collective-permute-start.15 = (bf16[4,6,1024]{2,1,0:T(8,128)(2,1)S(1)}, bf16[4,6,1024]{2,1,0:T(8,128)(2,1)S(1)}, u32[]{:S(2)}, u32[]{:S(2)}) collective-permute-start(bf16[4,6,1024]{2,1,0:T(8,128)(2,1)S(1)} %slice.79), channel_id=1, source_target_pairs={{0,64},{16,80},{32,96},{48,112},{64,0},{80,16},{96,32},{112,48},{1... | collective-permute-start | bytes 147464 | tf_op jit(solution)/shard_map/ppermute | solution.py:37
  173.0 2.2 %collective-permute-done.15 = bf16[4,6,1024]{2,1,0:T(8,128)(2,1)S(1)} collective-permute-done((bf16[4,6,1024]{2,1,0:T(8,128)(2,1)S(1)}, bf16[4,6,1024]{2,1,0:T(8,128)(2,1)S(1)}, u32[]{:S(2)}, u32[]{:S(2)}) %collective-permute-start.15) | collective-permute-done | bytes 49184 | tf_op jit(solution)/shard_map/ppermute | solution.py:37
  175.3 13.0 %collective-permute-start.16 = (bf16[2,6,1024]{2,1,0:T(8,128)(2,1)S(1)}, bf16[2,6,1024]{2,1,0:T(8,128)(2,1)S(1)}, u32[]{:S(2)}, u32[]{:S(2)}) collective-permute-start(bf16[2,6,1024]{2,1,0:T(8,128)(2,1)S(1)} %slice.80), channel_id=1, source_target_pairs={{0,128},{16,144},{32,160},{48,176},{64,192},{80,208},{96,224},{112... | collective-permute-start | bytes 73736 | tf_op jit(solution)/shard_map/ppermute | solution.py:37
  188.3 1.9 collective-permute-done.16
  190.2 5.1 %collective-permute-start.17 = (bf16[1,6,1024]{2,1,0:T(8,128)(2,1)S(1)}, bf16[1,6,1024]{2,1,0:T(8,128)(2,1)S(1)}, u32[]{:S(2)}, u32[]{:S(2)}) collective-permute-start(bf16[1,6,1024]{2,1,0:T(8,128)(2,1)S(1)} %slice.81), channel_id=1, source_target_pairs={{0,256},{16,272},{32,288},{48,304},{64,320},{80,336},{96,352},{112... | collective-permute-start | bytes 36872 | tf_op jit(solution)/shard_map/ppermute | solution.py:37
  195.3 2.8 %copy-done = bf16[3072,1024]{1,0:T(8,128)(2,1)S(1)} copy-done((bf16[3072,1024]{1,0:T(8,128)(2,1)S(1)}, bf16[3072,1024]{1,0:T(8,128)(2,1)}, u32[]{:S(2)}) %copy-start) | copy-done | bytes 6291480
  198.1 1.9 input_sum.1
  (46 shorter events, 1.1 us)
Async XLA Ops:
  7.2 106.3 %copy-start.2 = (bf16[1,128,1024]{2,1,0:T(8,128)(2,1)S(1)}, bf16[1,128,1024]{2,1,0:T(8,128)(2,1)}, u32[]{:S(2)}) copy-start(bf16[1,128,1024]{2,1,0:T(8,128)(2,1)} %param.5) | copy-start | bytes 786436
  7.2 98.8 %copy-start.9 = (s32[1,16,4]{1,2,0:T(4,128)S(1)}, s32[1,16,4]{1,2,0:T(4,128)}, u32[]{:S(2)}) copy-start(s32[1,16,4]{1,2,0:T(4,128)} %param.7) | copy-start | bytes 772
  7.2 106.3 %copy-start.7 = (s32[1,16]{1,0:T(1,128)S(1)}, s32[1,16]{1,0:T(1,128)}, u32[]{:S(2)}) copy-start(s32[1,16]{1,0:T(1,128)} %param.8) | copy-start | bytes 196
  7.2 38.3 %collective-permute-start = (bf16[128,1024]{1,0:T(8,128)(2,1)}, bf16[128,1024]{1,0:T(8,128)(2,1)S(1)}, u32[]{:S(2)}, u32[]{:S(2)}) collective-permute-start(bf16[128,1024]{1,0:T(8,128)(2,1)} %bitcast.27), channel_id=1, source_target_pairs={{0,1},{1,0},{2,3},{3,2},{4,5},{5,4},{6,7},{7,6},{8,9},{9,8},{10,11... | collective-permute-start | bytes 786440 | tf_op jit(solution)/shard_map/ppermute | solution.py:29
  12.0 33.5 %collective-permute-start.1 = (bf16[128,1024]{1,0:T(8,128)(2,1)}, bf16[128,1024]{1,0:T(8,128)(2,1)S(1)}, u32[]{:S(2)}, u32[]{:S(2)}) collective-permute-start(bf16[128,1024]{1,0:T(8,128)(2,1)} %bitcast.28), channel_id=1, source_target_pairs={{0,2},{1,3},{2,4},{3,5},{4,6},{5,7},{6,8},{7,9},{8,10},{9,11},{10,... | collective-permute-start | bytes 786440 | tf_op jit(solution)/shard_map/ppermute | solution.py:33
  16.3 29.2 %collective-permute-start.2 = (bf16[128,1024]{1,0:T(8,128)(2,1)}, bf16[128,1024]{1,0:T(8,128)(2,1)S(1)}, u32[]{:S(2)}, u32[]{:S(2)}) collective-permute-start(bf16[128,1024]{1,0:T(8,128)(2,1)} %bitcast.29), channel_id=1, source_target_pairs={{0,14},{1,15},{2,0},{3,1},{4,2},{5,3},{6,4},{7,5},{8,6},{9,7},{10,... | collective-permute-start | bytes 786440 | tf_op jit(solution)/shard_map/ppermute | solution.py:33
  24.9 20.6 %collective-permute-start.3 = (bf16[128,1024]{1,0:T(8,128)(2,1)}, bf16[128,1024]{1,0:T(8,128)(2,1)S(1)}, u32[]{:S(2)}, u32[]{:S(2)}) collective-permute-start(bf16[128,1024]{1,0:T(8,128)(2,1)} %bitcast.30), channel_id=1, source_target_pairs={{0,4},{1,5},{2,6},{3,7},{4,8},{5,9},{6,10},{7,11},{8,12},{9,13},{1... | collective-permute-start | bytes 786440 | tf_op jit(solution)/shard_map/ppermute | solution.py:33
  26.9 18.7 %collective-permute-start.4 = (bf16[128,1024]{1,0:T(8,128)(2,1)}, bf16[128,1024]{1,0:T(8,128)(2,1)S(1)}, u32[]{:S(2)}, u32[]{:S(2)}) collective-permute-start(bf16[128,1024]{1,0:T(8,128)(2,1)} %bitcast.31), channel_id=1, source_target_pairs={{0,12},{1,13},{2,14},{3,15},{4,0},{5,1},{6,2},{7,3},{8,4},{9,5},{1... | collective-permute-start | bytes 786440 | tf_op jit(solution)/shard_map/ppermute | solution.py:33
  35.6 24.4 %all-to-all-start = ((bf16[16,112,128]{2,1,0:T(8,128)(2,1)}), bf16[16,112,128]{2,1,0:T(8,128)(2,1)S(1)}, u32[]{:S(2)}, u32[]{:S(2)}) async-start(bf16[16,112,128]{2,1,0:T(8,128)(2,1)} %pad_maximum_fusion.2), calls=%async_computation | async-start | bytes 917504 | tf_op jit(solution)/shard_map/all_to_all | solution.py:224
  45.5 111.0 %all-gather.2.cloned.1.call-start = ((), (), s32[]{:S(2)}) async-start(), calls=%async_computation.3 | async-start | bytes 6488064 | tf_op jit(solution)/shard_map/all_gather | solution.py:227
  45.5 5.8 %copy-start.3 = (bf16[128,1024]{1,0:T(8,128)(2,1)}, bf16[128,1024]{1,0:T(8,128)(2,1)S(1)}, u32[]{:S(2)}) copy-start(bf16[128,1024]{1,0:T(8,128)(2,1)S(1)} %collective-permute-done.1.refs_2_) | copy-start | bytes 786436
  45.6 7.7 %copy-start.5 = (bf16[128,1024]{1,0:T(8,128)(2,1)}, bf16[128,1024]{1,0:T(8,128)(2,1)S(1)}, u32[]{:S(2)}) copy-start(bf16[128,1024]{1,0:T(8,128)(2,1)S(1)} %collective-permute-done.2.refs_3_) | copy-start | bytes 786436
  46.7 32.4 %collective-permute-start.6 = (bf16[256,1024]{1,0:T(8,128)(2,1)}, bf16[256,1024]{1,0:T(8,128)(2,1)S(1)}, u32[]{:S(2)}, u32[]{:S(2)}) collective-permute-start(bf16[256,1024]{1,0:T(8,128)(2,1)} %get-tuple-element.33), channel_id=1, source_target_pairs={{0,14},{1,15},{2,0},{3,1},{4,2},{5,3},{6,4},{7,5},{8,6},{9,7},{10,... | collective-permute-start | bytes 1572872 | tf_op jit(solution)/shard_map/ppermute | solution.py:33
  51.3 27.8 %collective-permute-start.5 = (bf16[256,1024]{1,0:T(8,128)(2,1)}, bf16[256,1024]{1,0:T(8,128)(2,1)S(1)}, u32[]{:S(2)}, u32[]{:S(2)}) collective-permute-start(bf16[256,1024]{1,0:T(8,128)(2,1)} %get-tuple-element.34), channel_id=1, source_target_pairs={{0,2},{1,3},{2,4},{3,5},{4,6},{5,7},{6,8},{7,9},{8,10},{9,11},{10,... | collective-permute-start | bytes 1572872 | tf_op jit(solution)/shard_map/ppermute | solution.py:33
  53.2 25.8 %collective-permute-start.8 = (bf16[128,1024]{1,0:T(8,128)(2,1)S(1)}, bf16[128,1024]{1,0:T(8,128)(2,1)S(1)}, u32[]{:S(2)}, u32[]{:S(2)}) collective-permute-start(bf16[128,1024]{1,0:T(8,128)(2,1)S(1)} %collective-permute-done.refs_1_), channel_id=1, source_target_pairs={{0,12},{1,13},{2,14},{3,15},{4,0},{5,1},{6,2},{7,3},{8,4},{9,5},{1... | collective-permute-start | bytes 786440 | tf_op jit(solution)/shard_map/ppermute | solution.py:33
  58.1 21.0 %collective-permute-start.7 = (bf16[128,1024]{1,0:T(8,128)(2,1)S(1)}, bf16[128,1024]{1,0:T(8,128)(2,1)S(1)}, u32[]{:S(2)}, u32[]{:S(2)}) collective-permute-start(bf16[128,1024]{1,0:T(8,128)(2,1)S(1)} %collective-permute-done.refs_1_), channel_id=1, source_target_pairs={{0,4},{1,5},{2,6},{3,7},{4,8},{5,9},{6,10},{7,11},{8,12},{9,13},{1... | collective-permute-start | bytes 786440 | tf_op jit(solution)/shard_map/ppermute | solution.py:33
  80.7 25.5 %all-to-all-start.1 = ((bf16[32,6,1024]{2,1,0:T(8,128)(2,1)}), bf16[32,6,1024]{2,1,0:T(8,128)(2,1)}, u32[]{:S(2)}, u32[]{:S(2)}) async-start(bf16[32,6,1024]{2,1,0:T(8,128)(2,1)} %broadcast_in_dim.25), calls=%async_computation.1 | async-start | bytes 1048576 | tf_op jit(solution)/shard_map/all_to_all | solution.py:42
  89.3 24.1 %collective-permute-start.10 = (bf16[192,1024]{1,0:T(8,128)(2,1)}, bf16[192,1024]{1,0:T(8,128)(2,1)}, u32[]{:S(2)}, u32[]{:S(2)}) collective-permute-start(bf16[192,1024]{1,0:T(8,128)(2,1)} %pad_maximum_fusion.4), channel_id=1, source_target_pairs={{0,14},{1,15},{2,0},{3,1},{4,2},{5,3},{6,4},{7,5},{8,6},{9,7},{10,... | collective-permute-start | bytes 1179656 | tf_op jit(solution)/shard_map/ppermute | solution.py:33
  94.7 18.7 %collective-permute-start.9 = (bf16[192,1024]{1,0:T(8,128)(2,1)}, bf16[192,1024]{1,0:T(8,128)(2,1)}, u32[]{:S(2)}, u32[]{:S(2)}) collective-permute-start(bf16[192,1024]{1,0:T(8,128)(2,1)} %pad_maximum_fusion.3), channel_id=1, source_target_pairs={{0,2},{1,3},{2,4},{3,5},{4,6},{5,7},{6,8},{7,9},{8,10},{9,11},{10,... | collective-permute-start | bytes 1179656 | tf_op jit(solution)/shard_map/ppermute | solution.py:33
  97.3 14.1 %collective-permute-start.11 = (bf16[64,1024]{1,0:T(8,128)(2,1)}, bf16[64,1024]{1,0:T(8,128)(2,1)}, u32[]{:S(2)}, u32[]{:S(2)}) collective-permute-start(bf16[64,1024]{1,0:T(8,128)(2,1)} %slice.58), channel_id=1, source_target_pairs={{0,4},{1,5},{2,6},{3,7},{4,8},{5,9},{6,10},{7,11},{8,12},{9,13},{1... | collective-permute-start | bytes 393224 | tf_op jit(solution)/shard_map/ppermute | solution.py:33
  102.8 10.7 %collective-permute-start.12 = (bf16[64,1024]{1,0:T(8,128)(2,1)}, bf16[64,1024]{1,0:T(8,128)(2,1)}, u32[]{:S(2)}, u32[]{:S(2)}) collective-permute-start(bf16[64,1024]{1,0:T(8,128)(2,1)} %slice.59), channel_id=1, source_target_pairs={{0,12},{1,13},{2,14},{3,15},{4,0},{5,1},{6,2},{7,3},{8,4},{9,5},{1... | collective-permute-start | bytes 393224 | tf_op jit(solution)/shard_map/ppermute | solution.py:33
  113.5 1.0 copy-start.4
  114.4 1.0 copy-start.6
  128.6 0.8 copy-start.1
  129.4 0.7 copy-start.8
  130.1 65.2 %all-to-all-start.2 = ((bf16[16,256,128]{2,1,0:T(8,128)(2,1)}), bf16[16,256,128]{2,1,0:T(8,128)(2,1)S(1)}, u32[]{:S(2)}, u32[]{:S(2)}) async-start(bf16[16,256,128]{2,1,0:T(8,128)(2,1)} %get-tuple-element.19), calls=%async_computation.2 | async-start | bytes 2097152 | tf_op jit(solution)/shard_map/all_to_all | solution.py:235
  141.5 3.6 %collective-permute-start.13 = (bf16[16,6,1024]{2,1,0:T(8,128)(2,1)}, bf16[16,6,1024]{2,1,0:T(8,128)(2,1)S(1)}, u32[]{:S(2)}, u32[]{:S(2)}) collective-permute-start(bf16[16,6,1024]{2,1,0:T(8,128)(2,1)} %copy-done.8), channel_id=1, source_target_pairs={{0,16},{16,0},{32,48},{48,32},{64,80},{80,64},{96,112},{112,96},{1... | collective-permute-start | bytes 589832 | tf_op jit(solution)/shard_map/ppermute | solution.py:37
  156.5 7.5 %collective-permute-start.14 = (bf16[8,6,1024]{2,1,0:T(8,128)(2,1)S(1)}, bf16[8,6,1024]{2,1,0:T(8,128)(2,1)S(1)}, u32[]{:S(2)}, u32[]{:S(2)}) collective-permute-start(bf16[8,6,1024]{2,1,0:T(8,128)(2,1)S(1)} %slice.78), channel_id=1, source_target_pairs={{0,32},{16,48},{32,0},{48,16},{64,96},{80,112},{96,64},{112,80},{1... | collective-permute-start | bytes 294920 | tf_op jit(solution)/shard_map/ppermute | solution.py:37
  164.1 11.2 %collective-permute-start.15 = (bf16[4,6,1024]{2,1,0:T(8,128)(2,1)S(1)}, bf16[4,6,1024]{2,1,0:T(8,128)(2,1)S(1)}, u32[]{:S(2)}, u32[]{:S(2)}) collective-permute-start(bf16[4,6,1024]{2,1,0:T(8,128)(2,1)S(1)} %slice.79), channel_id=1, source_target_pairs={{0,64},{16,80},{32,96},{48,112},{64,0},{80,16},{96,32},{112,48},{1... | collective-permute-start | bytes 147464 | tf_op jit(solution)/shard_map/ppermute | solution.py:37
  175.3 14.8 %collective-permute-start.16 = (bf16[2,6,1024]{2,1,0:T(8,128)(2,1)S(1)}, bf16[2,6,1024]{2,1,0:T(8,128)(2,1)S(1)}, u32[]{:S(2)}, u32[]{:S(2)}) collective-permute-start(bf16[2,6,1024]{2,1,0:T(8,128)(2,1)S(1)} %slice.80), channel_id=1, source_target_pairs={{0,128},{16,144},{32,160},{48,176},{64,192},{80,208},{96,224},{112... | collective-permute-start | bytes 73736 | tf_op jit(solution)/shard_map/ppermute | solution.py:37
  190.2 9.8 %collective-permute-start.17 = (bf16[1,6,1024]{2,1,0:T(8,128)(2,1)S(1)}, bf16[1,6,1024]{2,1,0:T(8,128)(2,1)S(1)}, u32[]{:S(2)}, u32[]{:S(2)}) collective-permute-start(bf16[1,6,1024]{2,1,0:T(8,128)(2,1)S(1)} %slice.81), channel_id=1, source_target_pairs={{0,256},{16,272},{32,288},{48,304},{64,320},{80,336},{96,352},{112... | collective-permute-start | bytes 36872 | tf_op jit(solution)/shard_map/ppermute | solution.py:37
  195.3 2.8 %copy-start = (bf16[3072,1024]{1,0:T(8,128)(2,1)S(1)}, bf16[3072,1024]{1,0:T(8,128)(2,1)}, u32[]{:S(2)}) copy-start(bf16[3072,1024]{1,0:T(8,128)(2,1)} %all-gather.2.cloned.1.call-done.w_ref) | copy-start | bytes 18874372
Sparse Core Ops, SparseCore 0:
  79.2 77.1 all-gather.1

commit v9 on v6

--- a/solution.py
+++ b/solution.py
@@ -78,7 +78,7 @@
 
 def attend(nblk, here_ref, order_ref, list_ref, count_ref, *refs):
     blocks = refs[:nblk]
-    w_ref, cot_ref, out_ref, sum_ref, kv_rows, kv_cols, q_cols, acc = refs[nblk:]
+    w_ref, cot_ref, out_ref, keep_ref, send_ref, kv_rows, kv_cols, q_cols, acc = refs[nblk:]
     scale = HEAD_DIM ** (-0.5)
     tiles = kv_rows.shape[0]
     w = w_ref[...]
@@ -138,23 +138,29 @@
         slot += n
         part = dot(jnp.concatenate(left, axis=1), blk, 1, 0)
         total = part if total is None else total + part
-    rows = sum_ref.shape[1]
+    rows = keep_ref.shape[1]
     here = here_ref[0]
-    for i in range(DP):
-        sum_ref[mirror(i) ^ here] = total[i * rows : (i + 1) * rows]
+    first = here < DP // 2
+    for i in range(0, DP, CORES):
+        even, odd = total[i * rows : (i + 1) * rows], total[(i + 1) * rows : (i + 2) * rows]
+        at = (mirror(i) ^ here) % (DP // 2)
+        keep_ref[at] = jnp.where(first, even, odd)
+        send_ref[at] = jnp.where(first, odd, even).astype(BF)
 
 
 def attention(here, order, tile_list, counts, blocks, w_head, cot_t):
     tiles = tile_list.shape[0]
     rows, depth = w_head.shape[0] // DP, w_head.shape[1]
+    outs = (
+        ((tiles, 4 * HEAD_DIM, TILE), BF),
+        ((DP // CORES, rows, depth), F32),
+        ((DP // CORES, rows, depth), BF),
+    )
     return pl.pallas_call(
         functools.partial(attend, len(blocks)),
-        out_shape=(
-            jax.ShapeDtypeStruct((tiles, 4 * HEAD_DIM, TILE), BF),
-            jax.ShapeDtypeStruct((DP, rows, depth), F32),
-        ),
+        out_shape=tuple(jax.ShapeDtypeStruct(*o) for o in outs),
+        out_specs=(VM,) * 3,
         in_specs=[SM, SM, SM, SM] + [VM] * (len(blocks) + 2),
-        out_specs=(VM, VM),
         scratch_shapes=[
             pltpu.VMEM((tiles, TILE, 2 * HEAD_DIM), BF),
             pltpu.VMEM((tiles, 2 * HEAD_DIM, TILE), BF),
@@ -223,14 +229,13 @@
 
     here = mirror(dp)[None].astype(jnp.int32)
     order = tile_places(z, y_hi)
-    both, sums = attention(here, order, key_tiles[0], key_counts[0], blocks, w_head, mixed)
+    both, keep, send = attention(here, order, key_tiles[0], key_counts[0], blocks, w_head, mixed)
     both = lax.all_to_all(both, "seq", 0, 0, tiled=True)
 
-    for bit in (1, 2, 4, 8, 16):
+    sums = keep + swap_dp(send, 1).astype(F32)
+    for bit in (2, 4, 8, 16):
         half = sums.shape[0] // 2
         sums = sums[:half] + swap_dp(sums[half:].astype(BF), bit).astype(F32)
-        if bit == 1:
-            w_all, sums = lax.optimization_barrier((w_all, sums))
     grad_weight = sums * grad_scale
 
     attended, grad_input = input_grad(both, w_all)

time: 190 us -> 180 us (0.947)
  the two profiles are of different devices: /device:TPU:314 before, /device:TPU:56 now
where the time goes in v9:
time: 180 us; the launch traced here: 179 us
  starting transfers between devices  91 us (51%)
  waiting for transfers between devices  41.3 us (23%)
  local copies, waits for them, and re-layouts  15.2 us (8%)
  between operations  14.5 us (8%)
  Pallas kernels  13.7 us (8%)
  other arithmetic  2.92 us (2%)
    ppermute x9, starting transfers between devices, shift_z(): return lax.ppermute(x, 'seq', [(s, (s + YH * k) % SEQ) for s in range(SEQ)])  39.9 us
    ppermute x9, waiting for transfers between devices, shift_z(): return lax.ppermute(x, 'seq', [(s, (s + YH * k) % SEQ) for s in range(SEQ)])  16.2 us
    ppermute x5, starting transfers between devices, swap_dp(): return lax.ppermute(x, 'dp', [(d, d ^ bit) for d in range(DP)])  15.8 us
    ppermute x5, waiting for transfers between devices, swap_dp(): return lax.ppermute(x, 'dp', [(d, d ^ bit) for d in range(DP)])  15.2 us
    all_to_all x1, starting transfers between devices, shards(): both = lax.all_to_all(both, 'seq', 0, 0, tiled=True)  12.8 us
    pallas_call x1, Pallas kernels, attention(): pl.pallas_call(functools.partial(attend, len(blocks)), out_shape=tuple((j...  11.9 us
    all_to_all x1, starting transfers between devices, shards(): mixed = lax.all_to_all(mixed, 'seq', 0, 0, tiled=True)  9.85 us
    unnamed x19, local copies, waits for them, and re-layouts  7.91 us
  transfers between devices with their start and end apart: 19, of which 9 were waited for; matrix products, arithmetic and copies ran while one was open for 6% of the time, Pallas kernels for 7%

profile of v9, /device:TPU:56, one launch (start us, length us, event | category | flops | bytes accessed | tf_op | source)
XLA Modules:
  0.0 178.6 jit_solution(8053471832239868316)
XLA Ops:
  7.2 4.8 %collective-permute-start = (bf16[128,1024]{1,0:T(8,128)(2,1)}, bf16[128,1024]{1,0:T(8,128)(2,1)S(1)}, u32[]{:S(2)}, u32[]{:S(2)}) collective-permute-start(bf16[128,1024]{1,0:T(8,128)(2,1)} %bitcast.27), channel_id=1, source_target_pairs={{0,1},{1,0},{2,3},{3,2},{4,5},{5,4},{6,7},{7,6},{8,9},{9,8},{10,11... | collective-permute-start | bytes 786440 | tf_op jit(solution)/shard_map/ppermute | solution.py:29
  12.0 4.3 %collective-permute-start.1 = (bf16[128,1024]{1,0:T(8,128)(2,1)}, bf16[128,1024]{1,0:T(8,128)(2,1)S(1)}, u32[]{:S(2)}, u32[]{:S(2)}) collective-permute-start(bf16[128,1024]{1,0:T(8,128)(2,1)} %bitcast.28), channel_id=1, source_target_pairs={{0,2},{1,3},{2,4},{3,5},{4,6},{5,7},{6,8},{7,9},{8,10},{9,11},{10,... | collective-permute-start | bytes 786440 | tf_op jit(solution)/shard_map/ppermute | solution.py:33
  16.3 8.6 %collective-permute-start.2 = (bf16[128,1024]{1,0:T(8,128)(2,1)}, bf16[128,1024]{1,0:T(8,128)(2,1)S(1)}, u32[]{:S(2)}, u32[]{:S(2)}) collective-permute-start(bf16[128,1024]{1,0:T(8,128)(2,1)} %bitcast.29), channel_id=1, source_target_pairs={{0,14},{1,15},{2,0},{3,1},{4,2},{5,3},{6,4},{7,5},{8,6},{9,7},{10,... | collective-permute-start | bytes 786440 | tf_op jit(solution)/shard_map/ppermute | solution.py:33
  24.9 1.1 copy.11
  26.1 0.8 broadcast_in_dim.23
  26.9 0.8 pad_maximum_fusion.2
  27.7 9.8 %all-to-all-start = ((bf16[16,112,128]{2,1,0:T(8,128)(2,1)}), bf16[16,112,128]{2,1,0:T(8,128)(2,1)S(1)}, u32[]{:S(2)}, u32[]{:S(2)}) async-start(bf16[16,112,128]{2,1,0:T(8,128)(2,1)} %pad_maximum_fusion.2), calls=%async_computation | async-start | bytes 917504 | tf_op jit(solution)/shard_map/all_to_all | solution.py:222
  37.6 0.9 pad_maximum_fusion.1
  38.5 3.4 %collective-permute-start.3 = (bf16[256,1024]{1,0:T(8,128)(2,1)}, bf16[256,1024]{1,0:T(8,128)(2,1)S(1)}, u32[]{:S(2)}, u32[]{:S(2)}) collective-permute-start(bf16[256,1024]{1,0:T(8,128)(2,1)} %get-tuple-element.24), channel_id=1, source_target_pairs={{0,2},{1,3},{2,4},{3,5},{4,6},{5,7},{6,8},{7,9},{8,10},{9,11},{10,... | collective-permute-start | bytes 1572872 | tf_op jit(solution)/shard_map/ppermute | solution.py:33
  41.9 3.7 %collective-permute-start.5 = (bf16[256,1024]{1,0:T(8,128)(2,1)S(1)}, bf16[256,1024]{1,0:T(8,128)(2,1)S(1)}, u32[]{:S(2)}, u32[]{:S(2)}) collective-permute-start(bf16[256,1024]{1,0:T(8,128)(2,1)S(1)} %get-tuple-element.23), channel_id=1, source_target_pairs={{0,14},{1,15},{2,0},{3,1},{4,2},{5,3},{6,4},{7,5},{8,6},{9,7},{10,... | collective-permute-start | bytes 1572872 | tf_op jit(solution)/shard_map/ppermute | solution.py:33
  45.6 6.5 %all-to-all-done.refs_12_ = bf16[16,112,128]{2,1,0:T(8,128)(2,1)S(1)} async-done(((bf16[16,112,128]{2,1,0:T(8,128)(2,1)}), bf16[16,112,128]{2,1,0:T(8,128)(2,1)S(1)}, u32[]{:S(2)}, u32[]{:S(2)}) %all-to-all-start) | async-done | bytes 458784 | tf_op jit(solution)/shard_map/all_to_all | solution.py:222
  52.0 0.8 reshape.19
  52.8 8.0 %collective-permute-done.3.refs_4_ = bf16[256,1024]{1,0:T(8,128)(2,1)S(1)} collective-permute-done((bf16[256,1024]{1,0:T(8,128)(2,1)}, bf16[256,1024]{1,0:T(8,128)(2,1)S(1)}, u32[]{:S(2)}, u32[]{:S(2)}) %collective-permute-start.3) | collective-permute-done | bytes 524320 | tf_op jit(solution)/shard_map/ppermute | solution.py:33
  60.8 3.8 %collective-permute-start.4 = (bf16[256,1024]{1,0:T(8,128)(2,1)S(1)}, bf16[256,1024]{1,0:T(8,128)(2,1)S(1)}, u32[]{:S(2)}, u32[]{:S(2)}) collective-permute-start(bf16[256,1024]{1,0:T(8,128)(2,1)S(1)} %collective-permute-done.3.refs_4_), channel_id=1, source_target_pairs={{0,2},{1,3},{2,4},{3,5},{4,6},{5,7},{6,8},{7,9},{8,10},{9,11},{10,... | collective-permute-start | bytes 1572872 | tf_op jit(solution)/shard_map/ppermute | solution.py:33
  64.6 3.2 %collective-permute-start.6 = (bf16[256,1024]{1,0:T(8,128)(2,1)S(1)}, bf16[256,1024]{1,0:T(8,128)(2,1)S(1)}, u32[]{:S(2)}, u32[]{:S(2)}) collective-permute-start(bf16[256,1024]{1,0:T(8,128)(2,1)S(1)} %collective-permute-done.5.refs_6_), channel_id=1, source_target_pairs={{0,14},{1,15},{2,0},{3,1},{4,2},{5,3},{6,4},{7,5},{8,6},{9,7},{10,... | collective-permute-start | bytes 1572872 | tf_op jit(solution)/shard_map/ppermute | solution.py:33
  67.9 1.6 broadcast_in_dim.25
  69.5 7.8 %all-to-all-start.1 = ((bf16[32,6,1024]{2,1,0:T(8,128)(2,1)}), bf16[32,6,1024]{2,1,0:T(8,128)(2,1)}, u32[]{:S(2)}, u32[]{:S(2)}) async-start(bf16[32,6,1024]{2,1,0:T(8,128)(2,1)} %broadcast_in_dim.25), calls=%async_computation.1 | async-start | bytes 1048576 | tf_op jit(solution)/shard_map/all_to_all | solution.py:42
  77.3 0.8 slice.48
  78.1 2.7 %collective-permute-start.7 = (bf16[192,1024]{1,0:T(8,128)(2,1)}, bf16[192,1024]{1,0:T(8,128)(2,1)}, u32[]{:S(2)}, u32[]{:S(2)}) collective-permute-start(bf16[192,1024]{1,0:T(8,128)(2,1)} %slice.48), channel_id=1, source_target_pairs={{0,2},{1,3},{2,4},{3,5},{4,6},{5,7},{6,8},{7,9},{8,10},{9,11},{10,... | collective-permute-start | bytes 1179656 | tf_op jit(solution)/shard_map/ppermute | solution.py:33
  80.9 0.8 slice.49
  81.6 4.3 %collective-permute-start.8 = (bf16[192,1024]{1,0:T(8,128)(2,1)}, bf16[192,1024]{1,0:T(8,128)(2,1)}, u32[]{:S(2)}, u32[]{:S(2)}) collective-permute-start(bf16[192,1024]{1,0:T(8,128)(2,1)} %slice.49), channel_id=1, source_target_pairs={{0,14},{1,15},{2,0},{3,1},{4,2},{5,3},{6,4},{7,5},{8,6},{9,7},{10,... | collective-permute-start | bytes 1179656 | tf_op jit(solution)/shard_map/ppermute | solution.py:33
  85.9 5.9 %collective-permute-start.9 = (bf16[128,1024]{1,0:T(8,128)(2,1)S(1)}, bf16[128,1024]{1,0:T(8,128)(2,1)}, u32[]{:S(2)}, u32[]{:S(2)}) collective-permute-start(bf16[128,1024]{1,0:T(8,128)(2,1)S(1)} %collective-permute-done.refs_1_), channel_id=1, source_target_pairs={{0,8},{1,9},{2,10},{3,11},{4,12},{5,13},{6,14},{7,15},{8,0},{9,1},... | collective-permute-start | bytes 786440 | tf_op jit(solution)/shard_map/ppermute | solution.py:33
  91.9 0.1 copy.12.list_ref
  92.0 0.1 stack.67.order_ref
  92.1 3.4 %all-to-all-done.1 = bf16[32,6,1024]{2,1,0:T(8,128)(2,1)} async-done(((bf16[32,6,1024]{2,1,0:T(8,128)(2,1)}), bf16[32,6,1024]{2,1,0:T(8,128)(2,1)}, u32[]{:S(2)}, u32[]{:S(2)}) %all-to-all-start.1) | async-done | bytes 393248 | tf_op jit(solution)/shard_map/all_to_all | solution.py:42
  95.6 1.2 reshape.18.refs_11_
  96.8 8.2 %collective-permute-done.9.refs_10_ = bf16[128,1024]{1,0:T(8,128)(2,1)} collective-permute-done((bf16[128,1024]{1,0:T(8,128)(2,1)S(1)}, bf16[128,1024]{1,0:T(8,128)(2,1)}, u32[]{:S(2)}, u32[]{:S(2)}) %collective-permute-start.9) | collective-permute-done | bytes 262176 | tf_op jit(solution)/shard_map/ppermute | solution.py:33
  105.0 1.0 copy-done.3
  106.0 1.0 copy-done.5
  107.0 11.9 %attend.1 = (bf16[16,256,128]{2,1,0:T(8,128)(2,1)S(1)}, f32[16,6,1024]{2,1,0:T(8,128)S(1)}, bf16[16,6,1024]{2,1,0:T(8,128)(2,1)S(1)}) custom-call(s32[1]{0:T(128)} %bitcast.here_ref, s32[16]{0:T(128)S(1)} %stack.67.order_ref, s32[16,4]{1,0:T(8,128)S(1)} %copy.12.list_ref, s32[16]{0:T(128)S(1)} %bitcast.31, bf16[128,1024]{1,0:T(8,128)(2,1)S(1)} %bitcast.30, ...), custom_call_target="tpu_custom_call" | custom-call | tf_op jit(solution)/shard_map/attend/pallas_call | solution.py:159
  118.9 1.0 copy-done.1
  119.8 0.8 copy-done.4
  120.7 0.7 copy-done.7
  121.4 12.8 %all-to-all-start.2 = ((bf16[16,256,128]{2,1,0:T(8,128)(2,1)}), bf16[16,256,128]{2,1,0:T(8,128)(2,1)S(1)}, u32[]{:S(2)}, u32[]{:S(2)}) async-start(bf16[16,256,128]{2,1,0:T(8,128)(2,1)} %copy-done.1), calls=%async_computation.2 | async-start | bytes 2097152 | tf_op jit(solution)/shard_map/all_to_all | solution.py:233
  134.2 1.9 %collective-permute-start.10 = (bf16[16,6,1024]{2,1,0:T(8,128)(2,1)}, bf16[16,6,1024]{2,1,0:T(8,128)(2,1)S(1)}, u32[]{:S(2)}, u32[]{:S(2)}) collective-permute-start(bf16[16,6,1024]{2,1,0:T(8,128)(2,1)} %copy-done.7), channel_id=1, source_target_pairs={{0,16},{16,0},{32,48},{48,32},{64,80},{80,64},{96,112},{112,96},{1... | collective-permute-start | bytes 589832 | tf_op jit(solution)/shard_map/ppermute | solution.py:37
  136.1 1.7 collective-permute-done.10
  137.8 1.1 convert_add_fusion
  138.9 3.4 %collective-permute-start.11 = (bf16[8,6,1024]{2,1,0:T(8,128)(2,1)S(1)}, bf16[8,6,1024]{2,1,0:T(8,128)(2,1)S(1)}, u32[]{:S(2)}, u32[]{:S(2)}) collective-permute-start(bf16[8,6,1024]{2,1,0:T(8,128)(2,1)S(1)} %slice.69), channel_id=1, source_target_pairs={{0,32},{16,48},{32,0},{48,16},{64,96},{80,112},{96,64},{112,80},{1... | collective-permute-start | bytes 294920 | tf_op jit(solution)/shard_map/ppermute | solution.py:37
  142.3 4.0 %collective-permute-done.11 = bf16[8,6,1024]{2,1,0:T(8,128)(2,1)S(1)} collective-permute-done((bf16[8,6,1024]{2,1,0:T(8,128)(2,1)S(1)}, bf16[8,6,1024]{2,1,0:T(8,128)(2,1)S(1)}, u32[]{:S(2)}, u32[]{:S(2)}) %collective-permute-start.11) | collective-permute-done | bytes 98336 | tf_op jit(solution)/shard_map/ppermute | solution.py:37
  146.4 4.9 %collective-permute-start.12 = (bf16[4,6,1024]{2,1,0:T(8,128)(2,1)S(1)}, bf16[4,6,1024]{2,1,0:T(8,128)(2,1)S(1)}, u32[]{:S(2)}, u32[]{:S(2)}) collective-permute-start(bf16[4,6,1024]{2,1,0:T(8,128)(2,1)S(1)} %slice.70), channel_id=1, source_target_pairs={{0,64},{16,80},{32,96},{48,112},{64,0},{80,16},{96,32},{112,48},{1... | collective-permute-start | bytes 147464 | tf_op jit(solution)/shard_map/ppermute | solution.py:37
  151.4 2.7 %collective-permute-done.12 = bf16[4,6,1024]{2,1,0:T(8,128)(2,1)S(1)} collective-permute-done((bf16[4,6,1024]{2,1,0:T(8,128)(2,1)S(1)}, bf16[4,6,1024]{2,1,0:T(8,128)(2,1)S(1)}, u32[]{:S(2)}, u32[]{:S(2)}) %collective-permute-start.12) | collective-permute-done | bytes 49184 | tf_op jit(solution)/shard_map/ppermute | solution.py:37
  154.1 3.1 %collective-permute-start.13 = (bf16[2,6,1024]{2,1,0:T(8,128)(2,1)S(1)}, bf16[2,6,1024]{2,1,0:T(8,128)(2,1)S(1)}, u32[]{:S(2)}, u32[]{:S(2)}) collective-permute-start(bf16[2,6,1024]{2,1,0:T(8,128)(2,1)S(1)} %slice.71), channel_id=1, source_target_pairs={{0,128},{16,144},{32,160},{48,176},{64,192},{80,208},{96,224},{112... | collective-permute-start | bytes 73736 | tf_op jit(solution)/shard_map/ppermute | solution.py:37
  157.2 2.7 %collective-permute-done.13 = bf16[2,6,1024]{2,1,0:T(8,128)(2,1)S(1)} collective-permute-done((bf16[2,6,1024]{2,1,0:T(8,128)(2,1)S(1)}, bf16[2,6,1024]{2,1,0:T(8,128)(2,1)S(1)}, u32[]{:S(2)}, u32[]{:S(2)}) %collective-permute-start.13) | collective-permute-done | bytes 24608 | tf_op jit(solution)/shard_map/ppermute | solution.py:37
  160.0 2.5 %collective-permute-start.14 = (bf16[1,6,1024]{2,1,0:T(8,128)(2,1)S(1)}, bf16[1,6,1024]{2,1,0:T(8,128)(2,1)S(1)}, u32[]{:S(2)}, u32[]{:S(2)}) collective-permute-start(bf16[1,6,1024]{2,1,0:T(8,128)(2,1)S(1)} %slice.72), channel_id=1, source_target_pairs={{0,256},{16,272},{32,288},{48,304},{64,320},{80,336},{96,352},{112... | collective-permute-start | bytes 36872 | tf_op jit(solution)/shard_map/ppermute | solution.py:37
  162.4 4.0 %collective-permute-done.14 = bf16[1,6,1024]{2,1,0:T(8,128)(2,1)S(1)} collective-permute-done((bf16[1,6,1024]{2,1,0:T(8,128)(2,1)S(1)}, bf16[1,6,1024]{2,1,0:T(8,128)(2,1)S(1)}, u32[]{:S(2)}, u32[]{:S(2)}) %collective-permute-start.14) | collective-permute-done | bytes 12320 | tf_op jit(solution)/shard_map/ppermute | solution.py:37
  166.5 0.6 copy.13
  167.1 2.8 %copy-done = bf16[3072,1024]{1,0:T(8,128)(2,1)S(1)} copy-done((bf16[3072,1024]{1,0:T(8,128)(2,1)S(1)}, bf16[3072,1024]{1,0:T(8,128)(2,1)}, u32[]{:S(2)}) %copy-start) | copy-done | bytes 6291480
  169.9 1.9 %input_sum.1 = (bf16[128,1024]{1,0:T(8,128)(2,1)}, bf16[128,1024]{1,0:T(8,128)(2,1)}) custom-call(bf16[16,256,128]{2,1,0:T(8,128)(2,1)S(1)} %all-to-all-done.2.both_ref, bf16[3072,1024]{1,0:T(8,128)(2,1)S(1)} %copy-done), custom_call_target="tpu_custom_call" | custom-call | tf_op jit(solution)/shard_map/input_sum/pallas_call | solution.py:192
  (34 shorter events, 0.3 us)
Async XLA Ops:
  7.2 84.8 %copy-start.8 = (s32[1,16,4]{1,2,0:T(4,128)S(1)}, s32[1,16,4]{1,2,0:T(4,128)}, u32[]{:S(2)}) copy-start(s32[1,16,4]{1,2,0:T(4,128)} %param.7) | copy-start | bytes 772
  7.2 97.8 %copy-start.6 = (s32[1,16]{1,0:T(1,128)S(1)}, s32[1,16]{1,0:T(1,128)}, u32[]{:S(2)}) copy-start(s32[1,16]{1,0:T(1,128)} %param.8) | copy-start | bytes 196
  7.2 30.4 %collective-permute-start = (bf16[128,1024]{1,0:T(8,128)(2,1)}, bf16[128,1024]{1,0:T(8,128)(2,1)S(1)}, u32[]{:S(2)}, u32[]{:S(2)}) collective-permute-start(bf16[128,1024]{1,0:T(8,128)(2,1)} %bitcast.27), channel_id=1, source_target_pairs={{0,1},{1,0},{2,3},{3,2},{4,5},{5,4},{6,7},{7,6},{8,9},{9,8},{10,11... | collective-permute-start | bytes 786440 | tf_op jit(solution)/shard_map/ppermute | solution.py:29
  12.0 25.5 %collective-permute-start.1 = (bf16[128,1024]{1,0:T(8,128)(2,1)}, bf16[128,1024]{1,0:T(8,128)(2,1)S(1)}, u32[]{:S(2)}, u32[]{:S(2)}) collective-permute-start(bf16[128,1024]{1,0:T(8,128)(2,1)} %bitcast.28), channel_id=1, source_target_pairs={{0,2},{1,3},{2,4},{3,5},{4,6},{5,7},{6,8},{7,9},{8,10},{9,11},{10,... | collective-permute-start | bytes 786440 | tf_op jit(solution)/shard_map/ppermute | solution.py:33
  16.3 21.3 %collective-permute-start.2 = (bf16[128,1024]{1,0:T(8,128)(2,1)}, bf16[128,1024]{1,0:T(8,128)(2,1)S(1)}, u32[]{:S(2)}, u32[]{:S(2)}) collective-permute-start(bf16[128,1024]{1,0:T(8,128)(2,1)} %bitcast.29), channel_id=1, source_target_pairs={{0,14},{1,15},{2,0},{3,1},{4,2},{5,3},{6,4},{7,5},{8,6},{9,7},{10,... | collective-permute-start | bytes 786440 | tf_op jit(solution)/shard_map/ppermute | solution.py:33
  27.7 24.3 %all-to-all-start = ((bf16[16,112,128]{2,1,0:T(8,128)(2,1)}), bf16[16,112,128]{2,1,0:T(8,128)(2,1)S(1)}, u32[]{:S(2)}, u32[]{:S(2)}) async-start(bf16[16,112,128]{2,1,0:T(8,128)(2,1)} %pad_maximum_fusion.2), calls=%async_computation | async-start | bytes 917504 | tf_op jit(solution)/shard_map/all_to_all | solution.py:222
  37.5 129.6 %all-gather.2.cloned.1.call-start = ((), (), s32[]{:S(2)}) async-start(), calls=%async_computation.3 | async-start | bytes 6488064 | tf_op jit(solution)/shard_map/all_gather | solution.py:225
  38.5 22.2 %collective-permute-start.3 = (bf16[256,1024]{1,0:T(8,128)(2,1)}, bf16[256,1024]{1,0:T(8,128)(2,1)S(1)}, u32[]{:S(2)}, u32[]{:S(2)}) collective-permute-start(bf16[256,1024]{1,0:T(8,128)(2,1)} %get-tuple-element.24), channel_id=1, source_target_pairs={{0,2},{1,3},{2,4},{3,5},{4,6},{5,7},{6,8},{7,9},{8,10},{9,11},{10,... | collective-permute-start | bytes 1572872 | tf_op jit(solution)/shard_map/ppermute | solution.py:33
  41.9 18.9 %collective-permute-start.5 = (bf16[256,1024]{1,0:T(8,128)(2,1)S(1)}, bf16[256,1024]{1,0:T(8,128)(2,1)S(1)}, u32[]{:S(2)}, u32[]{:S(2)}) collective-permute-start(bf16[256,1024]{1,0:T(8,128)(2,1)S(1)} %get-tuple-element.23), channel_id=1, source_target_pairs={{0,14},{1,15},{2,0},{3,1},{4,2},{5,3},{6,4},{7,5},{8,6},{9,7},{10,... | collective-permute-start | bytes 1572872 | tf_op jit(solution)/shard_map/ppermute | solution.py:33
  60.8 31.4 %copy-start.2 = (bf16[256,1024]{1,0:T(8,128)(2,1)}, bf16[256,1024]{1,0:T(8,128)(2,1)S(1)}, u32[]{:S(2)}) copy-start(bf16[256,1024]{1,0:T(8,128)(2,1)S(1)} %collective-permute-done.5.refs_6_) | copy-start | bytes 1572868
  60.8 16.5 %collective-permute-start.4 = (bf16[256,1024]{1,0:T(8,128)(2,1)S(1)}, bf16[256,1024]{1,0:T(8,128)(2,1)S(1)}, u32[]{:S(2)}, u32[]{:S(2)}) collective-permute-start(bf16[256,1024]{1,0:T(8,128)(2,1)S(1)} %collective-permute-done.3.refs_4_), channel_id=1, source_target_pairs={{0,2},{1,3},{2,4},{3,5},{4,6},{5,7},{6,8},{7,9},{8,10},{9,11},{10,... | collective-permute-start | bytes 1572872 | tf_op jit(solution)/shard_map/ppermute | solution.py:33
  64.6 16.2 %collective-permute-start.6 = (bf16[256,1024]{1,0:T(8,128)(2,1)S(1)}, bf16[256,1024]{1,0:T(8,128)(2,1)S(1)}, u32[]{:S(2)}, u32[]{:S(2)}) collective-permute-start(bf16[256,1024]{1,0:T(8,128)(2,1)S(1)} %collective-permute-done.5.refs_6_), channel_id=1, source_target_pairs={{0,14},{1,15},{2,0},{3,1},{4,2},{5,3},{6,4},{7,5},{8,6},{9,7},{10,... | collective-permute-start | bytes 1572872 | tf_op jit(solution)/shard_map/ppermute | solution.py:33
  69.5 26.1 %all-to-all-start.1 = ((bf16[32,6,1024]{2,1,0:T(8,128)(2,1)}), bf16[32,6,1024]{2,1,0:T(8,128)(2,1)}, u32[]{:S(2)}, u32[]{:S(2)}) async-start(bf16[32,6,1024]{2,1,0:T(8,128)(2,1)} %broadcast_in_dim.25), calls=%async_computation.1 | async-start | bytes 1048576 | tf_op jit(solution)/shard_map/all_to_all | solution.py:42
  78.1 26.9 %collective-permute-start.7 = (bf16[192,1024]{1,0:T(8,128)(2,1)}, bf16[192,1024]{1,0:T(8,128)(2,1)}, u32[]{:S(2)}, u32[]{:S(2)}) collective-permute-start(bf16[192,1024]{1,0:T(8,128)(2,1)} %slice.48), channel_id=1, source_target_pairs={{0,2},{1,3},{2,4},{3,5},{4,6},{5,7},{6,8},{7,9},{8,10},{9,11},{10,... | collective-permute-start | bytes 1179656 | tf_op jit(solution)/shard_map/ppermute | solution.py:33
  81.6 23.3 %collective-permute-start.8 = (bf16[192,1024]{1,0:T(8,128)(2,1)}, bf16[192,1024]{1,0:T(8,128)(2,1)}, u32[]{:S(2)}, u32[]{:S(2)}) collective-permute-start(bf16[192,1024]{1,0:T(8,128)(2,1)} %slice.49), channel_id=1, source_target_pairs={{0,14},{1,15},{2,0},{3,1},{4,2},{5,3},{6,4},{7,5},{8,6},{9,7},{10,... | collective-permute-start | bytes 1179656 | tf_op jit(solution)/shard_map/ppermute | solution.py:33
  85.9 19.0 %collective-permute-start.9 = (bf16[128,1024]{1,0:T(8,128)(2,1)S(1)}, bf16[128,1024]{1,0:T(8,128)(2,1)}, u32[]{:S(2)}, u32[]{:S(2)}) collective-permute-start(bf16[128,1024]{1,0:T(8,128)(2,1)S(1)} %collective-permute-done.refs_1_), channel_id=1, source_target_pairs={{0,8},{1,9},{2,10},{3,11},{4,12},{5,13},{6,14},{7,15},{8,0},{9,1},... | collective-permute-start | bytes 786440 | tf_op jit(solution)/shard_map/ppermute | solution.py:33
  105.0 1.0 copy-start.3
  106.0 1.0 copy-start.5
  118.9 1.0 copy-start.1
  119.8 0.8 copy-start.4
  120.7 0.7 copy-start.7
  121.4 45.8 %all-to-all-start.2 = ((bf16[16,256,128]{2,1,0:T(8,128)(2,1)}), bf16[16,256,128]{2,1,0:T(8,128)(2,1)S(1)}, u32[]{:S(2)}, u32[]{:S(2)}) async-start(bf16[16,256,128]{2,1,0:T(8,128)(2,1)} %copy-done.1), calls=%async_computation.2 | async-start | bytes 2097152 | tf_op jit(solution)/shard_map/all_to_all | solution.py:233
  134.2 3.6 %collective-permute-start.10 = (bf16[16,6,1024]{2,1,0:T(8,128)(2,1)}, bf16[16,6,1024]{2,1,0:T(8,128)(2,1)S(1)}, u32[]{:S(2)}, u32[]{:S(2)}) collective-permute-start(bf16[16,6,1024]{2,1,0:T(8,128)(2,1)} %copy-done.7), channel_id=1, source_target_pairs={{0,16},{16,0},{32,48},{48,32},{64,80},{80,64},{96,112},{112,96},{1... | collective-permute-start | bytes 589832 | tf_op jit(solution)/shard_map/ppermute | solution.py:37
  138.9 7.4 %collective-permute-start.11 = (bf16[8,6,1024]{2,1,0:T(8,128)(2,1)S(1)}, bf16[8,6,1024]{2,1,0:T(8,128)(2,1)S(1)}, u32[]{:S(2)}, u32[]{:S(2)}) collective-permute-start(bf16[8,6,1024]{2,1,0:T(8,128)(2,1)S(1)} %slice.69), channel_id=1, source_target_pairs={{0,32},{16,48},{32,0},{48,16},{64,96},{80,112},{96,64},{112,80},{1... | collective-permute-start | bytes 294920 | tf_op jit(solution)/shard_map/ppermute | solution.py:37
  146.4 7.7 %collective-permute-start.12 = (bf16[4,6,1024]{2,1,0:T(8,128)(2,1)S(1)}, bf16[4,6,1024]{2,1,0:T(8,128)(2,1)S(1)}, u32[]{:S(2)}, u32[]{:S(2)}) collective-permute-start(bf16[4,6,1024]{2,1,0:T(8,128)(2,1)S(1)} %slice.70), channel_id=1, source_target_pairs={{0,64},{16,80},{32,96},{48,112},{64,0},{80,16},{96,32},{112,48},{1... | collective-permute-start | bytes 147464 | tf_op jit(solution)/shard_map/ppermute | solution.py:37
  154.1 5.8 %collective-permute-start.13 = (bf16[2,6,1024]{2,1,0:T(8,128)(2,1)S(1)}, bf16[2,6,1024]{2,1,0:T(8,128)(2,1)S(1)}, u32[]{:S(2)}, u32[]{:S(2)}) collective-permute-start(bf16[2,6,1024]{2,1,0:T(8,128)(2,1)S(1)} %slice.71), channel_id=1, source_target_pairs={{0,128},{16,144},{32,160},{48,176},{64,192},{80,208},{96,224},{112... | collective-permute-start | bytes 73736 | tf_op jit(solution)/shard_map/ppermute | solution.py:37
  160.0 6.5 %collective-permute-start.14 = (bf16[1,6,1024]{2,1,0:T(8,128)(2,1)S(1)}, bf16[1,6,1024]{2,1,0:T(8,128)(2,1)S(1)}, u32[]{:S(2)}, u32[]{:S(2)}) collective-permute-start(bf16[1,6,1024]{2,1,0:T(8,128)(2,1)S(1)} %slice.72), channel_id=1, source_target_pairs={{0,256},{16,272},{32,288},{48,304},{64,320},{80,336},{96,352},{112... | collective-permute-start | bytes 36872 | tf_op jit(solution)/shard_map/ppermute | solution.py:37
  167.1 2.8 %copy-start = (bf16[3072,1024]{1,0:T(8,128)(2,1)S(1)}, bf16[3072,1024]{1,0:T(8,128)(2,1)}, u32[]{:S(2)}) copy-start(bf16[3072,1024]{1,0:T(8,128)(2,1)} %all-gather.2.cloned.1.call-done.w_ref) | copy-start | bytes 18874372
Sparse Core Ops, SparseCore 0:
  60.9 74.2 all-gather.1

commit v10 on v9

--- a/solution.py
+++ b/solution.py
@@ -232,11 +232,13 @@
     both, keep, send = attention(here, order, key_tiles[0], key_counts[0], blocks, w_head, mixed)
     both = lax.all_to_all(both, "seq", 0, 0, tiled=True)
 
-    sums = keep + swap_dp(send, 1).astype(F32)
+    came = swap_dp(send, 1)
     for bit in (2, 4, 8, 16):
-        half = sums.shape[0] // 2
-        sums = sums[:half] + swap_dp(sums[half:].astype(BF), bit).astype(F32)
-    grad_weight = sums * grad_scale
+        half = keep.shape[0] // 2
+        send = (keep[half:] + came[half:].astype(F32)).astype(BF)
+        keep = keep[:half] + came[:half].astype(F32)
+        came = swap_dp(send, bit)
+    grad_weight = (keep + came.astype(F32)) * grad_scale
 
     attended, grad_input = input_grad(both, w_all)
     return (attended[None], grad_input[None], grad_weight)

time: 180 us -> 180 us (level)
  no operation moved by 1% of the time
where the time goes in v10:
time: 180 us; the launch traced here: 179 us
  starting transfers between devices  91.1 us (51%)
  waiting for transfers between devices  41.2 us (23%)
  local copies, waits for them, and re-layouts  15.1 us (8%)
  between operations  14.4 us (8%)
  Pallas kernels  13.7 us (8%)
  other arithmetic  2.9 us (2%)
    ppermute x9, starting transfers between devices, shift_z(): return lax.ppermute(x, 'seq', [(s, (s + YH * k) % SEQ) for s in range(SEQ)])  39.9 us
    ppermute x9, waiting for transfers between devices, shift_z(): return lax.ppermute(x, 'seq', [(s, (s + YH * k) % SEQ) for s in range(SEQ)])  16.2 us
    ppermute x5, starting transfers between devices, swap_dp(): return lax.ppermute(x, 'dp', [(d, d ^ bit) for d in range(DP)])  15.9 us
    ppermute x5, waiting for transfers between devices, swap_dp(): return lax.ppermute(x, 'dp', [(d, d ^ bit) for d in range(DP)])  15.1 us
    all_to_all x1, starting transfers between devices, shards(): both = lax.all_to_all(both, 'seq', 0, 0, tiled=True)  12.8 us
    pallas_call x1, Pallas kernels, attention(): pl.pallas_call(functools.partial(attend, len(blocks)), out_shape=tuple((j...  11.9 us
    all_to_all x1, starting transfers between devices, shards(): mixed = lax.all_to_all(mixed, 'seq', 0, 0, tiled=True)  9.85 us
    unnamed x19, local copies, waits for them, and re-layouts  7.92 us
  transfers between devices with their start and end apart: 19, of which 9 were waited for; matrix products, arithmetic and copies ran while one was open for 6% of the time, Pallas kernels for 7%

profile of v10, /device:TPU:56, one launch (start us, length us, event | category | flops | bytes accessed | tf_op | source)
XLA Modules:
  0.0 178.5 jit_solution(8719761928613086649)
XLA Ops:
  7.2 4.8 %collective-permute-start = (bf16[128,1024]{1,0:T(8,128)(2,1)}, bf16[128,1024]{1,0:T(8,128)(2,1)S(1)}, u32[]{:S(2)}, u32[]{:S(2)}) collective-permute-start(bf16[128,1024]{1,0:T(8,128)(2,1)} %bitcast.27), channel_id=1, source_target_pairs={{0,1},{1,0},{2,3},{3,2},{4,5},{5,4},{6,7},{7,6},{8,9},{9,8},{10,11... | collective-permute-start | bytes 786440 | tf_op jit(solution)/shard_map/ppermute | solution.py:29
  12.0 4.3 %collective-permute-start.1 = (bf16[128,1024]{1,0:T(8,128)(2,1)}, bf16[128,1024]{1,0:T(8,128)(2,1)S(1)}, u32[]{:S(2)}, u32[]{:S(2)}) collective-permute-start(bf16[128,1024]{1,0:T(8,128)(2,1)} %bitcast.28), channel_id=1, source_target_pairs={{0,2},{1,3},{2,4},{3,5},{4,6},{5,7},{6,8},{7,9},{8,10},{9,11},{10,... | collective-permute-start | bytes 786440 | tf_op jit(solution)/shard_map/ppermute | solution.py:33
  16.3 8.6 %collective-permute-start.2 = (bf16[128,1024]{1,0:T(8,128)(2,1)}, bf16[128,1024]{1,0:T(8,128)(2,1)S(1)}, u32[]{:S(2)}, u32[]{:S(2)}) collective-permute-start(bf16[128,1024]{1,0:T(8,128)(2,1)} %bitcast.29), channel_id=1, source_target_pairs={{0,14},{1,15},{2,0},{3,1},{4,2},{5,3},{6,4},{7,5},{8,6},{9,7},{10,... | collective-permute-start | bytes 786440 | tf_op jit(solution)/shard_map/ppermute | solution.py:33
  24.9 1.1 copy.11
  26.1 0.8 broadcast_in_dim.23
  26.9 0.8 pad_maximum_fusion.2
  27.7 9.8 %all-to-all-start = ((bf16[16,112,128]{2,1,0:T(8,128)(2,1)}), bf16[16,112,128]{2,1,0:T(8,128)(2,1)S(1)}, u32[]{:S(2)}, u32[]{:S(2)}) async-start(bf16[16,112,128]{2,1,0:T(8,128)(2,1)} %pad_maximum_fusion.2), calls=%async_computation | async-start | bytes 917504 | tf_op jit(solution)/shard_map/all_to_all | solution.py:222
  37.6 0.9 pad_maximum_fusion.1
  38.5 3.4 %collective-permute-start.3 = (bf16[256,1024]{1,0:T(8,128)(2,1)}, bf16[256,1024]{1,0:T(8,128)(2,1)S(1)}, u32[]{:S(2)}, u32[]{:S(2)}) collective-permute-start(bf16[256,1024]{1,0:T(8,128)(2,1)} %get-tuple-element.28), channel_id=1, source_target_pairs={{0,2},{1,3},{2,4},{3,5},{4,6},{5,7},{6,8},{7,9},{8,10},{9,11},{10,... | collective-permute-start | bytes 1572872 | tf_op jit(solution)/shard_map/ppermute | solution.py:33
  41.9 3.7 %collective-permute-start.5 = (bf16[256,1024]{1,0:T(8,128)(2,1)S(1)}, bf16[256,1024]{1,0:T(8,128)(2,1)S(1)}, u32[]{:S(2)}, u32[]{:S(2)}) collective-permute-start(bf16[256,1024]{1,0:T(8,128)(2,1)S(1)} %get-tuple-element.27), channel_id=1, source_target_pairs={{0,14},{1,15},{2,0},{3,1},{4,2},{5,3},{6,4},{7,5},{8,6},{9,7},{10,... | collective-permute-start | bytes 1572872 | tf_op jit(solution)/shard_map/ppermute | solution.py:33
  45.6 6.4 %all-to-all-done.refs_12_ = bf16[16,112,128]{2,1,0:T(8,128)(2,1)S(1)} async-done(((bf16[16,112,128]{2,1,0:T(8,128)(2,1)}), bf16[16,112,128]{2,1,0:T(8,128)(2,1)S(1)}, u32[]{:S(2)}, u32[]{:S(2)}) %all-to-all-start) | async-done | bytes 458784 | tf_op jit(solution)/shard_map/all_to_all | solution.py:222
  52.0 0.8 reshape.19
  52.8 8.0 %collective-permute-done.3.refs_4_ = bf16[256,1024]{1,0:T(8,128)(2,1)S(1)} collective-permute-done((bf16[256,1024]{1,0:T(8,128)(2,1)}, bf16[256,1024]{1,0:T(8,128)(2,1)S(1)}, u32[]{:S(2)}, u32[]{:S(2)}) %collective-permute-start.3) | collective-permute-done | bytes 524320 | tf_op jit(solution)/shard_map/ppermute | solution.py:33
  60.8 3.8 %collective-permute-start.4 = (bf16[256,1024]{1,0:T(8,128)(2,1)S(1)}, bf16[256,1024]{1,0:T(8,128)(2,1)S(1)}, u32[]{:S(2)}, u32[]{:S(2)}) collective-permute-start(bf16[256,1024]{1,0:T(8,128)(2,1)S(1)} %collective-permute-done.3.refs_4_), channel_id=1, source_target_pairs={{0,2},{1,3},{2,4},{3,5},{4,6},{5,7},{6,8},{7,9},{8,10},{9,11},{10,... | collective-permute-start | bytes 1572872 | tf_op jit(solution)/shard_map/ppermute | solution.py:33
  64.6 3.2 %collective-permute-start.6 = (bf16[256,1024]{1,0:T(8,128)(2,1)S(1)}, bf16[256,1024]{1,0:T(8,128)(2,1)S(1)}, u32[]{:S(2)}, u32[]{:S(2)}) collective-permute-start(bf16[256,1024]{1,0:T(8,128)(2,1)S(1)} %collective-permute-done.5.refs_6_), channel_id=1, source_target_pairs={{0,14},{1,15},{2,0},{3,1},{4,2},{5,3},{6,4},{7,5},{8,6},{9,7},{10,... | collective-permute-start | bytes 1572872 | tf_op jit(solution)/shard_map/ppermute | solution.py:33
  67.8 1.6 broadcast_in_dim.25
  69.5 7.8 %all-to-all-start.1 = ((bf16[32,6,1024]{2,1,0:T(8,128)(2,1)}), bf16[32,6,1024]{2,1,0:T(8,128)(2,1)}, u32[]{:S(2)}, u32[]{:S(2)}) async-start(bf16[32,6,1024]{2,1,0:T(8,128)(2,1)} %broadcast_in_dim.25), calls=%async_computation.1 | async-start | bytes 1048576 | tf_op jit(solution)/shard_map/all_to_all | solution.py:42
  77.3 0.8 slice.76
  78.1 2.7 %collective-permute-start.7 = (bf16[192,1024]{1,0:T(8,128)(2,1)}, bf16[192,1024]{1,0:T(8,128)(2,1)}, u32[]{:S(2)}, u32[]{:S(2)}) collective-permute-start(bf16[192,1024]{1,0:T(8,128)(2,1)} %slice.76), channel_id=1, source_target_pairs={{0,2},{1,3},{2,4},{3,5},{4,6},{5,7},{6,8},{7,9},{8,10},{9,11},{10,... | collective-permute-start | bytes 1179656 | tf_op jit(solution)/shard_map/ppermute | solution.py:33
  80.9 0.8 slice.77
  81.6 4.3 %collective-permute-start.8 = (bf16[192,1024]{1,0:T(8,128)(2,1)}, bf16[192,1024]{1,0:T(8,128)(2,1)}, u32[]{:S(2)}, u32[]{:S(2)}) collective-permute-start(bf16[192,1024]{1,0:T(8,128)(2,1)} %slice.77), channel_id=1, source_target_pairs={{0,14},{1,15},{2,0},{3,1},{4,2},{5,3},{6,4},{7,5},{8,6},{9,7},{10,... | collective-permute-start | bytes 1179656 | tf_op jit(solution)/shard_map/ppermute | solution.py:33
  85.9 5.9 %collective-permute-start.9 = (bf16[128,1024]{1,0:T(8,128)(2,1)S(1)}, bf16[128,1024]{1,0:T(8,128)(2,1)}, u32[]{:S(2)}, u32[]{:S(2)}) collective-permute-start(bf16[128,1024]{1,0:T(8,128)(2,1)S(1)} %collective-permute-done.refs_1_), channel_id=1, source_target_pairs={{0,8},{1,9},{2,10},{3,11},{4,12},{5,13},{6,14},{7,15},{8,0},{9,1},... | collective-permute-start | bytes 786440 | tf_op jit(solution)/shard_map/ppermute | solution.py:33
  92.0 0.1 copy.12.list_ref
  92.0 0.1 stack.67.order_ref
  92.1 3.4 %all-to-all-done.1 = bf16[32,6,1024]{2,1,0:T(8,128)(2,1)} async-done(((bf16[32,6,1024]{2,1,0:T(8,128)(2,1)}), bf16[32,6,1024]{2,1,0:T(8,128)(2,1)}, u32[]{:S(2)}, u32[]{:S(2)}) %all-to-all-start.1) | async-done | bytes 393248 | tf_op jit(solution)/shard_map/all_to_all | solution.py:42
  95.6 1.2 reshape.18.refs_11_
  96.7 8.2 %collective-permute-done.9.refs_10_ = bf16[128,1024]{1,0:T(8,128)(2,1)} collective-permute-done((bf16[128,1024]{1,0:T(8,128)(2,1)S(1)}, bf16[128,1024]{1,0:T(8,128)(2,1)}, u32[]{:S(2)}, u32[]{:S(2)}) %collective-permute-start.9) | collective-permute-done | bytes 262176 | tf_op jit(solution)/shard_map/ppermute | solution.py:33
  105.0 1.0 copy-done.3
  106.1 1.0 copy-done.5
  107.0 11.9 %attend.1 = (bf16[16,256,128]{2,1,0:T(8,128)(2,1)S(1)}, f32[16,6,1024]{2,1,0:T(8,128)S(1)}, bf16[16,6,1024]{2,1,0:T(8,128)(2,1)S(1)}) custom-call(s32[1]{0:T(128)} %bitcast.here_ref, s32[16]{0:T(128)S(1)} %stack.67.order_ref, s32[16,4]{1,0:T(8,128)S(1)} %copy.12.list_ref, s32[16]{0:T(128)S(1)} %bitcast.31, bf16[128,1024]{1,0:T(8,128)(2,1)S(1)} %bitcast.30, ...), custom_call_target="tpu_custom_call" | custom-call | tf_op jit(solution)/shard_map/attend/pallas_call | solution.py:159
  118.9 1.0 copy-done.1
  119.9 0.8 copy-done.4
  120.7 0.7 copy-done.7
  121.4 12.8 %all-to-all-start.2 = ((bf16[16,256,128]{2,1,0:T(8,128)(2,1)}), bf16[16,256,128]{2,1,0:T(8,128)(2,1)S(1)}, u32[]{:S(2)}, u32[]{:S(2)}) async-start(bf16[16,256,128]{2,1,0:T(8,128)(2,1)} %copy-done.1), calls=%async_computation.2 | async-start | bytes 2097152 | tf_op jit(solution)/shard_map/all_to_all | solution.py:233
  134.2 1.9 %collective-permute-start.10 = (bf16[16,6,1024]{2,1,0:T(8,128)(2,1)}, bf16[16,6,1024]{2,1,0:T(8,128)(2,1)S(1)}, u32[]{:S(2)}, u32[]{:S(2)}) collective-permute-start(bf16[16,6,1024]{2,1,0:T(8,128)(2,1)} %copy-done.7), channel_id=1, source_target_pairs={{0,16},{16,0},{32,48},{48,32},{64,80},{80,64},{96,112},{112,96},{1... | collective-permute-start | bytes 589832 | tf_op jit(solution)/shard_map/ppermute | solution.py:37
  136.1 1.7 collective-permute-done.10
  137.8 1.1 add_convert_fusion
  138.9 3.4 %collective-permute-start.11 = (bf16[8,6,1024]{2,1,0:T(8,128)(2,1)S(1)}, bf16[8,6,1024]{2,1,0:T(8,128)(2,1)S(1)}, u32[]{:S(2)}, u32[]{:S(2)}) collective-permute-start(bf16[8,6,1024]{2,1,0:T(8,128)(2,1)S(1)} %get-tuple-element.23), channel_id=1, source_target_pairs={{0,32},{16,48},{32,0},{48,16},{64,96},{80,112},{96,64},{112,80},{1... | collective-permute-start | bytes 294920 | tf_op jit(solution)/shard_map/ppermute | solution.py:37
  142.3 4.0 %collective-permute-done.11 = bf16[8,6,1024]{2,1,0:T(8,128)(2,1)S(1)} collective-permute-done((bf16[8,6,1024]{2,1,0:T(8,128)(2,1)S(1)}, bf16[8,6,1024]{2,1,0:T(8,128)(2,1)S(1)}, u32[]{:S(2)}, u32[]{:S(2)}) %collective-permute-start.11) | collective-permute-done | bytes 98336 | tf_op jit(solution)/shard_map/ppermute | solution.py:37
  146.3 4.9 %collective-permute-start.12 = (bf16[4,6,1024]{2,1,0:T(8,128)(2,1)S(1)}, bf16[4,6,1024]{2,1,0:T(8,128)(2,1)S(1)}, u32[]{:S(2)}, u32[]{:S(2)}) collective-permute-start(bf16[4,6,1024]{2,1,0:T(8,128)(2,1)S(1)} %get-tuple-element.25), channel_id=1, source_target_pairs={{0,64},{16,80},{32,96},{48,112},{64,0},{80,16},{96,32},{112,48},{1... | collective-permute-start | bytes 147464 | tf_op jit(solution)/shard_map/ppermute | solution.py:37
  151.3 2.7 %collective-permute-done.12 = bf16[4,6,1024]{2,1,0:T(8,128)(2,1)S(1)} collective-permute-done((bf16[4,6,1024]{2,1,0:T(8,128)(2,1)S(1)}, bf16[4,6,1024]{2,1,0:T(8,128)(2,1)S(1)}, u32[]{:S(2)}, u32[]{:S(2)}) %collective-permute-start.12) | collective-permute-done | bytes 49184 | tf_op jit(solution)/shard_map/ppermute | solution.py:37
  154.0 3.1 %collective-permute-start.13 = (bf16[2,6,1024]{2,1,0:T(8,128)(2,1)S(1)}, bf16[2,6,1024]{2,1,0:T(8,128)(2,1)S(1)}, u32[]{:S(2)}, u32[]{:S(2)}) collective-permute-start(bf16[2,6,1024]{2,1,0:T(8,128)(2,1)S(1)} %get-tuple-element.29), channel_id=1, source_target_pairs={{0,128},{16,144},{32,160},{48,176},{64,192},{80,208},{96,224},{112... | collective-permute-start | bytes 73736 | tf_op jit(solution)/shard_map/ppermute | solution.py:37
  157.2 2.7 %collective-permute-done.13 = bf16[2,6,1024]{2,1,0:T(8,128)(2,1)S(1)} collective-permute-done((bf16[2,6,1024]{2,1,0:T(8,128)(2,1)S(1)}, bf16[2,6,1024]{2,1,0:T(8,128)(2,1)S(1)}, u32[]{:S(2)}, u32[]{:S(2)}) %collective-permute-start.13) | collective-permute-done | bytes 24608 | tf_op jit(solution)/shard_map/ppermute | solution.py:37
  159.8 2.6 %collective-permute-start.14 = (bf16[1,6,1024]{2,1,0:T(8,128)(2,1)S(1)}, bf16[1,6,1024]{2,1,0:T(8,128)(2,1)S(1)}, u32[]{:S(2)}, u32[]{:S(2)}) collective-permute-start(bf16[1,6,1024]{2,1,0:T(8,128)(2,1)S(1)} %fusion.2), channel_id=1, source_target_pairs={{0,256},{16,272},{32,288},{48,304},{64,320},{80,336},{96,352},{112... | collective-permute-start | bytes 36872 | tf_op jit(solution)/shard_map/ppermute | solution.py:37
  162.4 3.9 %collective-permute-done.14 = bf16[1,6,1024]{2,1,0:T(8,128)(2,1)S(1)} collective-permute-done((bf16[1,6,1024]{2,1,0:T(8,128)(2,1)S(1)}, bf16[1,6,1024]{2,1,0:T(8,128)(2,1)S(1)}, u32[]{:S(2)}, u32[]{:S(2)}) %collective-permute-start.14) | collective-permute-done | bytes 12320 | tf_op jit(solution)/shard_map/ppermute | solution.py:37
  166.4 0.6 copy.13
  167.0 2.8 %copy-done = bf16[3072,1024]{1,0:T(8,128)(2,1)S(1)} copy-done((bf16[3072,1024]{1,0:T(8,128)(2,1)S(1)}, bf16[3072,1024]{1,0:T(8,128)(2,1)}, u32[]{:S(2)}) %copy-start) | copy-done | bytes 6291480
  169.8 1.9 %input_sum.1 = (bf16[128,1024]{1,0:T(8,128)(2,1)}, bf16[128,1024]{1,0:T(8,128)(2,1)}) custom-call(bf16[16,256,128]{2,1,0:T(8,128)(2,1)S(1)} %all-to-all-done.2.both_ref, bf16[3072,1024]{1,0:T(8,128)(2,1)S(1)} %copy-done), custom_call_target="tpu_custom_call" | custom-call | tf_op jit(solution)/shard_map/input_sum/pallas_call | solution.py:192
  (30 shorter events, 0.2 us)
Async XLA Ops:
  7.2 84.8 %copy-start.8 = (s32[1,16,4]{1,2,0:T(4,128)S(1)}, s32[1,16,4]{1,2,0:T(4,128)}, u32[]{:S(2)}) copy-start(s32[1,16,4]{1,2,0:T(4,128)} %param.7) | copy-start | bytes 772
  7.2 97.8 %copy-start.6 = (s32[1,16]{1,0:T(1,128)S(1)}, s32[1,16]{1,0:T(1,128)}, u32[]{:S(2)}) copy-start(s32[1,16]{1,0:T(1,128)} %param.8) | copy-start | bytes 196
  7.2 30.4 %collective-permute-start = (bf16[128,1024]{1,0:T(8,128)(2,1)}, bf16[128,1024]{1,0:T(8,128)(2,1)S(1)}, u32[]{:S(2)}, u32[]{:S(2)}) collective-permute-start(bf16[128,1024]{1,0:T(8,128)(2,1)} %bitcast.27), channel_id=1, source_target_pairs={{0,1},{1,0},{2,3},{3,2},{4,5},{5,4},{6,7},{7,6},{8,9},{9,8},{10,11... | collective-permute-start | bytes 786440 | tf_op jit(solution)/shard_map/ppermute | solution.py:29
  12.0 25.5 %collective-permute-start.1 = (bf16[128,1024]{1,0:T(8,128)(2,1)}, bf16[128,1024]{1,0:T(8,128)(2,1)S(1)}, u32[]{:S(2)}, u32[]{:S(2)}) collective-permute-start(bf16[128,1024]{1,0:T(8,128)(2,1)} %bitcast.28), channel_id=1, source_target_pairs={{0,2},{1,3},{2,4},{3,5},{4,6},{5,7},{6,8},{7,9},{8,10},{9,11},{10,... | collective-permute-start | bytes 786440 | tf_op jit(solution)/shard_map/ppermute | solution.py:33
  16.3 21.2 %collective-permute-start.2 = (bf16[128,1024]{1,0:T(8,128)(2,1)}, bf16[128,1024]{1,0:T(8,128)(2,1)S(1)}, u32[]{:S(2)}, u32[]{:S(2)}) collective-permute-start(bf16[128,1024]{1,0:T(8,128)(2,1)} %bitcast.29), channel_id=1, source_target_pairs={{0,14},{1,15},{2,0},{3,1},{4,2},{5,3},{6,4},{7,5},{8,6},{9,7},{10,... | collective-permute-start | bytes 786440 | tf_op jit(solution)/shard_map/ppermute | solution.py:33
  27.7 24.3 %all-to-all-start = ((bf16[16,112,128]{2,1,0:T(8,128)(2,1)}), bf16[16,112,128]{2,1,0:T(8,128)(2,1)S(1)}, u32[]{:S(2)}, u32[]{:S(2)}) async-start(bf16[16,112,128]{2,1,0:T(8,128)(2,1)} %pad_maximum_fusion.2), calls=%async_computation | async-start | bytes 917504 | tf_op jit(solution)/shard_map/all_to_all | solution.py:222
  37.5 129.5 %all-gather.2.cloned.1.call-start = ((), (), s32[]{:S(2)}) async-start(), calls=%async_computation.3 | async-start | bytes 6488064 | tf_op jit(solution)/shard_map/all_gather | solution.py:225
  38.5 22.2 %collective-permute-start.3 = (bf16[256,1024]{1,0:T(8,128)(2,1)}, bf16[256,1024]{1,0:T(8,128)(2,1)S(1)}, u32[]{:S(2)}, u32[]{:S(2)}) collective-permute-start(bf16[256,1024]{1,0:T(8,128)(2,1)} %get-tuple-element.28), channel_id=1, source_target_pairs={{0,2},{1,3},{2,4},{3,5},{4,6},{5,7},{6,8},{7,9},{8,10},{9,11},{10,... | collective-permute-start | bytes 1572872 | tf_op jit(solution)/shard_map/ppermute | solution.py:33
  41.9 18.9 %collective-permute-start.5 = (bf16[256,1024]{1,0:T(8,128)(2,1)S(1)}, bf16[256,1024]{1,0:T(8,128)(2,1)S(1)}, u32[]{:S(2)}, u32[]{:S(2)}) collective-permute-start(bf16[256,1024]{1,0:T(8,128)(2,1)S(1)} %get-tuple-element.27), channel_id=1, source_target_pairs={{0,14},{1,15},{2,0},{3,1},{4,2},{5,3},{6,4},{7,5},{8,6},{9,7},{10,... | collective-permute-start | bytes 1572872 | tf_op jit(solution)/shard_map/ppermute | solution.py:33
  60.7 31.4 %copy-start.2 = (bf16[256,1024]{1,0:T(8,128)(2,1)}, bf16[256,1024]{1,0:T(8,128)(2,1)S(1)}, u32[]{:S(2)}) copy-start(bf16[256,1024]{1,0:T(8,128)(2,1)S(1)} %collective-permute-done.5.refs_6_) | copy-start | bytes 1572868
  60.8 16.5 %collective-permute-start.4 = (bf16[256,1024]{1,0:T(8,128)(2,1)S(1)}, bf16[256,1024]{1,0:T(8,128)(2,1)S(1)}, u32[]{:S(2)}, u32[]{:S(2)}) collective-permute-start(bf16[256,1024]{1,0:T(8,128)(2,1)S(1)} %collective-permute-done.3.refs_4_), channel_id=1, source_target_pairs={{0,2},{1,3},{2,4},{3,5},{4,6},{5,7},{6,8},{7,9},{8,10},{9,11},{10,... | collective-permute-start | bytes 1572872 | tf_op jit(solution)/shard_map/ppermute | solution.py:33
  64.6 16.2 %collective-permute-start.6 = (bf16[256,1024]{1,0:T(8,128)(2,1)S(1)}, bf16[256,1024]{1,0:T(8,128)(2,1)S(1)}, u32[]{:S(2)}, u32[]{:S(2)}) collective-permute-start(bf16[256,1024]{1,0:T(8,128)(2,1)S(1)} %collective-permute-done.5.refs_6_), channel_id=1, source_target_pairs={{0,14},{1,15},{2,0},{3,1},{4,2},{5,3},{6,4},{7,5},{8,6},{9,7},{10,... | collective-permute-start | bytes 1572872 | tf_op jit(solution)/shard_map/ppermute | solution.py:33
  69.5 26.1 %all-to-all-start.1 = ((bf16[32,6,1024]{2,1,0:T(8,128)(2,1)}), bf16[32,6,1024]{2,1,0:T(8,128)(2,1)}, u32[]{:S(2)}, u32[]{:S(2)}) async-start(bf16[32,6,1024]{2,1,0:T(8,128)(2,1)} %broadcast_in_dim.25), calls=%async_computation.1 | async-start | bytes 1048576 | tf_op jit(solution)/shard_map/all_to_all | solution.py:42
  78.1 26.9 %collective-permute-start.7 = (bf16[192,1024]{1,0:T(8,128)(2,1)}, bf16[192,1024]{1,0:T(8,128)(2,1)}, u32[]{:S(2)}, u32[]{:S(2)}) collective-permute-start(bf16[192,1024]{1,0:T(8,128)(2,1)} %slice.76), channel_id=1, source_target_pairs={{0,2},{1,3},{2,4},{3,5},{4,6},{5,7},{6,8},{7,9},{8,10},{9,11},{10,... | collective-permute-start | bytes 1179656 | tf_op jit(solution)/shard_map/ppermute | solution.py:33
  81.6 23.4 %collective-permute-start.8 = (bf16[192,1024]{1,0:T(8,128)(2,1)}, bf16[192,1024]{1,0:T(8,128)(2,1)}, u32[]{:S(2)}, u32[]{:S(2)}) collective-permute-start(bf16[192,1024]{1,0:T(8,128)(2,1)} %slice.77), channel_id=1, source_target_pairs={{0,14},{1,15},{2,0},{3,1},{4,2},{5,3},{6,4},{7,5},{8,6},{9,7},{10,... | collective-permute-start | bytes 1179656 | tf_op jit(solution)/shard_map/ppermute | solution.py:33
  85.9 19.1 %collective-permute-start.9 = (bf16[128,1024]{1,0:T(8,128)(2,1)S(1)}, bf16[128,1024]{1,0:T(8,128)(2,1)}, u32[]{:S(2)}, u32[]{:S(2)}) collective-permute-start(bf16[128,1024]{1,0:T(8,128)(2,1)S(1)} %collective-permute-done.refs_1_), channel_id=1, source_target_pairs={{0,8},{1,9},{2,10},{3,11},{4,12},{5,13},{6,14},{7,15},{8,0},{9,1},... | collective-permute-start | bytes 786440 | tf_op jit(solution)/shard_map/ppermute | solution.py:33
  105.0 1.0 copy-start.3
  106.0 1.0 copy-start.5
  118.9 1.0 copy-start.1
  119.9 0.8 copy-start.4
  120.7 0.7 copy-start.7
  121.4 45.6 %all-to-all-start.2 = ((bf16[16,256,128]{2,1,0:T(8,128)(2,1)}), bf16[16,256,128]{2,1,0:T(8,128)(2,1)S(1)}, u32[]{:S(2)}, u32[]{:S(2)}) async-start(bf16[16,256,128]{2,1,0:T(8,128)(2,1)} %copy-done.1), calls=%async_computation.2 | async-start | bytes 2097152 | tf_op jit(solution)/shard_map/all_to_all | solution.py:233
  134.2 3.6 %collective-permute-start.10 = (bf16[16,6,1024]{2,1,0:T(8,128)(2,1)}, bf16[16,6,1024]{2,1,0:T(8,128)(2,1)S(1)}, u32[]{:S(2)}, u32[]{:S(2)}) collective-permute-start(bf16[16,6,1024]{2,1,0:T(8,128)(2,1)} %copy-done.7), channel_id=1, source_target_pairs={{0,16},{16,0},{32,48},{48,32},{64,80},{80,64},{96,112},{112,96},{1... | collective-permute-start | bytes 589832 | tf_op jit(solution)/shard_map/ppermute | solution.py:37
  138.9 7.4 %collective-permute-start.11 = (bf16[8,6,1024]{2,1,0:T(8,128)(2,1)S(1)}, bf16[8,6,1024]{2,1,0:T(8,128)(2,1)S(1)}, u32[]{:S(2)}, u32[]{:S(2)}) collective-permute-start(bf16[8,6,1024]{2,1,0:T(8,128)(2,1)S(1)} %get-tuple-element.23), channel_id=1, source_target_pairs={{0,32},{16,48},{32,0},{48,16},{64,96},{80,112},{96,64},{112,80},{1... | collective-permute-start | bytes 294920 | tf_op jit(solution)/shard_map/ppermute | solution.py:37
  146.3 7.7 %collective-permute-start.12 = (bf16[4,6,1024]{2,1,0:T(8,128)(2,1)S(1)}, bf16[4,6,1024]{2,1,0:T(8,128)(2,1)S(1)}, u32[]{:S(2)}, u32[]{:S(2)}) collective-permute-start(bf16[4,6,1024]{2,1,0:T(8,128)(2,1)S(1)} %get-tuple-element.25), channel_id=1, source_target_pairs={{0,64},{16,80},{32,96},{48,112},{64,0},{80,16},{96,32},{112,48},{1... | collective-permute-start | bytes 147464 | tf_op jit(solution)/shard_map/ppermute | solution.py:37
  154.0 5.8 %collective-permute-start.13 = (bf16[2,6,1024]{2,1,0:T(8,128)(2,1)S(1)}, bf16[2,6,1024]{2,1,0:T(8,128)(2,1)S(1)}, u32[]{:S(2)}, u32[]{:S(2)}) collective-permute-start(bf16[2,6,1024]{2,1,0:T(8,128)(2,1)S(1)} %get-tuple-element.29), channel_id=1, source_target_pairs={{0,128},{16,144},{32,160},{48,176},{64,192},{80,208},{96,224},{112... | collective-permute-start | bytes 73736 | tf_op jit(solution)/shard_map/ppermute | solution.py:37
  159.8 6.5 %collective-permute-start.14 = (bf16[1,6,1024]{2,1,0:T(8,128)(2,1)S(1)}, bf16[1,6,1024]{2,1,0:T(8,128)(2,1)S(1)}, u32[]{:S(2)}, u32[]{:S(2)}) collective-permute-start(bf16[1,6,1024]{2,1,0:T(8,128)(2,1)S(1)} %fusion.2), channel_id=1, source_target_pairs={{0,256},{16,272},{32,288},{48,304},{64,320},{80,336},{96,352},{112... | collective-permute-start | bytes 36872 | tf_op jit(solution)/shard_map/ppermute | solution.py:37
  167.0 2.8 %copy-start = (bf16[3072,1024]{1,0:T(8,128)(2,1)S(1)}, bf16[3072,1024]{1,0:T(8,128)(2,1)}, u32[]{:S(2)}) copy-start(bf16[3072,1024]{1,0:T(8,128)(2,1)} %all-gather.2.cloned.1.call-done.w_ref) | copy-start | bytes 18874372
Sparse Core Ops, SparseCore 0:
  60.9 74.2 all-gather.1

commit v11 on v10

--- a/solution.py
+++ b/solution.py
@@ -234,6 +234,8 @@
 
     came = swap_dp(send, 1)
     for bit in (2, 4, 8, 16):
+        if bit == 16:
+            w_all, came = lax.optimization_barrier((w_all, came))
         half = keep.shape[0] // 2
         send = (keep[half:] + came[half:].astype(F32)).astype(BF)
         keep = keep[:half] + came[:half].astype(F32)

time: 180 us -> 181 us (level)
  the two profiles are of different devices: /device:TPU:56 before, /device:TPU:52 now
where the time goes in v11:
time: 181 us; the launch traced here: 180 us
  starting transfers between devices  87.5 us (48%)
  waiting for transfers between devices  46.1 us (25%)
  local copies, waits for them, and re-layouts  15.2 us (8%)
  between operations  14.4 us (8%)
  Pallas kernels  13.8 us (8%)
  other arithmetic  2.9 us (2%)
    ppermute x9, starting transfers between devices, shift_z(): return lax.ppermute(x, 'seq', [(s, (s + YH * k) % SEQ) for s in range(SEQ)])  41.5 us
    ppermute x9, waiting for transfers between devices, shift_z(): return lax.ppermute(x, 'seq', [(s, (s + YH * k) % SEQ) for s in range(SEQ)])  18.7 us
    ppermute x5, waiting for transfers between devices, swap_dp(): return lax.ppermute(x, 'dp', [(d, d ^ bit) for d in range(DP)])  14.4 us
    all_to_all x1, starting transfers between devices, shards(): both = lax.all_to_all(both, 'seq', 0, 0, tiled=True)  12.6 us
    ppermute x5, starting transfers between devices, swap_dp(): return lax.ppermute(x, 'dp', [(d, d ^ bit) for d in range(DP)])  12.1 us
    pallas_call x1, Pallas kernels, attention(): pl.pallas_call(functools.partial(attend, len(blocks)), out_shape=tuple((j...  11.9 us
    all_to_all x1, starting transfers between devices, shards(): mixed = lax.all_to_all(mixed, 'seq', 0, 0, tiled=True)  9.85 us
    unnamed x19, local copies, waits for them, and re-layouts  7.93 us
  transfers between devices with their start and end apart: 19, of which 9 were waited for; matrix products, arithmetic and copies ran while one was open for 6% of the time, Pallas kernels for 8%

profile of v11, /device:TPU:52, one launch (start us, length us, event | category | flops | bytes accessed | tf_op | source)
XLA Modules:
  0.0 179.8 jit_solution(13797341701933772241)
XLA Ops:
  7.2 3.9 %collective-permute-start = (bf16[128,1024]{1,0:T(8,128)(2,1)}, bf16[128,1024]{1,0:T(8,128)(2,1)S(1)}, u32[]{:S(2)}, u32[]{:S(2)}) collective-permute-start(bf16[128,1024]{1,0:T(8,128)(2,1)} %bitcast.27), channel_id=1, source_target_pairs={{0,1},{1,0},{2,3},{3,2},{4,5},{5,4},{6,7},{7,6},{8,9},{9,8},{10,11... | collective-permute-start | bytes 786440 | tf_op jit(solution)/shard_map/ppermute | solution.py:29
  11.1 4.3 %collective-permute-start.1 = (bf16[128,1024]{1,0:T(8,128)(2,1)}, bf16[128,1024]{1,0:T(8,128)(2,1)S(1)}, u32[]{:S(2)}, u32[]{:S(2)}) collective-permute-start(bf16[128,1024]{1,0:T(8,128)(2,1)} %bitcast.28), channel_id=1, source_target_pairs={{0,2},{1,3},{2,4},{3,5},{4,6},{5,7},{6,8},{7,9},{8,10},{9,11},{10,... | collective-permute-start | bytes 786440 | tf_op jit(solution)/shard_map/ppermute | solution.py:33
  15.4 8.6 %collective-permute-start.2 = (bf16[128,1024]{1,0:T(8,128)(2,1)}, bf16[128,1024]{1,0:T(8,128)(2,1)S(1)}, u32[]{:S(2)}, u32[]{:S(2)}) collective-permute-start(bf16[128,1024]{1,0:T(8,128)(2,1)} %bitcast.29), channel_id=1, source_target_pairs={{0,14},{1,15},{2,0},{3,1},{4,2},{5,3},{6,4},{7,5},{8,6},{9,7},{10,... | collective-permute-start | bytes 786440 | tf_op jit(solution)/shard_map/ppermute | solution.py:33
  24.0 1.1 copy.11
  25.2 0.8 broadcast_in_dim.23
  26.0 0.8 pad_maximum_fusion.2
  26.8 9.8 %all-to-all-start = ((bf16[16,112,128]{2,1,0:T(8,128)(2,1)}), bf16[16,112,128]{2,1,0:T(8,128)(2,1)S(1)}, u32[]{:S(2)}, u32[]{:S(2)}) async-start(bf16[16,112,128]{2,1,0:T(8,128)(2,1)} %pad_maximum_fusion.2), calls=%async_computation | async-start | bytes 917504 | tf_op jit(solution)/shard_map/all_to_all | solution.py:222
  36.7 0.9 pad_maximum_fusion.1
  37.6 3.4 %collective-permute-start.3 = (bf16[256,1024]{1,0:T(8,128)(2,1)}, bf16[256,1024]{1,0:T(8,128)(2,1)S(1)}, u32[]{:S(2)}, u32[]{:S(2)}) collective-permute-start(bf16[256,1024]{1,0:T(8,128)(2,1)} %get-tuple-element.32), channel_id=1, source_target_pairs={{0,2},{1,3},{2,4},{3,5},{4,6},{5,7},{6,8},{7,9},{8,10},{9,11},{10,... | collective-permute-start | bytes 1572872 | tf_op jit(solution)/shard_map/ppermute | solution.py:33
  41.0 3.7 %collective-permute-start.5 = (bf16[256,1024]{1,0:T(8,128)(2,1)S(1)}, bf16[256,1024]{1,0:T(8,128)(2,1)S(1)}, u32[]{:S(2)}, u32[]{:S(2)}) collective-permute-start(bf16[256,1024]{1,0:T(8,128)(2,1)S(1)} %get-tuple-element.31), channel_id=1, source_target_pairs={{0,14},{1,15},{2,0},{3,1},{4,2},{5,3},{6,4},{7,5},{8,6},{9,7},{10,... | collective-permute-start | bytes 1572872 | tf_op jit(solution)/shard_map/ppermute | solution.py:33
  44.7 7.0 %all-to-all-done.refs_12_ = bf16[16,112,128]{2,1,0:T(8,128)(2,1)S(1)} async-done(((bf16[16,112,128]{2,1,0:T(8,128)(2,1)}), bf16[16,112,128]{2,1,0:T(8,128)(2,1)S(1)}, u32[]{:S(2)}, u32[]{:S(2)}) %all-to-all-start) | async-done | bytes 458784 | tf_op jit(solution)/shard_map/all_to_all | solution.py:222
  51.7 0.8 reshape.19
  52.4 7.7 %collective-permute-done.3.refs_4_ = bf16[256,1024]{1,0:T(8,128)(2,1)S(1)} collective-permute-done((bf16[256,1024]{1,0:T(8,128)(2,1)}, bf16[256,1024]{1,0:T(8,128)(2,1)S(1)}, u32[]{:S(2)}, u32[]{:S(2)}) %collective-permute-start.3) | collective-permute-done | bytes 524320 | tf_op jit(solution)/shard_map/ppermute | solution.py:33
  60.2 3.2 %collective-permute-start.4 = (bf16[256,1024]{1,0:T(8,128)(2,1)S(1)}, bf16[256,1024]{1,0:T(8,128)(2,1)S(1)}, u32[]{:S(2)}, u32[]{:S(2)}) collective-permute-start(bf16[256,1024]{1,0:T(8,128)(2,1)S(1)} %collective-permute-done.3.refs_4_), channel_id=1, source_target_pairs={{0,2},{1,3},{2,4},{3,5},{4,6},{5,7},{6,8},{7,9},{8,10},{9,11},{10,... | collective-permute-start | bytes 1572872 | tf_op jit(solution)/shard_map/ppermute | solution.py:33
  63.4 3.8 %collective-permute-start.6 = (bf16[256,1024]{1,0:T(8,128)(2,1)S(1)}, bf16[256,1024]{1,0:T(8,128)(2,1)S(1)}, u32[]{:S(2)}, u32[]{:S(2)}) collective-permute-start(bf16[256,1024]{1,0:T(8,128)(2,1)S(1)} %collective-permute-done.5.refs_6_), channel_id=1, source_target_pairs={{0,14},{1,15},{2,0},{3,1},{4,2},{5,3},{6,4},{7,5},{8,6},{9,7},{10,... | collective-permute-start | bytes 1572872 | tf_op jit(solution)/shard_map/ppermute | solution.py:33
  67.2 1.6 broadcast_in_dim.25
  68.8 7.6 %all-to-all-start.1 = ((bf16[32,6,1024]{2,1,0:T(8,128)(2,1)}), bf16[32,6,1024]{2,1,0:T(8,128)(2,1)}, u32[]{:S(2)}, u32[]{:S(2)}) async-start(bf16[32,6,1024]{2,1,0:T(8,128)(2,1)} %broadcast_in_dim.25), calls=%async_computation.1 | async-start | bytes 1048576 | tf_op jit(solution)/shard_map/all_to_all | solution.py:42
  76.4 0.1 collective-permute-done.4.refs_5_
  76.5 0.8 slice.76
  77.3 2.5 %collective-permute-start.7 = (bf16[192,1024]{1,0:T(8,128)(2,1)}, bf16[192,1024]{1,0:T(8,128)(2,1)}, u32[]{:S(2)}, u32[]{:S(2)}) collective-permute-start(bf16[192,1024]{1,0:T(8,128)(2,1)} %slice.76), channel_id=1, source_target_pairs={{0,2},{1,3},{2,4},{3,5},{4,6},{5,7},{6,8},{7,9},{8,10},{9,11},{10,... | collective-permute-start | bytes 1179656 | tf_op jit(solution)/shard_map/ppermute | solution.py:33
  79.8 0.8 slice.77
  80.6 4.5 %collective-permute-start.8 = (bf16[192,1024]{1,0:T(8,128)(2,1)}, bf16[192,1024]{1,0:T(8,128)(2,1)}, u32[]{:S(2)}, u32[]{:S(2)}) collective-permute-start(bf16[192,1024]{1,0:T(8,128)(2,1)} %slice.77), channel_id=1, source_target_pairs={{0,14},{1,15},{2,0},{3,1},{4,2},{5,3},{6,4},{7,5},{8,6},{9,7},{10,... | collective-permute-start | bytes 1179656 | tf_op jit(solution)/shard_map/ppermute | solution.py:33
  85.1 7.5 %collective-permute-start.9 = (bf16[128,1024]{1,0:T(8,128)(2,1)S(1)}, bf16[128,1024]{1,0:T(8,128)(2,1)}, u32[]{:S(2)}, u32[]{:S(2)}) collective-permute-start(bf16[128,1024]{1,0:T(8,128)(2,1)S(1)} %collective-permute-done.refs_1_), channel_id=1, source_target_pairs={{0,8},{1,9},{2,10},{3,11},{4,12},{5,13},{6,14},{7,15},{8,0},{9,1},... | collective-permute-start | bytes 786440 | tf_op jit(solution)/shard_map/ppermute | solution.py:33
  92.7 0.1 copy.12.list_ref
  92.8 0.1 stack.67.order_ref
  92.9 1.2 reshape.18.refs_11_
  94.1 10.9 %collective-permute-done.9.refs_10_ = bf16[128,1024]{1,0:T(8,128)(2,1)} collective-permute-done((bf16[128,1024]{1,0:T(8,128)(2,1)S(1)}, bf16[128,1024]{1,0:T(8,128)(2,1)}, u32[]{:S(2)}, u32[]{:S(2)}) %collective-permute-start.9) | collective-permute-done | bytes 262176 | tf_op jit(solution)/shard_map/ppermute | solution.py:33
  105.1 1.0 copy-done.3
  106.1 1.0 copy-done.5
  107.1 11.9 %attend.1 = (bf16[16,256,128]{2,1,0:T(8,128)(2,1)S(1)}, f32[16,6,1024]{2,1,0:T(8,128)S(1)}, bf16[16,6,1024]{2,1,0:T(8,128)(2,1)S(1)}) custom-call(s32[1]{0:T(128)} %bitcast.here_ref, s32[16]{0:T(128)S(1)} %stack.67.order_ref, s32[16,4]{1,0:T(8,128)S(1)} %copy.12.list_ref, s32[16]{0:T(128)S(1)} %bitcast.31, bf16[128,1024]{1,0:T(8,128)(2,1)S(1)} %bitcast.30, ...), custom_call_target="tpu_custom_call" | custom-call | tf_op jit(solution)/shard_map/attend/pallas_call | solution.py:159
  119.0 1.0 copy-done.1
  119.9 0.8 copy-done.4
  120.8 0.7 copy-done.7
  121.5 12.6 %all-to-all-start.2 = ((bf16[16,256,128]{2,1,0:T(8,128)(2,1)}), bf16[16,256,128]{2,1,0:T(8,128)(2,1)S(1)}, u32[]{:S(2)}, u32[]{:S(2)}) async-start(bf16[16,256,128]{2,1,0:T(8,128)(2,1)} %copy-done.1), calls=%async_computation.2 | async-start | bytes 2097152 | tf_op jit(solution)/shard_map/all_to_all | solution.py:233
  134.0 1.9 %collective-permute-start.10 = (bf16[16,6,1024]{2,1,0:T(8,128)(2,1)}, bf16[16,6,1024]{2,1,0:T(8,128)(2,1)S(1)}, u32[]{:S(2)}, u32[]{:S(2)}) collective-permute-start(bf16[16,6,1024]{2,1,0:T(8,128)(2,1)} %copy-done.7), channel_id=1, source_target_pairs={{0,16},{16,0},{32,48},{48,32},{64,80},{80,64},{96,112},{112,96},{1... | collective-permute-start | bytes 589832 | tf_op jit(solution)/shard_map/ppermute | solution.py:37
  136.0 1.7 collective-permute-done.10
  137.7 1.1 add_convert_fusion
  138.8 3.1 %collective-permute-start.11 = (bf16[8,6,1024]{2,1,0:T(8,128)(2,1)S(1)}, bf16[8,6,1024]{2,1,0:T(8,128)(2,1)S(1)}, u32[]{:S(2)}, u32[]{:S(2)}) collective-permute-start(bf16[8,6,1024]{2,1,0:T(8,128)(2,1)S(1)} %get-tuple-element.27), channel_id=1, source_target_pairs={{0,32},{16,48},{32,0},{48,16},{64,96},{80,112},{96,64},{112,80},{1... | collective-permute-start | bytes 294920 | tf_op jit(solution)/shard_map/ppermute | solution.py:37
  141.9 4.3 %collective-permute-done.11 = bf16[8,6,1024]{2,1,0:T(8,128)(2,1)S(1)} collective-permute-done((bf16[8,6,1024]{2,1,0:T(8,128)(2,1)S(1)}, bf16[8,6,1024]{2,1,0:T(8,128)(2,1)S(1)}, u32[]{:S(2)}, u32[]{:S(2)}) %collective-permute-start.11) | collective-permute-done | bytes 98336 | tf_op jit(solution)/shard_map/ppermute | solution.py:37
  146.2 2.4 %collective-permute-start.12 = (bf16[4,6,1024]{2,1,0:T(8,128)(2,1)S(1)}, bf16[4,6,1024]{2,1,0:T(8,128)(2,1)S(1)}, u32[]{:S(2)}, u32[]{:S(2)}) collective-permute-start(bf16[4,6,1024]{2,1,0:T(8,128)(2,1)S(1)} %get-tuple-element.29), channel_id=1, source_target_pairs={{0,64},{16,80},{32,96},{48,112},{64,0},{80,16},{96,32},{112,48},{1... | collective-permute-start | bytes 147464 | tf_op jit(solution)/shard_map/ppermute | solution.py:37
  148.7 5.2 %collective-permute-done.12 = bf16[4,6,1024]{2,1,0:T(8,128)(2,1)S(1)} collective-permute-done((bf16[4,6,1024]{2,1,0:T(8,128)(2,1)S(1)}, bf16[4,6,1024]{2,1,0:T(8,128)(2,1)S(1)}, u32[]{:S(2)}, u32[]{:S(2)}) %collective-permute-start.12) | collective-permute-done | bytes 49184 | tf_op jit(solution)/shard_map/ppermute | solution.py:37
  153.9 2.7 %collective-permute-start.13 = (bf16[2,6,1024]{2,1,0:T(8,128)(2,1)S(1)}, bf16[2,6,1024]{2,1,0:T(8,128)(2,1)S(1)}, u32[]{:S(2)}, u32[]{:S(2)}) collective-permute-start(bf16[2,6,1024]{2,1,0:T(8,128)(2,1)S(1)} %get-tuple-element.34), channel_id=1, source_target_pairs={{0,128},{16,144},{32,160},{48,176},{64,192},{80,208},{96,224},{112... | collective-permute-start | bytes 73736 | tf_op jit(solution)/shard_map/ppermute | solution.py:37
  156.6 3.1 %collective-permute-done.13 = bf16[2,6,1024]{2,1,0:T(8,128)(2,1)S(1)} collective-permute-done((bf16[2,6,1024]{2,1,0:T(8,128)(2,1)S(1)}, bf16[2,6,1024]{2,1,0:T(8,128)(2,1)S(1)}, u32[]{:S(2)}, u32[]{:S(2)}) %collective-permute-start.13) | collective-permute-done | bytes 24608 | tf_op jit(solution)/shard_map/ppermute | solution.py:37
  159.7 1.9 %collective-permute-start.14 = (bf16[1,6,1024]{2,1,0:T(8,128)(2,1)S(1)}, bf16[1,6,1024]{2,1,0:T(8,128)(2,1)S(1)}, u32[]{:S(2)}, u32[]{:S(2)}) collective-permute-start(bf16[1,6,1024]{2,1,0:T(8,128)(2,1)S(1)} %fusion.2), channel_id=1, source_target_pairs={{0,256},{16,272},{32,288},{48,304},{64,320},{80,336},{96,352},{112... | collective-permute-start | bytes 36872 | tf_op jit(solution)/shard_map/ppermute | solution.py:37
  161.7 6.0 %all-to-all-done.2.both_ref = bf16[16,256,128]{2,1,0:T(8,128)(2,1)S(1)} async-done(((bf16[16,256,128]{2,1,0:T(8,128)(2,1)}), bf16[16,256,128]{2,1,0:T(8,128)(2,1)S(1)}, u32[]{:S(2)}, u32[]{:S(2)}) %all-to-all-start.2) | async-done | bytes 1048608 | tf_op jit(solution)/shard_map/all_to_all | solution.py:233
  167.6 2.8 %copy-done = bf16[3072,1024]{1,0:T(8,128)(2,1)S(1)} copy-done((bf16[3072,1024]{1,0:T(8,128)(2,1)S(1)}, bf16[3072,1024]{1,0:T(8,128)(2,1)}, u32[]{:S(2)}) %copy-start) | copy-done | bytes 6291480
  170.4 1.9 %input_sum.1 = (bf16[128,1024]{1,0:T(8,128)(2,1)}, bf16[128,1024]{1,0:T(8,128)(2,1)}) custom-call(bf16[16,256,128]{2,1,0:T(8,128)(2,1)S(1)} %all-to-all-done.2.both_ref, bf16[3072,1024]{1,0:T(8,128)(2,1)S(1)} %copy-done), custom_call_target="tpu_custom_call" | custom-call | tf_op jit(solution)/shard_map/input_sum/pallas_call | solution.py:192
  172.3 0.6 copy.13
  (30 shorter events, 0.2 us)
Async XLA Ops:
  7.2 85.6 %copy-start.8 = (s32[1,16,4]{1,2,0:T(4,128)S(1)}, s32[1,16,4]{1,2,0:T(4,128)}, u32[]{:S(2)}) copy-start(s32[1,16,4]{1,2,0:T(4,128)} %param.7) | copy-start | bytes 772
  7.2 97.9 %copy-start.6 = (s32[1,16]{1,0:T(1,128)S(1)}, s32[1,16]{1,0:T(1,128)}, u32[]{:S(2)}) copy-start(s32[1,16]{1,0:T(1,128)} %param.8) | copy-start | bytes 196
  7.2 29.5 %collective-permute-start = (bf16[128,1024]{1,0:T(8,128)(2,1)}, bf16[128,1024]{1,0:T(8,128)(2,1)S(1)}, u32[]{:S(2)}, u32[]{:S(2)}) collective-permute-start(bf16[128,1024]{1,0:T(8,128)(2,1)} %bitcast.27), channel_id=1, source_target_pairs={{0,1},{1,0},{2,3},{3,2},{4,5},{5,4},{6,7},{7,6},{8,9},{9,8},{10,11... | collective-permute-start | bytes 786440 | tf_op jit(solution)/shard_map/ppermute | solution.py:29
  11.1 25.5 %collective-permute-start.1 = (bf16[128,1024]{1,0:T(8,128)(2,1)}, bf16[128,1024]{1,0:T(8,128)(2,1)S(1)}, u32[]{:S(2)}, u32[]{:S(2)}) collective-permute-start(bf16[128,1024]{1,0:T(8,128)(2,1)} %bitcast.28), channel_id=1, source_target_pairs={{0,2},{1,3},{2,4},{3,5},{4,6},{5,7},{6,8},{7,9},{8,10},{9,11},{10,... | collective-permute-start | bytes 786440 | tf_op jit(solution)/shard_map/ppermute | solution.py:33
  15.4 21.2 %collective-permute-start.2 = (bf16[128,1024]{1,0:T(8,128)(2,1)}, bf16[128,1024]{1,0:T(8,128)(2,1)S(1)}, u32[]{:S(2)}, u32[]{:S(2)}) collective-permute-start(bf16[128,1024]{1,0:T(8,128)(2,1)} %bitcast.29), channel_id=1, source_target_pairs={{0,14},{1,15},{2,0},{3,1},{4,2},{5,3},{6,4},{7,5},{8,6},{9,7},{10,... | collective-permute-start | bytes 786440 | tf_op jit(solution)/shard_map/ppermute | solution.py:33
  26.8 24.9 %all-to-all-start = ((bf16[16,112,128]{2,1,0:T(8,128)(2,1)}), bf16[16,112,128]{2,1,0:T(8,128)(2,1)S(1)}, u32[]{:S(2)}, u32[]{:S(2)}) async-start(bf16[16,112,128]{2,1,0:T(8,128)(2,1)} %pad_maximum_fusion.2), calls=%async_computation | async-start | bytes 917504 | tf_op jit(solution)/shard_map/all_to_all | solution.py:222
  36.6 123.1 %all-gather.2.cloned.1.call-start = ((), (), s32[]{:S(2)}) async-start(), calls=%async_computation.3 | async-start | bytes 6488064 | tf_op jit(solution)/shard_map/all_gather | solution.py:225
  37.6 22.5 %collective-permute-start.3 = (bf16[256,1024]{1,0:T(8,128)(2,1)}, bf16[256,1024]{1,0:T(8,128)(2,1)S(1)}, u32[]{:S(2)}, u32[]{:S(2)}) collective-permute-start(bf16[256,1024]{1,0:T(8,128)(2,1)} %get-tuple-element.32), channel_id=1, source_target_pairs={{0,2},{1,3},{2,4},{3,5},{4,6},{5,7},{6,8},{7,9},{8,10},{9,11},{10,... | collective-permute-start | bytes 1572872 | tf_op jit(solution)/shard_map/ppermute | solution.py:33
  41.0 19.1 %collective-permute-start.5 = (bf16[256,1024]{1,0:T(8,128)(2,1)S(1)}, bf16[256,1024]{1,0:T(8,128)(2,1)S(1)}, u32[]{:S(2)}, u32[]{:S(2)}) collective-permute-start(bf16[256,1024]{1,0:T(8,128)(2,1)S(1)} %get-tuple-element.31), channel_id=1, source_target_pairs={{0,14},{1,15},{2,0},{3,1},{4,2},{5,3},{6,4},{7,5},{8,6},{9,7},{10,... | collective-permute-start | bytes 1572872 | tf_op jit(solution)/shard_map/ppermute | solution.py:33
  60.1 32.8 %copy-start.2 = (bf16[256,1024]{1,0:T(8,128)(2,1)}, bf16[256,1024]{1,0:T(8,128)(2,1)S(1)}, u32[]{:S(2)}) copy-start(bf16[256,1024]{1,0:T(8,128)(2,1)S(1)} %collective-permute-done.5.refs_6_) | copy-start | bytes 1572868
  60.2 16.4 %collective-permute-start.4 = (bf16[256,1024]{1,0:T(8,128)(2,1)S(1)}, bf16[256,1024]{1,0:T(8,128)(2,1)S(1)}, u32[]{:S(2)}, u32[]{:S(2)}) collective-permute-start(bf16[256,1024]{1,0:T(8,128)(2,1)S(1)} %collective-permute-done.3.refs_4_), channel_id=1, source_target_pairs={{0,2},{1,3},{2,4},{3,5},{4,6},{5,7},{6,8},{7,9},{8,10},{9,11},{10,... | collective-permute-start | bytes 1572872 | tf_op jit(solution)/shard_map/ppermute | solution.py:33
  63.4 16.4 %collective-permute-start.6 = (bf16[256,1024]{1,0:T(8,128)(2,1)S(1)}, bf16[256,1024]{1,0:T(8,128)(2,1)S(1)}, u32[]{:S(2)}, u32[]{:S(2)}) collective-permute-start(bf16[256,1024]{1,0:T(8,128)(2,1)S(1)} %collective-permute-done.5.refs_6_), channel_id=1, source_target_pairs={{0,14},{1,15},{2,0},{3,1},{4,2},{5,3},{6,4},{7,5},{8,6},{9,7},{10,... | collective-permute-start | bytes 1572872 | tf_op jit(solution)/shard_map/ppermute | solution.py:33
  68.8 24.1 %all-to-all-start.1 = ((bf16[32,6,1024]{2,1,0:T(8,128)(2,1)}), bf16[32,6,1024]{2,1,0:T(8,128)(2,1)}, u32[]{:S(2)}, u32[]{:S(2)}) async-start(bf16[32,6,1024]{2,1,0:T(8,128)(2,1)} %broadcast_in_dim.25), calls=%async_computation.1 | async-start | bytes 1048576 | tf_op jit(solution)/shard_map/all_to_all | solution.py:42
  77.3 27.7 %collective-permute-start.7 = (bf16[192,1024]{1,0:T(8,128)(2,1)}, bf16[192,1024]{1,0:T(8,128)(2,1)}, u32[]{:S(2)}, u32[]{:S(2)}) collective-permute-start(bf16[192,1024]{1,0:T(8,128)(2,1)} %slice.76), channel_id=1, source_target_pairs={{0,2},{1,3},{2,4},{3,5},{4,6},{5,7},{6,8},{7,9},{8,10},{9,11},{10,... | collective-permute-start | bytes 1179656 | tf_op jit(solution)/shard_map/ppermute | solution.py:33
  80.6 24.4 %collective-permute-start.8 = (bf16[192,1024]{1,0:T(8,128)(2,1)}, bf16[192,1024]{1,0:T(8,128)(2,1)}, u32[]{:S(2)}, u32[]{:S(2)}) collective-permute-start(bf16[192,1024]{1,0:T(8,128)(2,1)} %slice.77), channel_id=1, source_target_pairs={{0,14},{1,15},{2,0},{3,1},{4,2},{5,3},{6,4},{7,5},{8,6},{9,7},{10,... | collective-permute-start | bytes 1179656 | tf_op jit(solution)/shard_map/ppermute | solution.py:33
  85.1 19.9 %collective-permute-start.9 = (bf16[128,1024]{1,0:T(8,128)(2,1)S(1)}, bf16[128,1024]{1,0:T(8,128)(2,1)}, u32[]{:S(2)}, u32[]{:S(2)}) collective-permute-start(bf16[128,1024]{1,0:T(8,128)(2,1)S(1)} %collective-permute-done.refs_1_), channel_id=1, source_target_pairs={{0,8},{1,9},{2,10},{3,11},{4,12},{5,13},{6,14},{7,15},{8,0},{9,1},... | collective-permute-start | bytes 786440 | tf_op jit(solution)/shard_map/ppermute | solution.py:33
  105.0 1.1 copy-start.3
  106.1 1.0 copy-start.5
  119.0 1.0 copy-start.1
  119.9 0.8 copy-start.4
  120.8 0.7 copy-start.7
  121.5 46.2 %all-to-all-start.2 = ((bf16[16,256,128]{2,1,0:T(8,128)(2,1)}), bf16[16,256,128]{2,1,0:T(8,128)(2,1)S(1)}, u32[]{:S(2)}, u32[]{:S(2)}) async-start(bf16[16,256,128]{2,1,0:T(8,128)(2,1)} %copy-done.1), calls=%async_computation.2 | async-start | bytes 2097152 | tf_op jit(solution)/shard_map/all_to_all | solution.py:233
  134.0 3.6 %collective-permute-start.10 = (bf16[16,6,1024]{2,1,0:T(8,128)(2,1)}, bf16[16,6,1024]{2,1,0:T(8,128)(2,1)S(1)}, u32[]{:S(2)}, u32[]{:S(2)}) collective-permute-start(bf16[16,6,1024]{2,1,0:T(8,128)(2,1)} %copy-done.7), channel_id=1, source_target_pairs={{0,16},{16,0},{32,48},{48,32},{64,80},{80,64},{96,112},{112,96},{1... | collective-permute-start | bytes 589832 | tf_op jit(solution)/shard_map/ppermute | solution.py:37
  138.8 7.4 %collective-permute-start.11 = (bf16[8,6,1024]{2,1,0:T(8,128)(2,1)S(1)}, bf16[8,6,1024]{2,1,0:T(8,128)(2,1)S(1)}, u32[]{:S(2)}, u32[]{:S(2)}) collective-permute-start(bf16[8,6,1024]{2,1,0:T(8,128)(2,1)S(1)} %get-tuple-element.27), channel_id=1, source_target_pairs={{0,32},{16,48},{32,0},{48,16},{64,96},{80,112},{96,64},{112,80},{1... | collective-permute-start | bytes 294920 | tf_op jit(solution)/shard_map/ppermute | solution.py:37
  146.2 7.7 %collective-permute-start.12 = (bf16[4,6,1024]{2,1,0:T(8,128)(2,1)S(1)}, bf16[4,6,1024]{2,1,0:T(8,128)(2,1)S(1)}, u32[]{:S(2)}, u32[]{:S(2)}) collective-permute-start(bf16[4,6,1024]{2,1,0:T(8,128)(2,1)S(1)} %get-tuple-element.29), channel_id=1, source_target_pairs={{0,64},{16,80},{32,96},{48,112},{64,0},{80,16},{96,32},{112,48},{1... | collective-permute-start | bytes 147464 | tf_op jit(solution)/shard_map/ppermute | solution.py:37
  153.9 5.8 %collective-permute-start.13 = (bf16[2,6,1024]{2,1,0:T(8,128)(2,1)S(1)}, bf16[2,6,1024]{2,1,0:T(8,128)(2,1)S(1)}, u32[]{:S(2)}, u32[]{:S(2)}) collective-permute-start(bf16[2,6,1024]{2,1,0:T(8,128)(2,1)S(1)} %get-tuple-element.34), channel_id=1, source_target_pairs={{0,128},{16,144},{32,160},{48,176},{64,192},{80,208},{96,224},{112... | collective-permute-start | bytes 73736 | tf_op jit(solution)/shard_map/ppermute | solution.py:37
  159.7 12.5 %collective-permute-start.14 = (bf16[1,6,1024]{2,1,0:T(8,128)(2,1)S(1)}, bf16[1,6,1024]{2,1,0:T(8,128)(2,1)S(1)}, u32[]{:S(2)}, u32[]{:S(2)}) collective-permute-start(bf16[1,6,1024]{2,1,0:T(8,128)(2,1)S(1)} %fusion.2), channel_id=1, source_target_pairs={{0,256},{16,272},{32,288},{48,304},{64,320},{80,336},{96,352},{112... | collective-permute-start | bytes 36872 | tf_op jit(solution)/shard_map/ppermute | solution.py:37
  167.6 2.8 %copy-start = (bf16[3072,1024]{1,0:T(8,128)(2,1)S(1)}, bf16[3072,1024]{1,0:T(8,128)(2,1)}, u32[]{:S(2)}) copy-start(bf16[3072,1024]{1,0:T(8,128)(2,1)} %all-gather.2.cloned.1.call-done.w_ref) | copy-start | bytes 18874372
Sparse Core Ops, SparseCore 0:
  60.3 73.2 all-gather.1
